TPU v7x, 32 devices: a whole 2x2x4 slice. The times are simulated.
32 devices in a mesh: pool: 8 (over y, x, core), fft: 4 (over z).
Axes of the slice: x: 2, y: 2, z: 4, core: 2. Of those that a mesh axis runs over, the one named last changes fastest.
Arguments:
- orbitals: bfloat16 [2, 8, 64, 8192], P(None, 'pool', None, 'fft'), may hold values from -12 to 12
- box_index: int32 [8192], P('fft'), may hold values from 0 to 262143, as said below
- partner_pool: int32 [8], replicated, may hold values from 0 to 7, each once
- potential: float32 [64, 64, 128], replicated, may hold values from -9 to 9
Outputs:
- response: bfloat16 [2, 8, 64, 8192], P(None, 'pool', None, 'fft')
- coupling: float32 [2, 8, 64, 64], P(None, 'pool')
Inputs may be any that keep to these rules, and one draw needn't show every extreme that they name: `box_index`: entries are distinct. The 2048 entries of index d of fft lie on exactly 64 columns x * 64 + y of the box (a column is the 64 points of one x and y), and no column holds entries of two indices of fft. `partner_pool`: A permutation of the k-points.
All inputs are finite; a program needn't handle non-finite values.
Results may differ from a plain program's by a relative error of at most 0.02.
Values may be sent and summed in bfloat16 or wider, within the bound.
No kernel may reach another device: no remote copies, remote signals or barrier semaphores. Data moves between devices by JAX's collectives and lax.ppermute only.
A program may use at most 192 MiB of HBM per device.

v0:
```python
import jax
import jax.numpy as jnp
from jax import lax
from jax.sharding import PartitionSpec as P

STICK_DEV = 64


def tables(side, signum):
    points = jnp.arange(side, dtype=jnp.int32)
    products = points[:, None] * points[None, :] % side
    angles = 2.0 * jnp.pi / side * products.astype(jnp.float32)
    scaling = 1.0 / jnp.sqrt(jnp.float32(side))
    cosine = jnp.cos(angles) * scaling
    sines = jnp.sin(angles) * scaling
    rows_real = jnp.stack([cosine, -signum * sines], axis=1)
    rows_imag = jnp.stack([signum * sines, cosine], axis=1)
    return jnp.stack([rows_real, rows_imag], axis=0).astype(jnp.bfloat16)


def along_last(rows, weights):
    side = weights.shape[1]
    square = weights.reshape(2 * side, 2 * side)
    result = jnp.einsum("nkc,dc->nkd", rows, square, preferred_element_type=jnp.float32)
    return result.astype(jnp.bfloat16)


def modulate(grid, potential):
    side = potential.shape[0]
    field = potential.reshape(side, side, 2, side)
    lifted = grid.astype(jnp.float32)
    real_part = (
        field[None, :, :, 0] * lifted[:, :, :, 0] - field[None, :, :, 1] * lifted[:, :, :, 1]
    )
    imag_part = (
        field[None, :, :, 0] * lifted[:, :, :, 1] + field[None, :, :, 1] * lifted[:, :, :, 0]
    )
    return jnp.stack([real_part, imag_part], axis=3).astype(jnp.bfloat16)


def planes_work(sticks, stick_ids, potential, inverse_w, forward_w):
    bands = sticks.shape[0]
    side = potential.shape[0]
    flat_side = side * side
    grid = jnp.zeros((bands, flat_side, 2 * side), jnp.bfloat16).at[:, stick_ids].set(sticks)
    grid = grid.reshape(bands, side, side, 2, side)
    grid = jnp.einsum(
        "nxbsz,tasb->nxzta", grid, inverse_w, preferred_element_type=jnp.float32
    ).astype(jnp.bfloat16)
    grid = jnp.einsum(
        "nbzsy,tasb->nzyta", grid, inverse_w, preferred_element_type=jnp.float32
    ).astype(jnp.bfloat16)
    grid = modulate(grid, potential)
    grid = jnp.einsum(
        "nzysb,tasb->nzaty", grid, forward_w, preferred_element_type=jnp.float32
    ).astype(jnp.bfloat16)
    grid = jnp.einsum(
        "nzxsb,tasb->nxatz", grid, forward_w, preferred_element_type=jnp.float32
    ).astype(jnp.bfloat16)
    return grid.reshape(bands, flat_side, 2 * side)[:, stick_ids]


def stick_layout(table, side, count):
    column_of = table // side
    depth_of = table % side
    occupied = jnp.zeros((side * side,), jnp.int32).at[column_of].set(1)
    stick_ids = jnp.nonzero(occupied, size=count)[0].astype(jnp.int32)
    slot_table = jnp.cumsum(occupied) - 1
    base = slot_table[column_of] * (2 * side) + depth_of
    spots = jnp.concatenate([base, base + side])
    return (stick_ids, spots)


def to_sticks(coeffs, spots, count, side):
    bands = coeffs.shape[1]
    values = jnp.moveaxis(coeffs, 0, 1).reshape(bands, -1)
    filled = jnp.zeros((bands, count * 2 * side), jnp.bfloat16).at[:, spots].set(values)
    return filled.reshape(bands, count, 2 * side)


def from_sticks(sticks, spots):
    bands = sticks.shape[0]
    picked = sticks.reshape(bands, -1)[:, spots].reshape(bands, 2, -1)
    return jnp.moveaxis(picked, 0, 1)


def shards(orbitals, box_index, partner_pool, potential):
    fft_count = lax.axis_size("fft")
    coeffs = orbitals[:, 0]
    wave_count = coeffs.shape[2]
    box_side = potential.shape[0]
    inverse_w = tables(box_side, 1.0)
    forward_w = tables(box_side, -1.0)
    local_ids, spots = stick_layout(box_index, box_side, STICK_DEV)
    sticks = to_sticks(coeffs, spots, STICK_DEV, box_side)
    sticks = along_last(sticks, inverse_w)
    all_ids = lax.all_gather(local_ids, "fft", axis=0, tiled=True)
    whole = lax.all_to_all(sticks, "fft", split_axis=0, concat_axis=1, tiled=True)
    whole = planes_work(whole, all_ids, potential, inverse_w, forward_w)
    returned = lax.all_to_all(whole, "fft", split_axis=1, concat_axis=0, tiled=True)
    returned = along_last(returned, forward_w)
    response_rows = from_sticks(returned, spots)
    target = partner_pool[lax.axis_index("pool")]
    piece = lax.all_gather(orbitals, "pool", axis=1, tiled=True)
    source_rows = jnp.arange(piece.shape[1], dtype=jnp.int32)
    matches = (source_rows == target)[None, :, None, None]
    partner = jnp.sum(jnp.where(matches, piece, jnp.zeros_like(piece)), axis=1, keepdims=True)
    partner_rows = partner[:, 0]
    rotated = jnp.stack([response_rows[1], -response_rows[0]])
    real_part = jnp.einsum(
        "smp,snp->mn", partner_rows, response_rows, preferred_element_type=jnp.float32
    )
    imag_part = jnp.einsum("smp,snp->mn", partner_rows, rotated, preferred_element_type=jnp.float32)
    summed = lax.psum(jnp.stack([real_part, imag_part]).astype(jnp.bfloat16), "fft").astype(
        jnp.float32
    )
    coupling = (summed / jnp.sqrt(jnp.float32(wave_count * fft_count)))[:, None]
    return (response_rows[:, None], coupling)


def solution(mesh):
    placed = (P(None, "pool", None, "fft"), P("fft"), P(), P())
    return jax.shard_map(
        shards,
        mesh=mesh,
        in_specs=placed,
        out_specs=(P(None, "pool", None, "fft"), P(None, "pool", None, None)),
        check_vma=False,
    )
```

profile of v0, /device:TPU:0, one launch (start us, length us, event | category | flops | bytes accessed | tf_op | source)
XLA Modules:
  0.0 616.3 jit_solution(12357785768839009647)
XLA Ops:
  7.2 0.7 all-gather.2.cloned.1.call-update
  7.9 0.1 multiply_convert_fusion
  8.1 0.1 multiply_convert_fusion.1
  8.2 0.1 multiply_convert_fusion.2
  8.4 0.7 broadcast_clamp_fusion.1
  9.1 8.1 %scatter_custom_fusion = s32[4096]{0:T(1024)S(1)} fusion(s32[2048]{0:T(1024)S(1)} %get-tuple-element.9, s32[2048]{0:T(1024)S(1)} %ne.95, s32[]{:T(128)} %constant.94.clone.1), kind=kCustom, calls=%fused_computation.85 | custom fusion | bytes 16388 | tf_op jit(solution)/shard_map/scatter | solution.py:66
  17.2 0.3 reduce-window.34
  17.4 0.1 slice.55
  17.5 0.1 reduce-window.35
  17.6 0.1 slice_reduce_fusion
  17.7 0.1 add_bitcast_fusion
  17.8 11.8 %gather_fusion = s32[2048]{0:T(1024)S(1)} fusion(s32[4096]{0:T(1024)S(1)} %add_bitcast_fusion, s32[2048]{0:T(1024)S(1)} %get-tuple-element.8), kind=kCustom, calls=%fused_computation | custom fusion | bytes 24576 | tf_op jit(solution)/shard_map/gather | solution.py:69
  29.6 0.7 broadcast_add_fusion.1
  30.3 1.1 copy.51
  31.3 0.5 copy.18
  31.9 11.6 %scatter_custom_fusion.2 = bf16[64,8192]{0,1:T(8,128)(2,1)S(1)} fusion(s32[4096]{0:T(1024)S(1)} %bitcast.205, bf16[4096,64]{1,0:T(8,128)(2,1)S(1)} %copy.18, bf16[]{:T(256)} %constant.100.clone.1), kind=kCustom, calls=%fused_computation.33 | custom fusion | bytes 1048578 | tf_op jit(solution)/shard_map/scatter | solution.py:77
  43.4 1.7 copy.20
  45.2 0.7 pad_maximum_fusion
  45.8 0.1 copy.19
  45.9 0.1 reshape.376
  46.0 1.4 convolution_convert_fusion.1
  47.4 6.3 %all-to-all-start = ((bf16[64,64,128]{2,1,0:T(8,128)(2,1)}), bf16[64,64,128]{2,1,0:T(8,128)(2,1)S(1)}, u32[]{:S(2)}, u32[]{:S(2)}) async-start(bf16[64,64,128]{2,1,0:T(8,128)(2,1)} %convolution_convert_fusion.1), calls=%async_computation | async-start | bytes 2097152 | tf_op jit(solution)/shard_map/all_to_all | solution.py:98
  53.7 0.7 convert_reduce_fusion
  54.4 0.3 reduce-window.31
  54.7 0.1 slice.53
  54.8 0.1 slice_reduce_fusion.1
  54.9 0.1 broadcast_add_fusion
  55.1 28.8 %scatter_custom_fusion.1 = s32[64]{0:T(128)S(1)} fusion(s32[4096]{0:T(1024)S(1)} %bitcast.210, s32[4096]{0:T(1024)S(1)} %broadcast.247, s32[]{:T(128)} %constant.94.clone.1), kind=kCustom, calls=%fused_computation.100 | custom fusion | flops 4096 | bytes 260 | tf_op jit(solution)/shard_map/scatter-add | solution.py:67
  83.8 0.1 copy.16
  83.9 0.1 reduce-window.33
  84.0 0.1 reduce.2
  84.1 5.6 reshape.298
  89.8 0.6 dynamic-slice
  91.1 0.7 fusion.47
  91.8 8.8 %all-reduce = s32[256]{0:T(256)S(1)} all-reduce(s32[256]{0:T(256)S(1)} %fusion.47), channel_id=1, replica_groups=mesh['pool'=8,'fft'=4] {'fft'}, use_global_device_ids=true, to_apply=%add | all-reduce | flops 256 | bytes 2048
  100.6 0.6 pad_clamp_fusion
  101.2 9.2 %fusion.56 = (f32[64,64,1,64]{3,2,1,0:T(1,128)S(1)}, f32[64,64,1,64]{3,2,1,0:T(1,128)}) fusion(f32[64,64,2,64]{3,2,1,0:T(2,128)} %reshape.298), kind=kLoop, calls=%fused_computation.105 | loop fusion | bytes 4194304 | tf_op jit(solution)/shard_map/slice | solution.py:33
  110.3 1.7 copy.21
  112.0 6.0 broadcast_in_dim.26
  118.0 24.0 %scatter_fusion = bf16[16,4096,128]{2,0,1:T(8,128)(2,1)} fusion(bf16[16,4096,128]{2,0,1:T(8,128)(2,1)} %broadcast_in_dim.26, s32[256]{0:T(256)S(1)} %compare_select_fusion.3, bf16[256,16,128]{2,1,0:T(8,128)(2,1)S(1)} %bitcast.199), kind=kCustom, calls=%fused_computation.6 | custom fusion | bytes 3146752 | tf_op jit(solution)/shard_map/scatter | solution.py:45
  142.0 54.1 %reshape.377 = bf16[16,64,64,2,64,1]{4,3,0,2,1,5:T(2,128)(2,1)} reshape(bf16[16,4096,128]{2,0,1:T(8,128)(2,1)} %scatter_fusion) | data formatting | bytes 33554432 | tf_op jit(solution)/shard_map/reshape | solution.py:46
  196.1 87.3 %copy.33 = bf16[16,64,64,2,64,1]{2,1,3,5,4,0:T(8,128)(2,1)} copy(bf16[16,64,64,2,64,1]{4,3,0,2,1,5:T(2,128)(2,1)} %reshape.377) | data formatting | bytes 33554432 | tf_op jit(solution)/shard_map/reshape | solution.py:46
  283.5 39.9 %fusion.3 = f32[16,64,64,2,64]{4,2,3,1,0:T(8,128)} fusion(bf16[16,64,64,2,64,1]{2,1,3,5,4,0:T(8,128)(2,1)} %copy.33, bf16[1,64,2,64]{3,1,2,0:T(8,128)(2,1)S(1)} %get-tuple-element.19, bf16[1,64,2,64]{3,1,2,0:T(8,128)(2,1)S(1)} %get-tuple-element.22), kind=kOutput, calls=%fused_computation.13 | convolution fusion | flops 4320264192 | bytes 50364416 | tf_op jit(solution)/shard_map/nbzsy,tasb->nzyta/dot_general | solution.py:50
  323.3 33.1 %subtract_convert_fusion = (bf16[16,64,64,1,64]{4,2,3,1,0:T(8,128)(2,1)}, bf16[16,64,64,1,64]{4,2,3,1,0:T(8,128)(2,1)}) fusion(f32[16,64,64,2,64]{4,2,3,1,0:T(8,128)} %fusion.3, f32[64,64,64]{2,1,0:T(8,128)} %bitcast.194, f32[64,64,64]{2,1,0:T(8,128)S(1)} %bitcast.193), kind=kLoop, calls=%fused_computation.22 | loop fusion | flops 33554432 | bytes 52428800 | tf_op jit(solution)/shard_map/convert.5
  356.4 38.6 %fusion.7 = bf16[16,64,64,2,64]{1,2,4,0,3:T(8,128)(2,1)} fusion(bf16[16,64,64,1,64]{4,2,3,1,0:T(8,128)(2,1)} %get-tuple-element.13, bf16[16,64,64,1,64]{4,2,3,1,0:T(8,128)(2,1)} %get-tuple-element.12, bf16[1,64,2,64]{3,1,2,0:T(8,128)(2,1)S(1)} %get-tuple-element.23, bf16[1,64,2,64]{3,1,2,0:T(8,128)(2,1)S(1)} %get-tuple-element.18), kind=kOutput, calls=%fused_computation.16 | convolution fusion | flops 4345430016 | bytes 33587200 | tf_op jit(solution)/shard_map/nzxsb,tasb->nxatz/dot_general | solution.py:57
  395.1 90.8 %copy.43 = bf16[16,64,64,2,64]{4,3,0,2,1:T(2,128)(2,1)} copy(bf16[16,64,64,2,64]{1,2,4,0,3:T(8,128)(2,1)} %fusion.7) | data formatting | bytes 33554432 | tf_op jit(solution)/shard_map/reshape | solution.py:60
  485.9 52.5 %reshape.392 = bf16[16,4096,128]{2,0,1:T(8,128)(2,1)} reshape(bf16[16,64,64,2,64]{4,3,0,2,1:T(2,128)(2,1)} %copy.43) | data formatting | bytes 33554432 | tf_op jit(solution)/shard_map/reshape | solution.py:60
  538.4 7.7 %gather_fusion.1 = bf16[256,16,128]{2,1,0:T(8,128)(2,1)} fusion(bf16[16,4096,128]{2,0,1:T(8,128)(2,1)} %reshape.392, s32[1024]{0:T(1024)} %pad_clamp_fusion), kind=kCustom, calls=%fused_computation.1 | custom fusion | bytes 2098176 | tf_op jit(solution)/shard_map/gather | solution.py:60
  546.1 3.5 all-to-all-start.1
  549.6 0.1 copy.27
  549.7 0.1 reshape.387
  549.8 0.6 dynamic_slice.3
  550.4 0.6 iota_compare_fusion
  551.1 21.9 %all-to-all-done.1 = bf16[16,256,128]{2,0,1:T(8,128)(2,1)S(1)} async-done(((bf16[16,256,128]{2,0,1:T(8,128)(2,1)}), bf16[16,256,128]{2,0,1:T(8,128)(2,1)S(1)}, u32[]{:S(2)}, u32[]{:S(2)}) %all-to-all-start.1) | async-done | bytes 1048608 | tf_op jit(solution)/shard_map/all_to_all | solution.py:100
  573.0 0.3 copy.26
  573.3 0.4 convolution_convert_fusion
  573.7 1.5 copy.45
  575.2 12.1 %gather_fusion.2 = bf16[4096,64]{1,0:T(8,128)(2,1)S(1)} fusion(bf16[64,8192]{0,1:T(8,128)(2,1)S(1)} %bitcast.191, s32[4096]{0:T(1024)S(1)} %broadcast_clamp_fusion), kind=kCustom, calls=%fused_computation.2 | custom fusion | bytes 1064960 | tf_op jit(solution)/shard_map/gather | solution.py:83
  587.3 0.3 copy.30
  587.7 3.3 select_reduce_fusion
  591.1 0.3 fusion.20
  591.4 0.3 fusion.19
  591.7 17.1 %psum.7 = bf16[2,64,64]{2,1,0:T(8,128)(2,1)S(1)} all-reduce(bf16[2,64,64]{2,1,0:T(8,128)(2,1)S(1)} %pad_maximum_fusion.6), channel_id=1, replica_groups=mesh['pool'=8,'fft'=4] {'fft'}, use_global_device_ids=true, to_apply=%region_11.12 | all-reduce | flops 8192 | bytes 32768 | tf_op jit(solution)/shard_map/psum | solution.py:114
  608.8 0.6 multiply_bitcast_fusion
  (29 shorter events, 0.3 us)
Async XLA Ops:
  7.2 82.6 %copy-start.6 = (u32[32]{0:T(128)S(1)}, u32[32]{0:T(128)}, u32[]{:S(2)}) copy-start(u32[32]{0:T(128)} %constant.115) | copy-start | bytes 388
  7.2 580.5 %all-gather.2.cloned.1.call-start = ((), (), s32[]{:S(2)}) async-start(), calls=%async_computation.2 | async-start | bytes 4718592 | tf_op jit(solution)/shard_map/all_gather | solution.py:104
  31.9 11.6 %copy-start.3 = (s32[4096,1]{0,1:T(1,128)}, s32[4096,1]{0,1:T(1,128)S(1)}, u32[]{:S(2)}) copy-start(s32[4096,1]{0,1:T(1,128)S(1)} %compare_select_fusion) | copy-start | bytes 49156
  47.4 62.9 %all-to-all-start = ((bf16[64,64,128]{2,1,0:T(8,128)(2,1)}), bf16[64,64,128]{2,1,0:T(8,128)(2,1)S(1)}, u32[]{:S(2)}, u32[]{:S(2)}) async-start(bf16[64,64,128]{2,1,0:T(8,128)(2,1)} %convolution_convert_fusion.1), calls=%async_computation | async-start | bytes 2097152 | tf_op jit(solution)/shard_map/all_to_all | solution.py:98
  112.0 6.0 copy-start.1
  485.9 63.7 %copy-start.2 = (bf16[2,64,2,64]{3,1,2,0:T(8,128)(2,1)S(1)}, bf16[2,64,2,64]{3,1,2,0:T(8,128)(2,1)}, u32[]{:S(2)}) copy-start(bf16[2,64,2,64]{3,1,2,0:T(8,128)(2,1)} %get-tuple-element.24) | copy-start | bytes 98308
  485.9 63.9 %copy-start.5 = (s32[8]{0:T(128)S(1)}, s32[8]{0:T(128)}, u32[]{:S(2)}) copy-start(s32[8]{0:T(128)} %param.6) | copy-start | bytes 100
  485.9 65.1 %copy-start.4 = (s32[4096,1]{0,1:T(1,128)S(1)}, s32[4096,1]{0,1:T(1,128)}, u32[]{:S(2)}) copy-start(s32[4096,1]{0,1:T(1,128)} %copy-done.3) | copy-start | bytes 49156
  546.1 26.9 %all-to-all-start.1 = ((bf16[16,256,128]{2,0,1:T(8,128)(2,1)}), bf16[16,256,128]{2,0,1:T(8,128)(2,1)S(1)}, u32[]{:S(2)}, u32[]{:S(2)}) async-start(bf16[16,256,128]{2,0,1:T(8,128)(2,1)} %bitcast.44), calls=%async_computation.1 | async-start | bytes 2097152 | tf_op jit(solution)/shard_map/all_to_all | solution.py:100
  587.6 21.8 %copy-start = (bf16[64,2,2048]{2,0,1:T(8,128)(2,1)}, bf16[64,2,2048]{2,0,1:T(8,128)(2,1)S(1)}, u32[]{:S(2)}) copy-start(bf16[64,2,2048]{2,0,1:T(8,128)(2,1)S(1)} %copy.30) | copy-start | bytes 1572868
Sparse Core Ops, SparseCore 0:
  9.9 39.4 all-gather.1
where the time goes:
time: 625 us; the launch traced here: 616 us
  local copies, waits for them, and re-layouts  390 us (62%)
  matrix products  80.9 us (13%)
  other arithmetic  72.2 us (12%)
  blocking collectives  25.9 us (4%)
  waiting for transfers between devices  22.6 us (4%)
  between operations  15 us (2%)
  starting transfers between devices  9.88 us (2%)
    reshape x2, local copies, waits for them, and re-layouts, planes_work(): return grid.reshape(bands, flat_side, 2 * side)[:, stick_ids]  143 us
    reshape x2, local copies, waits for them, and re-layouts, planes_work(): grid = grid.reshape(bands, side, side, 2, side)  141 us
    dot_general x1, matrix products, planes_work(): jnp.einsum('nbzsy,tasb->nzyta', grid, inverse_w, preferred_element_type=j...  39.9 us
    dot_general x1, matrix products, planes_work(): jnp.einsum('nzxsb,tasb->nxatz', grid, forward_w, preferred_element_type=j...  38.6 us
    another operation x11, other arithmetic  34.5 us
    scatter-add x1, other arithmetic, stick_layout(): stick_ids = jnp.nonzero(occupied, size=count)[0].astype(jnp.int32)  28.8 us
    scatter x1, local copies, waits for them, and re-layouts, planes_work(): jnp.zeros((bands, flat_side, 2 * side), jnp.bfloat16).at[:, stick_ids]  24 us
    all_to_all x1, waiting for transfers between devices, shards(): lax.all_to_all(whole, 'fft', split_axis=1, concat_axis=0, tiled=True)  21.9 us
  transfers between devices with their start and end apart: 3, of which 1 were waited for; matrix products, arithmetic and copies ran while one was open for 87% of the time, Pallas kernels for 0%

commit v1 on v0

v1 whole, which is shorter than its diff:
```python
import functools

import jax
import jax.numpy as jnp
import ml_dtypes
import numpy as np
from jax import lax
from jax.experimental import pallas as pl
from jax.experimental.pallas import tpu as pltpu
from jax.sharding import PartitionSpec as P

STICK_DEV = 64
LANES = 128
BF16 = jnp.bfloat16
F32 = jnp.float32
VMEM_LIMIT = 48 * 1024 * 1024


def cos_sin(side):
    points = np.arange(side)
    angles = (2.0 * np.pi / side) * (points[:, None] * points[None, :] % side)
    scaling = 1.0 / np.sqrt(side)
    cosine = (np.cos(angles) * scaling).astype(ml_dtypes.bfloat16)
    sine = (np.sin(angles) * scaling).astype(ml_dtypes.bfloat16)
    return cosine, sine


def dot(a, b):
    return jnp.dot(a, b, preferred_element_type=F32)


def dot_nt(a, b):
    return lax.dot_general(a, b, (((1,), (1,)), ((), ())), preferred_element_type=F32)


def one_hot(row, count):
    places = lax.broadcasted_iota(jnp.int32, (count, row.shape[1]), 0)
    return jnp.where(places == row, 1.0, 0.0).astype(BF16)


def triangles(side):
    rows = lax.broadcasted_iota(jnp.int32, (side, side), 0)
    cols = lax.broadcasted_iota(jnp.int32, (side, side), 1)
    upper = jnp.where(rows < cols, 1.0, 0.0).astype(BF16)
    lower = jnp.where(rows > cols, 1.0, 0.0).astype(BF16)
    return upper, lower, jnp.ones((side, side), BF16)


def prefix(occupied, tri):
    upper, lower, ones = tri
    in_rows = dot(occupied, ones).astype(BF16)
    return dot(occupied, upper) + dot(lower, in_rows)


def locate(idx, side):
    bits = side.bit_length() - 1
    tri = triangles(side)
    xh = one_hot(idx >> (2 * bits), side)
    yh = one_hot((idx >> bits) & (side - 1), side)
    zh = one_hot(idx & (side - 1), side)
    columns = jnp.minimum(dot_nt(xh, yh), 1.0).astype(BF16)
    slots = prefix(columns, tri).astype(BF16)
    slot = jnp.sum(xh.astype(F32) * dot(slots, yh), axis=0, keepdims=True)
    ch = one_hot(slot.astype(jnp.int32), STICK_DEV)
    cells = dot_nt(zh, ch)
    ranks = prefix(cells.astype(BF16), tri)
    high = jnp.floor(ranks * (1.0 / side))
    low = ranks - high * side
    looked = dot(high.astype(BF16), ch) * side + dot(low.astype(BF16), ch)
    rank = jnp.sum(zh.astype(F32) * looked, axis=0, keepdims=True)
    return xh, yh, zh, ch, slot, cells, ranks, rank.astype(jnp.int32)


def sort_kernel(side, groups, idx_ref, x_ref, out_ref, rank_ref):
    rank = locate(idx_ref[...], side)[-1]
    rank_ref[...] = rank
    waves = rank.shape[1]
    rows = x_ref.shape[0]
    bands = rows // 2
    share = bands // groups
    low = one_hot(rank & 255, 256)
    for part in range(waves // 256):
        mask = jnp.where((rank >> 8) == part, 1.0, 0.0).astype(BF16)
        piece = dot_nt(x_ref[...] * mask, low)
        for q in range(groups):
            re = piece[q * share : (q + 1) * share]
            im = piece[bands + q * share : bands + (q + 1) * share]
            both = jnp.concatenate([re, im], axis=0).astype(BF16)
            out_ref[q, :, part * 256 : (part + 1) * 256] = both


def prep_kernel(
    side, chunks, idx_ref, pot_ref, cs_ref, cyr_ref, syr_ref,
    tab_ref, field_ref, spot_ref, col_ref, dep_ref,
):
    groups = idx_ref.shape[0]
    waves = idx_ref.shape[1]
    tiles = waves // LANES
    half = side // 2
    for d in range(groups):
        xh, yh, zh, ch, slot, cells, ranks, rank = locate(idx_ref[d : d + 1, :], side)
        at_x = jnp.minimum(dot_nt(ch, xh), 1.0).astype(BF16)
        at_y = jnp.minimum(dot_nt(ch, yh), 1.0).astype(BF16)
        both = dot(at_x, cs_ref[...])
        cx, sx = both[:, :LANES], both[:, LANES:]
        rows = slice(d * STICK_DEV, (d + 1) * STICK_DEV)
        for k in range(chunks):
            cy = dot(at_y, cyr_ref[:, k * LANES : (k + 1) * LANES])
            sy = dot(at_y, syr_ref[:, k * LANES : (k + 1) * LANES])
            base = 2 * k * LANES
            tab_ref[rows, base : base + LANES] = (cy * cx - sy * sx).astype(BF16)
            tab_ref[rows, base + LANES : base + 2 * LANES] = (cy * sx + sy * cx).astype(BF16)
        spot = ranks.astype(jnp.int32)
        spot_ref[d] = jnp.where(cells > 0.5, spot, spot - 4096)
        low = one_hot(rank & (LANES - 1), LANES)
        high = one_hot(rank >> 7, tiles)
        col = dot_nt(high * slot.astype(BF16), low).astype(jnp.int32)
        depth = jnp.sum(
            zh.astype(F32) * lax.broadcasted_iota(jnp.int32, zh.shape, 0).astype(F32),
            axis=0, keepdims=True,
        )
        dep = dot_nt(high * depth.astype(BF16), low).astype(jnp.int32)
        col_ref[d * tiles : (d + 1) * tiles, :] = col + (d % 2) * STICK_DEV
        dep_ref[d * tiles : (d + 1) * tiles, :] = dep
    lane = lax.broadcasted_iota(jnp.int32, (side, LANES), 1)
    first = lane < side
    flipped = (lane & side) + ((side - (lane & (side - 1))) & (side - 1))

    def pair(row_a, row_b):
        p = jnp.where(first, row_a, pltpu.roll(row_b, side, 1))
        q = jnp.where(first, pltpu.roll(row_a, side, 1), row_b)
        return p, q

    def plane(y):
        return pot_ref[pl.ds(y, side, stride=side), :]

    def mirror(y):
        if y == 0 or y >= half:
            return jnp.zeros((side, LANES), F32)
        return jnp.take_along_axis(plane(side - y), flipped, axis=1)

    zero = jnp.zeros((side, LANES), F32)
    for k in range(chunks):
        ya, yb = 2 * k, 2 * k + 1
        p, q = pair(plane(ya), plane(yb) if yb <= half else zero)
        field_ref[0, :, k * LANES : (k + 1) * LANES] = p
        field_ref[1, :, k * LANES : (k + 1) * LANES] = q
        p, q = pair(mirror(ya), mirror(yb))
        field_ref[2, :, k * LANES : (k + 1) * LANES] = p
        field_ref[3, :, k * LANES : (k + 1) * LANES] = q


def box_kernel(
    side, chunks, team, x_ref, tab_ref, field_ref, spot_ref, col_ref, dep_ref, start_s, dep_s,
    wz_ref, out_ref, xf, grid, t_scr, l_scr,
):
    groups, rows, waves = x_ref.shape
    bands = rows // 2
    tiles = waves // LANES
    blocks = rows // 8
    span = 2 * side
    xf[...] = x_ref[...].astype(F32)
    upper_half = lax.broadcasted_iota(jnp.int32, (1, LANES), 1) >= STICK_DEV

    def expand(z, carry):
        for dp in range(groups // 2):
            spot = jnp.concatenate(
                [spot_ref[2 * dp, pl.ds(z, 1), :], spot_ref[2 * dp + 1, pl.ds(z, 1), :]], axis=1
            )
            at = jnp.broadcast_to(spot & (LANES - 1), (8, LANES))
            tile = spot >> 7
            sources = []
            for dd in range(2):
                d = 2 * dp + dd
                t0 = (start_s[d, z, 0] & 4095) >> 7
                mine = upper_half if dd else jnp.logical_not(upper_half)
                for step in range(2):
                    chosen = jnp.broadcast_to(mine & (tile == t0 + step), (8, LANES))
                    where = jnp.minimum(t0 + step, tiles - 1)
                    sources.append((d, pl.multiple_of(where * LANES, LANES), chosen))
            for block in range(blocks):
                value = jnp.zeros((8, LANES), F32)
                for d, begin, chosen in sources:
                    source = xf[d, block * 8 : (block + 1) * 8, pl.ds(begin, LANES)]
                    value = jnp.where(chosen, jnp.take_along_axis(source, at, axis=1), value)
                grid[dp, pl.ds(block * 8 * side + z, 8, stride=side), :] = value
        return carry

    lax.fori_loop(0, side, expand, 0)

    def depth_in(b, carry):
        both = jnp.concatenate(
            [
                jnp.concatenate(
                    [grid[n, pl.ds(b * side, side), :], grid[n, pl.ds((bands + b) * side, side), :]],
                    axis=0,
                )
                for n in range(groups // 2)
            ],
            axis=1,
        ).astype(BF16)
        t_scr[pl.ds(b * span, span), :] = dot(wz_ref[0], both).astype(BF16)
        return carry

    lax.fori_loop(0, bands, depth_in, 0)

    def planes(g, carry):
        rows_g = pl.ds(g * team * span, team * span)
        sticks = t_scr[rows_g, :]
        for k in range(chunks):
            here = slice(k * LANES, (k + 1) * LANES)
            wide = slice(2 * k * LANES, 2 * (k + 1) * LANES)
            ab = dot(sticks, tab_ref[:, wide])
            p, q = field_ref[0, :, here], field_ref[1, :, here]
            p2, q2 = field_ref[2, :, here], field_ref[3, :, here]
            for b in range(team):
                u, x = ab[b * span : b * span + side, :LANES], ab[b * span : b * span + side, LANES:]
                w, v = ab[b * span + side : (b + 1) * span, :LANES], ab[b * span + side : (b + 1) * span, LANES:]
                pr, pi, mr, mi = u - v, w + x, u + v, w - x
                ar, ai = p * pr - q * pi, p * pi + q * pr
                br, bi = p2 * mr - q2 * mi, p2 * mi + q2 * mr
                even = jnp.concatenate([ar + br, ai + bi], axis=0).astype(BF16)
                odd = jnp.concatenate([ai - bi, br - ar], axis=0).astype(BF16)
                l_scr[b * span : (b + 1) * span, wide] = jnp.concatenate([even, odd], axis=1)
        back = dot_nt(l_scr[...], tab_ref[...]).astype(BF16)
        for b in range(team):
            done = dot(wz_ref[1], back[b * span : (b + 1) * span])
            for n in range(groups // 2):
                here = slice(n * LANES, (n + 1) * LANES)
                grid[n, pl.ds((g * team + b) * side, side), :] = done[:side, here]
                grid[n, pl.ds((bands + g * team + b) * side, side), :] = done[side:, here]
        return carry

    lax.fori_loop(0, bands // team, planes, 0)

    for d in range(groups):

        def collect(t, carry, d=d):
            row = d * tiles + t
            at = jnp.broadcast_to(col_ref[pl.ds(row, 1), :], (8, LANES))
            depth = jnp.broadcast_to(dep_ref[pl.ds(row, 1), :], (8, LANES))

            def level(z, values):
                mask = depth == z
                new = []
                for block in range(blocks):
                    source = grid[d // 2, pl.ds(block * 8 * side + z, 8, stride=side), :]
                    new.append(jnp.where(mask, jnp.take_along_axis(source, at, axis=1), values[block]))
                return tuple(new)

            values = lax.fori_loop(
                dep_s[row, 0], dep_s[row, LANES - 1] + 1, level,
                tuple(jnp.zeros((8, LANES), F32) for _ in range(blocks)),
            )
            out_ref[d, :, pl.ds(pl.multiple_of(t * LANES, LANES), LANES)] = jnp.concatenate(
                values, axis=0
            ).astype(BF16)
            return carry

        lax.fori_loop(0, tiles, collect, 0)


def finish_kernel(target_ref, y_ref, rank_ref, partner_ref, out_ref, g_ref):
    rank = rank_ref[...]
    waves = rank.shape[1]
    groups, rows, _ = y_ref.shape
    share = rows // 2
    low = one_hot(rank & 255, 256)
    total = None
    for part in range(waves // 256):
        pieces = [y_ref[q, :, part * 256 : (part + 1) * 256].astype(F32) for q in range(groups)]
        piece = jnp.concatenate(
            [piece[:share] for piece in pieces] + [piece[share:] for piece in pieces], axis=0
        ).astype(BF16)
        value = dot(piece, low)
        value = jnp.where((rank >> 8) == part, value, 0.0)
        total = value if total is None else total + value
    response = total.astype(BF16)
    out_ref[...] = response
    products = dot_nt(partner_ref[0], response)
    half = products.shape[0] // 2
    g_ref[0] = products[:half, :half] + products[half:, half:]
    g_ref[1] = products[:half, half:] - products[half:, :half]


def whole(memory=pltpu.VMEM):
    return pl.BlockSpec(memory_space=memory)


def params():
    return pltpu.CompilerParams(vmem_limit_bytes=VMEM_LIMIT)


def shards(orbitals, box_index, partner_pool, potential):
    fft_count = lax.axis_size("fft")
    side = potential.shape[0]
    bands = orbitals.shape[2]
    waves = orbitals.shape[3]
    share = bands // fft_count
    columns = STICK_DEV * fft_count
    chunks = (side // 2 + 1 + 1) // 2
    tiles = waves // LANES
    coeffs = orbitals.reshape(2 * bands, waves)

    cosine, sine = cos_sin(side)
    cs = jnp.asarray(np.concatenate([cosine, cosine, sine, sine], axis=1))
    half_points = (np.arange(2 * chunks * side) // side) % side
    cyr = jnp.asarray(cosine[:, half_points])
    syr = jnp.asarray(sine[:, half_points])
    inward = np.block([[cosine, -sine], [sine, cosine]])
    outward = np.block([[cosine, sine], [-sine, cosine]])
    wz = jnp.asarray(np.stack([inward, outward]))

    gathered = lax.all_gather(coeffs, "pool", axis=0)
    all_index = lax.all_gather(box_index, "fft", axis=0)

    ordered, rank = pl.pallas_call(
        functools.partial(sort_kernel, side, fft_count),
        out_shape=(
            jax.ShapeDtypeStruct((fft_count, 2 * share, waves), BF16),
            jax.ShapeDtypeStruct((1, waves), jnp.int32),
        ),
        in_specs=[whole(), whole()],
        out_specs=(whole(), whole()),
        compiler_params=params(),
        name="sort_waves",
    )(box_index.reshape(1, waves), coeffs)
    moved = lax.all_to_all(ordered, "fft", split_axis=0, concat_axis=0, tiled=True)

    tab, field, spot, col, dep = pl.pallas_call(
        functools.partial(prep_kernel, side, chunks),
        out_shape=(
            jax.ShapeDtypeStruct((columns, 2 * chunks * LANES), BF16),
            jax.ShapeDtypeStruct((4, side, chunks * LANES), F32),
            jax.ShapeDtypeStruct((fft_count, side, STICK_DEV), jnp.int32),
            jax.ShapeDtypeStruct((fft_count * tiles, LANES), jnp.int32),
            jax.ShapeDtypeStruct((fft_count * tiles, LANES), jnp.int32),
        ),
        in_specs=[whole()] * 5,
        out_specs=(whole(),) * 5,
        compiler_params=params(),
        cost_estimate=pl.CostEstimate(flops=10**9, bytes_accessed=10**7, transcendentals=0),
        name="prepare",
    )(all_index, potential.reshape(side * side, 2 * side), cs, cyr, syr)

    team = min(4, share)
    back = pl.pallas_call(
        functools.partial(box_kernel, side, chunks, team),
        out_shape=jax.ShapeDtypeStruct((fft_count, 2 * share, waves), BF16),
        in_specs=[whole()] * 6 + [whole(pltpu.SMEM)] * 2 + [whole()],
        out_specs=whole(),
        scratch_shapes=[
            pltpu.VMEM((fft_count, 2 * share, waves), F32),
            pltpu.VMEM((columns // LANES, 2 * share * side, LANES), F32),
            pltpu.VMEM((2 * share * side, columns), BF16),
            pltpu.VMEM((team * 2 * side, 2 * chunks * LANES), BF16),
        ],
        compiler_params=params(),
        cost_estimate=pl.CostEstimate(flops=10**10, bytes_accessed=10**7, transcendentals=0),
        name="box_work",
    )(moved, tab, field, spot, col, dep, spot[:, :, :1], dep, wz)
    returned = lax.all_to_all(back, "fft", split_axis=0, concat_axis=0, tiled=True)

    target = partner_pool[lax.axis_index("pool")].reshape(1)
    response, sums = pl.pallas_call(
        finish_kernel,
        grid_spec=pltpu.PrefetchScalarGridSpec(
            num_scalar_prefetch=1,
            grid=(1,),
            in_specs=[
                pl.BlockSpec((fft_count, 2 * share, waves), lambda i, t: (0, 0, 0)),
                pl.BlockSpec((1, waves), lambda i, t: (0, 0)),
                pl.BlockSpec((1, 2 * bands, waves), lambda i, t: (t[0], 0, 0)),
            ],
            out_specs=[
                pl.BlockSpec((2 * bands, waves), lambda i, t: (0, 0)),
                pl.BlockSpec((2, bands, bands), lambda i, t: (0, 0, 0)),
            ],
        ),
        out_shape=(
            jax.ShapeDtypeStruct((2 * bands, waves), BF16),
            jax.ShapeDtypeStruct((2, bands, bands), F32),
        ),
        compiler_params=params(),
        name="finish",
    )(target, returned, rank, gathered)
    summed = lax.psum(sums.astype(BF16), "fft").astype(F32)
    coupling = (summed / jnp.sqrt(jnp.float32(waves * fft_count)))[:, None]
    return response.reshape(2, 1, bands, waves), coupling


def solution(mesh):
    placed = (P(None, "pool", None, "fft"), P("fft"), P(), P())
    return jax.shard_map(
        shards,
        mesh=mesh,
        in_specs=placed,
        out_specs=(P(None, "pool", None, "fft"), P(None, "pool", None, None)),
        check_vma=False,
    )
```

time: 625 us -> 161 us (0.26); the launches traced: 616 us -> 160 us
  local copies, waits for them, and re-layouts: 390 us -> 8.73 us
  matrix products: 80.9 us -> 0 us
  Pallas kernels: 0 us -> 77.5 us
  other arithmetic: 72.2 us -> 0.64 us
  blocking collectives: 25.9 us -> 37.1 us
  waiting for transfers between devices: 22.6 us -> 11.9 us
    reshape x10 -> x0, local copies, waits for them, and re-layouts: 295 us -> none  [the longest x2 143 us: planes_work(): return grid.reshape(bands, flat_side, 2 * side)[:, stick_ids]]
    dot_general x6 -> x0, matrix products: 80.9 us -> none  [the longest x1 39.9 us: planes_work(): jnp.einsum('nbzsy,tasb->nzyta', grid, inverse_w, preferred_element_type=j...]
    pallas_call x0 -> x4, Pallas kernels: none -> 77.5 us  [the longest x1 58.8 us: shards(): pl.pallas_call(functools.partial(box_kernel, side, chunks, team), out_sha...]
    scatter x3 -> x0, local copies, waits for them, and re-layouts: 43.6 us -> none  [the longest x1 24 us: planes_work(): jnp.zeros((bands, flat_side, 2 * side), jnp.bfloat16).at[:, stick_ids]]
    another operation x14 -> x0, other arithmetic: 35.2 us -> none
    gather x3 -> x0, local copies, waits for them, and re-layouts: 31.6 us -> none  [the longest x1 12.1 us: from_sticks(): picked = sticks.reshape(bands, -1)[:, spots].reshape(bands, 2, -1)]
    scatter-add x1 -> x0, other arithmetic: 28.8 us -> none  [stick_layout(): stick_ids = jnp.nonzero(occupied, size=count)[0].astype(jnp.int32)]
    all_gather x0 -> x1, blocking collectives: none -> 20 us  [shards(): all_index = lax.all_gather(box_index, 'fft', axis=0)]
  transfers between devices with their start and end apart: 3 -> 3, of which waited for: 1 -> 1; matrix products, arithmetic and copies ran while one was open for 87% -> 0% of each run, Pallas kernels for 0% -> 47%
where the time goes in v1:
time: 161 us; the launch traced here: 160 us
  Pallas kernels  77.5 us (48%)
  blocking collectives  37.1 us (23%)
  between operations  14.1 us (9%)
  waiting for transfers between devices  11.9 us (7%)
  starting transfers between devices  10.1 us (6%)
  local copies, waits for them, and re-layouts  8.73 us (5%)
    pallas_call x1, Pallas kernels, shards(): pl.pallas_call(functools.partial(box_kernel, side, chunks, team), out_sha...  58.8 us
    all_gather x1, blocking collectives, shards(): all_index = lax.all_gather(box_index, 'fft', axis=0)  20 us
    psum x1, blocking collectives, shards(): summed = lax.psum(sums.astype(BF16), 'fft').astype(F32)  17.1 us
    all_to_all x1, waiting for transfers between devices, shards(): lax.all_to_all(back, 'fft', split_axis=0, concat_axis=0, tiled=True)  11.2 us
    pallas_call x1, Pallas kernels, shards(): pl.pallas_call(functools.partial(prep_kernel, side, chunks), out_shape=(j...  10.6 us
    unnamed x20, local copies, waits for them, and re-layouts  8.13 us
    all_to_all x1, starting transfers between devices, shards(): lax.all_to_all(ordered, 'fft', split_axis=0, concat_axis=0, tiled=True)  6.45 us
    pallas_call x1, Pallas kernels, shards(): pl.pallas_call(functools.partial(sort_kernel, side, fft_count), out_shape...  5.1 us
  transfers between devices with their start and end apart: 3, of which 1 were waited for; matrix products, arithmetic and copies ran while one was open for 0% of the time, Pallas kernels for 47%

profile of v1, /device:TPU:0, one launch (start us, length us, event | category | flops | bytes accessed | tf_op | source)
XLA Modules:
  0.0 160.1 jit_solution(4870721724988724272)
XLA Ops:
  7.2 0.0 copy-start.7
  7.2 0.0 copy-start.4
  7.2 0.0 all-gather.3.cloned.1.call-start
  7.2 0.7 all-gather.3.cloned.1.call-update
  7.9 0.0 copy-start.1
  7.9 1.0 copy-done.1
  9.0 0.0 copy-start.2
  9.0 0.7 copy-done.2
  9.7 5.1 %sort_waves.1 = (bf16[4,32,2048]{2,1,0:T(8,128)(2,1)}, s32[1,2048]{1,0:T(1,128)S(1)}) custom-call(s32[1,2048]{1,0:T(1,128)S(1)} %bitcast.14, bf16[128,2048]{1,0:T(8,128)(2,1)S(1)} %bitcast.13), custom_call_target="tpu_custom_call" | custom-call | tf_op jit(solution)/shard_map/sort_waves/pallas_call | solution.py:317
  14.8 0.0 copy-start.6
  14.8 6.4 %all-to-all-start = ((bf16[4,32,2048]{2,1,0:T(8,128)(2,1)}), bf16[4,32,2048]{2,1,0:T(8,128)(2,1)S(1)}, u32[]{:S(2)}, u32[]{:S(2)}) async-start(bf16[4,32,2048]{2,1,0:T(8,128)(2,1)} %get-tuple-element.11), calls=%async_computation | async-start | bytes 1048576 | tf_op jit(solution)/shard_map/all_to_all | solution.py:328
  21.2 20.0 %all-gather = s32[8192]{0:T(1024)S(1)} all-gather(s32[2048]{0:T(1024)} %param.9), channel_id=2, replica_groups=mesh['pool'=8,'fft'=4] {'fft'}, dimensions={0}, use_global_device_ids=true | all-gather | bytes 40960 | tf_op jit(solution)/shard_map/all_gather | solution.py:315
  41.2 0.0 copy-done.7
  41.2 0.0 copy-done.4
  41.2 0.0 copy-start.3
  41.2 1.6 %copy-done.3 = f32[64,64,128]{2,1,0:T(8,128)S(1)} copy-done((f32[64,64,128]{2,1,0:T(8,128)S(1)}, f32[64,64,128]{2,1,0:T(8,128)}, u32[]{:S(2)}) %copy-start.3) | copy-done | bytes 2097176
  42.8 0.0 copy-start.5
  42.8 1.0 copy-done.5
  43.8 10.6 %prepare.1 = (bf16[256,4352]{1,0:T(8,128)(2,1)S(1)}, f32[4,64,2176]{2,1,0:T(8,128)}, s32[4,64,64]{2,1,0:T(8,128)S(1)}, s32[64,128]{1,0:T(8,128)S(1)}, s32[64,128]{1,0:T(8,128)S(1)}) custom-call(s32[4,2048]{1,0:T(4,128)S(1)} %reshape.20.idx_ref, f32[4096,128]{1,0:T(8,128)S(1)} %bitcast.15, bf16[64,256]{1,0:T(8,128)(2,1)S(1)} %copy-done.7, ...), custom_call_target="tpu_custom_call" | custom-call | flops 1000000000 | bytes 10000000 | tf_op jit(solution)/shard_map/prepare/pallas_call | solution.py:330
  54.4 0.0 all-to-all-done.x_ref
  54.4 0.0 copy-done.6
  54.4 0.0 copy-start.8
  54.4 1.6 %copy-done.8 = f32[4,64,2176]{2,1,0:T(8,128)S(1)} copy-done((f32[4,64,2176]{2,1,0:T(8,128)S(1)}, f32[4,64,2176]{2,1,0:T(8,128)}, u32[]{:S(2)}) %copy-start.8) | copy-done | bytes 2228248
  56.1 0.0 copy-start.9
  56.1 58.8 %box_work.1 = bf16[4,32,2048]{2,1,0:T(8,128)(2,1)} custom-call(bf16[4,32,2048]{2,1,0:T(8,128)(2,1)S(1)} %all-to-all-done.x_ref, bf16[256,4352]{1,0:T(8,128)(2,1)S(1)} %get-tuple-element.12.tab_ref, f32[4,64,2176]{2,1,0:T(8,128)S(1)} %copy-done.8, s32[4,64,64]{2,1,0:T(8,128)S(1)} %get-tuple-element.14.spot_ref, s32[64,128]{1,0:T(8,128)S(1)} %get-tuple-element.15.col_ref, ...), custom_call_target="tpu_custom_call" | custom-call | flops 10000000000 | bytes 10000000 | tf_op jit(solution)/shard_map/box_work/pallas_call | solution.py:347
  114.9 3.7 %all-to-all-start.1 = ((bf16[4,32,2048]{2,1,0:T(8,128)(2,1)}), bf16[4,32,2048]{2,1,0:T(8,128)(2,1)S(1)}, u32[]{:S(2)}, u32[]{:S(2)}) async-start(bf16[4,32,2048]{2,1,0:T(8,128)(2,1)} %box_work.1), calls=%async_computation.1 | async-start | bytes 1048576 | tf_op jit(solution)/shard_map/all_to_all | solution.py:362
  118.6 0.0 copy-done.9
  118.6 0.6 dynamic_slice.3.target_ref
  119.2 11.2 %all-to-all-done.1.y_ref = bf16[4,32,2048]{2,1,0:T(8,128)(2,1)S(1)} async-done(((bf16[4,32,2048]{2,1,0:T(8,128)(2,1)}), bf16[4,32,2048]{2,1,0:T(8,128)(2,1)S(1)}, u32[]{:S(2)}, u32[]{:S(2)}) %all-to-all-start.1) | async-done | bytes 524320 | tf_op jit(solution)/shard_map/all_to_all | solution.py:362
  130.3 0.0 all-gather.3.cloned.1.call-done.partner_ref
  130.3 0.0 copy-start
  130.3 2.2 %copy-done = bf16[8,128,2048]{2,1,0:T(8,128)(2,1)S(1)} copy-done((bf16[8,128,2048]{2,1,0:T(8,128)(2,1)S(1)}, bf16[8,128,2048]{2,1,0:T(8,128)(2,1)}, u32[]{:S(2)}) %copy-start) | copy-done | bytes 4194328
  132.5 2.9 %finish.1 = (bf16[128,2048]{1,0:T(8,128)(2,1)}, f32[2,64,64]{2,1,0:T(8,128)S(1)}) custom-call(s32[1]{0:T(128)} %dynamic_slice.3.target_ref, bf16[4,32,2048]{2,1,0:T(8,128)(2,1)S(1)} %all-to-all-done.1.y_ref, s32[1,2048]{1,0:T(1,128)S(1)} %get-tuple-element.17.rank_ref, bf16[8,128,2048]{2,1,0:T(8,128)(2,1)S(1)} %copy-done), custom_call_target="tpu_custom_call" | custom-call | tf_op jit(solution)/shard_map/finish/pallas_call | solution.py:365
  135.5 17.1 %psum.7 = bf16[2,64,64]{2,1,0:T(8,128)(2,1)S(1)} all-reduce(bf16[2,64,64]{2,1,0:T(8,128)(2,1)S(1)} %convert_element_type.6), channel_id=1, replica_groups=mesh['pool'=8,'fft'=4] {'fft'}, use_global_device_ids=true, to_apply=%region_0.0 | all-reduce | flops 8192 | bytes 32768 | tf_op jit(solution)/shard_map/psum | solution.py:387
  152.6 0.6 multiply_bitcast_fusion
  (2 shorter events, 0.0 us)
Async XLA Ops:
  7.2 34.0 %copy-start.7 = (bf16[64,256]{1,0:T(8,128)(2,1)S(1)}, bf16[64,256]{1,0:T(8,128)(2,1)}, u32[]{:S(2)}) copy-start(bf16[64,256]{1,0:T(8,128)(2,1)} %constant.21.clone.cs_ref) | copy-start | bytes 98308
  7.2 34.0 %copy-start.4 = (bf16[64,2176]{1,0:T(8,128)(2,1)S(1)}, bf16[64,2176]{1,0:T(8,128)(2,1)}, u32[]{:S(2)}) copy-start(bf16[64,2176]{1,0:T(8,128)(2,1)} %constant.22.clone.cyr_ref) | copy-start | bytes 835588
  7.2 123.2 %all-gather.3.cloned.1.call-start = ((), (), s32[]{:S(2)}) async-start(), calls=%async_computation.2 | async-start | bytes 4718592 | tf_op jit(solution)/shard_map/all_gather | solution.py:314
  7.9 1.0 copy-start.1
  9.0 0.7 copy-start.2
  14.8 39.7 %copy-start.6 = (bf16[2,128,128]{2,1,0:T(8,128)(2,1)S(1)}, bf16[2,128,128]{2,1,0:T(8,128)(2,1)}, u32[]{:S(2)}) copy-start(bf16[2,128,128]{2,1,0:T(8,128)(2,1)} %constant.24.clone.wz_ref) | copy-start | bytes 196612
  14.8 39.7 %all-to-all-start = ((bf16[4,32,2048]{2,1,0:T(8,128)(2,1)}), bf16[4,32,2048]{2,1,0:T(8,128)(2,1)S(1)}, u32[]{:S(2)}, u32[]{:S(2)}) async-start(bf16[4,32,2048]{2,1,0:T(8,128)(2,1)} %get-tuple-element.11), calls=%async_computation | async-start | bytes 1048576 | tf_op jit(solution)/shard_map/all_to_all | solution.py:328
  41.2 1.6 %copy-start.3 = (f32[64,64,128]{2,1,0:T(8,128)S(1)}, f32[64,64,128]{2,1,0:T(8,128)}, u32[]{:S(2)}) copy-start(f32[64,64,128]{2,1,0:T(8,128)} %param.11) | copy-start | bytes 6291460
  42.8 1.0 copy-start.5
  54.4 1.6 %copy-start.8 = (f32[4,64,2176]{2,1,0:T(8,128)S(1)}, f32[4,64,2176]{2,1,0:T(8,128)}, u32[]{:S(2)}) copy-start(f32[4,64,2176]{2,1,0:T(8,128)} %get-tuple-element.13.field_ref) | copy-start | bytes 6684676
  56.1 62.5 %copy-start.9 = (s32[8]{0:T(128)S(1)}, s32[8]{0:T(128)}, u32[]{:S(2)}) copy-start(s32[8]{0:T(128)} %param.10) | copy-start | bytes 100
  114.9 15.4 %all-to-all-start.1 = ((bf16[4,32,2048]{2,1,0:T(8,128)(2,1)}), bf16[4,32,2048]{2,1,0:T(8,128)(2,1)S(1)}, u32[]{:S(2)}, u32[]{:S(2)}) async-start(bf16[4,32,2048]{2,1,0:T(8,128)(2,1)} %box_work.1), calls=%async_computation.1 | async-start | bytes 1048576 | tf_op jit(solution)/shard_map/all_to_all | solution.py:362
  130.3 2.2 %copy-start = (bf16[8,128,2048]{2,1,0:T(8,128)(2,1)S(1)}, bf16[8,128,2048]{2,1,0:T(8,128)(2,1)}, u32[]{:S(2)}) copy-start(bf16[8,128,2048]{2,1,0:T(8,128)(2,1)} %all-gather.3.cloned.1.call-done.partner_ref) | copy-start | bytes 12582916
Sparse Core Ops, SparseCore 0:
  9.9 39.4 all-gather.2

commit v2 on v1

--- a/solution.py
+++ b/solution.py
@@ -11,6 +11,7 @@
 
 STICK_DEV = 64
 LANES = 128
+UNROLL = 4
 BF16 = jnp.bfloat16
 F32 = jnp.float32
 VMEM_LIMIT = 48 * 1024 * 1024
@@ -68,7 +69,7 @@
     low = ranks - high * side
     looked = dot(high.astype(BF16), ch) * side + dot(low.astype(BF16), ch)
     rank = jnp.sum(zh.astype(F32) * looked, axis=0, keepdims=True)
-    return xh, yh, zh, ch, slot, cells, ranks, rank.astype(jnp.int32)
+    return xh, yh, ch, cells, ranks, rank.astype(jnp.int32)
 
 
 def sort_kernel(side, groups, idx_ref, x_ref, out_ref, rank_ref):
@@ -90,38 +91,33 @@
 
 
 def prep_kernel(
-    side, chunks, idx_ref, pot_ref, cs_ref, cyr_ref, syr_ref,
-    tab_ref, field_ref, spot_ref, col_ref, dep_ref,
+    side, chunks, groups, me_ref, *refs,
 ):
-    groups = idx_ref.shape[0]
-    waves = idx_ref.shape[1]
-    tiles = waves // LANES
+    idx_refs, refs = refs[:groups], refs[groups:]
+    pot_ref, cs_ref, cyr_ref, syr_ref, tab_ref, field_ref, spot_ref, start_ref = refs
     half = side // 2
-    for d in range(groups):
-        xh, yh, zh, ch, slot, cells, ranks, rank = locate(idx_ref[d : d + 1, :], side)
+    me = me_ref[0]
+    for shift in range(groups):
+        d = lax.rem(me + groups - shift, groups)
+        xh, yh, ch, cells, ranks = locate(idx_refs[shift][...], side)[:5]
         at_x = jnp.minimum(dot_nt(ch, xh), 1.0).astype(BF16)
         at_y = jnp.minimum(dot_nt(ch, yh), 1.0).astype(BF16)
         both = dot(at_x, cs_ref[...])
         cx, sx = both[:, :LANES], both[:, LANES:]
-        rows = slice(d * STICK_DEV, (d + 1) * STICK_DEV)
+        rows = pl.ds(pl.multiple_of(d * STICK_DEV, STICK_DEV), STICK_DEV)
         for k in range(chunks):
             cy = dot(at_y, cyr_ref[:, k * LANES : (k + 1) * LANES])
             sy = dot(at_y, syr_ref[:, k * LANES : (k + 1) * LANES])
             base = 2 * k * LANES
             tab_ref[rows, base : base + LANES] = (cy * cx - sy * sx).astype(BF16)
             tab_ref[rows, base + LANES : base + 2 * LANES] = (cy * sx + sy * cx).astype(BF16)
-        spot = ranks.astype(jnp.int32)
-        spot_ref[d] = jnp.where(cells > 0.5, spot, spot - 4096)
-        low = one_hot(rank & (LANES - 1), LANES)
-        high = one_hot(rank >> 7, tiles)
-        col = dot_nt(high * slot.astype(BF16), low).astype(jnp.int32)
-        depth = jnp.sum(
-            zh.astype(F32) * lax.broadcasted_iota(jnp.int32, zh.shape, 0).astype(F32),
-            axis=0, keepdims=True,
-        )
-        dep = dot_nt(high * depth.astype(BF16), low).astype(jnp.int32)
-        col_ref[d * tiles : (d + 1) * tiles, :] = col + (d % 2) * STICK_DEV
-        dep_ref[d * tiles : (d + 1) * tiles, :] = dep
+        block = float(STICK_DEV)
+        begins = jnp.floor(ranks[:, :1] * (1.0 / block))
+        spot = jnp.where(cells > 0.5, ranks - begins * block, -1.0)
+        spot_ref[d] = jnp.concatenate([spot, spot], axis=1)
+        level = dot_nt(jnp.ones((8, STICK_DEV), BF16), cells.astype(BF16))
+        before = dot(level.astype(BF16), triangles(side)[0])
+        start_ref[pl.ds(d, 1), :] = (before[:1] * (1.0 / block)).astype(jnp.int32)
     lane = lax.broadcasted_iota(jnp.int32, (side, LANES), 1)
     first = lane < side
     flipped = (lane & side) + ((side - (lane & (side - 1))) & (side - 1))
@@ -151,42 +147,66 @@
 
 
 def box_kernel(
-    side, chunks, team, x_ref, tab_ref, field_ref, spot_ref, col_ref, dep_ref, start_s, dep_s,
-    wz_ref, out_ref, xf, grid, t_scr, l_scr,
+    side, chunks, team, x_ref, tab_ref, field_ref, spot_ref, start_s, wz_ref,
+    out_ref, xf, grid, t_scr, l_scr, acc,
 ):
     groups, rows, waves = x_ref.shape
     bands = rows // 2
-    tiles = waves // LANES
     blocks = rows // 8
     span = 2 * side
-    xf[...] = x_ref[...].astype(F32)
-    upper_half = lax.broadcasted_iota(jnp.int32, (1, LANES), 1) >= STICK_DEV
-
-    def expand(z, carry):
+    xf[0] = x_ref[...]
+    for d in range(groups):
+        wide_x = x_ref[d].astype(F32)
+        xf[1, d] = jnp.concatenate([wide_x[:, STICK_DEV:], wide_x[:, :STICK_DEV]], axis=1).astype(BF16)
+        acc[0, d] = jnp.zeros((rows, waves), F32)
+        acc[1, d] = jnp.zeros((rows, waves), F32)
+    left = lax.broadcasted_iota(jnp.int32, (1, LANES), 1) < STICK_DEV
+    places = lax.broadcasted_iota(jnp.int32, (LANES, LANES), 0).astype(F32).astype(BF16)
+    one, none = jnp.ones((LANES, LANES), BF16), jnp.zeros((LANES, LANES), BF16)
+
+    def picks(z, dp):
+        row_a = jnp.where(left, spot_ref[2 * dp, pl.ds(z, 1), :], -1.0).astype(BF16)
+        row_b = jnp.where(left, -1.0, spot_ref[2 * dp + 1, pl.ds(z, 1), :]).astype(BF16)
+        return jnp.concatenate(
+            [jnp.where(places == row_a, one, none), jnp.where(places == row_b, one, none)], axis=0
+        )
+
+    def window(z, d):
+        begin = start_s[d, z]
+        return begin & 1, pl.ds(pl.multiple_of((begin >> 1) * LANES, LANES), LANES)
+
+    def expand(z):
         for dp in range(groups // 2):
-            spot = jnp.concatenate(
-                [spot_ref[2 * dp, pl.ds(z, 1), :], spot_ref[2 * dp + 1, pl.ds(z, 1), :]], axis=1
-            )
-            at = jnp.broadcast_to(spot & (LANES - 1), (8, LANES))
-            tile = spot >> 7
-            sources = []
+            pieces = []
+            for d in (2 * dp, 2 * dp + 1):
+                odd, lanes = window(z, d)
+                pieces.append(xf[odd, d, :, lanes])
+            value = dot(jnp.concatenate(pieces, axis=1), picks(z, dp))
+            for block in range(blocks):
+                rows_z = pl.ds(block * 8 * side + z, 8, stride=side)
+                grid[dp, rows_z, :] = value[block * 8 : (block + 1) * 8]
+
+    def collect(z):
+        for dp in range(groups // 2):
+            source = jnp.concatenate(
+                [grid[dp, pl.ds(block * 8 * side + z, 8, stride=side), :] for block in range(blocks)],
+                axis=0,
+            ).astype(BF16)
+            value = dot_nt(source, picks(z, dp))
             for dd in range(2):
                 d = 2 * dp + dd
-                t0 = (start_s[d, z, 0] & 4095) >> 7
-                mine = upper_half if dd else jnp.logical_not(upper_half)
-                for step in range(2):
-                    chosen = jnp.broadcast_to(mine & (tile == t0 + step), (8, LANES))
-                    where = jnp.minimum(t0 + step, tiles - 1)
-                    sources.append((d, pl.multiple_of(where * LANES, LANES), chosen))
-            for block in range(blocks):
-                value = jnp.zeros((8, LANES), F32)
-                for d, begin, chosen in sources:
-                    source = xf[d, block * 8 : (block + 1) * 8, pl.ds(begin, LANES)]
-                    value = jnp.where(chosen, jnp.take_along_axis(source, at, axis=1), value)
-                grid[dp, pl.ds(block * 8 * side + z, 8, stride=side), :] = value
-        return carry
-
-    lax.fori_loop(0, side, expand, 0)
+                odd, lanes = window(z, d)
+                acc[odd, d, :, lanes] += value[:, dd * LANES : (dd + 1) * LANES]
+
+    def levels(step):
+        def body(i, carry):
+            for j in range(UNROLL):
+                step(i * UNROLL + j)
+            return carry
+
+        lax.fori_loop(0, side // UNROLL, body, 0)
+
+    levels(expand)
 
     def depth_in(b, carry):
         both = jnp.concatenate(
@@ -233,34 +253,16 @@
 
     lax.fori_loop(0, bands // team, planes, 0)
 
+    levels(collect)
     for d in range(groups):
-
-        def collect(t, carry, d=d):
-            row = d * tiles + t
-            at = jnp.broadcast_to(col_ref[pl.ds(row, 1), :], (8, LANES))
-            depth = jnp.broadcast_to(dep_ref[pl.ds(row, 1), :], (8, LANES))
-
-            def level(z, values):
-                mask = depth == z
-                new = []
-                for block in range(blocks):
-                    source = grid[d // 2, pl.ds(block * 8 * side + z, 8, stride=side), :]
-                    new.append(jnp.where(mask, jnp.take_along_axis(source, at, axis=1), values[block]))
-                return tuple(new)
-
-            values = lax.fori_loop(
-                dep_s[row, 0], dep_s[row, LANES - 1] + 1, level,
-                tuple(jnp.zeros((8, LANES), F32) for _ in range(blocks)),
-            )
-            out_ref[d, :, pl.ds(pl.multiple_of(t * LANES, LANES), LANES)] = jnp.concatenate(
-                values, axis=0
-            ).astype(BF16)
-            return carry
-
-        lax.fori_loop(0, tiles, collect, 0)
-
-
-def finish_kernel(target_ref, y_ref, rank_ref, partner_ref, out_ref, g_ref):
+        late = acc[1, d]
+        late = jnp.concatenate([late[:, waves - STICK_DEV :], late[:, : waves - STICK_DEV]], axis=1)
+        out_ref[d] = (acc[0, d] + late).astype(BF16)
+
+
+def finish_kernel(target_ref, y_ref, rank_ref, all_ref, out_ref, g_ref, partner, sem):
+    fetch = pltpu.make_async_copy(all_ref.at[target_ref[0]], partner, sem)
+    fetch.start()
     rank = rank_ref[...]
     waves = rank.shape[1]
     groups, rows, _ = y_ref.shape
@@ -277,10 +279,11 @@
         total = value if total is None else total + value
     response = total.astype(BF16)
     out_ref[...] = response
-    products = dot_nt(partner_ref[0], response)
+    fetch.wait()
+    products = dot_nt(partner[...], response)
     half = products.shape[0] // 2
-    g_ref[0] = products[:half, :half] + products[half:, half:]
-    g_ref[1] = products[:half, half:] - products[half:, :half]
+    g_ref[0] = (products[:half, :half] + products[half:, half:]).astype(BF16)
+    g_ref[1] = (products[:half, half:] - products[half:, :half]).astype(BF16)
 
 
 def whole(memory=pltpu.VMEM):
@@ -311,8 +314,11 @@
     outward = np.block([[cosine, sine], [-sine, cosine]])
     wz = jnp.asarray(np.stack([inward, outward]))
 
+    me = lax.axis_index("fft")
+    shifts = [[(i, (i + s) % fft_count) for i in range(fft_count)] for s in range(1, fft_count)]
+    own_index = box_index.reshape(1, waves)
+    indices = [own_index] + [lax.ppermute(own_index, "fft", shift) for shift in shifts]
     gathered = lax.all_gather(coeffs, "pool", axis=0)
-    all_index = lax.all_gather(box_index, "fft", axis=0)
 
     ordered, rank = pl.pallas_call(
         functools.partial(sort_kernel, side, fft_count),
@@ -324,67 +330,65 @@
         out_specs=(whole(), whole()),
         compiler_params=params(),
         name="sort_waves",
-    )(box_index.reshape(1, waves), coeffs)
+    )(own_index, coeffs)
     moved = lax.all_to_all(ordered, "fft", split_axis=0, concat_axis=0, tiled=True)
 
-    tab, field, spot, col, dep = pl.pallas_call(
-        functools.partial(prep_kernel, side, chunks),
+    tab, field, spot, start = pl.pallas_call(
+        functools.partial(prep_kernel, side, chunks, fft_count),
         out_shape=(
             jax.ShapeDtypeStruct((columns, 2 * chunks * LANES), BF16),
             jax.ShapeDtypeStruct((4, side, chunks * LANES), F32),
-            jax.ShapeDtypeStruct((fft_count, side, STICK_DEV), jnp.int32),
-            jax.ShapeDtypeStruct((fft_count * tiles, LANES), jnp.int32),
-            jax.ShapeDtypeStruct((fft_count * tiles, LANES), jnp.int32),
+            jax.ShapeDtypeStruct((fft_count, side, 2 * STICK_DEV), F32),
+            jax.ShapeDtypeStruct((fft_count, side), jnp.int32),
         ),
-        in_specs=[whole()] * 5,
-        out_specs=(whole(),) * 5,
+        in_specs=[whole(pltpu.SMEM)] + [whole()] * (fft_count + 4),
+        out_specs=(whole(),) * 4,
         compiler_params=params(),
         cost_estimate=pl.CostEstimate(flops=10**9, bytes_accessed=10**7, transcendentals=0),
         name="prepare",
-    )(all_index, potential.reshape(side * side, 2 * side), cs, cyr, syr)
+    )(me.reshape(1), *indices, potential.reshape(side * side, 2 * side), cs, cyr, syr)
 
     team = min(4, share)
     back = pl.pallas_call(
         functools.partial(box_kernel, side, chunks, team),
         out_shape=jax.ShapeDtypeStruct((fft_count, 2 * share, waves), BF16),
-        in_specs=[whole()] * 6 + [whole(pltpu.SMEM)] * 2 + [whole()],
+        in_specs=[whole()] * 4 + [whole(pltpu.SMEM), whole()],
         out_specs=whole(),
         scratch_shapes=[
-            pltpu.VMEM((fft_count, 2 * share, waves), F32),
+            pltpu.VMEM((2, fft_count, 2 * share, waves), BF16),
             pltpu.VMEM((columns // LANES, 2 * share * side, LANES), F32),
             pltpu.VMEM((2 * share * side, columns), BF16),
             pltpu.VMEM((team * 2 * side, 2 * chunks * LANES), BF16),
+            pltpu.VMEM((2, fft_count, 2 * share, waves), F32),
         ],
         compiler_params=params(),
         cost_estimate=pl.CostEstimate(flops=10**10, bytes_accessed=10**7, transcendentals=0),
         name="box_work",
-    )(moved, tab, field, spot, col, dep, spot[:, :, :1], dep, wz)
+    )(moved, tab, field, spot, start, wz)
     returned = lax.all_to_all(back, "fft", split_axis=0, concat_axis=0, tiled=True)
 
     target = partner_pool[lax.axis_index("pool")].reshape(1)
     response, sums = pl.pallas_call(
         finish_kernel,
-        grid_spec=pltpu.PrefetchScalarGridSpec(
-            num_scalar_prefetch=1,
-            grid=(1,),
-            in_specs=[
-                pl.BlockSpec((fft_count, 2 * share, waves), lambda i, t: (0, 0, 0)),
-                pl.BlockSpec((1, waves), lambda i, t: (0, 0)),
-                pl.BlockSpec((1, 2 * bands, waves), lambda i, t: (t[0], 0, 0)),
-            ],
-            out_specs=[
-                pl.BlockSpec((2 * bands, waves), lambda i, t: (0, 0)),
-                pl.BlockSpec((2, bands, bands), lambda i, t: (0, 0, 0)),
-            ],
-        ),
         out_shape=(
             jax.ShapeDtypeStruct((2 * bands, waves), BF16),
-            jax.ShapeDtypeStruct((2, bands, bands), F32),
+            jax.ShapeDtypeStruct((2, bands, bands), BF16),
         ),
+        in_specs=[whole(pltpu.SMEM), whole(), whole(), whole(pltpu.HBM)],
+        out_specs=(whole(), whole()),
+        scratch_shapes=[pltpu.VMEM((2 * bands, waves), BF16), pltpu.SemaphoreType.DMA],
         compiler_params=params(),
         name="finish",
     )(target, returned, rank, gathered)
-    summed = lax.psum(sums.astype(BF16), "fft").astype(F32)
+    shares = [sums] + [lax.ppermute(sums, "fft", shift) for shift in shifts]
+    summed = None
+    for d in range(fft_count):
+        offset = lax.rem(me + fft_count - d, fft_count)
+        term = shares[0]
+        for s in range(1, fft_count):
+            term = jnp.where(offset == s, shares[s], term)
+        term = term.astype(F32)
+        summed = term if summed is None else summed + term
     coupling = (summed / jnp.sqrt(jnp.float32(waves * fft_count)))[:, None]
     return response.reshape(2, 1, bands, waves), coupling
 

time: 161 us -> 115 us (0.71)
  blocking collectives: 37.1 us -> 0 us
  Pallas kernels: 77.5 us -> 42.3 us
  waiting for transfers between devices: 11.9 us -> 28.3 us
  starting transfers between devices: 10.1 us -> 18 us
  local copies, waits for them, and re-layouts: 8.73 us -> 11.1 us
    pallas_call x1, Pallas kernels: 58.8 us -> 25.6 us  [shards(): pl.pallas_call(functools.partial(box_kernel, side, chunks, team), out_sha...]
    all_gather x1 -> x0, blocking collectives: 20 us -> none  [shards(): all_index = lax.all_gather(box_index, 'fft', axis=0)]
    psum x1 -> x0, blocking collectives: 17.1 us -> none  [shards(): summed = lax.psum(sums.astype(BF16), 'fft').astype(F32)]
    ppermute x0 -> x6, waiting for transfers between devices: none -> 14.3 us  [the longest x3 9.26 us: shards(): lax.ppermute(own_index, 'fft', shift)]
    ppermute x0 -> x6, starting transfers between devices: none -> 8 us  [the longest x3 5.85 us: shards(): lax.ppermute(own_index, 'fft', shift)]
    unnamed x20 -> x22, local copies, waits for them, and re-layouts: 8.13 us -> 10.5 us
    all_to_all x1, waiting for transfers between devices: 11.2 us -> 13.3 us  [shards(): lax.all_to_all(back, 'fft', split_axis=0, concat_axis=0, tiled=True)]
    pallas_call x2, Pallas kernels: 13.6 us -> 11.6 us  [the longest x1 8.62 us: shards(): pl.pallas_call(functools.partial(prep_kernel, side, chunks, fft_count), o...]
  transfers between devices with their start and end apart: 3 -> 9, of which waited for: 1 -> 6; matrix products, arithmetic and copies ran while one was open for 0% -> 1% of each run, Pallas kernels for 47% -> 34%
where the time goes in v2:
time: 115 us; the launch traced here: 114 us
  Pallas kernels  42.3 us (37%)
  waiting for transfers between devices  28.3 us (25%)
  starting transfers between devices  18 us (16%)
  between operations  14.1 us (12%)
  local copies, waits for them, and re-layouts  11.1 us (10%)
    pallas_call x1, Pallas kernels, shards(): pl.pallas_call(functools.partial(box_kernel, side, chunks, team), out_sha...  25.6 us
    all_to_all x1, waiting for transfers between devices, shards(): lax.all_to_all(back, 'fft', split_axis=0, concat_axis=0, tiled=True)  13.3 us
    unnamed x22, local copies, waits for them, and re-layouts  10.5 us
    ppermute x3, waiting for transfers between devices, shards(): lax.ppermute(own_index, 'fft', shift)  9.26 us
    pallas_call x1, Pallas kernels, shards(): pl.pallas_call(functools.partial(prep_kernel, side, chunks, fft_count), o...  8.62 us
    all_to_all x1, starting transfers between devices, shards(): lax.all_to_all(ordered, 'fft', split_axis=0, concat_axis=0, tiled=True)  6.45 us
    ppermute x3, starting transfers between devices, shards(): lax.ppermute(own_index, 'fft', shift)  5.85 us
    pallas_call x1, Pallas kernels, shards(): pl.pallas_call(functools.partial(sort_kernel, side, fft_count), out_shape...  5.1 us
  transfers between devices with their start and end apart: 9, of which 6 were waited for; matrix products, arithmetic and copies ran while one was open for 1% of the time, Pallas kernels for 34%

profile of v2, /device:TPU:0, one launch (start us, length us, event | category | flops | bytes accessed | tf_op | source)
XLA Modules:
  0.0 114.4 jit_solution(12069893475858101678)
XLA Ops:
  7.2 0.0 all-gather.2.cloned.1.call-start
  7.2 0.7 all-gather.2.cloned.1.call-update
  7.9 0.0 copy-start.1
  7.9 1.0 copy-done.1
  8.9 0.0 copy-start.2
  8.9 0.7 copy-done.2
  9.6 5.1 %sort_waves.1 = (bf16[4,32,2048]{2,1,0:T(8,128)(2,1)}, s32[1,2048]{1,0:T(1,128)S(1)}) custom-call(s32[1,2048]{1,0:T(1,128)S(1)} %bitcast.17, bf16[128,2048]{1,0:T(8,128)(2,1)S(1)} %bitcast.13), custom_call_target="tpu_custom_call" | custom-call | tf_op jit(solution)/shard_map/sort_waves/pallas_call | solution.py:323
  14.7 0.0 copy-start.7
  14.7 6.4 %all-to-all-start = ((bf16[4,32,2048]{2,1,0:T(8,128)(2,1)}), bf16[4,32,2048]{2,1,0:T(8,128)(2,1)S(1)}, u32[]{:S(2)}, u32[]{:S(2)}) async-start(bf16[4,32,2048]{2,1,0:T(8,128)(2,1)} %get-tuple-element.10), calls=%async_computation | async-start | bytes 1048576 | tf_op jit(solution)/shard_map/all_to_all | solution.py:334
  21.2 2.0 %collective-permute-start = (s32[1,2048]{1,0:T(1,128)}, s32[1,2048]{1,0:T(1,128)S(1)}, u32[]{:S(2)}, u32[]{:S(2)}) collective-permute-start(s32[1,2048]{1,0:T(1,128)} %bitcast.14), channel_id=1, source_target_pairs={{0,1},{1,2},{2,3},{3,0},{4,5},{5,6},{6,7},{7,4},{8,9},{9,10},{10,1... | collective-permute-start | bytes 24584 | tf_op jit(solution)/shard_map/ppermute | solution.py:320
  23.2 2.4 %collective-permute-start.1 = (s32[1,2048]{1,0:T(1,128)}, s32[1,2048]{1,0:T(1,128)S(1)}, u32[]{:S(2)}, u32[]{:S(2)}) collective-permute-start(s32[1,2048]{1,0:T(1,128)} %bitcast.15), channel_id=1, source_target_pairs={{0,2},{1,3},{2,0},{3,1},{4,6},{5,7},{6,4},{7,5},{8,10},{9,11},{10,... | collective-permute-start | bytes 24584 | tf_op jit(solution)/shard_map/ppermute | solution.py:320
  25.6 1.5 %collective-permute-start.2 = (s32[1,2048]{1,0:T(1,128)}, s32[1,2048]{1,0:T(1,128)S(1)}, u32[]{:S(2)}, u32[]{:S(2)}) collective-permute-start(s32[1,2048]{1,0:T(1,128)} %bitcast.16), channel_id=1, source_target_pairs={{0,3},{1,0},{2,1},{3,2},{4,7},{5,4},{6,5},{7,6},{8,11},{9,8},{10,9... | collective-permute-start | bytes 24584 | tf_op jit(solution)/shard_map/ppermute | solution.py:320
  27.0 7.1 %collective-permute-done.refs_1_ = s32[1,2048]{1,0:T(1,128)S(1)} collective-permute-done((s32[1,2048]{1,0:T(1,128)}, s32[1,2048]{1,0:T(1,128)S(1)}, u32[]{:S(2)}, u32[]{:S(2)}) %collective-permute-start) | collective-permute-done | bytes 8224 | tf_op jit(solution)/shard_map/ppermute | solution.py:320
  34.2 2.1 %collective-permute-done.1.refs_2_ = s32[1,2048]{1,0:T(1,128)S(1)} collective-permute-done((s32[1,2048]{1,0:T(1,128)}, s32[1,2048]{1,0:T(1,128)S(1)}, u32[]{:S(2)}, u32[]{:S(2)}) %collective-permute-start.1) | collective-permute-done | bytes 8224 | tf_op jit(solution)/shard_map/ppermute | solution.py:320
  36.3 0.0 collective-permute-done.2.refs_3_
  36.3 0.0 copy-start.3
  36.3 0.7 copy-done.3
  37.0 0.0 copy-start.4
  37.0 1.6 %copy-done.4 = f32[64,64,128]{2,1,0:T(8,128)S(1)} copy-done((f32[64,64,128]{2,1,0:T(8,128)S(1)}, f32[64,64,128]{2,1,0:T(8,128)}, u32[]{:S(2)}) %copy-start.4) | copy-done | bytes 2097176
  38.6 0.0 copy-start.5
  38.6 1.0 copy-done.5
  39.5 0.0 copy-start.6
  39.5 1.0 copy-done.6
  40.5 0.0 copy-start.8
  40.5 0.8 copy-done.8
  41.3 8.6 %prepare.1 = (bf16[256,4352]{1,0:T(8,128)(2,1)S(1)}, f32[4,64,2176]{2,1,0:T(8,128)}, f32[4,64,128]{2,1,0:T(8,128)S(1)}, s32[4,64]{1,0:T(4,128)S(1)}) custom-call(s32[1]{0:T(128)} %bitcast.2.me_ref, s32[1,2048]{1,0:T(1,128)S(1)} %bitcast.18, s32[1,2048]{1,0:T(1,128)S(1)} %collective-permute-done.refs_1_, s32[1,2048]{1,0:T(1,128)S(1)} %collective-permute-done.1.refs_2_, ...), custom_call_target="tpu_custom_call" | custom-call | flops 1000000000 | bytes 10000000 | tf_op jit(solution)/shard_map/prepare/pallas_call | solution.py:336
  49.9 0.0 all-to-all-done.x_ref
  49.9 0.0 copy-done.7
  49.9 0.0 copy-start.9
  49.9 1.6 %copy-done.9 = f32[4,64,2176]{2,1,0:T(8,128)S(1)} copy-done((f32[4,64,2176]{2,1,0:T(8,128)S(1)}, f32[4,64,2176]{2,1,0:T(8,128)}, u32[]{:S(2)}) %copy-start.9) | copy-done | bytes 2228248
  51.5 0.0 copy-start.10
  51.5 25.6 %box_work.1 = bf16[4,32,2048]{2,1,0:T(8,128)(2,1)} custom-call(bf16[4,32,2048]{2,1,0:T(8,128)(2,1)S(1)} %all-to-all-done.x_ref, bf16[256,4352]{1,0:T(8,128)(2,1)S(1)} %get-tuple-element.11.tab_ref, f32[4,64,2176]{2,1,0:T(8,128)S(1)} %copy-done.9, f32[4,64,128]{2,1,0:T(8,128)S(1)} %get-tuple-element.13.spot_ref, s32[4,64]{1,0:T(4,128)S(1)} %get-tuple-element.14.start_s, ...), custom_call_target="tpu_custom_call" | custom-call | flops 10000000000 | bytes 10000000 | tf_op jit(solution)/shard_map/box_work/pallas_call | solution.py:352
  77.1 3.5 %all-to-all-start.1 = ((bf16[4,32,2048]{2,1,0:T(8,128)(2,1)}), bf16[4,32,2048]{2,1,0:T(8,128)(2,1)S(1)}, u32[]{:S(2)}, u32[]{:S(2)}) async-start(bf16[4,32,2048]{2,1,0:T(8,128)(2,1)} %box_work.1), calls=%async_computation.1 | async-start | bytes 1048576 | tf_op jit(solution)/shard_map/all_to_all | solution.py:368
  80.6 0.0 copy-done.10
  80.6 0.6 dynamic_slice.3.target_ref
  81.2 13.3 %all-to-all-done.1.y_ref = bf16[4,32,2048]{2,1,0:T(8,128)(2,1)S(1)} async-done(((bf16[4,32,2048]{2,1,0:T(8,128)(2,1)}), bf16[4,32,2048]{2,1,0:T(8,128)(2,1)S(1)}, u32[]{:S(2)}, u32[]{:S(2)}) %all-to-all-start.1) | async-done | bytes 524320 | tf_op jit(solution)/shard_map/all_to_all | solution.py:368
  94.5 0.0 all-gather.2.cloned.1.call-done.all_ref
  94.5 0.0 copy-start
  94.5 2.2 %copy-done = bf16[8,128,2048]{2,1,0:T(8,128)(2,1)S(1)} copy-done((bf16[8,128,2048]{2,1,0:T(8,128)(2,1)S(1)}, bf16[8,128,2048]{2,1,0:T(8,128)(2,1)}, u32[]{:S(2)}) %copy-start) | copy-done | bytes 4194328
  96.7 3.0 %finish.1 = (bf16[128,2048]{1,0:T(8,128)(2,1)}, bf16[2,64,64]{2,1,0:T(8,128)(2,1)S(1)}) custom-call(s32[1]{0:T(128)} %dynamic_slice.3.target_ref, bf16[4,32,2048]{2,1,0:T(8,128)(2,1)S(1)} %all-to-all-done.1.y_ref, s32[1,2048]{1,0:T(1,128)S(1)} %get-tuple-element.15.rank_ref, bf16[8,128,2048]{2,1,0:T(8,128)(2,1)S(1)} %copy-done), custom_call_target="tpu_custom_call" | custom-call | tf_op jit(solution)/shard_map/finish/pallas_call | solution.py:371
  99.6 1.5 %collective-permute-start.3 = (bf16[2,64,64]{2,1,0:T(8,128)(2,1)S(1)}, bf16[2,64,64]{2,1,0:T(8,128)(2,1)S(1)}, u32[]{:S(2)}, u32[]{:S(2)}) collective-permute-start(bf16[2,64,64]{2,1,0:T(8,128)(2,1)S(1)} %get-tuple-element.17), channel_id=1, source_target_pairs={{0,3},{1,0},{2,1},{3,2},{4,7},{5,4},{6,5},{7,6},{8,11},{9,8},{10,9... | collective-permute-start | bytes 49160 | tf_op jit(solution)/shard_map/ppermute | solution.py:383
  101.2 0.0 collective-permute-start.4
  101.2 0.6 collective-permute-start.5
  101.8 1.8 %collective-permute-done.3 = bf16[2,64,64]{2,1,0:T(8,128)(2,1)S(1)} collective-permute-done((bf16[2,64,64]{2,1,0:T(8,128)(2,1)S(1)}, bf16[2,64,64]{2,1,0:T(8,128)(2,1)S(1)}, u32[]{:S(2)}, u32[]{:S(2)}) %collective-permute-start.3) | collective-permute-done | bytes 16416 | tf_op jit(solution)/shard_map/ppermute | solution.py:383
  103.6 2.7 %collective-permute-done.4 = bf16[2,64,64]{2,1,0:T(8,128)(2,1)S(1)} collective-permute-done((bf16[2,64,64]{2,1,0:T(8,128)(2,1)S(1)}, bf16[2,64,64]{2,1,0:T(8,128)(2,1)S(1)}, u32[]{:S(2)}, u32[]{:S(2)}) %collective-permute-start.4) | collective-permute-done | bytes 16416 | tf_op jit(solution)/shard_map/ppermute | solution.py:383
  106.3 0.6 collective-permute-done.5
  106.9 0.7 multiply_bitcast_fusion
Async XLA Ops:
  7.2 87.3 %all-gather.2.cloned.1.call-start = ((), (), s32[]{:S(2)}) async-start(), calls=%async_computation.2 | async-start | bytes 4718592 | tf_op jit(solution)/shard_map/all_gather | solution.py:321
  7.9 1.0 copy-start.1
  8.9 0.7 copy-start.2
  14.7 35.1 %copy-start.7 = (bf16[2,128,128]{2,1,0:T(8,128)(2,1)S(1)}, bf16[2,128,128]{2,1,0:T(8,128)(2,1)}, u32[]{:S(2)}) copy-start(bf16[2,128,128]{2,1,0:T(8,128)(2,1)} %constant.49.clone.wz_ref) | copy-start | bytes 196612
  14.7 35.1 %all-to-all-start = ((bf16[4,32,2048]{2,1,0:T(8,128)(2,1)}), bf16[4,32,2048]{2,1,0:T(8,128)(2,1)S(1)}, u32[]{:S(2)}, u32[]{:S(2)}) async-start(bf16[4,32,2048]{2,1,0:T(8,128)(2,1)} %get-tuple-element.10), calls=%async_computation | async-start | bytes 1048576 | tf_op jit(solution)/shard_map/all_to_all | solution.py:334
  21.2 13.0 %collective-permute-start = (s32[1,2048]{1,0:T(1,128)}, s32[1,2048]{1,0:T(1,128)S(1)}, u32[]{:S(2)}, u32[]{:S(2)}) collective-permute-start(s32[1,2048]{1,0:T(1,128)} %bitcast.14), channel_id=1, source_target_pairs={{0,1},{1,2},{2,3},{3,0},{4,5},{5,6},{6,7},{7,4},{8,9},{9,10},{10,1... | collective-permute-start | bytes 24584 | tf_op jit(solution)/shard_map/ppermute | solution.py:320
  23.2 13.1 %collective-permute-start.1 = (s32[1,2048]{1,0:T(1,128)}, s32[1,2048]{1,0:T(1,128)S(1)}, u32[]{:S(2)}, u32[]{:S(2)}) collective-permute-start(s32[1,2048]{1,0:T(1,128)} %bitcast.15), channel_id=1, source_target_pairs={{0,2},{1,3},{2,0},{3,1},{4,6},{5,7},{6,4},{7,5},{8,10},{9,11},{10,... | collective-permute-start | bytes 24584 | tf_op jit(solution)/shard_map/ppermute | solution.py:320
  25.6 10.7 %collective-permute-start.2 = (s32[1,2048]{1,0:T(1,128)}, s32[1,2048]{1,0:T(1,128)S(1)}, u32[]{:S(2)}, u32[]{:S(2)}) collective-permute-start(s32[1,2048]{1,0:T(1,128)} %bitcast.16), channel_id=1, source_target_pairs={{0,3},{1,0},{2,1},{3,2},{4,7},{5,4},{6,5},{7,6},{8,11},{9,8},{10,9... | collective-permute-start | bytes 24584 | tf_op jit(solution)/shard_map/ppermute | solution.py:320
  36.3 0.7 copy-start.3
  37.0 1.6 %copy-start.4 = (f32[64,64,128]{2,1,0:T(8,128)S(1)}, f32[64,64,128]{2,1,0:T(8,128)}, u32[]{:S(2)}) copy-start(f32[64,64,128]{2,1,0:T(8,128)} %param.11) | copy-start | bytes 6291460
  38.6 1.0 copy-start.5
  39.5 1.0 copy-start.6
  40.5 0.8 copy-start.8
  49.9 1.6 %copy-start.9 = (f32[4,64,2176]{2,1,0:T(8,128)S(1)}, f32[4,64,2176]{2,1,0:T(8,128)}, u32[]{:S(2)}) copy-start(f32[4,64,2176]{2,1,0:T(8,128)} %get-tuple-element.12.field_ref) | copy-start | bytes 6684676
  51.5 29.1 %copy-start.10 = (s32[8]{0:T(128)S(1)}, s32[8]{0:T(128)}, u32[]{:S(2)}) copy-start(s32[8]{0:T(128)} %param.10) | copy-start | bytes 100
  77.1 17.4 %all-to-all-start.1 = ((bf16[4,32,2048]{2,1,0:T(8,128)(2,1)}), bf16[4,32,2048]{2,1,0:T(8,128)(2,1)S(1)}, u32[]{:S(2)}, u32[]{:S(2)}) async-start(bf16[4,32,2048]{2,1,0:T(8,128)(2,1)} %box_work.1), calls=%async_computation.1 | async-start | bytes 1048576 | tf_op jit(solution)/shard_map/all_to_all | solution.py:368
  94.5 2.2 %copy-start = (bf16[8,128,2048]{2,1,0:T(8,128)(2,1)S(1)}, bf16[8,128,2048]{2,1,0:T(8,128)(2,1)}, u32[]{:S(2)}) copy-start(bf16[8,128,2048]{2,1,0:T(8,128)(2,1)} %all-gather.2.cloned.1.call-done.all_ref) | copy-start | bytes 12582916
  99.6 4.0 %collective-permute-start.3 = (bf16[2,64,64]{2,1,0:T(8,128)(2,1)S(1)}, bf16[2,64,64]{2,1,0:T(8,128)(2,1)S(1)}, u32[]{:S(2)}, u32[]{:S(2)}) collective-permute-start(bf16[2,64,64]{2,1,0:T(8,128)(2,1)S(1)} %get-tuple-element.17), channel_id=1, source_target_pairs={{0,3},{1,0},{2,1},{3,2},{4,7},{5,4},{6,5},{7,6},{8,11},{9,8},{10,9... | collective-permute-start | bytes 49160 | tf_op jit(solution)/shard_map/ppermute | solution.py:383
  101.2 5.2 %collective-permute-start.4 = (bf16[2,64,64]{2,1,0:T(8,128)(2,1)S(1)}, bf16[2,64,64]{2,1,0:T(8,128)(2,1)S(1)}, u32[]{:S(2)}, u32[]{:S(2)}) collective-permute-start(bf16[2,64,64]{2,1,0:T(8,128)(2,1)S(1)} %get-tuple-element.17), channel_id=1, source_target_pairs={{0,2},{1,3},{2,0},{3,1},{4,6},{5,7},{6,4},{7,5},{8,10},{9,11},{10,... | collective-permute-start | bytes 49160 | tf_op jit(solution)/shard_map/ppermute | solution.py:383
  101.2 5.7 %collective-permute-start.5 = (bf16[2,64,64]{2,1,0:T(8,128)(2,1)S(1)}, bf16[2,64,64]{2,1,0:T(8,128)(2,1)S(1)}, u32[]{:S(2)}, u32[]{:S(2)}) collective-permute-start(bf16[2,64,64]{2,1,0:T(8,128)(2,1)S(1)} %get-tuple-element.17), channel_id=1, source_target_pairs={{0,1},{1,2},{2,3},{3,0},{4,5},{5,6},{6,7},{7,4},{8,9},{9,10},{10,1... | collective-permute-start | bytes 49160 | tf_op jit(solution)/shard_map/ppermute | solution.py:383
Sparse Core Ops, SparseCore 0:
  9.9 39.4 all-gather.1

commit v3 on v2

--- a/solution.py
+++ b/solution.py
@@ -14,7 +14,7 @@
 UNROLL = 4
 BF16 = jnp.bfloat16
 F32 = jnp.float32
-VMEM_LIMIT = 48 * 1024 * 1024
+VMEM_LIMIT = 36 * 1024 * 1024
 
 
 def cos_sin(side):
@@ -72,17 +72,38 @@
     return xh, yh, ch, cells, ranks, rank.astype(jnp.int32)
 
 
-def sort_kernel(side, groups, idx_ref, x_ref, out_ref, rank_ref):
-    rank = locate(idx_ref[...], side)[-1]
+def sort_block(x_ref, rank, low, part):
+    mask = jnp.where((rank >> 8) == part, 1.0, 0.0).astype(BF16)
+    return dot_nt(x_ref[...] * mask, low)
+
+
+def sort_kernel(side, groups, idx_ref, x_hbm, out_ref, rank_ref, x_ref, sem):
+    fetch = pltpu.make_async_copy(x_hbm, x_ref, sem)
+    fetch.start()
+    xh, yh, ch, cells, ranks, rank = locate(idx_ref[...], side)
     rank_ref[...] = rank
     waves = rank.shape[1]
-    rows = x_ref.shape[0]
-    bands = rows // 2
+    bands = x_ref.shape[0] // 2
     share = bands // groups
+    rows = 2 * share
+    lane = lax.broadcasted_iota(jnp.int32, (STICK_DEV, side), 1).astype(F32)
+    cells = jnp.concatenate([cells[i : i + rows] for i in range(0, side, rows)], axis=1)
+    slot = lax.broadcasted_iota(jnp.int32, (rows, LANES), 1) // rows
+    place = jnp.zeros((rows, LANES), F32)
+    count = 0
+    for hot in (xh, yh):
+        at = jnp.minimum(dot_nt(ch, hot), 1.0)
+        value = jnp.sum(at * lane, axis=1, keepdims=True)
+        for i in range(0, STICK_DEV, rows):
+            place = jnp.where(slot == count, value[i : i + rows], place)
+            count += 1
+    extra = jnp.concatenate([cells, place], axis=1).astype(BF16)
     low = one_hot(rank & 255, 256)
+    fetch.wait()
+    for q in range(groups):
+        out_ref[q, :, waves:] = extra
     for part in range(waves // 256):
-        mask = jnp.where((rank >> 8) == part, 1.0, 0.0).astype(BF16)
-        piece = dot_nt(x_ref[...] * mask, low)
+        piece = sort_block(x_ref, rank, low, part)
         for q in range(groups):
             re = piece[q * share : (q + 1) * share]
             im = piece[bands + q * share : bands + (q + 1) * share]
@@ -90,34 +111,8 @@
             out_ref[q, :, part * 256 : (part + 1) * 256] = both
 
 
-def prep_kernel(
-    side, chunks, groups, me_ref, *refs,
-):
-    idx_refs, refs = refs[:groups], refs[groups:]
-    pot_ref, cs_ref, cyr_ref, syr_ref, tab_ref, field_ref, spot_ref, start_ref = refs
+def field_kernel(side, chunks, pot_ref, field_ref):
     half = side // 2
-    me = me_ref[0]
-    for shift in range(groups):
-        d = lax.rem(me + groups - shift, groups)
-        xh, yh, ch, cells, ranks = locate(idx_refs[shift][...], side)[:5]
-        at_x = jnp.minimum(dot_nt(ch, xh), 1.0).astype(BF16)
-        at_y = jnp.minimum(dot_nt(ch, yh), 1.0).astype(BF16)
-        both = dot(at_x, cs_ref[...])
-        cx, sx = both[:, :LANES], both[:, LANES:]
-        rows = pl.ds(pl.multiple_of(d * STICK_DEV, STICK_DEV), STICK_DEV)
-        for k in range(chunks):
-            cy = dot(at_y, cyr_ref[:, k * LANES : (k + 1) * LANES])
-            sy = dot(at_y, syr_ref[:, k * LANES : (k + 1) * LANES])
-            base = 2 * k * LANES
-            tab_ref[rows, base : base + LANES] = (cy * cx - sy * sx).astype(BF16)
-            tab_ref[rows, base + LANES : base + 2 * LANES] = (cy * sx + sy * cx).astype(BF16)
-        block = float(STICK_DEV)
-        begins = jnp.floor(ranks[:, :1] * (1.0 / block))
-        spot = jnp.where(cells > 0.5, ranks - begins * block, -1.0)
-        spot_ref[d] = jnp.concatenate([spot, spot], axis=1)
-        level = dot_nt(jnp.ones((8, STICK_DEV), BF16), cells.astype(BF16))
-        before = dot(level.astype(BF16), triangles(side)[0])
-        start_ref[pl.ds(d, 1), :] = (before[:1] * (1.0 / block)).astype(jnp.int32)
     lane = lax.broadcasted_iota(jnp.int32, (side, LANES), 1)
     first = lane < side
     flipped = (lane & side) + ((side - (lane & (side - 1))) & (side - 1))
@@ -138,25 +133,72 @@
     zero = jnp.zeros((side, LANES), F32)
     for k in range(chunks):
         ya, yb = 2 * k, 2 * k + 1
-        p, q = pair(plane(ya), plane(yb) if yb <= half else zero)
-        field_ref[0, :, k * LANES : (k + 1) * LANES] = p
-        field_ref[1, :, k * LANES : (k + 1) * LANES] = q
-        p, q = pair(mirror(ya), mirror(yb))
-        field_ref[2, :, k * LANES : (k + 1) * LANES] = p
-        field_ref[3, :, k * LANES : (k + 1) * LANES] = q
+        here = slice(k * LANES, (k + 1) * LANES)
+        field_ref[0, :, here], field_ref[1, :, here] = pair(
+            plane(ya), plane(yb) if yb <= half else zero
+        )
+        field_ref[2, :, here], field_ref[3, :, here] = pair(mirror(ya), mirror(yb))
+
+
+def select_kernel(order_ref, in_ref, out_ref, sems):
+    copies = []
+    for i in range(out_ref.shape[0]):
+        copy = pltpu.make_async_copy(in_ref.at[order_ref[i]], out_ref.at[i], sems.at[i])
+        copy.start()
+        copies.append(copy)
+    for copy in copies:
+        copy.wait()
 
 
 def box_kernel(
-    side, chunks, team, x_ref, tab_ref, field_ref, spot_ref, start_s, wz_ref,
-    out_ref, xf, grid, t_scr, l_scr, acc,
+    side, chunks, team, waves, x_ref, field_ref, cs_ref, cyr_ref, syr_ref, wz_ref,
+    out_ref, xf, grid, t_scr, l_scr, acc, tab_ref, spot_ref, start_v, start_s, sem,
 ):
-    groups, rows, waves = x_ref.shape
+    groups, rows, _ = x_ref.shape
     bands = rows // 2
     blocks = rows // 8
     span = 2 * side
-    xf[0] = x_ref[...]
+    tri = triangles(side)
+    parts = side // rows
+    cells_end = waves + parts * STICK_DEV
+    lane_f = lax.broadcasted_iota(jnp.int32, (STICK_DEV, side), 1).astype(F32)
+    at_x, at_y = [], []
     for d in range(groups):
-        wide_x = x_ref[d].astype(F32)
+        cells = jnp.concatenate(
+            [x_ref[d, :, waves + i * STICK_DEV : waves + (i + 1) * STICK_DEV].astype(F32) for i in range(parts)],
+            axis=0,
+        )
+        place = x_ref[d, :, cells_end : cells_end + LANES].astype(F32)
+        for which, hots in enumerate((at_x, at_y)):
+            value = jnp.concatenate(
+                [place[:, i * rows : i * rows + 1] for i in range(which * parts, (which + 1) * parts)],
+                axis=0,
+            )
+            hots.append(jnp.where(lane_f == value, 1.0, 0.0))
+        ranks = prefix(cells.astype(BF16), tri)
+        begins = jnp.floor(ranks[:, :1] * (1.0 / STICK_DEV))
+        spot = jnp.where(cells > 0.5, ranks - begins * STICK_DEV, -1.0)
+        spot_ref[d] = jnp.concatenate([spot, spot], axis=1)
+        level = dot_nt(jnp.ones((8, STICK_DEV), BF16), cells.astype(BF16))
+        before = dot(level.astype(BF16), tri[0])
+        start_v[d : d + 1, :side] = (before[:1] * (1.0 / STICK_DEV)).astype(jnp.int32)
+    to_scalars = pltpu.make_async_copy(start_v, start_s, sem)
+    to_scalars.start()
+    at_x = jnp.concatenate(at_x, axis=0).astype(BF16)
+    at_y = jnp.concatenate(at_y, axis=0).astype(BF16)
+    both = dot(at_x, cs_ref[...])
+    cx, sx = both[:, :LANES], both[:, LANES:]
+    for k in range(chunks):
+        cy = dot(at_y, cyr_ref[:, k * LANES : (k + 1) * LANES])
+        sy = dot(at_y, syr_ref[:, k * LANES : (k + 1) * LANES])
+        base = 2 * k * LANES
+        tab_ref[:, base : base + LANES] = (cy * cx - sy * sx).astype(BF16)
+        tab_ref[:, base + LANES : base + 2 * LANES] = (cy * sx + sy * cx).astype(BF16)
+    to_scalars.wait()
+
+    xf[0] = x_ref[:, :, :waves]
+    for d in range(groups):
+        wide_x = x_ref[d, :, :waves].astype(F32)
         xf[1, d] = jnp.concatenate([wide_x[:, STICK_DEV:], wide_x[:, :STICK_DEV]], axis=1).astype(BF16)
         acc[0, d] = jnp.zeros((rows, waves), F32)
         acc[1, d] = jnp.zeros((rows, waves), F32)
@@ -260,30 +302,38 @@
         out_ref[d] = (acc[0, d] + late).astype(BF16)
 
 
-def finish_kernel(target_ref, y_ref, rank_ref, all_ref, out_ref, g_ref, partner, sem):
-    fetch = pltpu.make_async_copy(all_ref.at[target_ref[0]], partner, sem)
-    fetch.start()
+def partner_kernel(x_ref, rank_ref, out_ref):
     rank = rank_ref[...]
-    waves = rank.shape[1]
-    groups, rows, _ = y_ref.shape
-    share = rows // 2
     low = one_hot(rank & 255, 256)
-    total = None
-    for part in range(waves // 256):
-        pieces = [y_ref[q, :, part * 256 : (part + 1) * 256].astype(F32) for q in range(groups)]
-        piece = jnp.concatenate(
-            [piece[:share] for piece in pieces] + [piece[share:] for piece in pieces], axis=0
-        ).astype(BF16)
-        value = dot(piece, low)
-        value = jnp.where((rank >> 8) == part, value, 0.0)
-        total = value if total is None else total + value
-    response = total.astype(BF16)
-    out_ref[...] = response
-    fetch.wait()
-    products = dot_nt(partner[...], response)
+    for part in range(rank.shape[1] // 256):
+        out_ref[:, part * 256 : (part + 1) * 256] = sort_block(x_ref, rank, low, part).astype(BF16)
+
+
+def by_part(blocks):
+    share = blocks[0].shape[0] // 2
+    return jnp.concatenate(
+        [block[:share] for block in blocks] + [block[share:] for block in blocks], axis=0
+    ).astype(BF16)
+
+
+def couple_kernel(y_ref, partner_ref, g_ref):
+    response = by_part([y_ref[q].astype(F32) for q in range(y_ref.shape[0])])
+    products = dot_nt(partner_ref[...], response)
     half = products.shape[0] // 2
     g_ref[0] = (products[:half, :half] + products[half:, half:]).astype(BF16)
     g_ref[1] = (products[:half, half:] - products[half:, :half]).astype(BF16)
+
+
+def unsort_kernel(y_ref, rank_ref, out_ref):
+    rank = rank_ref[...]
+    low = one_hot(rank & 255, 256)
+    total = None
+    for part in range(rank.shape[1] // 256):
+        here = slice(part * 256, (part + 1) * 256)
+        piece = by_part([y_ref[q, :, here].astype(F32) for q in range(y_ref.shape[0])])
+        value = jnp.where((rank >> 8) == part, dot(piece, low), 0.0)
+        total = value if total is None else total + value
+    out_ref[...] = total.astype(BF16)
 
 
 def whole(memory=pltpu.VMEM):
@@ -302,7 +352,6 @@
     share = bands // fft_count
     columns = STICK_DEV * fft_count
     chunks = (side // 2 + 1 + 1) // 2
-    tiles = waves // LANES
     coeffs = orbitals.reshape(2 * bands, waves)
 
     cosine, sine = cos_sin(side)
@@ -316,71 +365,99 @@
 
     me = lax.axis_index("fft")
     shifts = [[(i, (i + s) % fft_count) for i in range(fft_count)] for s in range(1, fft_count)]
-    own_index = box_index.reshape(1, waves)
-    indices = [own_index] + [lax.ppermute(own_index, "fft", shift) for shift in shifts]
-    gathered = lax.all_gather(coeffs, "pool", axis=0)
+    pool_count = lax.axis_size("pool")
+    rows = 2 * share
+    packed = waves + side * STICK_DEV // rows + LANES
 
     ordered, rank = pl.pallas_call(
         functools.partial(sort_kernel, side, fft_count),
         out_shape=(
-            jax.ShapeDtypeStruct((fft_count, 2 * share, waves), BF16),
+            jax.ShapeDtypeStruct((fft_count, rows, packed), BF16),
             jax.ShapeDtypeStruct((1, waves), jnp.int32),
         ),
-        in_specs=[whole(), whole()],
+        in_specs=[whole(), whole(pltpu.HBM)],
         out_specs=(whole(), whole()),
+        scratch_shapes=[pltpu.VMEM((2 * bands, waves), BF16), pltpu.SemaphoreType.DMA],
         compiler_params=params(),
         name="sort_waves",
-    )(own_index, coeffs)
+    )(box_index.reshape(1, waves), coeffs)
     moved = lax.all_to_all(ordered, "fft", split_axis=0, concat_axis=0, tiled=True)
 
-    tab, field, spot, start = pl.pallas_call(
-        functools.partial(prep_kernel, side, chunks, fft_count),
-        out_shape=(
-            jax.ShapeDtypeStruct((columns, 2 * chunks * LANES), BF16),
-            jax.ShapeDtypeStruct((4, side, chunks * LANES), F32),
-            jax.ShapeDtypeStruct((fft_count, side, 2 * STICK_DEV), F32),
-            jax.ShapeDtypeStruct((fft_count, side), jnp.int32),
-        ),
-        in_specs=[whole(pltpu.SMEM)] + [whole()] * (fft_count + 4),
-        out_specs=(whole(),) * 4,
+    spread = lax.all_to_all(
+        coeffs.reshape(pool_count, 2 * bands // pool_count, waves), "pool", 0, 0, tiled=True
+    )
+    chosen = pl.pallas_call(
+        select_kernel,
+        out_shape=jax.ShapeDtypeStruct(spread.shape, BF16),
+        in_specs=[whole(pltpu.SMEM), whole(pl.ANY)],
+        out_specs=whole(pl.ANY),
+        scratch_shapes=[pltpu.SemaphoreType.DMA((pool_count,))],
+        compiler_params=params(),
+        name="select_partner",
+    )(partner_pool, spread)
+    partner = lax.all_to_all(chosen, "pool", 0, 0, tiled=True).reshape(2 * bands, waves)
+
+    field = pl.pallas_call(
+        functools.partial(field_kernel, side, chunks),
+        out_shape=jax.ShapeDtypeStruct((4, side, chunks * LANES), F32),
+        in_specs=[whole()],
+        out_specs=whole(),
         compiler_params=params(),
         cost_estimate=pl.CostEstimate(flops=10**9, bytes_accessed=10**7, transcendentals=0),
-        name="prepare",
-    )(me.reshape(1), *indices, potential.reshape(side * side, 2 * side), cs, cyr, syr)
+        name="field_pairs",
+    )(potential.reshape(side * side, 2 * side))
 
     team = min(4, share)
     back = pl.pallas_call(
-        functools.partial(box_kernel, side, chunks, team),
-        out_shape=jax.ShapeDtypeStruct((fft_count, 2 * share, waves), BF16),
-        in_specs=[whole()] * 4 + [whole(pltpu.SMEM), whole()],
+        functools.partial(box_kernel, side, chunks, team, waves),
+        out_shape=jax.ShapeDtypeStruct((fft_count, rows, waves), BF16),
+        in_specs=[whole()] * 6,
         out_specs=whole(),
         scratch_shapes=[
-            pltpu.VMEM((2, fft_count, 2 * share, waves), BF16),
-            pltpu.VMEM((columns // LANES, 2 * share * side, LANES), F32),
-            pltpu.VMEM((2 * share * side, columns), BF16),
+            pltpu.VMEM((2, fft_count, rows, waves), BF16),
+            pltpu.VMEM((columns // LANES, rows * side, LANES), F32),
+            pltpu.VMEM((rows * side, columns), BF16),
             pltpu.VMEM((team * 2 * side, 2 * chunks * LANES), BF16),
-            pltpu.VMEM((2, fft_count, 2 * share, waves), F32),
+            pltpu.VMEM((2, fft_count, rows, waves), F32),
+            pltpu.VMEM((columns, 2 * chunks * LANES), BF16),
+            pltpu.VMEM((fft_count, side, 2 * STICK_DEV), F32),
+            pltpu.VMEM((fft_count, LANES), jnp.int32),
+            pltpu.SMEM((fft_count, LANES), jnp.int32),
+            pltpu.SemaphoreType.DMA,
         ],
         compiler_params=params(),
         cost_estimate=pl.CostEstimate(flops=10**10, bytes_accessed=10**7, transcendentals=0),
         name="box_work",
-    )(moved, tab, field, spot, start, wz)
+    )(moved, field, cs, cyr, syr, wz)
     returned = lax.all_to_all(back, "fft", split_axis=0, concat_axis=0, tiled=True)
 
-    target = partner_pool[lax.axis_index("pool")].reshape(1)
-    response, sums = pl.pallas_call(
-        finish_kernel,
-        out_shape=(
-            jax.ShapeDtypeStruct((2 * bands, waves), BF16),
-            jax.ShapeDtypeStruct((2, bands, bands), BF16),
-        ),
-        in_specs=[whole(pltpu.SMEM), whole(), whole(), whole(pltpu.HBM)],
-        out_specs=(whole(), whole()),
-        scratch_shapes=[pltpu.VMEM((2 * bands, waves), BF16), pltpu.SemaphoreType.DMA],
-        compiler_params=params(),
-        name="finish",
-    )(target, returned, rank, gathered)
+    ordered_partner = pl.pallas_call(
+        partner_kernel,
+        out_shape=jax.ShapeDtypeStruct((2 * bands, waves), BF16),
+        in_specs=[whole(), whole()],
+        out_specs=whole(),
+        compiler_params=params(),
+        cost_estimate=pl.CostEstimate(flops=10**9, bytes_accessed=10**7, transcendentals=0),
+        name="sort_partner",
+    )(partner, rank)
+    sums = pl.pallas_call(
+        couple_kernel,
+        out_shape=jax.ShapeDtypeStruct((2, bands, bands), BF16),
+        in_specs=[whole(), whole()],
+        out_specs=whole(),
+        compiler_params=params(),
+        name="couple",
+    )(returned, ordered_partner)
     shares = [sums] + [lax.ppermute(sums, "fft", shift) for shift in shifts]
+    response = pl.pallas_call(
+        unsort_kernel,
+        out_shape=jax.ShapeDtypeStruct((2 * bands, waves), BF16),
+        in_specs=[whole(), whole()],
+        out_specs=whole(),
+        compiler_params=params(),
+        cost_estimate=pl.CostEstimate(flops=10**9, bytes_accessed=10**7, transcendentals=0),
+        name="unsort",
+    )(returned, rank)
     summed = None
     for d in range(fft_count):
         offset = lax.rem(me + fft_count - d, fft_count)

time: 115 us -> 94.4 us (0.82)
  between operations: 14.1 us -> 0.76 us
  local copies, waits for them, and re-layouts: 11.1 us -> 6.08 us
  Pallas kernels: 42.3 us -> 39.9 us
  starting transfers between devices: 18 us -> 19.5 us
  waiting for transfers between devices: 28.3 us -> 26.9 us
    ppermute x3 -> x0, waiting for transfers between devices: 9.26 us -> none  [shards(): lax.ppermute(own_index, 'fft', shift)]
    all_to_all x1, waiting for transfers between devices: 0.01 us -> 9.24 us  [shards(): lax.all_to_all(ordered, 'fft', split_axis=0, concat_axis=0, tiled=True)]
    all_to_all x0 -> x2, starting transfers between devices: none -> 9.02 us  [the longest x1 5.18 us: shards(): lax.all_to_all(coeffs.reshape(pool_count, 2 * bands // pool_count, waves)...]
    ppermute x3 -> x0, starting transfers between devices: 5.85 us -> none  [shards(): lax.ppermute(own_index, 'fft', shift)]
    unnamed x22 -> x18, local copies, waits for them, and re-layouts: 10.5 us -> 6.08 us
    pallas_call x3 -> x6, Pallas kernels: 37.2 us -> 34.2 us  [the longest x1 25.3 us: shards(): pl.pallas_call(functools.partial(box_kernel, side, chunks, team, waves),...]
    all_to_all x0 -> x2, waiting for transfers between devices: none -> 2.32 us  [the longest x1 2.32 us: shards(): lax.all_to_all(coeffs.reshape(pool_count, 2 * bands // pool_count, waves)...]
    ppermute x3, waiting for transfers between devices: 5.07 us -> 2.87 us  [shards(): shares = [sums] + [lax.ppermute(sums, 'fft', shift) for shift in shifts]]
  transfers between devices with their start and end apart: 9 -> 7, of which waited for: 6 -> 5; matrix products, arithmetic and copies ran while one was open for 1% -> 0% of each run, Pallas kernels for 34% -> 42%
where the time goes in v3:
time: 94.4 us; the launch traced here: 93.8 us
  Pallas kernels  39.9 us (42%)
  waiting for transfers between devices  26.9 us (28%)
  starting transfers between devices  19.5 us (21%)
  local copies, waits for them, and re-layouts  6.08 us (6%)
    pallas_call x1, Pallas kernels, shards(): pl.pallas_call(functools.partial(box_kernel, side, chunks, team, waves),...  25.3 us
    all_to_all x1, waiting for transfers between devices, shards(): lax.all_to_all(back, 'fft', split_axis=0, concat_axis=0, tiled=True)  12.5 us
    all_to_all x1, waiting for transfers between devices, shards(): lax.all_to_all(ordered, 'fft', split_axis=0, concat_axis=0, tiled=True)  9.24 us
    unnamed x18, local copies, waits for them, and re-layouts  6.08 us
    pallas_call x1, Pallas kernels, shards(): pl.pallas_call(functools.partial(sort_kernel, side, fft_count), out_shape...  5.64 us
    all_to_all x1, starting transfers between devices, shards(): lax.all_to_all(coeffs.reshape(pool_count, 2 * bands // pool_count, waves)...  5.18 us
    all_to_all x1, starting transfers between devices, shards(): lax.all_to_all(ordered, 'fft', split_axis=0, concat_axis=0, tiled=True)  4.87 us
    all_to_all x1, starting transfers between devices, shards(): lax.all_to_all(chosen, 'pool', 0, 0, tiled=True).reshape(2 * bands, waves)  3.84 us
  transfers between devices with their start and end apart: 7, of which 5 were waited for; matrix products, arithmetic and copies ran while one was open for 0% of the time, Pallas kernels for 42%

profile of v3, /device:TPU:0, one launch (start us, length us, event | category | flops | bytes accessed | tf_op | source)
XLA Modules:
  0.0 93.8 jit_solution(4993910406442183089)
XLA Ops:
  0.6 5.2 %all-to-all-start.2 = ((bf16[8,16,2048]{2,1,0:T(8,128)(2,1)}), bf16[8,16,2048]{2,1,0:T(8,128)(2,1)S(1)}, u32[]{:S(2)}, u32[]{:S(2)}) async-start(bf16[8,16,2048]{2,1,0:T(8,128)(2,1)} %bitcast.13), calls=%async_computation.2 | async-start | bytes 1048576 | tf_op jit(solution)/shard_map/all_to_all | solution.py:386
  5.8 0.0 copy-start.1
  5.8 1.1 %copy-done.1 = bf16[2,1,64,2048]{3,2,1,0:T(8,128)(2,1)S(1)} copy-done((bf16[2,1,64,2048]{3,2,1,0:T(8,128)(2,1)S(1)}, bf16[2,1,64,2048]{3,2,1,0:T(8,128)(2,1)}, u32[]{:S(2)}) %copy-start.1) | copy-done | bytes 524312
  6.9 0.0 copy-start.3
  6.9 0.7 copy-done.3
  7.6 5.6 %sort_waves.1 = (bf16[4,32,2304]{2,1,0:T(8,128)(2,1)}, s32[1,2048]{1,0:T(1,128)S(1)}) custom-call(s32[1,2048]{1,0:T(1,128)S(1)} %bitcast.16, bf16[128,2048]{1,0:T(8,128)(2,1)S(1)} %bitcast.14), custom_call_target="tpu_custom_call" | custom-call | tf_op jit(solution)/shard_map/sort_waves/pallas_call | solution.py:372
  13.2 2.3 %all-to-all-done.2.in_ref = bf16[8,16,2048]{2,1,0:T(8,128)(2,1)S(1)} async-done(((bf16[8,16,2048]{2,1,0:T(8,128)(2,1)}), bf16[8,16,2048]{2,1,0:T(8,128)(2,1)S(1)}, u32[]{:S(2)}, u32[]{:S(2)}) %all-to-all-start.2) | async-done | bytes 524320 | tf_op jit(solution)/shard_map/all_to_all | solution.py:386
  15.6 4.9 %all-to-all-start = ((bf16[4,32,2304]{2,1,0:T(8,128)(2,1)}), bf16[4,32,2304]{2,1,0:T(8,128)(2,1)S(1)}, u32[]{:S(2)}, u32[]{:S(2)}) async-start(bf16[4,32,2304]{2,1,0:T(8,128)(2,1)} %get-tuple-element.4), calls=%async_computation | async-start | bytes 1179648 | tf_op jit(solution)/shard_map/all_to_all | solution.py:384
  20.4 0.0 copy-start.4
  20.4 0.0 copy-start
  20.4 1.6 %copy-done = f32[64,64,128]{2,1,0:T(8,128)S(1)} copy-done((f32[64,64,128]{2,1,0:T(8,128)S(1)}, f32[64,64,128]{2,1,0:T(8,128)}, u32[]{:S(2)}) %copy-start) | copy-done | bytes 2097176
  22.0 0.0 copy-start.7
  22.0 0.0 copy-start.8
  22.0 2.0 %field_pairs.1.field_ref = f32[4,64,2176]{2,1,0:T(8,128)S(1)} custom-call(f32[4096,128]{1,0:T(8,128)S(1)} %bitcast.12), custom_call_target="tpu_custom_call" | custom-call | flops 1000000000 | bytes 10000000 | tf_op jit(solution)/shard_map/field_pairs/pallas_call | solution.py:400
  24.0 0.0 copy-done.4
  24.0 1.4 %select_partner.1 = bf16[8,16,2048]{2,1,0:T(8,128)(2,1)} custom-call(s32[8]{0:T(128)S(1)} %copy-done.4, bf16[8,16,2048]{2,1,0:T(8,128)(2,1)S(1)} %all-to-all-done.2.in_ref), custom_call_target="tpu_custom_call" | custom-call | tf_op jit(solution)/shard_map/select_partner/pallas_call | solution.py:389
  25.5 9.2 %all-to-all-done.x_ref = bf16[4,32,2304]{2,1,0:T(8,128)(2,1)S(1)} async-done(((bf16[4,32,2304]{2,1,0:T(8,128)(2,1)}), bf16[4,32,2304]{2,1,0:T(8,128)(2,1)S(1)}, u32[]{:S(2)}, u32[]{:S(2)}) %all-to-all-start) | async-done | bytes 589856 | tf_op jit(solution)/shard_map/all_to_all | solution.py:384
  34.7 3.8 %all-to-all-start.3 = ((bf16[8,16,2048]{2,1,0:T(8,128)(2,1)}), bf16[8,16,2048]{2,1,0:T(8,128)(2,1)S(1)}, u32[]{:S(2)}, u32[]{:S(2)}) async-start(bf16[8,16,2048]{2,1,0:T(8,128)(2,1)} %select_partner.1), calls=%async_computation.3 | async-start | bytes 1048576 | tf_op jit(solution)/shard_map/all_to_all | solution.py:398
  38.5 0.0 copy-done.7
  38.5 0.0 copy-done.8
  38.5 0.0 copy-start.5
  38.6 0.9 %copy-done.5 = bf16[64,2176]{1,0:T(8,128)(2,1)S(1)} copy-done((bf16[64,2176]{1,0:T(8,128)(2,1)S(1)}, bf16[64,2176]{1,0:T(8,128)(2,1)}, u32[]{:S(2)}) %copy-start.5) | copy-done | bytes 278552
  39.5 0.0 copy-start.6
  39.5 1.0 %copy-done.6 = bf16[64,2176]{1,0:T(8,128)(2,1)S(1)} copy-done((bf16[64,2176]{1,0:T(8,128)(2,1)S(1)}, bf16[64,2176]{1,0:T(8,128)(2,1)}, u32[]{:S(2)}) %copy-start.6) | copy-done | bytes 278552
  40.5 25.3 %box_work.1 = bf16[4,32,2048]{2,1,0:T(8,128)(2,1)S(1)} custom-call(bf16[4,32,2304]{2,1,0:T(8,128)(2,1)S(1)} %all-to-all-done.x_ref, f32[4,64,2176]{2,1,0:T(8,128)S(1)} %field_pairs.1.field_ref, bf16[64,256]{1,0:T(8,128)(2,1)S(1)} %copy-done.8, bf16[64,2176]{1,0:T(8,128)(2,1)S(1)} %copy-done.5, bf16[64,2176]{1,0:T(8,128)(2,1)S(1)} %copy-done.6, ...), custom_call_target="tpu_custom_call" | custom-call | flops 10000000000 | bytes 10000000 | tf_op jit(solution)/shard_map/box_work/pallas_call | solution.py:411
  65.8 0.0 copy-start.2
  65.8 0.8 copy-done.2
  66.6 0.0 all-to-all-done.3
  66.6 3.5 %all-to-all-start.1 = ((bf16[4,32,2048]{2,1,0:T(8,128)(2,1)}), bf16[4,32,2048]{2,1,0:T(8,128)(2,1)S(1)}, u32[]{:S(2)}, u32[]{:S(2)}) async-start(bf16[4,32,2048]{2,1,0:T(8,128)(2,1)} %copy-done.2), calls=%async_computation.1 | async-start | bytes 1048576 | tf_op jit(solution)/shard_map/all_to_all | solution.py:432
  70.1 2.8 %sort_partner.1.partner_ref = bf16[128,2048]{1,0:T(8,128)(2,1)S(1)} custom-call(bf16[128,2048]{1,0:T(8,128)(2,1)S(1)} %bitcast.15, s32[1,2048]{1,0:T(1,128)S(1)} %get-tuple-element.5.rank_ref), custom_call_target="tpu_custom_call" | custom-call | flops 1000000000 | bytes 10000000 | tf_op jit(solution)/shard_map/sort_partner/pallas_call | solution.py:434
  73.0 12.5 %all-to-all-done.1.y_ref = bf16[4,32,2048]{2,1,0:T(8,128)(2,1)S(1)} async-done(((bf16[4,32,2048]{2,1,0:T(8,128)(2,1)}), bf16[4,32,2048]{2,1,0:T(8,128)(2,1)S(1)}, u32[]{:S(2)}, u32[]{:S(2)}) %all-to-all-start.1) | async-done | bytes 524320 | tf_op jit(solution)/shard_map/all_to_all | solution.py:432
  85.5 0.4 couple.1
  85.9 1.5 %collective-permute-start = (bf16[2,64,64]{2,1,0:T(8,128)(2,1)S(1)}, bf16[2,64,64]{2,1,0:T(8,128)(2,1)S(1)}, u32[]{:S(2)}, u32[]{:S(2)}) collective-permute-start(bf16[2,64,64]{2,1,0:T(8,128)(2,1)S(1)} %couple.1), channel_id=1, source_target_pairs={{0,3},{1,0},{2,1},{3,2},{4,7},{5,4},{6,5},{7,6},{8,11},{9,8},{10,9... | collective-permute-start | bytes 49160 | tf_op jit(solution)/shard_map/ppermute | solution.py:451
  87.4 0.0 collective-permute-start.1
  87.4 0.6 collective-permute-start.2
  88.0 2.2 %unsort.1 = bf16[128,2048]{1,0:T(8,128)(2,1)} custom-call(bf16[4,32,2048]{2,1,0:T(8,128)(2,1)S(1)} %all-to-all-done.1.y_ref, s32[1,2048]{1,0:T(1,128)S(1)} %get-tuple-element.5.rank_ref), custom_call_target="tpu_custom_call" | custom-call | flops 1000000000 | bytes 10000000 | tf_op jit(solution)/shard_map/unsort/pallas_call | solution.py:452
  90.2 0.0 collective-permute-done
  90.3 2.3 %collective-permute-done.1 = bf16[2,64,64]{2,1,0:T(8,128)(2,1)S(1)} collective-permute-done((bf16[2,64,64]{2,1,0:T(8,128)(2,1)S(1)}, bf16[2,64,64]{2,1,0:T(8,128)(2,1)S(1)}, u32[]{:S(2)}, u32[]{:S(2)}) %collective-permute-start.1) | collective-permute-done | bytes 16416 | tf_op jit(solution)/shard_map/ppermute | solution.py:451
  92.6 0.6 collective-permute-done.2
  93.1 0.7 multiply_bitcast_fusion
Async XLA Ops:
  0.6 14.9 %all-to-all-start.2 = ((bf16[8,16,2048]{2,1,0:T(8,128)(2,1)}), bf16[8,16,2048]{2,1,0:T(8,128)(2,1)S(1)}, u32[]{:S(2)}, u32[]{:S(2)}) async-start(bf16[8,16,2048]{2,1,0:T(8,128)(2,1)} %bitcast.13), calls=%async_computation.2 | async-start | bytes 1048576 | tf_op jit(solution)/shard_map/all_to_all | solution.py:386
  5.8 1.1 %copy-start.1 = (bf16[2,1,64,2048]{3,2,1,0:T(8,128)(2,1)S(1)}, bf16[2,1,64,2048]{3,2,1,0:T(8,128)(2,1)}, u32[]{:S(2)}) copy-start(bf16[2,1,64,2048]{3,2,1,0:T(8,128)(2,1)} %param.8) | copy-start | bytes 1572868
  6.9 0.7 copy-start.3
  15.6 19.1 %all-to-all-start = ((bf16[4,32,2304]{2,1,0:T(8,128)(2,1)}), bf16[4,32,2304]{2,1,0:T(8,128)(2,1)S(1)}, u32[]{:S(2)}, u32[]{:S(2)}) async-start(bf16[4,32,2304]{2,1,0:T(8,128)(2,1)} %get-tuple-element.4), calls=%async_computation | async-start | bytes 1179648 | tf_op jit(solution)/shard_map/all_to_all | solution.py:384
  20.4 3.6 %copy-start.4 = (s32[8]{0:T(128)S(1)}, s32[8]{0:T(128)}, u32[]{:S(2)}) copy-start(s32[8]{0:T(128)} %order_ref.1) | copy-start | bytes 100
  20.4 1.6 %copy-start = (f32[64,64,128]{2,1,0:T(8,128)S(1)}, f32[64,64,128]{2,1,0:T(8,128)}, u32[]{:S(2)}) copy-start(f32[64,64,128]{2,1,0:T(8,128)} %param.11) | copy-start | bytes 6291460
  22.0 16.5 %copy-start.7 = (bf16[2,128,128]{2,1,0:T(8,128)(2,1)S(1)}, bf16[2,128,128]{2,1,0:T(8,128)(2,1)}, u32[]{:S(2)}) copy-start(bf16[2,128,128]{2,1,0:T(8,128)(2,1)} %constant.41.clone.wz_ref) | copy-start | bytes 196612
  22.0 16.5 %copy-start.8 = (bf16[64,256]{1,0:T(8,128)(2,1)S(1)}, bf16[64,256]{1,0:T(8,128)(2,1)}, u32[]{:S(2)}) copy-start(bf16[64,256]{1,0:T(8,128)(2,1)} %constant.38.clone.cs_ref) | copy-start | bytes 98308
  34.7 31.9 %all-to-all-start.3 = ((bf16[8,16,2048]{2,1,0:T(8,128)(2,1)}), bf16[8,16,2048]{2,1,0:T(8,128)(2,1)S(1)}, u32[]{:S(2)}, u32[]{:S(2)}) async-start(bf16[8,16,2048]{2,1,0:T(8,128)(2,1)} %select_partner.1), calls=%async_computation.3 | async-start | bytes 1048576 | tf_op jit(solution)/shard_map/all_to_all | solution.py:398
  38.5 1.0 %copy-start.5 = (bf16[64,2176]{1,0:T(8,128)(2,1)S(1)}, bf16[64,2176]{1,0:T(8,128)(2,1)}, u32[]{:S(2)}) copy-start(bf16[64,2176]{1,0:T(8,128)(2,1)} %constant.39.clone.cyr_ref) | copy-start | bytes 835588
  39.5 1.0 %copy-start.6 = (bf16[64,2176]{1,0:T(8,128)(2,1)S(1)}, bf16[64,2176]{1,0:T(8,128)(2,1)}, u32[]{:S(2)}) copy-start(bf16[64,2176]{1,0:T(8,128)(2,1)} %constant.40.clone.syr_ref) | copy-start | bytes 835588
  65.8 0.8 copy-start.2
  66.6 18.9 %all-to-all-start.1 = ((bf16[4,32,2048]{2,1,0:T(8,128)(2,1)}), bf16[4,32,2048]{2,1,0:T(8,128)(2,1)S(1)}, u32[]{:S(2)}, u32[]{:S(2)}) async-start(bf16[4,32,2048]{2,1,0:T(8,128)(2,1)} %copy-done.2), calls=%async_computation.1 | async-start | bytes 1048576 | tf_op jit(solution)/shard_map/all_to_all | solution.py:432
  85.9 4.3 %collective-permute-start = (bf16[2,64,64]{2,1,0:T(8,128)(2,1)S(1)}, bf16[2,64,64]{2,1,0:T(8,128)(2,1)S(1)}, u32[]{:S(2)}, u32[]{:S(2)}) collective-permute-start(bf16[2,64,64]{2,1,0:T(8,128)(2,1)S(1)} %couple.1), channel_id=1, source_target_pairs={{0,3},{1,0},{2,1},{3,2},{4,7},{5,4},{6,5},{7,6},{8,11},{9,8},{10,9... | collective-permute-start | bytes 49160 | tf_op jit(solution)/shard_map/ppermute | solution.py:451
  87.4 5.2 %collective-permute-start.1 = (bf16[2,64,64]{2,1,0:T(8,128)(2,1)S(1)}, bf16[2,64,64]{2,1,0:T(8,128)(2,1)S(1)}, u32[]{:S(2)}, u32[]{:S(2)}) collective-permute-start(bf16[2,64,64]{2,1,0:T(8,128)(2,1)S(1)} %couple.1), channel_id=1, source_target_pairs={{0,2},{1,3},{2,0},{3,1},{4,6},{5,7},{6,4},{7,5},{8,10},{9,11},{10,... | collective-permute-start | bytes 49160 | tf_op jit(solution)/shard_map/ppermute | solution.py:451
  87.4 5.7 %collective-permute-start.2 = (bf16[2,64,64]{2,1,0:T(8,128)(2,1)S(1)}, bf16[2,64,64]{2,1,0:T(8,128)(2,1)S(1)}, u32[]{:S(2)}, u32[]{:S(2)}) collective-permute-start(bf16[2,64,64]{2,1,0:T(8,128)(2,1)S(1)} %couple.1), channel_id=1, source_target_pairs={{0,1},{1,2},{2,3},{3,0},{4,5},{5,6},{6,7},{7,4},{8,9},{9,10},{10,1... | collective-permute-start | bytes 49160 | tf_op jit(solution)/shard_map/ppermute | solution.py:451

commit v4 on v3

--- a/solution.py
+++ b/solution.py
@@ -14,7 +14,8 @@
 UNROLL = 4
 BF16 = jnp.bfloat16
 F32 = jnp.float32
-VMEM_LIMIT = 36 * 1024 * 1024
+VMEM_LIMIT = 24 * 1024 * 1024
+SORT_LIMIT = 60 * 1024 * 1024
 
 
 def cos_sin(side):
@@ -72,18 +73,15 @@
     return xh, yh, ch, cells, ranks, rank.astype(jnp.int32)
 
 
-def sort_block(x_ref, rank, low, part):
-    mask = jnp.where((rank >> 8) == part, 1.0, 0.0).astype(BF16)
-    return dot_nt(x_ref[...] * mask, low)
-
-
-def sort_kernel(side, groups, idx_ref, x_hbm, out_ref, rank_ref, x_ref, sem):
+def sort_kernel(side, groups, me_ref, idx_ref, x_hbm, *refs):
+    outs, (all_ref, rank_ref, x_ref, wide, pieces, sem) = refs[:groups], refs[groups:]
     fetch = pltpu.make_async_copy(x_hbm, x_ref, sem)
     fetch.start()
     xh, yh, ch, cells, ranks, rank = locate(idx_ref[...], side)
     rank_ref[...] = rank
     waves = rank.shape[1]
-    bands = x_ref.shape[0] // 2
+    both = x_ref.shape[0]
+    bands = both // 2
     share = bands // groups
     rows = 2 * share
     lane = lax.broadcasted_iota(jnp.int32, (STICK_DEV, side), 1).astype(F32)
@@ -99,20 +97,35 @@
             count += 1
     extra = jnp.concatenate([cells, place], axis=1).astype(BF16)
     low = one_hot(rank & 255, 256)
+    for out in outs:
+        out[:, waves:] = extra
     fetch.wait()
-    for q in range(groups):
-        out_ref[q, :, waves:] = extra
-    for part in range(waves // 256):
-        piece = sort_block(x_ref, rank, low, part)
-        for q in range(groups):
-            re = piece[q * share : (q + 1) * share]
-            im = piece[bands + q * share : bands + (q + 1) * share]
-            both = jnp.concatenate([re, im], axis=0).astype(BF16)
-            out_ref[q, :, part * 256 : (part + 1) * 256] = both
-
-
-def field_kernel(side, chunks, pot_ref, field_ref):
+    parts = waves // 256
+    for part in range(parts):
+        mask = jnp.where((rank >> 8) == part, 1.0, 0.0).astype(BF16)
+        wide[part * both : (part + 1) * both] = x_ref[...] * mask
+    pieces[...] = dot_nt(wide[...], low)
+    for part in range(parts):
+        here = slice(part * 256, (part + 1) * 256)
+        all_ref[:, here] = pieces[part * both : (part + 1) * both].astype(BF16)
+        for shift, out in enumerate(outs):
+            q = lax.rem(me_ref[0] + shift, groups)
+            begin = pl.multiple_of(part * both + q * share, 8)
+            re = pieces[pl.ds(begin, share)]
+            im = pieces[pl.ds(begin + bands, share)]
+            out[:, here] = jnp.concatenate([re, im], axis=0).astype(BF16)
+
+
+def field_kernel(side, chunks, pot_ref, cs_ref, field_ref, cyr_ref, syr_ref):
     half = side // 2
+    left = lax.broadcasted_iota(jnp.int32, (side, LANES), 1) < side
+    for ref, begin in ((cyr_ref, 0), (syr_ref, LANES)):
+        table = cs_ref[:, begin : begin + side].astype(F32)
+        for k in range(chunks):
+            ya, yb = (2 * k) % side, (2 * k + 1) % side
+            ref[:, k * LANES : (k + 1) * LANES] = jnp.where(
+                left, table[:, ya : ya + 1], table[:, yb : yb + 1]
+            ).astype(BF16)
     lane = lax.broadcasted_iota(jnp.int32, (side, LANES), 1)
     first = lane < side
     flipped = (lane & side) + ((side - (lane & (side - 1))) & (side - 1))
@@ -151,10 +164,13 @@
 
 
 def box_kernel(
-    side, chunks, team, waves, x_ref, field_ref, cs_ref, cyr_ref, syr_ref, wz_ref,
-    out_ref, xf, grid, t_scr, l_scr, acc, tab_ref, spot_ref, start_v, start_s, sem,
+    side, chunks, team, waves, groups, *refs,
 ):
-    groups, rows, _ = x_ref.shape
+    x_refs, refs = refs[:groups], refs[groups:]
+    (field_ref, cs_ref, cyr_ref, syr_ref, wz_ref), refs = refs[:5], refs[5:]
+    out_refs, refs = refs[:groups], refs[groups:]
+    xf, grid, t_scr, l_scr, acc, tab_ref, spot_ref, start_v, start_s, sem = refs
+    rows = x_refs[0].shape[0]
     bands = rows // 2
     blocks = rows // 8
     span = 2 * side
@@ -165,10 +181,10 @@
     at_x, at_y = [], []
     for d in range(groups):
         cells = jnp.concatenate(
-            [x_ref[d, :, waves + i * STICK_DEV : waves + (i + 1) * STICK_DEV].astype(F32) for i in range(parts)],
+            [x_refs[d][:, waves + i * STICK_DEV : waves + (i + 1) * STICK_DEV].astype(F32) for i in range(parts)],
             axis=0,
         )
-        place = x_ref[d, :, cells_end : cells_end + LANES].astype(F32)
+        place = x_refs[d][:, cells_end : cells_end + LANES].astype(F32)
         for which, hots in enumerate((at_x, at_y)):
             value = jnp.concatenate(
                 [place[:, i * rows : i * rows + 1] for i in range(which * parts, (which + 1) * parts)],
@@ -196,9 +212,9 @@
         tab_ref[:, base + LANES : base + 2 * LANES] = (cy * sx + sy * cx).astype(BF16)
     to_scalars.wait()
 
-    xf[0] = x_ref[:, :, :waves]
     for d in range(groups):
-        wide_x = x_ref[d, :, :waves].astype(F32)
+        xf[0, d] = x_refs[d][:, :waves]
+        wide_x = x_refs[d][:, :waves].astype(F32)
         xf[1, d] = jnp.concatenate([wide_x[:, STICK_DEV:], wide_x[:, :STICK_DEV]], axis=1).astype(BF16)
         acc[0, d] = jnp.zeros((rows, waves), F32)
         acc[1, d] = jnp.zeros((rows, waves), F32)
@@ -299,49 +315,46 @@
     for d in range(groups):
         late = acc[1, d]
         late = jnp.concatenate([late[:, waves - STICK_DEV :], late[:, : waves - STICK_DEV]], axis=1)
-        out_ref[d] = (acc[0, d] + late).astype(BF16)
-
-
-def partner_kernel(x_ref, rank_ref, out_ref):
-    rank = rank_ref[...]
-    low = one_hot(rank & 255, 256)
-    for part in range(rank.shape[1] // 256):
-        out_ref[:, part * 256 : (part + 1) * 256] = sort_block(x_ref, rank, low, part).astype(BF16)
-
-
-def by_part(blocks):
-    share = blocks[0].shape[0] // 2
-    return jnp.concatenate(
-        [block[:share] for block in blocks] + [block[share:] for block in blocks], axis=0
-    ).astype(BF16)
-
-
-def couple_kernel(y_ref, partner_ref, g_ref):
-    response = by_part([y_ref[q].astype(F32) for q in range(y_ref.shape[0])])
+        out_refs[d][...] = (acc[0, d] + late).astype(BF16)
+
+
+def couple_kernel(groups, me_ref, *refs):
+    y_refs, (partner_ref, sorted_ref, g_ref, rows_scr) = refs[:groups], refs[groups:]
+    share = y_refs[0].shape[0] // 2
+    half = groups * share
+    for shift, y_ref in enumerate(y_refs):
+        begin = pl.multiple_of(lax.rem(me_ref[0] + shift, groups) * share, 8)
+        value = y_ref[...].astype(F32)
+        rows_scr[pl.ds(begin, share)] = value[:share]
+        rows_scr[pl.ds(begin + half, share)] = value[share:]
+    response = rows_scr[...].astype(BF16)
+    sorted_ref[...] = response
     products = dot_nt(partner_ref[...], response)
-    half = products.shape[0] // 2
     g_ref[0] = (products[:half, :half] + products[half:, half:]).astype(BF16)
     g_ref[1] = (products[:half, half:] - products[half:, :half]).astype(BF16)
 
 
 def unsort_kernel(y_ref, rank_ref, out_ref):
-    rank = rank_ref[...]
-    low = one_hot(rank & 255, 256)
-    total = None
-    for part in range(rank.shape[1] // 256):
-        here = slice(part * 256, (part + 1) * 256)
-        piece = by_part([y_ref[q, :, here].astype(F32) for q in range(y_ref.shape[0])])
-        value = jnp.where((rank >> 8) == part, dot(piece, low), 0.0)
-        total = value if total is None else total + value
-    out_ref[...] = total.astype(BF16)
+    both, waves = y_ref.shape
+    parts = waves // 256
+    stacked = jnp.concatenate([y_ref[:, i * 256 : (i + 1) * 256] for i in range(parts)], axis=0)
+    for tile in range(parts):
+        here = slice(tile * 256, (tile + 1) * 256)
+        rank = rank_ref[:, here]
+        values = dot(stacked, one_hot(rank & 255, 256))
+        total = None
+        for part in range(parts):
+            value = jnp.where((rank >> 8) == part, values[part * both : (part + 1) * both], 0.0)
+            total = value if total is None else total + value
+        out_ref[:, here] = total.astype(BF16)
 
 
 def whole(memory=pltpu.VMEM):
     return pl.BlockSpec(memory_space=memory)
 
 
-def params():
-    return pltpu.CompilerParams(vmem_limit_bytes=VMEM_LIMIT)
+def params(limit=VMEM_LIMIT):
+    return pltpu.CompilerParams(vmem_limit_bytes=limit)
 
 
 def shards(orbitals, box_index, partner_pool, potential):
@@ -356,40 +369,46 @@
 
     cosine, sine = cos_sin(side)
     cs = jnp.asarray(np.concatenate([cosine, cosine, sine, sine], axis=1))
-    half_points = (np.arange(2 * chunks * side) // side) % side
-    cyr = jnp.asarray(cosine[:, half_points])
-    syr = jnp.asarray(sine[:, half_points])
     inward = np.block([[cosine, -sine], [sine, cosine]])
     outward = np.block([[cosine, sine], [-sine, cosine]])
     wz = jnp.asarray(np.stack([inward, outward]))
 
     me = lax.axis_index("fft")
-    shifts = [[(i, (i + s) % fft_count) for i in range(fft_count)] for s in range(1, fft_count)]
+    me_row = me.reshape(1)
+    onward = [[(i, (i + s) % fft_count) for i in range(fft_count)] for s in range(fft_count)]
+    home = [[(j, i) for i, j in pairs] for pairs in onward]
     pool_count = lax.axis_size("pool")
     rows = 2 * share
     packed = waves + side * STICK_DEV // rows + LANES
-
-    ordered, rank = pl.pallas_call(
+    scalars, blocks = whole(pltpu.SMEM), [whole()] * fft_count
+
+    *ordered, ordered_all, rank = pl.pallas_call(
         functools.partial(sort_kernel, side, fft_count),
-        out_shape=(
-            jax.ShapeDtypeStruct((fft_count, rows, packed), BF16),
+        out_shape=[jax.ShapeDtypeStruct((rows, packed), BF16)] * fft_count
+        + [
+            jax.ShapeDtypeStruct((2 * bands, waves), BF16),
             jax.ShapeDtypeStruct((1, waves), jnp.int32),
-        ),
-        in_specs=[whole(), whole(pltpu.HBM)],
-        out_specs=(whole(), whole()),
-        scratch_shapes=[pltpu.VMEM((2 * bands, waves), BF16), pltpu.SemaphoreType.DMA],
-        compiler_params=params(),
+        ],
+        in_specs=[scalars, whole(), whole(pltpu.HBM)],
+        out_specs=blocks + [whole(), whole()],
+        scratch_shapes=[
+            pltpu.VMEM((2 * bands, waves), BF16),
+            pltpu.VMEM((waves // 256 * 2 * bands, waves), BF16),
+            pltpu.VMEM((waves // 256 * 2 * bands, 256), F32),
+            pltpu.SemaphoreType.DMA,
+        ],
+        compiler_params=params(SORT_LIMIT),
         name="sort_waves",
-    )(box_index.reshape(1, waves), coeffs)
-    moved = lax.all_to_all(ordered, "fft", split_axis=0, concat_axis=0, tiled=True)
+    )(me_row, box_index.reshape(1, waves), coeffs)
+    moved = [ordered[0]] + [lax.ppermute(ordered[s], "fft", onward[s]) for s in range(1, fft_count)]
 
     spread = lax.all_to_all(
-        coeffs.reshape(pool_count, 2 * bands // pool_count, waves), "pool", 0, 0, tiled=True
+        ordered_all.reshape(pool_count, 2 * bands // pool_count, waves), "pool", 0, 0, tiled=True
     )
     chosen = pl.pallas_call(
         select_kernel,
         out_shape=jax.ShapeDtypeStruct(spread.shape, BF16),
-        in_specs=[whole(pltpu.SMEM), whole(pl.ANY)],
+        in_specs=[scalars, whole(pl.ANY)],
         out_specs=whole(pl.ANY),
         scratch_shapes=[pltpu.SemaphoreType.DMA((pool_count,))],
         compiler_params=params(),
@@ -397,22 +416,26 @@
     )(partner_pool, spread)
     partner = lax.all_to_all(chosen, "pool", 0, 0, tiled=True).reshape(2 * bands, waves)
 
-    field = pl.pallas_call(
+    field, cyr, syr = pl.pallas_call(
         functools.partial(field_kernel, side, chunks),
-        out_shape=jax.ShapeDtypeStruct((4, side, chunks * LANES), F32),
-        in_specs=[whole()],
-        out_specs=whole(),
+        out_shape=(
+            jax.ShapeDtypeStruct((4, side, chunks * LANES), F32),
+            jax.ShapeDtypeStruct((side, chunks * LANES), BF16),
+            jax.ShapeDtypeStruct((side, chunks * LANES), BF16),
+        ),
+        in_specs=[whole(), whole()],
+        out_specs=(whole(),) * 3,
         compiler_params=params(),
         cost_estimate=pl.CostEstimate(flops=10**9, bytes_accessed=10**7, transcendentals=0),
         name="field_pairs",
-    )(potential.reshape(side * side, 2 * side))
+    )(potential.reshape(side * side, 2 * side), cs)
 
     team = min(4, share)
     back = pl.pallas_call(
-        functools.partial(box_kernel, side, chunks, team, waves),
-        out_shape=jax.ShapeDtypeStruct((fft_count, rows, waves), BF16),
-        in_specs=[whole()] * 6,
-        out_specs=whole(),
+        functools.partial(box_kernel, side, chunks, team, waves, fft_count),
+        out_shape=[jax.ShapeDtypeStruct((rows, waves), BF16)] * fft_count,
+        in_specs=blocks + [whole()] * 5,
+        out_specs=blocks,
         scratch_shapes=[
             pltpu.VMEM((2, fft_count, rows, waves), BF16),
             pltpu.VMEM((columns // LANES, rows * side, LANES), F32),
@@ -428,27 +451,22 @@
         compiler_params=params(),
         cost_estimate=pl.CostEstimate(flops=10**10, bytes_accessed=10**7, transcendentals=0),
         name="box_work",
-    )(moved, field, cs, cyr, syr, wz)
-    returned = lax.all_to_all(back, "fft", split_axis=0, concat_axis=0, tiled=True)
-
-    ordered_partner = pl.pallas_call(
-        partner_kernel,
-        out_shape=jax.ShapeDtypeStruct((2 * bands, waves), BF16),
-        in_specs=[whole(), whole()],
-        out_specs=whole(),
-        compiler_params=params(),
-        cost_estimate=pl.CostEstimate(flops=10**9, bytes_accessed=10**7, transcendentals=0),
-        name="sort_partner",
-    )(partner, rank)
-    sums = pl.pallas_call(
-        couple_kernel,
-        out_shape=jax.ShapeDtypeStruct((2, bands, bands), BF16),
-        in_specs=[whole(), whole()],
-        out_specs=whole(),
+    )(*moved, field, cs, cyr, syr, wz)
+    returned = [back[0]] + [lax.ppermute(back[s], "fft", home[s]) for s in range(1, fft_count)]
+
+    sorted_response, sums = pl.pallas_call(
+        functools.partial(couple_kernel, fft_count),
+        out_shape=(
+            jax.ShapeDtypeStruct((2 * bands, waves), BF16),
+            jax.ShapeDtypeStruct((2, bands, bands), BF16),
+        ),
+        in_specs=[scalars] + blocks + [whole()],
+        out_specs=(whole(), whole()),
+        scratch_shapes=[pltpu.VMEM((2 * bands, waves), F32)],
         compiler_params=params(),
         name="couple",
-    )(returned, ordered_partner)
-    shares = [sums] + [lax.ppermute(sums, "fft", shift) for shift in shifts]
+    )(me_row, *returned, partner)
+    shares = [sums] + [lax.ppermute(sums, "fft", onward[s]) for s in range(1, fft_count)]
     response = pl.pallas_call(
         unsort_kernel,
         out_shape=jax.ShapeDtypeStruct((2 * bands, waves), BF16),
@@ -457,7 +475,7 @@
         compiler_params=params(),
         cost_estimate=pl.CostEstimate(flops=10**9, bytes_accessed=10**7, transcendentals=0),
         name="unsort",
-    )(returned, rank)
+    )(sorted_response, rank)
     summed = None
     for d in range(fft_count):
         offset = lax.rem(me + fft_count - d, fft_count)

time: 94.4 us -> 79.2 us (0.84)
  waiting for transfers between devices: 26.9 us -> 13.3 us
  Pallas kernels: 39.9 us -> 37.4 us
  starting transfers between devices: 19.5 us -> 21.2 us
    all_to_all x3 -> x1, waiting for transfers between devices: 24.1 us -> 0.01 us  [shards(): lax.all_to_all(ordered_all.reshape(pool_count, 2 * bands // pool_count, w...]
    ppermute x3 -> x9, waiting for transfers between devices: 2.87 us -> 13.3 us  [the longest x3 11.6 us: shards(): lax.ppermute(back[s], 'fft', home[s])]
    ppermute x3 -> x9, starting transfers between devices: 2.13 us -> 11.8 us  [the longest x3 5.51 us: shards(): lax.ppermute(ordered[s], 'fft', onward[s])]
    all_to_all x3 -> x1, starting transfers between devices: 13.5 us -> 5.19 us  [shards(): lax.all_to_all(ordered_all.reshape(pool_count, 2 * bands // pool_count, w...]
    pallas_call x4 -> x3, Pallas kernels: 30.6 us -> 28.8 us  [the longest x1 25.9 us: shards(): pl.pallas_call(functools.partial(box_kernel, side, chunks, team, waves, f...]
  transfers between devices with their start and end apart: 7 -> 11, of which waited for: 5 -> 3; matrix products, arithmetic and copies ran while one was open for 0% -> 0% of each run, Pallas kernels for 42% -> 40%
where the time goes in v4:
time: 79.2 us; the launch traced here: 78.8 us
  Pallas kernels  37.4 us (47%)
  starting transfers between devices  21.2 us (27%)
  waiting for transfers between devices  13.3 us (17%)
  local copies, waits for them, and re-layouts  5.38 us (7%)
    pallas_call x1, Pallas kernels, shards(): pl.pallas_call(functools.partial(box_kernel, side, chunks, team, waves, f...  25.9 us
    ppermute x3, waiting for transfers between devices, shards(): lax.ppermute(back[s], 'fft', home[s])  11.6 us
    ppermute x3, starting transfers between devices, shards(): lax.ppermute(ordered[s], 'fft', onward[s])  5.51 us
    unnamed x18, local copies, waits for them, and re-layouts  5.38 us
    all_to_all x1, starting transfers between devices, shards(): lax.all_to_all(ordered_all.reshape(pool_count, 2 * bands // pool_count, w...  5.19 us
    pallas_call x1, Pallas kernels, shards(): pl.pallas_call(functools.partial(sort_kernel, side, fft_count), out_shape...  5.14 us
    all_to_all x1, starting transfers between devices, shards(): lax.all_to_all(chosen, 'pool', 0, 0, tiled=True).reshape(2 * bands, waves)  4.21 us
    ppermute x3, starting transfers between devices, shards(): lax.ppermute(sums, 'fft', onward[s])  3.43 us
  transfers between devices with their start and end apart: 11, of which 3 were waited for; matrix products, arithmetic and copies ran while one was open for 0% of the time, Pallas kernels for 40%

profile of v4, /device:TPU:0, one launch (start us, length us, event | category | flops | bytes accessed | tf_op | source)
XLA Modules:
  0.0 78.8 jit_solution(4345690300810339990)
XLA Ops:
  0.6 5.1 %sort_waves.1 = (bf16[32,2304]{1,0:T(8,128)(2,1)}, bf16[32,2304]{1,0:T(8,128)(2,1)}, bf16[32,2304]{1,0:T(8,128)(2,1)}, bf16[32,2304]{1,0:T(8,128)(2,1)}, bf16[128,2048]{1,0:T(8,128)(2,1)}, /*index=5*/s32[1,2048]{1,0:T(1,128)}) custom-call(s32[1]{0:T(128)} %bitcast.me_ref, s32[1,2048]{1,0:T(1,128)} %bitcast.17, bf16[128,2048]{1,0:T(8,128)(2,1)} %bitcast.15), custom_call_target="tpu_custom_call" | custom-call | tf_op jit(solution)/shard_map/sort_waves/pallas_call | solution.py:385
  5.8 0.0 copy-start
  5.8 5.2 %all-to-all-start = ((bf16[8,16,2048]{2,1,0:T(8,128)(2,1)}), bf16[8,16,2048]{2,1,0:T(8,128)(2,1)S(1)}, u32[]{:S(2)}, u32[]{:S(2)}) async-start(bf16[8,16,2048]{2,1,0:T(8,128)(2,1)} %bitcast.16), calls=%async_computation | async-start | bytes 1048576 | tf_op jit(solution)/shard_map/all_to_all | solution.py:405
  11.0 1.6 %collective-permute-start = (bf16[32,2304]{1,0:T(8,128)(2,1)}, bf16[32,2304]{1,0:T(8,128)(2,1)S(1)}, u32[]{:S(2)}, u32[]{:S(2)}) collective-permute-start(bf16[32,2304]{1,0:T(8,128)(2,1)} %get-tuple-element.18), channel_id=1, source_target_pairs={{0,1},{1,2},{2,3},{3,0},{4,5},{5,6},{6,7},{7,4},{8,9},{9,10},{10,1... | collective-permute-start | bytes 442376 | tf_op jit(solution)/shard_map/ppermute | solution.py:403
  12.5 2.6 %collective-permute-start.1 = (bf16[32,2304]{1,0:T(8,128)(2,1)}, bf16[32,2304]{1,0:T(8,128)(2,1)S(1)}, u32[]{:S(2)}, u32[]{:S(2)}) collective-permute-start(bf16[32,2304]{1,0:T(8,128)(2,1)} %get-tuple-element.19), channel_id=1, source_target_pairs={{0,2},{1,3},{2,0},{3,1},{4,6},{5,7},{6,4},{7,5},{8,10},{9,11},{10,... | collective-permute-start | bytes 442376 | tf_op jit(solution)/shard_map/ppermute | solution.py:403
  15.2 1.3 %collective-permute-start.2 = (bf16[32,2304]{1,0:T(8,128)(2,1)}, bf16[32,2304]{1,0:T(8,128)(2,1)S(1)}, u32[]{:S(2)}, u32[]{:S(2)}) collective-permute-start(bf16[32,2304]{1,0:T(8,128)(2,1)} %get-tuple-element.20), channel_id=1, source_target_pairs={{0,3},{1,0},{2,1},{3,2},{4,7},{5,4},{6,5},{7,6},{8,11},{9,8},{10,9... | collective-permute-start | bytes 442376 | tf_op jit(solution)/shard_map/ppermute | solution.py:403
  16.5 0.0 copy-start.1
  16.5 1.6 %copy-done.1 = f32[64,64,128]{2,1,0:T(8,128)S(1)} copy-done((f32[64,64,128]{2,1,0:T(8,128)S(1)}, f32[64,64,128]{2,1,0:T(8,128)}, u32[]{:S(2)}) %copy-start.1) | copy-done | bytes 2097176
  18.1 0.0 copy-start.5
  18.1 0.8 copy-done.5
  18.8 0.0 copy-start.2
  18.8 0.0 copy-start.4
  18.8 0.0 copy-start.6
  18.8 2.3 %field_pairs.1 = (f32[4,64,2176]{2,1,0:T(8,128)S(1)}, bf16[64,2176]{1,0:T(8,128)(2,1)S(1)}, bf16[64,2176]{1,0:T(8,128)(2,1)S(1)}) custom-call(f32[4096,128]{1,0:T(8,128)S(1)} %bitcast.14, bf16[64,256]{1,0:T(8,128)(2,1)S(1)} %copy-done.5), custom_call_target="tpu_custom_call" | custom-call | flops 1000000000 | bytes 10000000 | tf_op jit(solution)/shard_map/field_pairs/pallas_call | solution.py:419
  21.2 0.0 copy-start.7
  21.2 1.4 %copy-done.7 = f32[4,64,2176]{2,1,0:T(8,128)} copy-done((f32[4,64,2176]{2,1,0:T(8,128)}, f32[4,64,2176]{2,1,0:T(8,128)S(1)}, u32[]{:S(2)}) %copy-start.7) | copy-done | bytes 2228248
  22.6 0.0 all-to-all-done.in_ref
  22.6 0.0 copy-done
  22.6 1.4 %select_partner.1 = bf16[8,16,2048]{2,1,0:T(8,128)(2,1)} custom-call(s32[8]{0:T(128)S(1)} %copy-done, bf16[8,16,2048]{2,1,0:T(8,128)(2,1)S(1)} %all-to-all-done.in_ref), custom_call_target="tpu_custom_call" | custom-call | tf_op jit(solution)/shard_map/select_partner/pallas_call | solution.py:408
  24.0 4.2 %all-to-all-start.1 = ((bf16[8,16,2048]{2,1,0:T(8,128)(2,1)}), bf16[8,16,2048]{2,1,0:T(8,128)(2,1)S(1)}, u32[]{:S(2)}, u32[]{:S(2)}) async-start(bf16[8,16,2048]{2,1,0:T(8,128)(2,1)} %select_partner.1), calls=%async_computation.1 | async-start | bytes 1048576 | tf_op jit(solution)/shard_map/all_to_all | solution.py:417
  28.2 0.0 collective-permute-done.refs_1_
  28.2 0.0 collective-permute-done.1.refs_2_
  28.2 0.0 collective-permute-done.2.refs_3_
  28.2 0.0 copy-done.2
  28.2 0.0 copy-done.4
  28.2 0.0 copy-done.6
  28.2 0.0 copy-start.8
  28.2 1.6 %copy-done.8 = f32[4,64,2176]{2,1,0:T(8,128)S(1)} copy-done((f32[4,64,2176]{2,1,0:T(8,128)S(1)}, f32[4,64,2176]{2,1,0:T(8,128)}, u32[]{:S(2)}) %copy-start.8) | copy-done | bytes 2228248
  29.9 0.0 copy-start.3
  29.9 25.9 %box_work.1 = (bf16[32,2048]{1,0:T(8,128)(2,1)S(1)}, bf16[32,2048]{1,0:T(8,128)(2,1)S(1)}, bf16[32,2048]{1,0:T(8,128)(2,1)S(1)}, bf16[32,2048]{1,0:T(8,128)(2,1)S(1)}) custom-call(bf16[32,2304]{1,0:T(8,128)(2,1)S(1)} %copy-done.2, bf16[32,2304]{1,0:T(8,128)(2,1)S(1)} %collective-permute-done.refs_1_, bf16[32,2304]{1,0:T(8,128)(2,1)S(1)} %collective-permute-done.1.refs_2_, ...), custom_call_target="tpu_custom_call" | custom-call | flops 10000000000 | bytes 10000000 | tf_op jit(solution)/shard_map/box_work/pallas_call | solution.py:434
  55.8 2.3 %collective-permute-start.3 = (bf16[32,2048]{1,0:T(8,128)(2,1)S(1)}, bf16[32,2048]{1,0:T(8,128)(2,1)S(1)}, u32[]{:S(2)}, u32[]{:S(2)}) collective-permute-start(bf16[32,2048]{1,0:T(8,128)(2,1)S(1)} %get-tuple-element.25), channel_id=1, source_target_pairs={{1,0},{2,1},{3,2},{0,3},{5,4},{6,5},{7,6},{4,7},{9,8},{10,9},{11,1... | collective-permute-start | bytes 393224 | tf_op jit(solution)/shard_map/ppermute | solution.py:455
  58.0 0.4 collective-permute-start.4
  58.4 0.2 collective-permute-start.5
  58.6 3.4 %collective-permute-done.3.refs_1_ = bf16[32,2048]{1,0:T(8,128)(2,1)S(1)} collective-permute-done((bf16[32,2048]{1,0:T(8,128)(2,1)S(1)}, bf16[32,2048]{1,0:T(8,128)(2,1)S(1)}, u32[]{:S(2)}, u32[]{:S(2)}) %collective-permute-start.3) | collective-permute-done | bytes 131104 | tf_op jit(solution)/shard_map/ppermute | solution.py:455
  62.0 8.2 %collective-permute-done.4.refs_2_ = bf16[32,2048]{1,0:T(8,128)(2,1)S(1)} collective-permute-done((bf16[32,2048]{1,0:T(8,128)(2,1)S(1)}, bf16[32,2048]{1,0:T(8,128)(2,1)S(1)}, u32[]{:S(2)}, u32[]{:S(2)}) %collective-permute-start.4) | collective-permute-done | bytes 131104 | tf_op jit(solution)/shard_map/ppermute | solution.py:455
  70.3 0.0 collective-permute-done.5.refs_3_
  70.3 0.0 all-to-all-done.1
  70.3 0.6 couple.1
  70.9 0.4 collective-permute-start.6
  71.3 1.1 %collective-permute-start.7 = (bf16[2,64,64]{2,1,0:T(8,128)(2,1)S(1)}, bf16[2,64,64]{2,1,0:T(8,128)(2,1)S(1)}, u32[]{:S(2)}, u32[]{:S(2)}) collective-permute-start(bf16[2,64,64]{2,1,0:T(8,128)(2,1)S(1)} %get-tuple-element.31), channel_id=1, source_target_pairs={{0,2},{1,3},{2,0},{3,1},{4,6},{5,7},{6,4},{7,5},{8,10},{9,11},{10,... | collective-permute-start | bytes 49160 | tf_op jit(solution)/shard_map/ppermute | solution.py:469
  72.4 1.9 %collective-permute-start.8 = (bf16[2,64,64]{2,1,0:T(8,128)(2,1)S(1)}, bf16[2,64,64]{2,1,0:T(8,128)(2,1)S(1)}, u32[]{:S(2)}, u32[]{:S(2)}) collective-permute-start(bf16[2,64,64]{2,1,0:T(8,128)(2,1)S(1)} %get-tuple-element.31), channel_id=1, source_target_pairs={{0,1},{1,2},{2,3},{3,0},{4,5},{5,6},{6,7},{7,4},{8,9},{9,10},{10,1... | collective-permute-start | bytes 49160 | tf_op jit(solution)/shard_map/ppermute | solution.py:469
  74.3 0.0 copy-done.3
  74.3 2.1 %unsort.1 = bf16[128,2048]{1,0:T(8,128)(2,1)} custom-call(bf16[128,2048]{1,0:T(8,128)(2,1)S(1)} %get-tuple-element.29.y_ref, s32[1,2048]{1,0:T(1,128)S(1)} %copy-done.3), custom_call_target="tpu_custom_call" | custom-call | flops 1000000000 | bytes 10000000 | tf_op jit(solution)/shard_map/unsort/pallas_call | solution.py:470
  76.4 0.0 collective-permute-done.6
  76.4 0.0 collective-permute-done.7
  76.4 1.7 %collective-permute-done.8 = bf16[2,64,64]{2,1,0:T(8,128)(2,1)S(1)} collective-permute-done((bf16[2,64,64]{2,1,0:T(8,128)(2,1)S(1)}, bf16[2,64,64]{2,1,0:T(8,128)(2,1)S(1)}, u32[]{:S(2)}, u32[]{:S(2)}) %collective-permute-start.8) | collective-permute-done | bytes 16416 | tf_op jit(solution)/shard_map/ppermute | solution.py:469
  78.1 0.7 multiply_bitcast_fusion
Async XLA Ops:
  5.8 16.8 %copy-start = (s32[8]{0:T(128)S(1)}, s32[8]{0:T(128)}, u32[]{:S(2)}) copy-start(s32[8]{0:T(128)} %order_ref.1) | copy-start | bytes 100
  5.8 16.8 %all-to-all-start = ((bf16[8,16,2048]{2,1,0:T(8,128)(2,1)}), bf16[8,16,2048]{2,1,0:T(8,128)(2,1)S(1)}, u32[]{:S(2)}, u32[]{:S(2)}) async-start(bf16[8,16,2048]{2,1,0:T(8,128)(2,1)} %bitcast.16), calls=%async_computation | async-start | bytes 1048576 | tf_op jit(solution)/shard_map/all_to_all | solution.py:405
  11.0 17.2 %collective-permute-start = (bf16[32,2304]{1,0:T(8,128)(2,1)}, bf16[32,2304]{1,0:T(8,128)(2,1)S(1)}, u32[]{:S(2)}, u32[]{:S(2)}) collective-permute-start(bf16[32,2304]{1,0:T(8,128)(2,1)} %get-tuple-element.18), channel_id=1, source_target_pairs={{0,1},{1,2},{2,3},{3,0},{4,5},{5,6},{6,7},{7,4},{8,9},{9,10},{10,1... | collective-permute-start | bytes 442376 | tf_op jit(solution)/shard_map/ppermute | solution.py:403
  12.5 15.6 %collective-permute-start.1 = (bf16[32,2304]{1,0:T(8,128)(2,1)}, bf16[32,2304]{1,0:T(8,128)(2,1)S(1)}, u32[]{:S(2)}, u32[]{:S(2)}) collective-permute-start(bf16[32,2304]{1,0:T(8,128)(2,1)} %get-tuple-element.19), channel_id=1, source_target_pairs={{0,2},{1,3},{2,0},{3,1},{4,6},{5,7},{6,4},{7,5},{8,10},{9,11},{10,... | collective-permute-start | bytes 442376 | tf_op jit(solution)/shard_map/ppermute | solution.py:403
  15.2 13.0 %collective-permute-start.2 = (bf16[32,2304]{1,0:T(8,128)(2,1)}, bf16[32,2304]{1,0:T(8,128)(2,1)S(1)}, u32[]{:S(2)}, u32[]{:S(2)}) collective-permute-start(bf16[32,2304]{1,0:T(8,128)(2,1)} %get-tuple-element.20), channel_id=1, source_target_pairs={{0,3},{1,0},{2,1},{3,2},{4,7},{5,4},{6,5},{7,6},{8,11},{9,8},{10,9... | collective-permute-start | bytes 442376 | tf_op jit(solution)/shard_map/ppermute | solution.py:403
  16.5 1.6 %copy-start.1 = (f32[64,64,128]{2,1,0:T(8,128)S(1)}, f32[64,64,128]{2,1,0:T(8,128)}, u32[]{:S(2)}) copy-start(f32[64,64,128]{2,1,0:T(8,128)} %param.9) | copy-start | bytes 6291460
  18.1 0.8 copy-start.5
  18.8 9.4 %copy-start.2 = (bf16[32,2304]{1,0:T(8,128)(2,1)S(1)}, bf16[32,2304]{1,0:T(8,128)(2,1)}, u32[]{:S(2)}) copy-start(bf16[32,2304]{1,0:T(8,128)(2,1)} %get-tuple-element.17.refs_0_) | copy-start | bytes 442372
  18.8 9.4 %copy-start.4 = (bf16[2,128,128]{2,1,0:T(8,128)(2,1)S(1)}, bf16[2,128,128]{2,1,0:T(8,128)(2,1)}, u32[]{:S(2)}) copy-start(bf16[2,128,128]{2,1,0:T(8,128)(2,1)} %constant.35.clone.refs_8_) | copy-start | bytes 196612
  18.8 9.4 %copy-start.6 = (bf16[64,256]{1,0:T(8,128)(2,1)S(1)}, bf16[64,256]{1,0:T(8,128)(2,1)}, u32[]{:S(2)}) copy-start(bf16[64,256]{1,0:T(8,128)(2,1)} %constant.34.clone.cs_ref.refs_5_) | copy-start | bytes 98308
  21.2 1.4 %copy-start.7 = (f32[4,64,2176]{2,1,0:T(8,128)}, f32[4,64,2176]{2,1,0:T(8,128)S(1)}, u32[]{:S(2)}) copy-start(f32[4,64,2176]{2,1,0:T(8,128)S(1)} %get-tuple-element.21.refs_4_) | copy-start | bytes 6684676
  24.0 46.3 %all-to-all-start.1 = ((bf16[8,16,2048]{2,1,0:T(8,128)(2,1)}), bf16[8,16,2048]{2,1,0:T(8,128)(2,1)S(1)}, u32[]{:S(2)}, u32[]{:S(2)}) async-start(bf16[8,16,2048]{2,1,0:T(8,128)(2,1)} %select_partner.1), calls=%async_computation.1 | async-start | bytes 1048576 | tf_op jit(solution)/shard_map/all_to_all | solution.py:417
  28.2 1.6 %copy-start.8 = (f32[4,64,2176]{2,1,0:T(8,128)S(1)}, f32[4,64,2176]{2,1,0:T(8,128)}, u32[]{:S(2)}) copy-start(f32[4,64,2176]{2,1,0:T(8,128)} %copy-done.7) | copy-start | bytes 6684676
  29.9 44.5 %copy-start.3 = (s32[1,2048]{1,0:T(1,128)S(1)}, s32[1,2048]{1,0:T(1,128)}, u32[]{:S(2)}) copy-start(s32[1,2048]{1,0:T(1,128)} %get-tuple-element.30.rank_ref) | copy-start | bytes 24580
  55.8 6.3 %collective-permute-start.3 = (bf16[32,2048]{1,0:T(8,128)(2,1)S(1)}, bf16[32,2048]{1,0:T(8,128)(2,1)S(1)}, u32[]{:S(2)}, u32[]{:S(2)}) collective-permute-start(bf16[32,2048]{1,0:T(8,128)(2,1)S(1)} %get-tuple-element.25), channel_id=1, source_target_pairs={{1,0},{2,1},{3,2},{0,3},{5,4},{6,5},{7,6},{4,7},{9,8},{10,9},{11,1... | collective-permute-start | bytes 393224 | tf_op jit(solution)/shard_map/ppermute | solution.py:455
  58.0 12.3 %collective-permute-start.4 = (bf16[32,2048]{1,0:T(8,128)(2,1)S(1)}, bf16[32,2048]{1,0:T(8,128)(2,1)S(1)}, u32[]{:S(2)}, u32[]{:S(2)}) collective-permute-start(bf16[32,2048]{1,0:T(8,128)(2,1)S(1)} %get-tuple-element.26), channel_id=1, source_target_pairs={{2,0},{3,1},{0,2},{1,3},{6,4},{7,5},{4,6},{5,7},{10,8},{11,9},{8,1... | collective-permute-start | bytes 393224 | tf_op jit(solution)/shard_map/ppermute | solution.py:455
  58.4 11.9 %collective-permute-start.5 = (bf16[32,2048]{1,0:T(8,128)(2,1)S(1)}, bf16[32,2048]{1,0:T(8,128)(2,1)S(1)}, u32[]{:S(2)}, u32[]{:S(2)}) collective-permute-start(bf16[32,2048]{1,0:T(8,128)(2,1)S(1)} %get-tuple-element.27), channel_id=1, source_target_pairs={{3,0},{0,1},{1,2},{2,3},{7,4},{4,5},{5,6},{6,7},{11,8},{8,9},{9,10... | collective-permute-start | bytes 393224 | tf_op jit(solution)/shard_map/ppermute | solution.py:455
  70.9 5.5 %collective-permute-start.6 = (bf16[2,64,64]{2,1,0:T(8,128)(2,1)S(1)}, bf16[2,64,64]{2,1,0:T(8,128)(2,1)S(1)}, u32[]{:S(2)}, u32[]{:S(2)}) collective-permute-start(bf16[2,64,64]{2,1,0:T(8,128)(2,1)S(1)} %get-tuple-element.31), channel_id=1, source_target_pairs={{0,3},{1,0},{2,1},{3,2},{4,7},{5,4},{6,5},{7,6},{8,11},{9,8},{10,9... | collective-permute-start | bytes 49160 | tf_op jit(solution)/shard_map/ppermute | solution.py:469
  71.3 5.1 %collective-permute-start.7 = (bf16[2,64,64]{2,1,0:T(8,128)(2,1)S(1)}, bf16[2,64,64]{2,1,0:T(8,128)(2,1)S(1)}, u32[]{:S(2)}, u32[]{:S(2)}) collective-permute-start(bf16[2,64,64]{2,1,0:T(8,128)(2,1)S(1)} %get-tuple-element.31), channel_id=1, source_target_pairs={{0,2},{1,3},{2,0},{3,1},{4,6},{5,7},{6,4},{7,5},{8,10},{9,11},{10,... | collective-permute-start | bytes 49160 | tf_op jit(solution)/shard_map/ppermute | solution.py:469
  72.4 5.7 %collective-permute-start.8 = (bf16[2,64,64]{2,1,0:T(8,128)(2,1)S(1)}, bf16[2,64,64]{2,1,0:T(8,128)(2,1)S(1)}, u32[]{:S(2)}, u32[]{:S(2)}) collective-permute-start(bf16[2,64,64]{2,1,0:T(8,128)(2,1)S(1)} %get-tuple-element.31), channel_id=1, source_target_pairs={{0,1},{1,2},{2,3},{3,0},{4,5},{5,6},{6,7},{7,4},{8,9},{9,10},{10,1... | collective-permute-start | bytes 49160 | tf_op jit(solution)/shard_map/ppermute | solution.py:469

commit v5 on v4

--- a/solution.py
+++ b/solution.py
@@ -11,11 +11,12 @@
 
 STICK_DEV = 64
 LANES = 128
-UNROLL = 4
+UNROLL = 16
 BF16 = jnp.bfloat16
 F32 = jnp.float32
 VMEM_LIMIT = 24 * 1024 * 1024
 SORT_LIMIT = 60 * 1024 * 1024
+ARRANGE_COST = 10**11
 
 
 def cos_sin(side):
@@ -109,14 +110,15 @@
         here = slice(part * 256, (part + 1) * 256)
         all_ref[:, here] = pieces[part * both : (part + 1) * both].astype(BF16)
         for shift, out in enumerate(outs):
-            q = lax.rem(me_ref[0] + shift, groups)
+            q = me_ref[0] ^ shift
             begin = pl.multiple_of(part * both + q * share, 8)
             re = pieces[pl.ds(begin, share)]
             im = pieces[pl.ds(begin + bands, share)]
             out[:, here] = jnp.concatenate([re, im], axis=0).astype(BF16)
 
 
-def field_kernel(side, chunks, pot_ref, cs_ref, field_ref, cyr_ref, syr_ref):
+def field_kernel(side, chunks, pot_ref, cs_ref, waves_ref, field_ref, cyr_ref, syr_ref, copy_ref):
+    copy_ref[...] = waves_ref[...]
     half = side // 2
     left = lax.broadcasted_iota(jnp.int32, (side, LANES), 1) < side
     for ref, begin in ((cyr_ref, 0), (syr_ref, LANES)):
@@ -318,18 +320,21 @@
         out_refs[d][...] = (acc[0, d] + late).astype(BF16)
 
 
-def couple_kernel(groups, me_ref, *refs):
-    y_refs, (partner_ref, sorted_ref, g_ref, rows_scr) = refs[:groups], refs[groups:]
+def arrange_kernel(groups, me_ref, *refs):
+    y_refs, (sorted_ref, rows_scr) = refs[:groups], refs[groups:]
     share = y_refs[0].shape[0] // 2
     half = groups * share
     for shift, y_ref in enumerate(y_refs):
-        begin = pl.multiple_of(lax.rem(me_ref[0] + shift, groups) * share, 8)
+        begin = pl.multiple_of((me_ref[0] ^ shift) * share, 8)
         value = y_ref[...].astype(F32)
         rows_scr[pl.ds(begin, share)] = value[:share]
         rows_scr[pl.ds(begin + half, share)] = value[share:]
-    response = rows_scr[...].astype(BF16)
-    sorted_ref[...] = response
-    products = dot_nt(partner_ref[...], response)
+    sorted_ref[...] = rows_scr[...].astype(BF16)
+
+
+def couple_kernel(partner_ref, sorted_ref, g_ref):
+    products = dot_nt(partner_ref[...], sorted_ref[...])
+    half = products.shape[0] // 2
     g_ref[0] = (products[:half, :half] + products[half:, half:]).astype(BF16)
     g_ref[1] = (products[:half, half:] - products[half:, :half]).astype(BF16)
 
@@ -375,8 +380,7 @@
 
     me = lax.axis_index("fft")
     me_row = me.reshape(1)
-    onward = [[(i, (i + s) % fft_count) for i in range(fft_count)] for s in range(fft_count)]
-    home = [[(j, i) for i, j in pairs] for pairs in onward]
+    pairs = [[(i, i ^ s) for i in range(fft_count)] for s in range(fft_count)]
     pool_count = lax.axis_size("pool")
     rows = 2 * share
     packed = waves + side * STICK_DEV // rows + LANES
@@ -400,35 +404,22 @@
         compiler_params=params(SORT_LIMIT),
         name="sort_waves",
     )(me_row, box_index.reshape(1, waves), coeffs)
-    moved = [ordered[0]] + [lax.ppermute(ordered[s], "fft", onward[s]) for s in range(1, fft_count)]
-
-    spread = lax.all_to_all(
-        ordered_all.reshape(pool_count, 2 * bands // pool_count, waves), "pool", 0, 0, tiled=True
-    )
-    chosen = pl.pallas_call(
-        select_kernel,
-        out_shape=jax.ShapeDtypeStruct(spread.shape, BF16),
-        in_specs=[scalars, whole(pl.ANY)],
-        out_specs=whole(pl.ANY),
-        scratch_shapes=[pltpu.SemaphoreType.DMA((pool_count,))],
-        compiler_params=params(),
-        name="select_partner",
-    )(partner_pool, spread)
-    partner = lax.all_to_all(chosen, "pool", 0, 0, tiled=True).reshape(2 * bands, waves)
-
-    field, cyr, syr = pl.pallas_call(
+    moved = [ordered[0]] + [lax.ppermute(ordered[s], "fft", pairs[s]) for s in range(1, fft_count)]
+
+    field, cyr, syr, passed = pl.pallas_call(
         functools.partial(field_kernel, side, chunks),
         out_shape=(
             jax.ShapeDtypeStruct((4, side, chunks * LANES), F32),
             jax.ShapeDtypeStruct((side, chunks * LANES), BF16),
             jax.ShapeDtypeStruct((side, chunks * LANES), BF16),
+            jax.ShapeDtypeStruct((2 * bands, waves), BF16),
         ),
-        in_specs=[whole(), whole()],
-        out_specs=(whole(),) * 3,
+        in_specs=[whole()] * 3,
+        out_specs=(whole(),) * 4,
         compiler_params=params(),
         cost_estimate=pl.CostEstimate(flops=10**9, bytes_accessed=10**7, transcendentals=0),
         name="field_pairs",
-    )(potential.reshape(side * side, 2 * side), cs)
+    )(potential.reshape(side * side, 2 * side), cs, ordered_all)
 
     team = min(4, share)
     back = pl.pallas_call(
@@ -452,21 +443,41 @@
         cost_estimate=pl.CostEstimate(flops=10**10, bytes_accessed=10**7, transcendentals=0),
         name="box_work",
     )(*moved, field, cs, cyr, syr, wz)
-    returned = [back[0]] + [lax.ppermute(back[s], "fft", home[s]) for s in range(1, fft_count)]
-
-    sorted_response, sums = pl.pallas_call(
-        functools.partial(couple_kernel, fft_count),
-        out_shape=(
-            jax.ShapeDtypeStruct((2 * bands, waves), BF16),
-            jax.ShapeDtypeStruct((2, bands, bands), BF16),
-        ),
-        in_specs=[scalars] + blocks + [whole()],
-        out_specs=(whole(), whole()),
+    spread = lax.all_to_all(
+        passed.reshape(pool_count, 2 * bands // pool_count, waves), "pool", 0, 0, tiled=True
+    )
+    chosen = pl.pallas_call(
+        select_kernel,
+        out_shape=jax.ShapeDtypeStruct(spread.shape, BF16),
+        in_specs=[scalars, whole(pl.ANY)],
+        out_specs=whole(pl.ANY),
+        scratch_shapes=[pltpu.SemaphoreType.DMA((pool_count,))],
+        compiler_params=params(),
+        name="select_partner",
+    )(partner_pool, spread)
+    partner = lax.all_to_all(chosen, "pool", 0, 0, tiled=True).reshape(2 * bands, waves)
+
+    returned = [back[0]] + [lax.ppermute(back[s], "fft", pairs[s]) for s in range(1, fft_count)]
+
+    sorted_response = pl.pallas_call(
+        functools.partial(arrange_kernel, fft_count),
+        out_shape=jax.ShapeDtypeStruct((2 * bands, waves), BF16),
+        in_specs=[scalars] + blocks,
+        out_specs=whole(),
         scratch_shapes=[pltpu.VMEM((2 * bands, waves), F32)],
         compiler_params=params(),
+        cost_estimate=pl.CostEstimate(flops=ARRANGE_COST, bytes_accessed=10**6, transcendentals=0),
+        name="arrange",
+    )(me_row, *returned)
+    sums = pl.pallas_call(
+        couple_kernel,
+        out_shape=jax.ShapeDtypeStruct((2, bands, bands), BF16),
+        in_specs=[whole(), whole()],
+        out_specs=whole(),
+        compiler_params=params(),
         name="couple",
-    )(me_row, *returned, partner)
-    shares = [sums] + [lax.ppermute(sums, "fft", onward[s]) for s in range(1, fft_count)]
+    )(partner, sorted_response)
+    shares = [sums] + [lax.ppermute(sums, "fft", pairs[s]) for s in range(1, fft_count)]
     response = pl.pallas_call(
         unsort_kernel,
         out_shape=jax.ShapeDtypeStruct((2 * bands, waves), BF16),
@@ -478,7 +489,7 @@
     )(sorted_response, rank)
     summed = None
     for d in range(fft_count):
-        offset = lax.rem(me + fft_count - d, fft_count)
+        offset = me ^ d
         term = shares[0]
         for s in range(1, fft_count):
             term = jnp.where(offset == s, shares[s], term)

time: 79.2 us -> 76.9 us (0.971)
  Pallas kernels: 37.4 us -> 34.3 us
  waiting for transfers between devices: 13.3 us -> 11.6 us
  starting transfers between devices: 21.2 us -> 22.7 us
  local copies, waits for them, and re-layouts: 5.38 us -> 6.42 us
    ppermute x9, waiting for transfers between devices: 13.3 us -> 6.97 us  [the longest x3 5.02 us: shards(): lax.ppermute(back[s], 'fft', pairs[s])]
    all_to_all x1, waiting for transfers between devices: 0.01 us -> 4.59 us  [shards(): lax.all_to_all(chosen, 'pool', 0, 0, tiled=True).reshape(2 * bands, waves)]
    pallas_call x1, Pallas kernels: 25.9 us -> 22.2 us  [shards(): pl.pallas_call(functools.partial(box_kernel, side, chunks, team, waves, f...]
    ppermute x9, starting transfers between devices: 11.8 us -> 14.7 us  [the longest x3 5.7 us: shards(): lax.ppermute(ordered[s], 'fft', pairs[s])]
    all_to_all x1, starting transfers between devices: 5.19 us -> 3.93 us  [shards(): lax.all_to_all(passed.reshape(pool_count, 2 * bands // pool_count, waves)...]
    unnamed x18 -> x20, local copies, waits for them, and re-layouts: 5.38 us -> 6.42 us
  transfers between devices with their start and end apart: 11 -> 11, of which waited for: 3 -> 3; matrix products, arithmetic and copies ran while one was open for 0% -> 0% of each run, Pallas kernels for 40% -> 38%
where the time goes in v5:
time: 76.9 us; the launch traced here: 76.4 us
  Pallas kernels  34.3 us (45%)
  starting transfers between devices  22.7 us (30%)
  waiting for transfers between devices  11.6 us (15%)
  local copies, waits for them, and re-layouts  6.42 us (8%)
    pallas_call x1, Pallas kernels, shards(): pl.pallas_call(functools.partial(box_kernel, side, chunks, team, waves, f...  22.2 us
    unnamed x20, local copies, waits for them, and re-layouts  6.42 us
    ppermute x3, starting transfers between devices, shards(): lax.ppermute(ordered[s], 'fft', pairs[s])  5.7 us
    pallas_call x1, Pallas kernels, shards(): pl.pallas_call(functools.partial(sort_kernel, side, fft_count), out_shape...  5.07 us
    ppermute x3, waiting for transfers between devices, shards(): lax.ppermute(back[s], 'fft', pairs[s])  5.02 us
    ppermute x3, starting transfers between devices, shards(): lax.ppermute(back[s], 'fft', pairs[s])  4.63 us
    all_to_all x1, waiting for transfers between devices, shards(): lax.all_to_all(chosen, 'pool', 0, 0, tiled=True).reshape(2 * bands, waves)  4.59 us
    ppermute x3, starting transfers between devices, shards(): lax.ppermute(sums, 'fft', pairs[s])  4.42 us
  transfers between devices with their start and end apart: 11, of which 3 were waited for; matrix products, arithmetic and copies ran while one was open for 0% of the time, Pallas kernels for 38%

profile of v5, /device:TPU:0, one launch (start us, length us, event | category | flops | bytes accessed | tf_op | source)
XLA Modules:
  0.0 76.4 jit_solution(15660939746047635719)
XLA Ops:
  0.6 5.1 %sort_waves.1 = (bf16[32,2304]{1,0:T(8,128)(2,1)}, bf16[32,2304]{1,0:T(8,128)(2,1)}, bf16[32,2304]{1,0:T(8,128)(2,1)}, bf16[32,2304]{1,0:T(8,128)(2,1)}, bf16[128,2048]{1,0:T(8,128)(2,1)}, /*index=5*/s32[1,2048]{1,0:T(1,128)}) custom-call(s32[1]{0:T(128)} %bitcast.me_ref, s32[1,2048]{1,0:T(1,128)} %bitcast.16, bf16[128,2048]{1,0:T(8,128)(2,1)} %bitcast.15), custom_call_target="tpu_custom_call" | custom-call | tf_op jit(solution)/shard_map/sort_waves/pallas_call | solution.py:389
  5.7 3.1 %collective-permute-start = (bf16[32,2304]{1,0:T(8,128)(2,1)}, bf16[32,2304]{1,0:T(8,128)(2,1)S(1)}, u32[]{:S(2)}, u32[]{:S(2)}) collective-permute-start(bf16[32,2304]{1,0:T(8,128)(2,1)} %get-tuple-element.17), channel_id=1, source_target_pairs={{0,1},{1,0},{2,3},{3,2},{4,5},{5,4},{6,7},{7,6},{8,9},{9,8},{10,11... | collective-permute-start | bytes 442376 | tf_op jit(solution)/shard_map/ppermute | solution.py:407
  8.8 2.6 %collective-permute-start.1 = (bf16[32,2304]{1,0:T(8,128)(2,1)}, bf16[32,2304]{1,0:T(8,128)(2,1)S(1)}, u32[]{:S(2)}, u32[]{:S(2)}) collective-permute-start(bf16[32,2304]{1,0:T(8,128)(2,1)} %get-tuple-element.18), channel_id=1, source_target_pairs={{0,2},{1,3},{2,0},{3,1},{4,6},{5,7},{6,4},{7,5},{8,10},{9,11},{10,... | collective-permute-start | bytes 442376 | tf_op jit(solution)/shard_map/ppermute | solution.py:407
  11.4 0.0 collective-permute-start.2
  11.4 0.0 copy-start.1
  11.4 1.6 %copy-done.1 = f32[64,64,128]{2,1,0:T(8,128)S(1)} copy-done((f32[64,64,128]{2,1,0:T(8,128)S(1)}, f32[64,64,128]{2,1,0:T(8,128)}, u32[]{:S(2)}) %copy-start.1) | copy-done | bytes 2097176
  13.0 0.0 copy-start.2
  13.0 1.0 %copy-done.2 = bf16[128,2048]{1,0:T(8,128)(2,1)S(1)} copy-done((bf16[128,2048]{1,0:T(8,128)(2,1)S(1)}, bf16[128,2048]{1,0:T(8,128)(2,1)}, u32[]{:S(2)}) %copy-start.2) | copy-done | bytes 524312
  14.0 0.0 copy-start.6
  14.0 0.8 copy-done.6
  14.8 0.0 copy-start.3
  14.8 0.0 copy-start.5
  14.8 0.0 copy-start.7
  14.8 3.0 %field_pairs.1 = (f32[4,64,2176]{2,1,0:T(8,128)S(1)}, bf16[64,2176]{1,0:T(8,128)(2,1)S(1)}, bf16[64,2176]{1,0:T(8,128)(2,1)S(1)}, bf16[128,2048]{1,0:T(8,128)(2,1)}) custom-call(f32[4096,128]{1,0:T(8,128)S(1)} %bitcast.14, bf16[64,256]{1,0:T(8,128)(2,1)S(1)} %copy-done.6, bf16[128,2048]{1,0:T(8,128)(2,1)S(1)} %copy-done.2), custom_call_target="tpu_custom_call" | custom-call | flops 1000000000 | bytes 10000000 | tf_op jit(solution)/shard_map/field_pairs/pallas_call | solution.py:409
  17.8 0.0 copy-start.8
  17.9 1.4 %copy-done.8 = f32[4,64,2176]{2,1,0:T(8,128)} copy-done((f32[4,64,2176]{2,1,0:T(8,128)}, f32[4,64,2176]{2,1,0:T(8,128)S(1)}, u32[]{:S(2)}) %copy-start.8) | copy-done | bytes 2228248
  19.2 3.9 %all-to-all-start = ((bf16[8,16,2048]{2,1,0:T(8,128)(2,1)}), bf16[8,16,2048]{2,1,0:T(8,128)(2,1)S(1)}, u32[]{:S(2)}, u32[]{:S(2)}) async-start(bf16[8,16,2048]{2,1,0:T(8,128)(2,1)} %bitcast.6), calls=%async_computation | async-start | bytes 1048576 | tf_op jit(solution)/shard_map/all_to_all | solution.py:446
  23.2 0.0 collective-permute-done.refs_1_
  23.2 0.0 collective-permute-done.1.refs_2_
  23.2 0.0 collective-permute-done.2.refs_3_
  23.2 0.0 copy-done.3
  23.2 0.0 copy-done.5
  23.2 0.0 copy-done.7
  23.2 0.0 copy-start.9
  23.2 1.6 %copy-done.9 = f32[4,64,2176]{2,1,0:T(8,128)S(1)} copy-done((f32[4,64,2176]{2,1,0:T(8,128)S(1)}, f32[4,64,2176]{2,1,0:T(8,128)}, u32[]{:S(2)}) %copy-start.9) | copy-done | bytes 2228248
  24.9 0.0 copy-start
  24.9 22.2 %box_work.1 = (bf16[32,2048]{1,0:T(8,128)(2,1)S(1)}, bf16[32,2048]{1,0:T(8,128)(2,1)S(1)}, bf16[32,2048]{1,0:T(8,128)(2,1)S(1)}, bf16[32,2048]{1,0:T(8,128)(2,1)S(1)}) custom-call(bf16[32,2304]{1,0:T(8,128)(2,1)S(1)} %copy-done.3, bf16[32,2304]{1,0:T(8,128)(2,1)S(1)} %collective-permute-done.refs_1_, bf16[32,2304]{1,0:T(8,128)(2,1)S(1)} %collective-permute-done.1.refs_2_, ...), custom_call_target="tpu_custom_call" | custom-call | flops 10000000000 | bytes 10000000 | tf_op jit(solution)/shard_map/box_work/pallas_call | solution.py:425
  47.0 2.2 %collective-permute-start.3 = (bf16[32,2048]{1,0:T(8,128)(2,1)S(1)}, bf16[32,2048]{1,0:T(8,128)(2,1)S(1)}, u32[]{:S(2)}, u32[]{:S(2)}) collective-permute-start(bf16[32,2048]{1,0:T(8,128)(2,1)S(1)} %get-tuple-element.25), channel_id=1, source_target_pairs={{0,1},{1,0},{2,3},{3,2},{4,5},{5,4},{6,7},{7,6},{8,9},{9,8},{10,11... | collective-permute-start | bytes 393224 | tf_op jit(solution)/shard_map/ppermute | solution.py:460
  49.2 2.1 %collective-permute-start.4 = (bf16[32,2048]{1,0:T(8,128)(2,1)S(1)}, bf16[32,2048]{1,0:T(8,128)(2,1)S(1)}, u32[]{:S(2)}, u32[]{:S(2)}) collective-permute-start(bf16[32,2048]{1,0:T(8,128)(2,1)S(1)} %get-tuple-element.26), channel_id=1, source_target_pairs={{0,2},{1,3},{2,0},{3,1},{4,6},{5,7},{6,4},{7,5},{8,10},{9,11},{10,... | collective-permute-start | bytes 393224 | tf_op jit(solution)/shard_map/ppermute | solution.py:460
  51.3 0.4 collective-permute-start.5
  51.7 0.0 all-to-all-done.in_ref
  51.7 0.0 copy-done
  51.7 1.4 %select_partner.1 = bf16[8,16,2048]{2,1,0:T(8,128)(2,1)} custom-call(s32[8]{0:T(128)S(1)} %copy-done, bf16[8,16,2048]{2,1,0:T(8,128)(2,1)S(1)} %all-to-all-done.in_ref), custom_call_target="tpu_custom_call" | custom-call | tf_op jit(solution)/shard_map/select_partner/pallas_call | solution.py:449
  53.1 4.0 %all-to-all-start.1 = ((bf16[8,16,2048]{2,1,0:T(8,128)(2,1)}), bf16[8,16,2048]{2,1,0:T(8,128)(2,1)S(1)}, u32[]{:S(2)}, u32[]{:S(2)}) async-start(bf16[8,16,2048]{2,1,0:T(8,128)(2,1)} %select_partner.1), calls=%async_computation.1 | async-start | bytes 1048576 | tf_op jit(solution)/shard_map/all_to_all | solution.py:458
  57.1 0.0 collective-permute-done.3.refs_1_
  57.1 5.0 %collective-permute-done.4.refs_2_ = bf16[32,2048]{1,0:T(8,128)(2,1)S(1)} collective-permute-done((bf16[32,2048]{1,0:T(8,128)(2,1)S(1)}, bf16[32,2048]{1,0:T(8,128)(2,1)S(1)}, u32[]{:S(2)}, u32[]{:S(2)}) %collective-permute-start.4) | collective-permute-done | bytes 131104 | tf_op jit(solution)/shard_map/ppermute | solution.py:460
  62.1 0.0 collective-permute-done.5.refs_3_
  62.1 0.0 copy-start.4
  62.1 0.1 arrange.1.y_ref.sorted_ref
  62.3 4.6 %all-to-all-done.1 = bf16[8,16,2048]{2,1,0:T(8,128)(2,1)S(1)} async-done(((bf16[8,16,2048]{2,1,0:T(8,128)(2,1)}), bf16[8,16,2048]{2,1,0:T(8,128)(2,1)S(1)}, u32[]{:S(2)}, u32[]{:S(2)}) %all-to-all-start.1) | async-done | bytes 524320 | tf_op jit(solution)/shard_map/all_to_all | solution.py:458
  66.8 0.4 couple.1
  67.3 3.6 %collective-permute-start.6 = (bf16[2,64,64]{2,1,0:T(8,128)(2,1)S(1)}, bf16[2,64,64]{2,1,0:T(8,128)(2,1)S(1)}, u32[]{:S(2)}, u32[]{:S(2)}) collective-permute-start(bf16[2,64,64]{2,1,0:T(8,128)(2,1)S(1)} %couple.1), channel_id=1, source_target_pairs={{0,3},{1,2},{2,1},{3,0},{4,7},{5,6},{6,5},{7,4},{8,11},{9,10},{10,... | collective-permute-start | bytes 49160 | tf_op jit(solution)/shard_map/ppermute | solution.py:480
  70.9 0.0 collective-permute-start.7
  70.9 0.8 %collective-permute-start.8 = (bf16[2,64,64]{2,1,0:T(8,128)(2,1)S(1)}, bf16[2,64,64]{2,1,0:T(8,128)(2,1)S(1)}, u32[]{:S(2)}, u32[]{:S(2)}) collective-permute-start(bf16[2,64,64]{2,1,0:T(8,128)(2,1)S(1)} %couple.1), channel_id=1, source_target_pairs={{0,1},{1,0},{2,3},{3,2},{4,5},{5,4},{6,7},{7,6},{8,9},{9,8},{10,11... | collective-permute-start | bytes 49160 | tf_op jit(solution)/shard_map/ppermute | solution.py:480
  71.7 0.0 copy-done.4
  71.7 2.1 %unsort.1 = bf16[128,2048]{1,0:T(8,128)(2,1)} custom-call(bf16[128,2048]{1,0:T(8,128)(2,1)S(1)} %arrange.1.y_ref.sorted_ref, s32[1,2048]{1,0:T(1,128)S(1)} %copy-done.4), custom_call_target="tpu_custom_call" | custom-call | flops 1000000000 | bytes 10000000 | tf_op jit(solution)/shard_map/unsort/pallas_call | solution.py:481
  73.8 0.0 collective-permute-done.6
  73.8 1.9 %collective-permute-done.7 = bf16[2,64,64]{2,1,0:T(8,128)(2,1)S(1)} collective-permute-done((bf16[2,64,64]{2,1,0:T(8,128)(2,1)S(1)}, bf16[2,64,64]{2,1,0:T(8,128)(2,1)S(1)}, u32[]{:S(2)}, u32[]{:S(2)}) %collective-permute-start.7) | collective-permute-done | bytes 16416 | tf_op jit(solution)/shard_map/ppermute | solution.py:480
  75.7 0.0 collective-permute-done.8
  75.7 0.7 multiply_bitcast_fusion
Async XLA Ops:
  5.7 17.5 %collective-permute-start = (bf16[32,2304]{1,0:T(8,128)(2,1)}, bf16[32,2304]{1,0:T(8,128)(2,1)S(1)}, u32[]{:S(2)}, u32[]{:S(2)}) collective-permute-start(bf16[32,2304]{1,0:T(8,128)(2,1)} %get-tuple-element.17), channel_id=1, source_target_pairs={{0,1},{1,0},{2,3},{3,2},{4,5},{5,4},{6,7},{7,6},{8,9},{9,8},{10,11... | collective-permute-start | bytes 442376 | tf_op jit(solution)/shard_map/ppermute | solution.py:407
  8.8 14.4 %collective-permute-start.1 = (bf16[32,2304]{1,0:T(8,128)(2,1)}, bf16[32,2304]{1,0:T(8,128)(2,1)S(1)}, u32[]{:S(2)}, u32[]{:S(2)}) collective-permute-start(bf16[32,2304]{1,0:T(8,128)(2,1)} %get-tuple-element.18), channel_id=1, source_target_pairs={{0,2},{1,3},{2,0},{3,1},{4,6},{5,7},{6,4},{7,5},{8,10},{9,11},{10,... | collective-permute-start | bytes 442376 | tf_op jit(solution)/shard_map/ppermute | solution.py:407
  11.4 11.8 %collective-permute-start.2 = (bf16[32,2304]{1,0:T(8,128)(2,1)}, bf16[32,2304]{1,0:T(8,128)(2,1)S(1)}, u32[]{:S(2)}, u32[]{:S(2)}) collective-permute-start(bf16[32,2304]{1,0:T(8,128)(2,1)} %get-tuple-element.19), channel_id=1, source_target_pairs={{0,3},{1,2},{2,1},{3,0},{4,7},{5,6},{6,5},{7,4},{8,11},{9,10},{10,... | collective-permute-start | bytes 442376 | tf_op jit(solution)/shard_map/ppermute | solution.py:407
  11.4 1.6 %copy-start.1 = (f32[64,64,128]{2,1,0:T(8,128)S(1)}, f32[64,64,128]{2,1,0:T(8,128)}, u32[]{:S(2)}) copy-start(f32[64,64,128]{2,1,0:T(8,128)} %param.9) | copy-start | bytes 6291460
  13.0 1.0 %copy-start.2 = (bf16[128,2048]{1,0:T(8,128)(2,1)S(1)}, bf16[128,2048]{1,0:T(8,128)(2,1)}, u32[]{:S(2)}) copy-start(bf16[128,2048]{1,0:T(8,128)(2,1)} %get-tuple-element.20.waves_ref) | copy-start | bytes 1572868
  14.0 0.8 copy-start.6
  14.8 8.4 %copy-start.3 = (bf16[32,2304]{1,0:T(8,128)(2,1)S(1)}, bf16[32,2304]{1,0:T(8,128)(2,1)}, u32[]{:S(2)}) copy-start(bf16[32,2304]{1,0:T(8,128)(2,1)} %get-tuple-element.16.refs_0_) | copy-start | bytes 442372
  14.8 8.4 %copy-start.5 = (bf16[2,128,128]{2,1,0:T(8,128)(2,1)S(1)}, bf16[2,128,128]{2,1,0:T(8,128)(2,1)}, u32[]{:S(2)}) copy-start(bf16[2,128,128]{2,1,0:T(8,128)(2,1)} %constant.18.clone.refs_8_) | copy-start | bytes 196612
  14.8 8.4 %copy-start.7 = (bf16[64,256]{1,0:T(8,128)(2,1)S(1)}, bf16[64,256]{1,0:T(8,128)(2,1)}, u32[]{:S(2)}) copy-start(bf16[64,256]{1,0:T(8,128)(2,1)} %constant.17.clone.cs_ref.refs_5_) | copy-start | bytes 98308
  17.8 1.4 %copy-start.8 = (f32[4,64,2176]{2,1,0:T(8,128)}, f32[4,64,2176]{2,1,0:T(8,128)S(1)}, u32[]{:S(2)}) copy-start(f32[4,64,2176]{2,1,0:T(8,128)S(1)} %get-tuple-element.21.refs_4_) | copy-start | bytes 6684676
  19.2 32.4 %all-to-all-start = ((bf16[8,16,2048]{2,1,0:T(8,128)(2,1)}), bf16[8,16,2048]{2,1,0:T(8,128)(2,1)S(1)}, u32[]{:S(2)}, u32[]{:S(2)}) async-start(bf16[8,16,2048]{2,1,0:T(8,128)(2,1)} %bitcast.6), calls=%async_computation | async-start | bytes 1048576 | tf_op jit(solution)/shard_map/all_to_all | solution.py:446
  23.2 1.6 %copy-start.9 = (f32[4,64,2176]{2,1,0:T(8,128)S(1)}, f32[4,64,2176]{2,1,0:T(8,128)}, u32[]{:S(2)}) copy-start(f32[4,64,2176]{2,1,0:T(8,128)} %copy-done.8) | copy-start | bytes 6684676
  24.9 26.8 %copy-start = (s32[8]{0:T(128)S(1)}, s32[8]{0:T(128)}, u32[]{:S(2)}) copy-start(s32[8]{0:T(128)} %order_ref.1) | copy-start | bytes 100
  47.0 10.1 %collective-permute-start.3 = (bf16[32,2048]{1,0:T(8,128)(2,1)S(1)}, bf16[32,2048]{1,0:T(8,128)(2,1)S(1)}, u32[]{:S(2)}, u32[]{:S(2)}) collective-permute-start(bf16[32,2048]{1,0:T(8,128)(2,1)S(1)} %get-tuple-element.25), channel_id=1, source_target_pairs={{0,1},{1,0},{2,3},{3,2},{4,5},{5,4},{6,7},{7,6},{8,9},{9,8},{10,11... | collective-permute-start | bytes 393224 | tf_op jit(solution)/shard_map/ppermute | solution.py:460
  49.2 12.9 %collective-permute-start.4 = (bf16[32,2048]{1,0:T(8,128)(2,1)S(1)}, bf16[32,2048]{1,0:T(8,128)(2,1)S(1)}, u32[]{:S(2)}, u32[]{:S(2)}) collective-permute-start(bf16[32,2048]{1,0:T(8,128)(2,1)S(1)} %get-tuple-element.26), channel_id=1, source_target_pairs={{0,2},{1,3},{2,0},{3,1},{4,6},{5,7},{6,4},{7,5},{8,10},{9,11},{10,... | collective-permute-start | bytes 393224 | tf_op jit(solution)/shard_map/ppermute | solution.py:460
  51.3 10.9 %collective-permute-start.5 = (bf16[32,2048]{1,0:T(8,128)(2,1)S(1)}, bf16[32,2048]{1,0:T(8,128)(2,1)S(1)}, u32[]{:S(2)}, u32[]{:S(2)}) collective-permute-start(bf16[32,2048]{1,0:T(8,128)(2,1)S(1)} %get-tuple-element.27), channel_id=1, source_target_pairs={{0,3},{1,2},{2,1},{3,0},{4,7},{5,6},{6,5},{7,4},{8,11},{9,10},{10,... | collective-permute-start | bytes 393224 | tf_op jit(solution)/shard_map/ppermute | solution.py:460
  53.1 13.8 %all-to-all-start.1 = ((bf16[8,16,2048]{2,1,0:T(8,128)(2,1)}), bf16[8,16,2048]{2,1,0:T(8,128)(2,1)S(1)}, u32[]{:S(2)}, u32[]{:S(2)}) async-start(bf16[8,16,2048]{2,1,0:T(8,128)(2,1)} %select_partner.1), calls=%async_computation.1 | async-start | bytes 1048576 | tf_op jit(solution)/shard_map/all_to_all | solution.py:458
  62.1 9.6 %copy-start.4 = (s32[1,2048]{1,0:T(1,128)S(1)}, s32[1,2048]{1,0:T(1,128)}, u32[]{:S(2)}) copy-start(s32[1,2048]{1,0:T(1,128)} %get-tuple-element.28.rank_ref) | copy-start | bytes 24580
  67.3 6.5 %collective-permute-start.6 = (bf16[2,64,64]{2,1,0:T(8,128)(2,1)S(1)}, bf16[2,64,64]{2,1,0:T(8,128)(2,1)S(1)}, u32[]{:S(2)}, u32[]{:S(2)}) collective-permute-start(bf16[2,64,64]{2,1,0:T(8,128)(2,1)S(1)} %couple.1), channel_id=1, source_target_pairs={{0,3},{1,2},{2,1},{3,0},{4,7},{5,6},{6,5},{7,4},{8,11},{9,10},{10,... | collective-permute-start | bytes 49160 | tf_op jit(solution)/shard_map/ppermute | solution.py:480
  70.9 4.8 %collective-permute-start.7 = (bf16[2,64,64]{2,1,0:T(8,128)(2,1)S(1)}, bf16[2,64,64]{2,1,0:T(8,128)(2,1)S(1)}, u32[]{:S(2)}, u32[]{:S(2)}) collective-permute-start(bf16[2,64,64]{2,1,0:T(8,128)(2,1)S(1)} %couple.1), channel_id=1, source_target_pairs={{0,2},{1,3},{2,0},{3,1},{4,6},{5,7},{6,4},{7,5},{8,10},{9,11},{10,... | collective-permute-start | bytes 49160 | tf_op jit(solution)/shard_map/ppermute | solution.py:480
  70.9 4.8 %collective-permute-start.8 = (bf16[2,64,64]{2,1,0:T(8,128)(2,1)S(1)}, bf16[2,64,64]{2,1,0:T(8,128)(2,1)S(1)}, u32[]{:S(2)}, u32[]{:S(2)}) collective-permute-start(bf16[2,64,64]{2,1,0:T(8,128)(2,1)S(1)} %couple.1), channel_id=1, source_target_pairs={{0,1},{1,0},{2,3},{3,2},{4,5},{5,4},{6,7},{7,6},{8,9},{9,8},{10,11... | collective-permute-start | bytes 49160 | tf_op jit(solution)/shard_map/ppermute | solution.py:480

commit v6 on v5

--- a/solution.py
+++ b/solution.py
@@ -11,12 +11,14 @@
 
 STICK_DEV = 64
 LANES = 128
-UNROLL = 16
+UNROLL = 8
+CHUNKS = 2
 BF16 = jnp.bfloat16
 F32 = jnp.float32
 VMEM_LIMIT = 24 * 1024 * 1024
 SORT_LIMIT = 60 * 1024 * 1024
-ARRANGE_COST = 10**11
+ARRANGE_COST = 3*10**9
+JOIN_COST = 10**7
 
 
 def cos_sin(side):
@@ -71,20 +73,20 @@
     low = ranks - high * side
     looked = dot(high.astype(BF16), ch) * side + dot(low.astype(BF16), ch)
     rank = jnp.sum(zh.astype(F32) * looked, axis=0, keepdims=True)
-    return xh, yh, ch, cells, ranks, rank.astype(jnp.int32)
+    return xh, yh, ch, slot, cells, rank.astype(jnp.int32)
 
 
 def sort_kernel(side, groups, me_ref, idx_ref, x_hbm, *refs):
-    outs, (all_ref, rank_ref, x_ref, wide, pieces, sem) = refs[:groups], refs[groups:]
+    outs, (all_ref, rank_ref, x_ref, wide, pieces, sem) = refs[: groups * CHUNKS], refs[groups * CHUNKS :]
     fetch = pltpu.make_async_copy(x_hbm, x_ref, sem)
     fetch.start()
-    xh, yh, ch, cells, ranks, rank = locate(idx_ref[...], side)
+    xh, yh, ch, slot_of, cells, rank = locate(idx_ref[...], side)
     rank_ref[...] = rank
     waves = rank.shape[1]
     both = x_ref.shape[0]
     bands = both // 2
     share = bands // groups
-    rows = 2 * share
+    rows = 2 * share // CHUNKS
     lane = lax.broadcasted_iota(jnp.int32, (STICK_DEV, side), 1).astype(F32)
     cells = jnp.concatenate([cells[i : i + rows] for i in range(0, side, rows)], axis=1)
     slot = lax.broadcasted_iota(jnp.int32, (rows, LANES), 1) // rows
@@ -96,29 +98,36 @@
         for i in range(0, STICK_DEV, rows):
             place = jnp.where(slot == count, value[i : i + rows], place)
             count += 1
-    extra = jnp.concatenate([cells, place], axis=1).astype(BF16)
+    tiles = waves // LANES
+    in_tile = one_hot(rank & (LANES - 1), LANES)
+    col = dot_nt(one_hot(rank >> 7, tiles) * slot_of.astype(BF16), in_tile)
+    col = [col[i : i + rows] for i in range(0, tiles, rows)]
+    extra = jnp.concatenate([cells, place] + col, axis=1).astype(BF16)
     low = one_hot(rank & 255, 256)
-    for out in outs:
-        out[:, waves:] = extra
+    for shift in range(groups):
+        outs[shift * CHUNKS][:, waves:] = extra
     fetch.wait()
     parts = waves // 256
     for part in range(parts):
         mask = jnp.where((rank >> 8) == part, 1.0, 0.0).astype(BF16)
         wide[part * both : (part + 1) * both] = x_ref[...] * mask
     pieces[...] = dot_nt(wide[...], low)
+    half = share // CHUNKS
     for part in range(parts):
         here = slice(part * 256, (part + 1) * 256)
         all_ref[:, here] = pieces[part * both : (part + 1) * both].astype(BF16)
-        for shift, out in enumerate(outs):
-            q = me_ref[0] ^ shift
-            begin = pl.multiple_of(part * both + q * share, 8)
+        for shift in range(groups):
+            begin = pl.multiple_of(part * both + (me_ref[0] ^ shift) * share, 8)
             re = pieces[pl.ds(begin, share)]
             im = pieces[pl.ds(begin + bands, share)]
-            out[:, here] = jnp.concatenate([re, im], axis=0).astype(BF16)
-
-
-def field_kernel(side, chunks, pot_ref, cs_ref, waves_ref, field_ref, cyr_ref, syr_ref, copy_ref):
-    copy_ref[...] = waves_ref[...]
+            for c in range(CHUNKS):
+                mine = slice(c * half, (c + 1) * half)
+                outs[shift * CHUNKS + c][:, here] = jnp.concatenate(
+                    [re[mine], im[mine]], axis=0
+                ).astype(BF16)
+
+
+def field_kernel(side, chunks, pot_ref, cs_ref, field_ref, cyr_ref, syr_ref):
     half = side // 2
     left = lax.broadcasted_iota(jnp.int32, (side, LANES), 1) < side
     for ref, begin in ((cyr_ref, 0), (syr_ref, LANES)):
@@ -149,10 +158,9 @@
     for k in range(chunks):
         ya, yb = 2 * k, 2 * k + 1
         here = slice(k * LANES, (k + 1) * LANES)
-        field_ref[0, :, here], field_ref[1, :, here] = pair(
-            plane(ya), plane(yb) if yb <= half else zero
-        )
-        field_ref[2, :, here], field_ref[3, :, here] = pair(mirror(ya), mirror(yb))
+        values = pair(plane(ya), plane(yb) if yb <= half else zero) + pair(mirror(ya), mirror(yb))
+        for i, value in enumerate(values):
+            field_ref[i, :, here] = value.astype(BF16)
 
 
 def select_kernel(order_ref, in_ref, out_ref, sems):
@@ -165,28 +173,26 @@
         copy.wait()
 
 
-def box_kernel(
-    side, chunks, team, waves, groups, *refs,
-):
-    x_refs, refs = refs[:groups], refs[groups:]
-    (field_ref, cs_ref, cyr_ref, syr_ref, wz_ref), refs = refs[:5], refs[5:]
-    out_refs, refs = refs[:groups], refs[groups:]
-    xf, grid, t_scr, l_scr, acc, tab_ref, spot_ref, start_v, start_s, sem = refs
+def build_tables(side, chunks, waves, x_refs, cs_ref, cyr_ref, syr_ref, tab_ref, spot_ref, col_ref, start_ref):
     rows = x_refs[0].shape[0]
-    bands = rows // 2
-    blocks = rows // 8
-    span = 2 * side
+    parts = side // rows
+    tiles = waves // LANES
+    cells_end = waves + parts * STICK_DEV
     tri = triangles(side)
-    parts = side // rows
-    cells_end = waves + parts * STICK_DEV
     lane_f = lax.broadcasted_iota(jnp.int32, (STICK_DEV, side), 1).astype(F32)
+    ahead = jnp.where(
+        lax.broadcasted_iota(jnp.int32, (side, LANES), 0)
+        < lax.broadcasted_iota(jnp.int32, (side, LANES), 1),
+        1.0, 0.0,
+    ).astype(BF16)
+    left = lax.broadcasted_iota(jnp.int32, (tiles, LANES), 1) < STICK_DEV
     at_x, at_y = [], []
-    for d in range(groups):
+    for d, x_ref in enumerate(x_refs):
         cells = jnp.concatenate(
-            [x_refs[d][:, waves + i * STICK_DEV : waves + (i + 1) * STICK_DEV].astype(F32) for i in range(parts)],
+            [x_ref[:, waves + i * STICK_DEV : waves + (i + 1) * STICK_DEV].astype(F32) for i in range(parts)],
             axis=0,
         )
-        place = x_refs[d][:, cells_end : cells_end + LANES].astype(F32)
+        place = x_ref[:, cells_end : cells_end + LANES].astype(F32)
         for which, hots in enumerate((at_x, at_y)):
             value = jnp.concatenate(
                 [place[:, i * rows : i * rows + 1] for i in range(which * parts, (which + 1) * parts)],
@@ -194,14 +200,20 @@
             )
             hots.append(jnp.where(lane_f == value, 1.0, 0.0))
         ranks = prefix(cells.astype(BF16), tri)
-        begins = jnp.floor(ranks[:, :1] * (1.0 / STICK_DEV))
+        begins = jnp.minimum(jnp.floor(ranks[:, :1] * (1.0 / STICK_DEV)), waves // STICK_DEV - 1.0)
         spot = jnp.where(cells > 0.5, ranks - begins * STICK_DEV, -1.0)
         spot_ref[d] = jnp.concatenate([spot, spot], axis=1)
         level = dot_nt(jnp.ones((8, STICK_DEV), BF16), cells.astype(BF16))
-        before = dot(level.astype(BF16), tri[0])
-        start_v[d : d + 1, :side] = (before[:1] * (1.0 / STICK_DEV)).astype(jnp.int32)
-    to_scalars = pltpu.make_async_copy(start_v, start_s, sem)
-    to_scalars.start()
+        start_ref[d : d + 1, :] = dot(level.astype(BF16), ahead)[:1].astype(jnp.int32)
+        begin = cells_end + LANES
+        col = jnp.concatenate(
+            [x_ref[:, begin + i * LANES : begin + (i + 1) * LANES].astype(F32) for i in range(tiles // rows)],
+            axis=0,
+        ) + float((d % 2) * STICK_DEV)
+        turned = pltpu.roll(col, STICK_DEV, 1)
+        after = jnp.concatenate([turned[1:], turned[:1]], axis=0)
+        col_ref[0, d] = col.astype(jnp.int32)
+        col_ref[1, d] = jnp.where(left, turned, after).astype(jnp.int32)
     at_x = jnp.concatenate(at_x, axis=0).astype(BF16)
     at_y = jnp.concatenate(at_y, axis=0).astype(BF16)
     both = dot(at_x, cs_ref[...])
@@ -212,51 +224,90 @@
         base = 2 * k * LANES
         tab_ref[:, base : base + LANES] = (cy * cx - sy * sx).astype(BF16)
         tab_ref[:, base + LANES : base + 2 * LANES] = (cy * sx + sy * cx).astype(BF16)
+
+
+def box_first_kernel(side, chunks, team, waves, groups, *refs):
+    x_refs, refs = refs[:groups], refs[groups:]
+    (field_ref, cs_ref, cyr_ref, syr_ref, wz_ref), refs = refs[:5], refs[5:]
+    out_refs, refs = refs[:groups], refs[groups:]
+    (tab_ref, spot_ref, col_ref, start_ref), refs = refs[:4], refs[4:]
+    *scratch, start_s, sem = refs
+    build_tables(
+        side, chunks, waves, x_refs, cs_ref, cyr_ref, syr_ref, tab_ref, spot_ref, col_ref, start_ref
+    )
+    to_scalars = pltpu.make_async_copy(start_ref, start_s, sem)
+    to_scalars.start()
     to_scalars.wait()
-
+    box_work(
+        side, chunks, team, waves, x_refs, field_ref, wz_ref, tab_ref, spot_ref, col_ref, start_s,
+        out_refs, *scratch,
+    )
+
+
+def box_next_kernel(side, chunks, team, waves, groups, *refs):
+    x_refs, refs = refs[:groups], refs[groups:]
+    (field_ref, wz_ref, tab_ref, spot_ref, col_ref, start_s), refs = refs[:6], refs[6:]
+    out_refs, scratch = refs[:groups], refs[groups:]
+    box_work(
+        side, chunks, team, waves, x_refs, field_ref, wz_ref, tab_ref, spot_ref, col_ref, start_s,
+        out_refs, *scratch,
+    )
+
+
+def box_work(
+    side, chunks, team, waves, x_refs, field_ref, wz_ref, tab_ref, spot_ref, col_ref, start_s,
+    out_refs, xf, grid, t_scr, l_scr, acc,
+):
+    groups = len(x_refs)
+    rows = x_refs[0].shape[0]
+    bands = rows // 2
+    blocks = rows // 8
+    span = 2 * side
     for d in range(groups):
-        xf[0, d] = x_refs[d][:, :waves]
-        wide_x = x_refs[d][:, :waves].astype(F32)
-        xf[1, d] = jnp.concatenate([wide_x[:, STICK_DEV:], wide_x[:, :STICK_DEV]], axis=1).astype(BF16)
+        value = x_refs[d][:, :waves].astype(F32)
+        xf[0, d] = value
+        xf[1, d] = jnp.concatenate([value[:, STICK_DEV:], value[:, :STICK_DEV]], axis=1)
         acc[0, d] = jnp.zeros((rows, waves), F32)
         acc[1, d] = jnp.zeros((rows, waves), F32)
-    left = lax.broadcasted_iota(jnp.int32, (1, LANES), 1) < STICK_DEV
-    places = lax.broadcasted_iota(jnp.int32, (LANES, LANES), 0).astype(F32).astype(BF16)
-    one, none = jnp.ones((LANES, LANES), BF16), jnp.zeros((LANES, LANES), BF16)
-
-    def picks(z, dp):
-        row_a = jnp.where(left, spot_ref[2 * dp, pl.ds(z, 1), :], -1.0).astype(BF16)
-        row_b = jnp.where(left, -1.0, spot_ref[2 * dp + 1, pl.ds(z, 1), :]).astype(BF16)
-        return jnp.concatenate(
-            [jnp.where(places == row_a, one, none), jnp.where(places == row_b, one, none)], axis=0
-        )
+    lane = lax.broadcasted_iota(jnp.int32, (8, LANES), 1)
+    left = lane < STICK_DEV
 
     def window(z, d):
-        begin = start_s[d, z]
-        return begin & 1, pl.ds(pl.multiple_of((begin >> 1) * LANES, LANES), LANES)
+        begin = jnp.minimum(start_s[d, z] >> 6, waves // STICK_DEV - 1)
+        tile = begin >> 1
+        return begin & 1, tile, pl.ds(pl.multiple_of(tile * LANES, LANES), LANES), begin * STICK_DEV
 
     def expand(z):
         for dp in range(groups // 2):
-            pieces = []
-            for d in (2 * dp, 2 * dp + 1):
-                odd, lanes = window(z, d)
-                pieces.append(xf[odd, d, :, lanes])
-            value = dot(jnp.concatenate(pieces, axis=1), picks(z, dp))
+            spot = jnp.where(
+                left,
+                jnp.broadcast_to(spot_ref[2 * dp, pl.ds(z, 1), :], (8, LANES)),
+                jnp.broadcast_to(spot_ref[2 * dp + 1, pl.ds(z, 1), :], (8, LANES)),
+            )
+            valid = spot >= 0.0
+            at = jnp.maximum(spot, 0.0).astype(jnp.int32)
+            odd_a, _, lanes_a, _ = window(z, 2 * dp)
+            odd_b, _, lanes_b, _ = window(z, 2 * dp + 1)
             for block in range(blocks):
-                rows_z = pl.ds(block * 8 * side + z, 8, stride=side)
-                grid[dp, rows_z, :] = value[block * 8 : (block + 1) * 8]
+                part = slice(block * 8, (block + 1) * 8)
+                a = jnp.take_along_axis(xf[odd_a, 2 * dp, part, lanes_a], at, axis=1)
+                b = jnp.take_along_axis(xf[odd_b, 2 * dp + 1, part, lanes_b], at, axis=1)
+                value = jnp.where(valid, jnp.where(left, a, b), 0.0)
+                grid[dp, pl.ds(block * 8 * side + z, 8, stride=side), :] = value
 
     def collect(z):
         for dp in range(groups // 2):
-            source = jnp.concatenate(
-                [grid[dp, pl.ds(block * 8 * side + z, 8, stride=side), :] for block in range(blocks)],
-                axis=0,
-            ).astype(BF16)
-            value = dot_nt(source, picks(z, dp))
-            for dd in range(2):
-                d = 2 * dp + dd
-                odd, lanes = window(z, d)
-                acc[odd, d, :, lanes] += value[:, dd * LANES : (dd + 1) * LANES]
+            sources = [
+                grid[dp, pl.ds(block * 8 * side + z, 8, stride=side), :] for block in range(blocks)
+            ]
+            for d in (2 * dp, 2 * dp + 1):
+                odd, tile, lanes, base = window(z, d)
+                at = jnp.broadcast_to(col_ref[odd, d, pl.ds(tile, 1), :], (8, LANES))
+                mask = (lane >= start_s[d, z] - base) & (lane < start_s[d, z + 1] - base)
+                for block in range(blocks):
+                    part = slice(block * 8, (block + 1) * 8)
+                    value = jnp.take_along_axis(sources[block], at, axis=1)
+                    acc[odd, d, part, lanes] = jnp.where(mask, value, acc[odd, d, part, lanes])
 
     def levels(step):
         def body(i, carry):
@@ -296,11 +347,11 @@
             for b in range(team):
                 u, x = ab[b * span : b * span + side, :LANES], ab[b * span : b * span + side, LANES:]
                 w, v = ab[b * span + side : (b + 1) * span, :LANES], ab[b * span + side : (b + 1) * span, LANES:]
-                pr, pi, mr, mi = u - v, w + x, u + v, w - x
+                pr, pi, mr, mi = [t.astype(BF16) for t in (u - v, w + x, u + v, w - x)]
                 ar, ai = p * pr - q * pi, p * pi + q * pr
                 br, bi = p2 * mr - q2 * mi, p2 * mi + q2 * mr
-                even = jnp.concatenate([ar + br, ai + bi], axis=0).astype(BF16)
-                odd = jnp.concatenate([ai - bi, br - ar], axis=0).astype(BF16)
+                even = jnp.concatenate([ar + br, ai + bi], axis=0)
+                odd = jnp.concatenate([ai - bi, br - ar], axis=0)
                 l_scr[b * span : (b + 1) * span, wide] = jnp.concatenate([even, odd], axis=1)
         back = dot_nt(l_scr[...], tab_ref[...]).astype(BF16)
         for b in range(team):
@@ -321,15 +372,28 @@
 
 
 def arrange_kernel(groups, me_ref, *refs):
-    y_refs, (sorted_ref, rows_scr) = refs[:groups], refs[groups:]
-    share = y_refs[0].shape[0] // 2
-    half = groups * share
-    for shift, y_ref in enumerate(y_refs):
-        begin = pl.multiple_of((me_ref[0] ^ shift) * share, 8)
-        value = y_ref[...].astype(F32)
-        rows_scr[pl.ds(begin, share)] = value[:share]
-        rows_scr[pl.ds(begin + half, share)] = value[share:]
-    sorted_ref[...] = rows_scr[...].astype(BF16)
+    y_refs, (rows_ref,) = refs[:groups], refs[groups:]
+    part = y_refs[0].shape[0] // 2
+    half = groups * part
+    me = me_ref[0]
+    for j in range(groups // 2):
+        one, other = y_refs[2 * j][...].astype(F32), y_refs[2 * j + 1][...].astype(F32)
+        low = jnp.where((me & 1) == 0, one, other)
+        high = jnp.where((me & 1) == 0, other, one)
+        begin = pl.multiple_of(((me >> 1) ^ j) * (2 * part), 8)
+        rows_ref[pl.ds(begin, 2 * part)] = jnp.concatenate([low[:part], high[:part]], axis=0)
+        rows_ref[pl.ds(begin + half, 2 * part)] = jnp.concatenate([low[part:], high[part:]], axis=0)
+
+
+def join_kernel(groups, me_ref, *refs):
+    rows_refs, refs = refs[: CHUNKS - 1], refs[CHUNKS - 1 :]
+    sorted_ref, rows_scr = refs[groups:]
+    arrange_kernel(groups, me_ref, *refs[:groups], rows_scr)
+    values = [ref[...] for ref in (*rows_refs, rows_scr)]
+    part = values[0].shape[0] // (2 * groups)
+    sorted_ref[...] = jnp.concatenate(
+        [v[i * part : (i + 1) * part] for i in range(2 * groups) for v in values], axis=0
+    ).astype(BF16)
 
 
 def couple_kernel(partner_ref, sorted_ref, g_ref):
@@ -382,19 +446,24 @@
     me_row = me.reshape(1)
     pairs = [[(i, i ^ s) for i in range(fft_count)] for s in range(fft_count)]
     pool_count = lax.axis_size("pool")
-    rows = 2 * share
-    packed = waves + side * STICK_DEV // rows + LANES
+    rows = 2 * share // CHUNKS
+    tiles = waves // LANES
+    packed = waves + side * STICK_DEV // rows + LANES + tiles * LANES // rows
     scalars, blocks = whole(pltpu.SMEM), [whole()] * fft_count
 
     *ordered, ordered_all, rank = pl.pallas_call(
         functools.partial(sort_kernel, side, fft_count),
-        out_shape=[jax.ShapeDtypeStruct((rows, packed), BF16)] * fft_count
+        out_shape=[
+            jax.ShapeDtypeStruct((rows, waves if c else packed), BF16)
+            for _ in range(fft_count)
+            for c in range(CHUNKS)
+        ]
         + [
             jax.ShapeDtypeStruct((2 * bands, waves), BF16),
             jax.ShapeDtypeStruct((1, waves), jnp.int32),
         ],
         in_specs=[scalars, whole(), whole(pltpu.HBM)],
-        out_specs=blocks + [whole(), whole()],
+        out_specs=blocks * CHUNKS + [whole(), whole()],
         scratch_shapes=[
             pltpu.VMEM((2 * bands, waves), BF16),
             pltpu.VMEM((waves // 256 * 2 * bands, waves), BF16),
@@ -404,47 +473,70 @@
         compiler_params=params(SORT_LIMIT),
         name="sort_waves",
     )(me_row, box_index.reshape(1, waves), coeffs)
-    moved = [ordered[0]] + [lax.ppermute(ordered[s], "fft", pairs[s]) for s in range(1, fft_count)]
-
-    field, cyr, syr, passed = pl.pallas_call(
+    moved = [
+        [ordered[c]] + [lax.ppermute(ordered[s * CHUNKS + c], "fft", pairs[s]) for s in range(1, fft_count)]
+        for c in range(CHUNKS)
+    ]
+
+    field, cyr, syr = pl.pallas_call(
         functools.partial(field_kernel, side, chunks),
         out_shape=(
-            jax.ShapeDtypeStruct((4, side, chunks * LANES), F32),
+            jax.ShapeDtypeStruct((4, side, chunks * LANES), BF16),
             jax.ShapeDtypeStruct((side, chunks * LANES), BF16),
             jax.ShapeDtypeStruct((side, chunks * LANES), BF16),
-            jax.ShapeDtypeStruct((2 * bands, waves), BF16),
         ),
-        in_specs=[whole()] * 3,
-        out_specs=(whole(),) * 4,
+        in_specs=[whole()] * 2,
+        out_specs=(whole(),) * 3,
         compiler_params=params(),
         cost_estimate=pl.CostEstimate(flops=10**9, bytes_accessed=10**7, transcendentals=0),
         name="field_pairs",
-    )(potential.reshape(side * side, 2 * side), cs, ordered_all)
-
-    team = min(4, share)
-    back = pl.pallas_call(
-        functools.partial(box_kernel, side, chunks, team, waves, fft_count),
-        out_shape=[jax.ShapeDtypeStruct((rows, waves), BF16)] * fft_count,
+    )(potential.reshape(side * side, 2 * side), cs)
+
+    team = min(4, rows // 2)
+    scratch = [
+        pltpu.VMEM((2, fft_count, rows, waves), F32),
+        pltpu.VMEM((columns // LANES, rows * side, LANES), F32),
+        pltpu.VMEM((rows * side, columns), BF16),
+        pltpu.VMEM((team * 2 * side, 2 * chunks * LANES), BF16),
+        pltpu.VMEM((2, fft_count, rows, waves), F32),
+    ]
+    cost = pl.CostEstimate(flops=10**10, bytes_accessed=10**7, transcendentals=0)
+    shapes = [jax.ShapeDtypeStruct((rows, waves), BF16)] * fft_count
+    *back, tab, spot, col, start = pl.pallas_call(
+        functools.partial(box_first_kernel, side, chunks, team, waves, fft_count),
+        out_shape=shapes
+        + [
+            jax.ShapeDtypeStruct((columns, 2 * chunks * LANES), BF16),
+            jax.ShapeDtypeStruct((fft_count, side, 2 * STICK_DEV), F32),
+            jax.ShapeDtypeStruct((2, fft_count, tiles, LANES), jnp.int32),
+            jax.ShapeDtypeStruct((fft_count, LANES), jnp.int32),
+        ],
         in_specs=blocks + [whole()] * 5,
-        out_specs=blocks,
-        scratch_shapes=[
-            pltpu.VMEM((2, fft_count, rows, waves), BF16),
-            pltpu.VMEM((columns // LANES, rows * side, LANES), F32),
-            pltpu.VMEM((rows * side, columns), BF16),
-            pltpu.VMEM((team * 2 * side, 2 * chunks * LANES), BF16),
-            pltpu.VMEM((2, fft_count, rows, waves), F32),
-            pltpu.VMEM((columns, 2 * chunks * LANES), BF16),
-            pltpu.VMEM((fft_count, side, 2 * STICK_DEV), F32),
-            pltpu.VMEM((fft_count, LANES), jnp.int32),
-            pltpu.SMEM((fft_count, LANES), jnp.int32),
-            pltpu.SemaphoreType.DMA,
-        ],
+        out_specs=blocks + [whole()] * 4,
+        scratch_shapes=scratch
+        + [pltpu.SMEM((fft_count, LANES), jnp.int32), pltpu.SemaphoreType.DMA],
         compiler_params=params(),
-        cost_estimate=pl.CostEstimate(flops=10**10, bytes_accessed=10**7, transcendentals=0),
-        name="box_work",
-    )(*moved, field, cs, cyr, syr, wz)
+        cost_estimate=cost,
+        name="box_first",
+    )(*moved[0], field, cs, cyr, syr, wz)
+    returned = [[back[0]] + [lax.ppermute(back[s], "fft", pairs[s]) for s in range(1, fft_count)]]
+    for c in range(1, CHUNKS):
+        back = pl.pallas_call(
+            functools.partial(box_next_kernel, side, chunks, team, waves, fft_count),
+            out_shape=shapes,
+            in_specs=blocks + [whole()] * 5 + [scalars],
+            out_specs=blocks,
+            scratch_shapes=scratch,
+            compiler_params=params(),
+            cost_estimate=cost,
+            name="box_next",
+        )(*moved[c], field, wz, tab, spot, col, start)
+        returned.append(
+            [back[0]] + [lax.ppermute(back[s], "fft", pairs[s]) for s in range(1, fft_count)]
+        )
+
     spread = lax.all_to_all(
-        passed.reshape(pool_count, 2 * bands // pool_count, waves), "pool", 0, 0, tiled=True
+        ordered_all.reshape(pool_count, 2 * bands // pool_count, waves), "pool", 0, 0, tiled=True
     )
     chosen = pl.pallas_call(
         select_kernel,
@@ -457,18 +549,30 @@
     )(partner_pool, spread)
     partner = lax.all_to_all(chosen, "pool", 0, 0, tiled=True).reshape(2 * bands, waves)
 
-    returned = [back[0]] + [lax.ppermute(back[s], "fft", pairs[s]) for s in range(1, fft_count)]
-
+    arranged = [
+        pl.pallas_call(
+            functools.partial(arrange_kernel, fft_count),
+            out_shape=jax.ShapeDtypeStruct((rows * fft_count, waves), F32),
+            in_specs=[scalars] + blocks,
+            out_specs=whole(),
+            compiler_params=params(),
+            cost_estimate=pl.CostEstimate(
+                flops=ARRANGE_COST, bytes_accessed=10**6, transcendentals=0
+            ),
+            name="arrange",
+        )(me_row, *returned[c])
+        for c in range(CHUNKS - 1)
+    ]
     sorted_response = pl.pallas_call(
-        functools.partial(arrange_kernel, fft_count),
+        functools.partial(join_kernel, fft_count),
         out_shape=jax.ShapeDtypeStruct((2 * bands, waves), BF16),
-        in_specs=[scalars] + blocks,
+        in_specs=[scalars] + [whole()] * (CHUNKS - 1) + blocks,
         out_specs=whole(),
-        scratch_shapes=[pltpu.VMEM((2 * bands, waves), F32)],
+        scratch_shapes=[pltpu.VMEM((rows * fft_count, waves), F32)],
         compiler_params=params(),
-        cost_estimate=pl.CostEstimate(flops=ARRANGE_COST, bytes_accessed=10**6, transcendentals=0),
-        name="arrange",
-    )(me_row, *returned)
+        cost_estimate=pl.CostEstimate(flops=JOIN_COST, bytes_accessed=10**6, transcendentals=0),
+        name="join",
+    )(me_row, *arranged, *returned[-1])
     sums = pl.pallas_call(
         couple_kernel,
         out_shape=jax.ShapeDtypeStruct((2, bands, bands), BF16),

time: 76.9 us -> 80.8 us (1.051)
  starting transfers between devices: 22.7 us -> 31.5 us
  waiting for transfers between devices: 11.6 us -> 5.64 us
  Pallas kernels: 34.3 us -> 36.3 us
  local copies, waits for them, and re-layouts: 6.42 us -> 5.38 us
    ppermute x3 -> x6, starting transfers between devices: 5.7 us -> 10.4 us  [shards(): lax.ppermute(ordered[s * CHUNKS + c], 'fft', pairs[s])]
    all_to_all x1, waiting for transfers between devices: 4.59 us -> 0.01 us  [shards(): lax.all_to_all(chosen, 'pool', 0, 0, tiled=True).reshape(2 * bands, waves)]
    ppermute x3 -> x6, starting transfers between devices: 4.63 us -> 8.69 us  [shards(): lax.ppermute(back[s], 'fft', pairs[s])]
    pallas_call x1 -> x3, Pallas kernels: 22.2 us -> 24.9 us  [the longest x1 12.8 us: shards(): pl.pallas_call(functools.partial(box_first_kernel, side, chunks, team, wa...]
    ppermute x3, waiting for transfers between devices: 1.94 us -> 0.7 us  [shards(): lax.ppermute(sums, 'fft', pairs[s])]
    unnamed x20 -> x22, local copies, waits for them, and re-layouts: 6.42 us -> 5.38 us
    pallas_call x1, Pallas kernels: 3.04 us -> 2.08 us  [shards(): pl.pallas_call(functools.partial(field_kernel, side, chunks), out_shape=(...]
    ppermute x3 -> x6, waiting for transfers between devices: 5.02 us -> 4.92 us  [shards(): lax.ppermute(back[s], 'fft', pairs[s])]
  transfers between devices with their start and end apart: 11 -> 17, of which waited for: 3 -> 3; matrix products, arithmetic and copies ran while one was open for 0% -> 0% of each run, Pallas kernels for 38% -> 38%
where the time goes in v6:
time: 80.8 us; the launch traced here: 80.3 us
  Pallas kernels  36.3 us (45%)
  starting transfers between devices  31.5 us (39%)
  waiting for transfers between devices  5.64 us (7%)
  local copies, waits for them, and re-layouts  5.38 us (7%)
    pallas_call x1, Pallas kernels, shards(): pl.pallas_call(functools.partial(box_first_kernel, side, chunks, team, wa...  12.8 us
    pallas_call x1, Pallas kernels, shards(): pl.pallas_call(functools.partial(box_next_kernel, side, chunks, team, wav...  12 us
    ppermute x6, starting transfers between devices, shards(): lax.ppermute(ordered[s * CHUNKS + c], 'fft', pairs[s])  10.4 us
    ppermute x6, starting transfers between devices, shards(): lax.ppermute(back[s], 'fft', pairs[s])  8.69 us
    unnamed x22, local copies, waits for them, and re-layouts  5.38 us
    pallas_call x1, Pallas kernels, shards(): pl.pallas_call(functools.partial(sort_kernel, side, fft_count), out_shape...  5.33 us
    ppermute x6, waiting for transfers between devices, shards(): lax.ppermute(back[s], 'fft', pairs[s])  4.92 us
    ppermute x3, starting transfers between devices, shards(): lax.ppermute(sums, 'fft', pairs[s])  4.42 us
  transfers between devices with their start and end apart: 17, of which 3 were waited for; matrix products, arithmetic and copies ran while one was open for 0% of the time, Pallas kernels for 38%

profile of v6, /device:TPU:0, one launch (start us, length us, event | category | flops | bytes accessed | tf_op | source)
XLA Modules:
  0.0 80.3 jit_solution(18036828309188477290)
XLA Ops:
  0.6 5.3 %sort_waves.1 = (bf16[16,2560]{1,0:T(8,128)(2,1)}, bf16[16,2048]{1,0:T(8,128)(2,1)}, bf16[16,2560]{1,0:T(8,128)(2,1)}, bf16[16,2048]{1,0:T(8,128)(2,1)}, bf16[16...) custom-call(s32[1]{0:T(128)} %bitcast.me_ref, ...), custom_call_target="tpu_custom_call" | custom-call | tf_op jit(solution)/shard_map/sort_waves/pallas_call | solution.py:454
  6.0 3.1 %collective-permute-start = (bf16[16,2560]{1,0:T(8,128)(2,1)}, bf16[16,2560]{1,0:T(8,128)(2,1)S(1)}, u32[]{:S(2)}, u32[]{:S(2)}) collective-permute-start(bf16[16,2560]{1,0:T(8,128)(2,1)} %get-tuple-element.28), channel_id=1, source_target_pairs={{0,1},{1,0},{2,3},{3,2},{4,5},{5,4},{6,7},{7,6},{8,9},{9,8},{10,11... | collective-permute-start | bytes 245768 | tf_op jit(solution)/shard_map/ppermute | solution.py:477
  9.1 2.6 %collective-permute-start.1 = (bf16[16,2560]{1,0:T(8,128)(2,1)}, bf16[16,2560]{1,0:T(8,128)(2,1)S(1)}, u32[]{:S(2)}, u32[]{:S(2)}) collective-permute-start(bf16[16,2560]{1,0:T(8,128)(2,1)} %get-tuple-element.29), channel_id=1, source_target_pairs={{0,2},{1,3},{2,0},{3,1},{4,6},{5,7},{6,4},{7,5},{8,10},{9,11},{10,... | collective-permute-start | bytes 245768 | tf_op jit(solution)/shard_map/ppermute | solution.py:477
  11.7 0.0 collective-permute-start.2
  11.7 0.9 %collective-permute-start.6 = (bf16[16,2048]{1,0:T(8,128)(2,1)}, bf16[16,2048]{1,0:T(8,128)(2,1)S(1)}, u32[]{:S(2)}, u32[]{:S(2)}) collective-permute-start(bf16[16,2048]{1,0:T(8,128)(2,1)} %get-tuple-element.39), channel_id=1, source_target_pairs={{0,1},{1,0},{2,3},{3,2},{4,5},{5,4},{6,7},{7,6},{8,9},{9,8},{10,11... | collective-permute-start | bytes 196616 | tf_op jit(solution)/shard_map/ppermute | solution.py:477
  12.6 3.5 %collective-permute-start.7 = (bf16[16,2048]{1,0:T(8,128)(2,1)}, bf16[16,2048]{1,0:T(8,128)(2,1)S(1)}, u32[]{:S(2)}, u32[]{:S(2)}) collective-permute-start(bf16[16,2048]{1,0:T(8,128)(2,1)} %get-tuple-element.40), channel_id=1, source_target_pairs={{0,2},{1,3},{2,0},{3,1},{4,6},{5,7},{6,4},{7,5},{8,10},{9,11},{10,... | collective-permute-start | bytes 196616 | tf_op jit(solution)/shard_map/ppermute | solution.py:477
  16.0 0.0 copy-start.10
  16.0 0.0 copy-start.2
  16.0 0.0 copy-start.5
  16.0 0.0 copy-start.7
  16.1 3.9 %all-to-all-start = ((bf16[8,16,2048]{2,1,0:T(8,128)(2,1)}), bf16[8,16,2048]{2,1,0:T(8,128)(2,1)S(1)}, u32[]{:S(2)}, u32[]{:S(2)}) async-start(bf16[8,16,2048]{2,1,0:T(8,128)(2,1)} %bitcast.16), calls=%async_computation | async-start | bytes 1048576 | tf_op jit(solution)/shard_map/all_to_all | solution.py:538
  19.9 0.0 copy-start.1
  19.9 1.6 %copy-done.1 = f32[64,64,128]{2,1,0:T(8,128)S(1)} copy-done((f32[64,64,128]{2,1,0:T(8,128)S(1)}, f32[64,64,128]{2,1,0:T(8,128)}, u32[]{:S(2)}) %copy-start.1) | copy-done | bytes 2097176
  21.5 0.8 copy-done.6
  22.3 2.1 %field_pairs.1 = (bf16[4,64,2176]{2,1,0:T(8,128)(2,1)S(1)}, bf16[64,2176]{1,0:T(8,128)(2,1)S(1)}, bf16[64,2176]{1,0:T(8,128)(2,1)S(1)}) custom-call(f32[4096,128]{1,0:T(8,128)S(1)} %bitcast.14, bf16[64,256]{1,0:T(8,128)(2,1)S(1)} %copy-done.6), custom_call_target="tpu_custom_call" | custom-call | flops 1000000000 | bytes 10000000 | tf_op jit(solution)/shard_map/field_pairs/pallas_call | solution.py:481
  24.4 0.0 collective-permute-done.refs_1_
  24.4 0.0 copy-done.10
  24.4 0.3 collective-permute-start.8
  24.7 0.0 collective-permute-done.1.refs_2_
  24.7 0.0 collective-permute-done.2.refs_3_
  24.7 0.0 copy-done.2
  24.7 0.0 copy-done.5
  24.7 0.0 copy-done.7
  24.7 0.0 copy-start
  24.7 12.8 %box_first.1 = (bf16[16,2048]{1,0:T(8,128)(2,1)S(1)}, bf16[16,2048]{1,0:T(8,128)(2,1)S(1)}, bf16[16,2048]{1,0:T(8,128)(2,1)S(1)}, bf16[16,2048]{1,0:T(8,128)(2,1...) custom-call(bf16[16,2560]{1,0:T(8,128)(2,1)S(1)} %copy-done.2, ...), custom_call_target="tpu_custom_call" | custom-call | flops 10000000000 | bytes 10000000 | tf_op jit(solution)/shard_map/box_first/pallas_call | solution.py:505
  37.5 0.0 copy-start.8
  37.5 1.4 %copy-done.8 = bf16[256,4352]{1,0:T(8,128)(2,1)} copy-done((bf16[256,4352]{1,0:T(8,128)(2,1)}, bf16[256,4352]{1,0:T(8,128)(2,1)S(1)}, u32[]{:S(2)}) %copy-start.8) | copy-done | bytes 2228248
  38.9 0.4 collective-permute-start.3
  39.3 3.8 %collective-permute-start.4 = (bf16[16,2048]{1,0:T(8,128)(2,1)S(1)}, bf16[16,2048]{1,0:T(8,128)(2,1)S(1)}, u32[]{:S(2)}, u32[]{:S(2)}) collective-permute-start(bf16[16,2048]{1,0:T(8,128)(2,1)S(1)} %get-tuple-element.36), channel_id=1, source_target_pairs={{0,2},{1,3},{2,0},{3,1},{4,6},{5,7},{6,4},{7,5},{8,10},{9,11},{10,... | collective-permute-start | bytes 196616 | tf_op jit(solution)/shard_map/ppermute | solution.py:522
  43.1 0.0 all-to-all-done.in_ref
  43.1 0.0 copy-done
  43.1 1.4 %select_partner.1 = bf16[8,16,2048]{2,1,0:T(8,128)(2,1)} custom-call(s32[8]{0:T(128)S(1)} %copy-done, bf16[8,16,2048]{2,1,0:T(8,128)(2,1)S(1)} %all-to-all-done.in_ref), custom_call_target="tpu_custom_call" | custom-call | tf_op jit(solution)/shard_map/select_partner/pallas_call | solution.py:541
  44.5 4.2 %all-to-all-start.1 = ((bf16[8,16,2048]{2,1,0:T(8,128)(2,1)}), bf16[8,16,2048]{2,1,0:T(8,128)(2,1)S(1)}, u32[]{:S(2)}, u32[]{:S(2)}) async-start(bf16[8,16,2048]{2,1,0:T(8,128)(2,1)} %select_partner.1), calls=%async_computation.1 | async-start | bytes 1048576 | tf_op jit(solution)/shard_map/all_to_all | solution.py:550
  48.7 0.0 collective-permute-done.6.refs_1_
  48.7 0.3 collective-permute-start.5
  49.0 0.0 collective-permute-done.7.refs_2_
  49.0 0.0 collective-permute-done.8.refs_3_
  49.0 0.0 copy-done.3
  49.0 0.0 copy-start.9
  49.0 1.6 %copy-done.9 = bf16[256,4352]{1,0:T(8,128)(2,1)S(1)} copy-done((bf16[256,4352]{1,0:T(8,128)(2,1)S(1)}, bf16[256,4352]{1,0:T(8,128)(2,1)}, u32[]{:S(2)}) %copy-start.9) | copy-done | bytes 2228248
  50.6 12.0 %box_next.1 = (bf16[16,2048]{1,0:T(8,128)(2,1)S(1)}, bf16[16,2048]{1,0:T(8,128)(2,1)S(1)}, bf16[16,2048]{1,0:T(8,128)(2,1)S(1)}, bf16[16,2048]{1,0:T(8,128)(2,1)S(1)}) custom-call(bf16[16,2048]{1,0:T(8,128)(2,1)S(1)} %copy-done.3, bf16[16,2048]{1,0:T(8,128)(2,1)S(1)} %collective-permute-done.6.refs_1_, bf16[16,2048]{1,0:T(8,128)(2,1)S(1)} %collective-permute-done.7.refs_2_, ...), custom_call_target="tpu_custom_call" | custom-call | flops 10000000000 | bytes 10000000 | tf_op jit(solution)/shard_map/box_next/pallas_call | solution.py:524
  62.7 1.3 %collective-permute-start.10 = (bf16[16,2048]{1,0:T(8,128)(2,1)S(1)}, bf16[16,2048]{1,0:T(8,128)(2,1)S(1)}, u32[]{:S(2)}, u32[]{:S(2)}) collective-permute-start(bf16[16,2048]{1,0:T(8,128)(2,1)S(1)} %get-tuple-element.48), channel_id=1, source_target_pairs={{0,2},{1,3},{2,0},{3,1},{4,6},{5,7},{6,4},{7,5},{8,10},{9,11},{10,... | collective-permute-start | bytes 196616 | tf_op jit(solution)/shard_map/ppermute | solution.py:535
  64.0 2.4 %collective-permute-start.11 = (bf16[16,2048]{1,0:T(8,128)(2,1)S(1)}, bf16[16,2048]{1,0:T(8,128)(2,1)S(1)}, u32[]{:S(2)}, u32[]{:S(2)}) collective-permute-start(bf16[16,2048]{1,0:T(8,128)(2,1)S(1)} %get-tuple-element.49), channel_id=1, source_target_pairs={{0,3},{1,2},{2,1},{3,0},{4,7},{5,6},{6,5},{7,4},{8,11},{9,10},{10,... | collective-permute-start | bytes 196616 | tf_op jit(solution)/shard_map/ppermute | solution.py:535
  66.4 0.0 collective-permute-done.3.refs_1_
  66.4 0.5 collective-permute-start.9
  66.9 0.0 collective-permute-done.4.refs_2_
  66.9 0.0 collective-permute-done.5.refs_3_
  66.9 0.1 arrange.1.refs_0_
  67.0 0.0 copy-start.4
  67.0 4.2 %collective-permute-done.10.refs_3_ = bf16[16,2048]{1,0:T(8,128)(2,1)S(1)} collective-permute-done((bf16[16,2048]{1,0:T(8,128)(2,1)S(1)}, bf16[16,2048]{1,0:T(8,128)(2,1)S(1)}, u32[]{:S(2)}, u32[]{:S(2)}) %collective-permute-start.10) | collective-permute-done | bytes 65568 | tf_op jit(solution)/shard_map/ppermute | solution.py:535
  71.2 0.0 collective-permute-done.11.refs_4_
  71.2 0.7 collective-permute-done.9.refs_2_
  71.9 0.1 join.1.y_ref.sorted_ref
  72.0 0.0 all-to-all-done.1
  72.0 0.4 couple.1
  72.4 2.4 %collective-permute-start.12 = (bf16[2,64,64]{2,1,0:T(8,128)(2,1)S(1)}, bf16[2,64,64]{2,1,0:T(8,128)(2,1)S(1)}, u32[]{:S(2)}, u32[]{:S(2)}) collective-permute-start(bf16[2,64,64]{2,1,0:T(8,128)(2,1)S(1)} %couple.1), channel_id=1, source_target_pairs={{0,3},{1,2},{2,1},{3,0},{4,7},{5,6},{6,5},{7,4},{8,11},{9,10},{10,... | collective-permute-start | bytes 49160 | tf_op jit(solution)/shard_map/ppermute | solution.py:584
  74.8 0.0 collective-permute-start.13
  74.8 2.0 %collective-permute-start.14 = (bf16[2,64,64]{2,1,0:T(8,128)(2,1)S(1)}, bf16[2,64,64]{2,1,0:T(8,128)(2,1)S(1)}, u32[]{:S(2)}, u32[]{:S(2)}) collective-permute-start(bf16[2,64,64]{2,1,0:T(8,128)(2,1)S(1)} %couple.1), channel_id=1, source_target_pairs={{0,1},{1,0},{2,3},{3,2},{4,5},{5,4},{6,7},{7,6},{8,9},{9,8},{10,11... | collective-permute-start | bytes 49160 | tf_op jit(solution)/shard_map/ppermute | solution.py:584
  76.9 0.0 copy-done.4
  76.9 2.1 %unsort.1 = bf16[128,2048]{1,0:T(8,128)(2,1)} custom-call(bf16[128,2048]{1,0:T(8,128)(2,1)S(1)} %join.1.y_ref.sorted_ref, s32[1,2048]{1,0:T(1,128)S(1)} %copy-done.4), custom_call_target="tpu_custom_call" | custom-call | flops 1000000000 | bytes 10000000 | tf_op jit(solution)/shard_map/unsort/pallas_call | solution.py:585
  78.9 0.0 collective-permute-done.12
  79.0 0.7 collective-permute-done.13
  79.6 0.0 collective-permute-done.14
  79.6 0.7 multiply_bitcast_fusion
  (2 shorter events, 0.0 us)
Async XLA Ops:
  6.0 18.4 %collective-permute-start = (bf16[16,2560]{1,0:T(8,128)(2,1)}, bf16[16,2560]{1,0:T(8,128)(2,1)S(1)}, u32[]{:S(2)}, u32[]{:S(2)}) collective-permute-start(bf16[16,2560]{1,0:T(8,128)(2,1)} %get-tuple-element.28), channel_id=1, source_target_pairs={{0,1},{1,0},{2,3},{3,2},{4,5},{5,4},{6,7},{7,6},{8,9},{9,8},{10,11... | collective-permute-start | bytes 245768 | tf_op jit(solution)/shard_map/ppermute | solution.py:477
  9.1 15.6 %collective-permute-start.1 = (bf16[16,2560]{1,0:T(8,128)(2,1)}, bf16[16,2560]{1,0:T(8,128)(2,1)S(1)}, u32[]{:S(2)}, u32[]{:S(2)}) collective-permute-start(bf16[16,2560]{1,0:T(8,128)(2,1)} %get-tuple-element.29), channel_id=1, source_target_pairs={{0,2},{1,3},{2,0},{3,1},{4,6},{5,7},{6,4},{7,5},{8,10},{9,11},{10,... | collective-permute-start | bytes 245768 | tf_op jit(solution)/shard_map/ppermute | solution.py:477
  11.7 13.0 %collective-permute-start.2 = (bf16[16,2560]{1,0:T(8,128)(2,1)}, bf16[16,2560]{1,0:T(8,128)(2,1)S(1)}, u32[]{:S(2)}, u32[]{:S(2)}) collective-permute-start(bf16[16,2560]{1,0:T(8,128)(2,1)} %get-tuple-element.30), channel_id=1, source_target_pairs={{0,3},{1,2},{2,1},{3,0},{4,7},{5,6},{6,5},{7,4},{8,11},{9,10},{10,... | collective-permute-start | bytes 245768 | tf_op jit(solution)/shard_map/ppermute | solution.py:477
  11.7 37.0 %collective-permute-start.6 = (bf16[16,2048]{1,0:T(8,128)(2,1)}, bf16[16,2048]{1,0:T(8,128)(2,1)S(1)}, u32[]{:S(2)}, u32[]{:S(2)}) collective-permute-start(bf16[16,2048]{1,0:T(8,128)(2,1)} %get-tuple-element.39), channel_id=1, source_target_pairs={{0,1},{1,0},{2,3},{3,2},{4,5},{5,4},{6,7},{7,6},{8,9},{9,8},{10,11... | collective-permute-start | bytes 196616 | tf_op jit(solution)/shard_map/ppermute | solution.py:477
  12.6 36.4 %collective-permute-start.7 = (bf16[16,2048]{1,0:T(8,128)(2,1)}, bf16[16,2048]{1,0:T(8,128)(2,1)S(1)}, u32[]{:S(2)}, u32[]{:S(2)}) collective-permute-start(bf16[16,2048]{1,0:T(8,128)(2,1)} %get-tuple-element.40), channel_id=1, source_target_pairs={{0,2},{1,3},{2,0},{3,1},{4,6},{5,7},{6,4},{7,5},{8,10},{9,11},{10,... | collective-permute-start | bytes 196616 | tf_op jit(solution)/shard_map/ppermute | solution.py:477
  16.0 8.3 %copy-start.10 = (bf16[16,2048]{1,0:T(8,128)(2,1)S(1)}, bf16[16,2048]{1,0:T(8,128)(2,1)}, u32[]{:S(2)}) copy-start(bf16[16,2048]{1,0:T(8,128)(2,1)} %get-tuple-element.41) | copy-start | bytes 196612
  16.0 8.6 %copy-start.2 = (bf16[16,2560]{1,0:T(8,128)(2,1)S(1)}, bf16[16,2560]{1,0:T(8,128)(2,1)}, u32[]{:S(2)}) copy-start(bf16[16,2560]{1,0:T(8,128)(2,1)} %get-tuple-element.27.refs_0_) | copy-start | bytes 245764
  16.0 8.6 %copy-start.5 = (bf16[2,128,128]{2,1,0:T(8,128)(2,1)S(1)}, bf16[2,128,128]{2,1,0:T(8,128)(2,1)}, u32[]{:S(2)}) copy-start(bf16[2,128,128]{2,1,0:T(8,128)(2,1)} %constant.18.clone.refs_8_.refs_5_) | copy-start | bytes 196612
  16.0 8.6 %copy-start.7 = (bf16[64,256]{1,0:T(8,128)(2,1)S(1)}, bf16[64,256]{1,0:T(8,128)(2,1)}, u32[]{:S(2)}) copy-start(bf16[64,256]{1,0:T(8,128)(2,1)} %constant.17.clone.cs_ref.refs_5_) | copy-start | bytes 98308
  16.1 27.0 %all-to-all-start = ((bf16[8,16,2048]{2,1,0:T(8,128)(2,1)}), bf16[8,16,2048]{2,1,0:T(8,128)(2,1)S(1)}, u32[]{:S(2)}, u32[]{:S(2)}) async-start(bf16[8,16,2048]{2,1,0:T(8,128)(2,1)} %bitcast.16), calls=%async_computation | async-start | bytes 1048576 | tf_op jit(solution)/shard_map/all_to_all | solution.py:538
  19.9 1.6 %copy-start.1 = (f32[64,64,128]{2,1,0:T(8,128)S(1)}, f32[64,64,128]{2,1,0:T(8,128)}, u32[]{:S(2)}) copy-start(f32[64,64,128]{2,1,0:T(8,128)} %param.9) | copy-start | bytes 6291460
  21.5 0.8 copy-start.6
  24.4 24.6 %collective-permute-start.8 = (bf16[16,2048]{1,0:T(8,128)(2,1)S(1)}, bf16[16,2048]{1,0:T(8,128)(2,1)S(1)}, u32[]{:S(2)}, u32[]{:S(2)}) collective-permute-start(bf16[16,2048]{1,0:T(8,128)(2,1)S(1)} %copy-done.10), channel_id=1, source_target_pairs={{0,3},{1,2},{2,1},{3,0},{4,7},{5,6},{6,5},{7,4},{8,11},{9,10},{10,... | collective-permute-start | bytes 196616 | tf_op jit(solution)/shard_map/ppermute | solution.py:477
  24.7 18.4 %copy-start = (s32[8]{0:T(128)S(1)}, s32[8]{0:T(128)}, u32[]{:S(2)}) copy-start(s32[8]{0:T(128)} %order_ref.1) | copy-start | bytes 100
  37.5 1.4 %copy-start.8 = (bf16[256,4352]{1,0:T(8,128)(2,1)}, bf16[256,4352]{1,0:T(8,128)(2,1)S(1)}, u32[]{:S(2)}) copy-start(bf16[256,4352]{1,0:T(8,128)(2,1)S(1)} %get-tuple-element.42.refs_6_) | copy-start | bytes 6684676
  38.9 10.1 %copy-start.3 = (bf16[16,2048]{1,0:T(8,128)(2,1)S(1)}, bf16[16,2048]{1,0:T(8,128)(2,1)}, u32[]{:S(2)}) copy-start(bf16[16,2048]{1,0:T(8,128)(2,1)} %get-tuple-element.38.refs_0_) | copy-start | bytes 196612
  38.9 27.5 %collective-permute-start.3 = (bf16[16,2048]{1,0:T(8,128)(2,1)S(1)}, bf16[16,2048]{1,0:T(8,128)(2,1)S(1)}, u32[]{:S(2)}, u32[]{:S(2)}) collective-permute-start(bf16[16,2048]{1,0:T(8,128)(2,1)S(1)} %get-tuple-element.35), channel_id=1, source_target_pairs={{0,1},{1,0},{2,3},{3,2},{4,5},{5,4},{6,7},{7,6},{8,9},{9,8},{10,11... | collective-permute-start | bytes 196616 | tf_op jit(solution)/shard_map/ppermute | solution.py:522
  39.3 27.6 %collective-permute-start.4 = (bf16[16,2048]{1,0:T(8,128)(2,1)S(1)}, bf16[16,2048]{1,0:T(8,128)(2,1)S(1)}, u32[]{:S(2)}, u32[]{:S(2)}) collective-permute-start(bf16[16,2048]{1,0:T(8,128)(2,1)S(1)} %get-tuple-element.36), channel_id=1, source_target_pairs={{0,2},{1,3},{2,0},{3,1},{4,6},{5,7},{6,4},{7,5},{8,10},{9,11},{10,... | collective-permute-start | bytes 196616 | tf_op jit(solution)/shard_map/ppermute | solution.py:522
  44.5 27.5 %all-to-all-start.1 = ((bf16[8,16,2048]{2,1,0:T(8,128)(2,1)}), bf16[8,16,2048]{2,1,0:T(8,128)(2,1)S(1)}, u32[]{:S(2)}, u32[]{:S(2)}) async-start(bf16[8,16,2048]{2,1,0:T(8,128)(2,1)} %select_partner.1), calls=%async_computation.1 | async-start | bytes 1048576 | tf_op jit(solution)/shard_map/all_to_all | solution.py:550
  48.7 18.2 %collective-permute-start.5 = (bf16[16,2048]{1,0:T(8,128)(2,1)S(1)}, bf16[16,2048]{1,0:T(8,128)(2,1)S(1)}, u32[]{:S(2)}, u32[]{:S(2)}) collective-permute-start(bf16[16,2048]{1,0:T(8,128)(2,1)S(1)} %get-tuple-element.37), channel_id=1, source_target_pairs={{0,3},{1,2},{2,1},{3,0},{4,7},{5,6},{6,5},{7,4},{8,11},{9,10},{10,... | collective-permute-start | bytes 196616 | tf_op jit(solution)/shard_map/ppermute | solution.py:522
  49.0 1.6 %copy-start.9 = (bf16[256,4352]{1,0:T(8,128)(2,1)S(1)}, bf16[256,4352]{1,0:T(8,128)(2,1)}, u32[]{:S(2)}) copy-start(bf16[256,4352]{1,0:T(8,128)(2,1)} %copy-done.8) | copy-start | bytes 6684676
  62.7 8.5 %collective-permute-start.10 = (bf16[16,2048]{1,0:T(8,128)(2,1)S(1)}, bf16[16,2048]{1,0:T(8,128)(2,1)S(1)}, u32[]{:S(2)}, u32[]{:S(2)}) collective-permute-start(bf16[16,2048]{1,0:T(8,128)(2,1)S(1)} %get-tuple-element.48), channel_id=1, source_target_pairs={{0,2},{1,3},{2,0},{3,1},{4,6},{5,7},{6,4},{7,5},{8,10},{9,11},{10,... | collective-permute-start | bytes 196616 | tf_op jit(solution)/shard_map/ppermute | solution.py:535
  64.0 7.2 %collective-permute-start.11 = (bf16[16,2048]{1,0:T(8,128)(2,1)S(1)}, bf16[16,2048]{1,0:T(8,128)(2,1)S(1)}, u32[]{:S(2)}, u32[]{:S(2)}) collective-permute-start(bf16[16,2048]{1,0:T(8,128)(2,1)S(1)} %get-tuple-element.49), channel_id=1, source_target_pairs={{0,3},{1,2},{2,1},{3,0},{4,7},{5,6},{6,5},{7,4},{8,11},{9,10},{10,... | collective-permute-start | bytes 196616 | tf_op jit(solution)/shard_map/ppermute | solution.py:535
  66.4 5.5 %collective-permute-start.9 = (bf16[16,2048]{1,0:T(8,128)(2,1)S(1)}, bf16[16,2048]{1,0:T(8,128)(2,1)S(1)}, u32[]{:S(2)}, u32[]{:S(2)}) collective-permute-start(bf16[16,2048]{1,0:T(8,128)(2,1)S(1)} %get-tuple-element.47), channel_id=1, source_target_pairs={{0,1},{1,0},{2,3},{3,2},{4,5},{5,4},{6,7},{7,6},{8,9},{9,8},{10,11... | collective-permute-start | bytes 196616 | tf_op jit(solution)/shard_map/ppermute | solution.py:535
  67.0 9.9 %copy-start.4 = (s32[1,2048]{1,0:T(1,128)S(1)}, s32[1,2048]{1,0:T(1,128)}, u32[]{:S(2)}) copy-start(s32[1,2048]{1,0:T(1,128)} %get-tuple-element.50.rank_ref) | copy-start | bytes 24580
  72.4 6.5 %collective-permute-start.12 = (bf16[2,64,64]{2,1,0:T(8,128)(2,1)S(1)}, bf16[2,64,64]{2,1,0:T(8,128)(2,1)S(1)}, u32[]{:S(2)}, u32[]{:S(2)}) collective-permute-start(bf16[2,64,64]{2,1,0:T(8,128)(2,1)S(1)} %couple.1), channel_id=1, source_target_pairs={{0,3},{1,2},{2,1},{3,0},{4,7},{5,6},{6,5},{7,4},{8,11},{9,10},{10,... | collective-permute-start | bytes 49160 | tf_op jit(solution)/shard_map/ppermute | solution.py:584
  74.8 4.8 %collective-permute-start.13 = (bf16[2,64,64]{2,1,0:T(8,128)(2,1)S(1)}, bf16[2,64,64]{2,1,0:T(8,128)(2,1)S(1)}, u32[]{:S(2)}, u32[]{:S(2)}) collective-permute-start(bf16[2,64,64]{2,1,0:T(8,128)(2,1)S(1)} %couple.1), channel_id=1, source_target_pairs={{0,2},{1,3},{2,0},{3,1},{4,6},{5,7},{6,4},{7,5},{8,10},{9,11},{10,... | collective-permute-start | bytes 49160 | tf_op jit(solution)/shard_map/ppermute | solution.py:584
  74.8 4.8 %collective-permute-start.14 = (bf16[2,64,64]{2,1,0:T(8,128)(2,1)S(1)}, bf16[2,64,64]{2,1,0:T(8,128)(2,1)S(1)}, u32[]{:S(2)}, u32[]{:S(2)}) collective-permute-start(bf16[2,64,64]{2,1,0:T(8,128)(2,1)S(1)} %couple.1), channel_id=1, source_target_pairs={{0,1},{1,0},{2,3},{3,2},{4,5},{5,4},{6,7},{7,6},{8,9},{9,8},{10,11... | collective-permute-start | bytes 49160 | tf_op jit(solution)/shard_map/ppermute | solution.py:584

commit v7 on v6

--- a/solution.py
+++ b/solution.py
@@ -12,7 +12,7 @@
 STICK_DEV = 64
 LANES = 128
 UNROLL = 8
-CHUNKS = 2
+CHUNKS = 1
 BF16 = jnp.bfloat16
 F32 = jnp.float32
 VMEM_LIMIT = 24 * 1024 * 1024
@@ -87,22 +87,19 @@
     bands = both // 2
     share = bands // groups
     rows = 2 * share // CHUNKS
-    lane = lax.broadcasted_iota(jnp.int32, (STICK_DEV, side), 1).astype(F32)
     cells = jnp.concatenate([cells[i : i + rows] for i in range(0, side, rows)], axis=1)
-    slot = lax.broadcasted_iota(jnp.int32, (rows, LANES), 1) // rows
-    place = jnp.zeros((rows, LANES), F32)
-    count = 0
-    for hot in (xh, yh):
-        at = jnp.minimum(dot_nt(ch, hot), 1.0)
-        value = jnp.sum(at * lane, axis=1, keepdims=True)
-        for i in range(0, STICK_DEV, rows):
-            place = jnp.where(slot == count, value[i : i + rows], place)
-            count += 1
     tiles = waves // LANES
     in_tile = one_hot(rank & (LANES - 1), LANES)
     col = dot_nt(one_hot(rank >> 7, tiles) * slot_of.astype(BF16), in_tile)
-    col = [col[i : i + rows] for i in range(0, tiles, rows)]
-    extra = jnp.concatenate([cells, place] + col, axis=1).astype(BF16)
+    steps = lax.broadcasted_iota(jnp.int32, (8, side), 1).astype(F32).astype(BF16)
+    place = [dot_nt(steps, jnp.minimum(dot_nt(ch, hot), 1.0).astype(BF16)) for hot in (xh, yh)]
+    lines = [col, jnp.concatenate(place, axis=1)]
+    spare = -(tiles + 8) % rows
+    if spare:
+        lines.append(jnp.zeros((spare, LANES), F32))
+    lines = jnp.concatenate(lines, axis=0)
+    lines = [lines[i : i + rows] for i in range(0, lines.shape[0], rows)]
+    extra = jnp.concatenate([cells] + lines, axis=1).astype(BF16)
     low = one_hot(rank & 255, 256)
     for shift in range(groups):
         outs[shift * CHUNKS][:, waves:] = extra
@@ -179,7 +176,6 @@
     tiles = waves // LANES
     cells_end = waves + parts * STICK_DEV
     tri = triangles(side)
-    lane_f = lax.broadcasted_iota(jnp.int32, (STICK_DEV, side), 1).astype(F32)
     ahead = jnp.where(
         lax.broadcasted_iota(jnp.int32, (side, LANES), 0)
         < lax.broadcasted_iota(jnp.int32, (side, LANES), 1),
@@ -192,24 +188,23 @@
             [x_ref[:, waves + i * STICK_DEV : waves + (i + 1) * STICK_DEV].astype(F32) for i in range(parts)],
             axis=0,
         )
-        place = x_ref[:, cells_end : cells_end + LANES].astype(F32)
-        for which, hots in enumerate((at_x, at_y)):
-            value = jnp.concatenate(
-                [place[:, i * rows : i * rows + 1] for i in range(which * parts, (which + 1) * parts)],
-                axis=0,
-            )
-            hots.append(jnp.where(lane_f == value, 1.0, 0.0))
+        lines = jnp.concatenate(
+            [
+                x_ref[:, i : i + LANES].astype(F32)
+                for i in range(cells_end, cells_end + -(-(tiles + 8) // rows) * LANES, LANES)
+            ],
+            axis=0,
+        )
+        place = lines[tiles : tiles + 1].astype(jnp.int32)
+        at_x.append(one_hot(place[:, :side], side).astype(F32).T)
+        at_y.append(one_hot(place[:, side:], side).astype(F32).T)
         ranks = prefix(cells.astype(BF16), tri)
         begins = jnp.minimum(jnp.floor(ranks[:, :1] * (1.0 / STICK_DEV)), waves // STICK_DEV - 1.0)
         spot = jnp.where(cells > 0.5, ranks - begins * STICK_DEV, -1.0)
         spot_ref[d] = jnp.concatenate([spot, spot], axis=1)
         level = dot_nt(jnp.ones((8, STICK_DEV), BF16), cells.astype(BF16))
         start_ref[d : d + 1, :] = dot(level.astype(BF16), ahead)[:1].astype(jnp.int32)
-        begin = cells_end + LANES
-        col = jnp.concatenate(
-            [x_ref[:, begin + i * LANES : begin + (i + 1) * LANES].astype(F32) for i in range(tiles // rows)],
-            axis=0,
-        ) + float((d % 2) * STICK_DEV)
+        col = lines[:tiles] + float((d % 2) * STICK_DEV)
         turned = pltpu.roll(col, STICK_DEV, 1)
         after = jnp.concatenate([turned[1:], turned[:1]], axis=0)
         col_ref[0, d] = col.astype(jnp.int32)
@@ -319,21 +314,25 @@
 
     levels(expand)
 
-    def depth_in(b, carry):
-        both = jnp.concatenate(
-            [
-                jnp.concatenate(
-                    [grid[n, pl.ds(b * side, side), :], grid[n, pl.ds((bands + b) * side, side), :]],
-                    axis=0,
-                )
-                for n in range(groups // 2)
-            ],
-            axis=1,
-        ).astype(BF16)
-        t_scr[pl.ds(b * span, span), :] = dot(wz_ref[0], both).astype(BF16)
+    def depth_in(g, carry):
+        for b in [g * team + i for i in range(team)]:
+            both = jnp.concatenate(
+                [
+                    jnp.concatenate(
+                        [
+                            grid[n, pl.ds(b * side, side), :].astype(BF16),
+                            grid[n, pl.ds((bands + b) * side, side), :].astype(BF16),
+                        ],
+                        axis=0,
+                    )
+                    for n in range(groups // 2)
+                ],
+                axis=1,
+            )
+            t_scr[pl.ds(b * span, span), :] = dot(wz_ref[0], both).astype(BF16)
         return carry
 
-    lax.fori_loop(0, bands, depth_in, 0)
+    lax.fori_loop(0, bands // team, depth_in, 0)
 
     def planes(g, carry):
         rows_g = pl.ds(g * team * span, team * span)
@@ -399,8 +398,10 @@
 def couple_kernel(partner_ref, sorted_ref, g_ref):
     products = dot_nt(partner_ref[...], sorted_ref[...])
     half = products.shape[0] // 2
-    g_ref[0] = (products[:half, :half] + products[half:, half:]).astype(BF16)
-    g_ref[1] = (products[:half, half:] - products[half:, :half]).astype(BF16)
+    re = products[:half, :half] + products[half:, half:]
+    im = products[:half, half:] - products[half:, :half]
+    for i in range(g_ref.shape[0]):
+        g_ref[i] = jnp.concatenate([re, im], axis=1).astype(BF16)
 
 
 def unsort_kernel(y_ref, rank_ref, out_ref):
@@ -448,7 +449,7 @@
     pool_count = lax.axis_size("pool")
     rows = 2 * share // CHUNKS
     tiles = waves // LANES
-    packed = waves + side * STICK_DEV // rows + LANES + tiles * LANES // rows
+    packed = waves + side * STICK_DEV // rows + -(-(tiles + 8) // rows) * LANES
     scalars, blocks = whole(pltpu.SMEM), [whole()] * fft_count
 
     *ordered, ordered_all, rank = pl.pallas_call(
@@ -575,13 +576,13 @@
     )(me_row, *arranged, *returned[-1])
     sums = pl.pallas_call(
         couple_kernel,
-        out_shape=jax.ShapeDtypeStruct((2, bands, bands), BF16),
+        out_shape=jax.ShapeDtypeStruct((fft_count, bands, 2 * bands), BF16),
         in_specs=[whole(), whole()],
         out_specs=whole(),
         compiler_params=params(),
         name="couple",
     )(partner, sorted_response)
-    shares = [sums] + [lax.ppermute(sums, "fft", pairs[s]) for s in range(1, fft_count)]
+    shares = lax.all_to_all(sums, "fft", 0, 0, tiled=True)
     response = pl.pallas_call(
         unsort_kernel,
         out_shape=jax.ShapeDtypeStruct((2 * bands, waves), BF16),
@@ -591,14 +592,8 @@
         cost_estimate=pl.CostEstimate(flops=10**9, bytes_accessed=10**7, transcendentals=0),
         name="unsort",
     )(sorted_response, rank)
-    summed = None
-    for d in range(fft_count):
-        offset = me ^ d
-        term = shares[0]
-        for s in range(1, fft_count):
-            term = jnp.where(offset == s, shares[s], term)
-        term = term.astype(F32)
-        summed = term if summed is None else summed + term
+    summed = jnp.sum(shares.astype(F32), axis=0)
+    summed = jnp.stack([summed[:, :bands], summed[:, bands:]])
     coupling = (summed / jnp.sqrt(jnp.float32(waves * fft_count)))[:, None]
     return response.reshape(2, 1, bands, waves), coupling
 

time: 80.8 us -> 76.1 us (0.942)
  waiting for transfers between devices: 5.64 us -> 15.6 us
  starting transfers between devices: 31.5 us -> 22.8 us
  local copies, waits for them, and re-layouts: 5.38 us -> 2.44 us
  Pallas kernels: 36.3 us -> 33.4 us
    pallas_call x3 -> x1, Pallas kernels: 12.5 us -> 1 us  [shards(): pl.pallas_call(couple_kernel, out_shape=jax.ShapeDtypeStruct((fft_count,...]
    pallas_call x1, Pallas kernels: 12.8 us -> 21.2 us  [shards(): pl.pallas_call(functools.partial(box_first_kernel, side, chunks, team, wa...]
    ppermute x6 -> x3, starting transfers between devices: 10.4 us -> 4.45 us  [shards(): lax.ppermute(ordered[s * CHUNKS + c], 'fft', pairs[s])]
    ppermute x6 -> x3, waiting for transfers between devices: 4.92 us -> 9.93 us  [shards(): lax.ppermute(back[s], 'fft', pairs[s])]
    ppermute x3 -> x0, starting transfers between devices: 4.42 us -> none  [shards(): lax.ppermute(sums, 'fft', pairs[s])]
    all_to_all x0 -> x1, starting transfers between devices: none -> 4.2 us  [shards(): shares = lax.all_to_all(sums, 'fft', 0, 0, tiled=True)]
    all_to_all x0 -> x1, waiting for transfers between devices: none -> 3.66 us  [shards(): shares = lax.all_to_all(sums, 'fft', 0, 0, tiled=True)]
    ppermute x6 -> x3, starting transfers between devices: 8.69 us -> 5.48 us  [shards(): lax.ppermute(back[s], 'fft', pairs[s])]
  transfers between devices with their start and end apart: 17 -> 9, of which waited for: 3 -> 5; matrix products, arithmetic and copies ran while one was open for 0% -> 0% of each run, Pallas kernels for 38% -> 36%
where the time goes in v7:
time: 76.1 us; the launch traced here: 75.6 us
  Pallas kernels  33.4 us (44%)
  starting transfers between devices  22.8 us (30%)
  waiting for transfers between devices  15.6 us (20%)
  local copies, waits for them, and re-layouts  2.44 us (3%)
    pallas_call x1, Pallas kernels, shards(): pl.pallas_call(functools.partial(box_first_kernel, side, chunks, team, wa...  21.2 us
    ppermute x3, waiting for transfers between devices, shards(): lax.ppermute(back[s], 'fft', pairs[s])  9.93 us
    ppermute x3, starting transfers between devices, shards(): lax.ppermute(back[s], 'fft', pairs[s])  5.48 us
    pallas_call x1, Pallas kernels, shards(): pl.pallas_call(functools.partial(sort_kernel, side, fft_count), out_shape...  5.46 us
    all_to_all x1, starting transfers between devices, shards(): lax.all_to_all(ordered_all.reshape(pool_count, 2 * bands // pool_count, w...  5.17 us
    ppermute x3, starting transfers between devices, shards(): lax.ppermute(ordered[s * CHUNKS + c], 'fft', pairs[s])  4.45 us
    all_to_all x1, starting transfers between devices, shards(): shares = lax.all_to_all(sums, 'fft', 0, 0, tiled=True)  4.2 us
    all_to_all x1, waiting for transfers between devices, shards(): shares = lax.all_to_all(sums, 'fft', 0, 0, tiled=True)  3.66 us
  transfers between devices with their start and end apart: 9, of which 5 were waited for; matrix products, arithmetic and copies ran while one was open for 0% of the time, Pallas kernels for 36%

profile of v7, /device:TPU:0, one launch (start us, length us, event | category | flops | bytes accessed | tf_op | source)
XLA Modules:
  0.0 75.6 jit_solution(15061814399319434758)
XLA Ops:
  0.6 5.5 %sort_waves.1 = (bf16[32,2304]{1,0:T(8,128)(2,1)}, bf16[32,2304]{1,0:T(8,128)(2,1)}, bf16[32,2304]{1,0:T(8,128)(2,1)}, bf16[32,2304]{1,0:T(8,128)(2,1)}, bf16[128,2048]{1,0:T(8,128)(2,1)}, /*index=5*/s32[1,2048]{1,0:T(1,128)}) custom-call(s32[1]{0:T(128)} %bitcast.me_ref, s32[1,2048]{1,0:T(1,128)} %bitcast.17, bf16[128,2048]{1,0:T(8,128)(2,1)} %bitcast.15), custom_call_target="tpu_custom_call" | custom-call | tf_op jit(solution)/shard_map/sort_waves/pallas_call | solution.py:455
  6.1 5.2 %all-to-all-start = ((bf16[8,16,2048]{2,1,0:T(8,128)(2,1)}), bf16[8,16,2048]{2,1,0:T(8,128)(2,1)S(1)}, u32[]{:S(2)}, u32[]{:S(2)}) async-start(bf16[8,16,2048]{2,1,0:T(8,128)(2,1)} %bitcast.16), calls=%async_computation | async-start | bytes 1048576 | tf_op jit(solution)/shard_map/all_to_all | solution.py:539
  11.3 0.0 copy-start
  11.3 1.6 %collective-permute-start = (bf16[32,2304]{1,0:T(8,128)(2,1)}, bf16[32,2304]{1,0:T(8,128)(2,1)S(1)}, u32[]{:S(2)}, u32[]{:S(2)}) collective-permute-start(bf16[32,2304]{1,0:T(8,128)(2,1)} %get-tuple-element.16), channel_id=1, source_target_pairs={{0,1},{1,0},{2,3},{3,2},{4,5},{5,4},{6,7},{7,6},{8,9},{9,8},{10,11... | collective-permute-start | bytes 442376 | tf_op jit(solution)/shard_map/ppermute | solution.py:478
  12.9 2.6 %collective-permute-start.1 = (bf16[32,2304]{1,0:T(8,128)(2,1)}, bf16[32,2304]{1,0:T(8,128)(2,1)S(1)}, u32[]{:S(2)}, u32[]{:S(2)}) collective-permute-start(bf16[32,2304]{1,0:T(8,128)(2,1)} %get-tuple-element.17), channel_id=1, source_target_pairs={{0,2},{1,3},{2,0},{3,1},{4,6},{5,7},{6,4},{7,5},{8,10},{9,11},{10,... | collective-permute-start | bytes 442376 | tf_op jit(solution)/shard_map/ppermute | solution.py:478
  15.5 0.2 collective-permute-start.2
  15.7 0.0 copy-start.1
  15.7 1.6 %copy-done.1 = f32[64,64,128]{2,1,0:T(8,128)S(1)} copy-done((f32[64,64,128]{2,1,0:T(8,128)S(1)}, f32[64,64,128]{2,1,0:T(8,128)}, u32[]{:S(2)}) %copy-start.1) | copy-done | bytes 2097176
  17.3 0.0 copy-start.5
  17.3 0.8 copy-done.5
  18.1 0.0 copy-start.2
  18.1 0.0 copy-start.4
  18.1 0.0 copy-start.6
  18.1 2.1 %field_pairs.1 = (bf16[4,64,2176]{2,1,0:T(8,128)(2,1)S(1)}, bf16[64,2176]{1,0:T(8,128)(2,1)S(1)}, bf16[64,2176]{1,0:T(8,128)(2,1)S(1)}) custom-call(f32[4096,128]{1,0:T(8,128)S(1)} %bitcast.14, bf16[64,256]{1,0:T(8,128)(2,1)S(1)} %copy-done.5), custom_call_target="tpu_custom_call" | custom-call | flops 1000000000 | bytes 10000000 | tf_op jit(solution)/shard_map/field_pairs/pallas_call | solution.py:482
  20.2 0.8 %all-to-all-done.in_ref = bf16[8,16,2048]{2,1,0:T(8,128)(2,1)S(1)} async-done(((bf16[8,16,2048]{2,1,0:T(8,128)(2,1)}), bf16[8,16,2048]{2,1,0:T(8,128)(2,1)S(1)}, u32[]{:S(2)}, u32[]{:S(2)}) %all-to-all-start) | async-done | bytes 524320 | tf_op jit(solution)/shard_map/all_to_all | solution.py:539
  21.0 0.0 copy-done
  21.0 1.4 %select_partner.1 = bf16[8,16,2048]{2,1,0:T(8,128)(2,1)} custom-call(s32[8]{0:T(128)S(1)} %copy-done, bf16[8,16,2048]{2,1,0:T(8,128)(2,1)S(1)} %all-to-all-done.in_ref), custom_call_target="tpu_custom_call" | custom-call | tf_op jit(solution)/shard_map/select_partner/pallas_call | solution.py:542
  22.4 3.5 %all-to-all-start.1 = ((bf16[8,16,2048]{2,1,0:T(8,128)(2,1)}), bf16[8,16,2048]{2,1,0:T(8,128)(2,1)S(1)}, u32[]{:S(2)}, u32[]{:S(2)}) async-start(bf16[8,16,2048]{2,1,0:T(8,128)(2,1)} %select_partner.1), calls=%async_computation.1 | async-start | bytes 1048576 | tf_op jit(solution)/shard_map/all_to_all | solution.py:551
  25.9 0.0 collective-permute-done.refs_1_
  25.9 1.1 %collective-permute-done.1.refs_2_ = bf16[32,2304]{1,0:T(8,128)(2,1)S(1)} collective-permute-done((bf16[32,2304]{1,0:T(8,128)(2,1)}, bf16[32,2304]{1,0:T(8,128)(2,1)S(1)}, u32[]{:S(2)}, u32[]{:S(2)}) %collective-permute-start.1) | collective-permute-done | bytes 147488 | tf_op jit(solution)/shard_map/ppermute | solution.py:478
  27.1 0.0 collective-permute-done.2.refs_3_
  27.1 0.0 copy-done.2
  27.1 0.0 copy-done.4
  27.1 0.0 copy-done.6
  27.1 21.2 %box_first.1 = (bf16[32,2048]{1,0:T(8,128)(2,1)S(1)}, bf16[32,2048]{1,0:T(8,128)(2,1)S(1)}, bf16[32,2048]{1,0:T(8,128)(2,1)S(1)}, bf16[32,2048]{1,0:T(8,128)(2,1...) custom-call(bf16[32,2304]{1,0:T(8,128)(2,1)S(1)} %copy-done.2, ...), custom_call_target="tpu_custom_call" | custom-call | flops 10000000000 | bytes 10000000 | tf_op jit(solution)/shard_map/box_first/pallas_call | solution.py:506
  48.3 0.0 copy-start.3
  48.3 3.0 %collective-permute-start.3 = (bf16[32,2048]{1,0:T(8,128)(2,1)S(1)}, bf16[32,2048]{1,0:T(8,128)(2,1)S(1)}, u32[]{:S(2)}, u32[]{:S(2)}) collective-permute-start(bf16[32,2048]{1,0:T(8,128)(2,1)S(1)} %get-tuple-element.23), channel_id=1, source_target_pairs={{0,1},{1,0},{2,3},{3,2},{4,5},{5,4},{6,7},{7,6},{8,9},{9,8},{10,11... | collective-permute-start | bytes 393224 | tf_op jit(solution)/shard_map/ppermute | solution.py:523
  51.3 1.1 %collective-permute-start.4 = (bf16[32,2048]{1,0:T(8,128)(2,1)S(1)}, bf16[32,2048]{1,0:T(8,128)(2,1)S(1)}, u32[]{:S(2)}, u32[]{:S(2)}) collective-permute-start(bf16[32,2048]{1,0:T(8,128)(2,1)S(1)} %get-tuple-element.24), channel_id=1, source_target_pairs={{0,2},{1,3},{2,0},{3,1},{4,6},{5,7},{6,4},{7,5},{8,10},{9,11},{10,... | collective-permute-start | bytes 393224 | tf_op jit(solution)/shard_map/ppermute | solution.py:523
  52.4 1.4 %collective-permute-start.5 = (bf16[32,2048]{1,0:T(8,128)(2,1)S(1)}, bf16[32,2048]{1,0:T(8,128)(2,1)S(1)}, u32[]{:S(2)}, u32[]{:S(2)}) collective-permute-start(bf16[32,2048]{1,0:T(8,128)(2,1)S(1)} %get-tuple-element.25), channel_id=1, source_target_pairs={{0,3},{1,2},{2,1},{3,0},{4,7},{5,6},{6,5},{7,4},{8,11},{9,10},{10,... | collective-permute-start | bytes 393224 | tf_op jit(solution)/shard_map/ppermute | solution.py:523
  53.8 1.8 %collective-permute-done.3.refs_1_ = bf16[32,2048]{1,0:T(8,128)(2,1)S(1)} collective-permute-done((bf16[32,2048]{1,0:T(8,128)(2,1)S(1)}, bf16[32,2048]{1,0:T(8,128)(2,1)S(1)}, u32[]{:S(2)}, u32[]{:S(2)}) %collective-permute-start.3) | collective-permute-done | bytes 131104 | tf_op jit(solution)/shard_map/ppermute | solution.py:523
  55.6 8.1 %collective-permute-done.4.refs_2_ = bf16[32,2048]{1,0:T(8,128)(2,1)S(1)} collective-permute-done((bf16[32,2048]{1,0:T(8,128)(2,1)S(1)}, bf16[32,2048]{1,0:T(8,128)(2,1)S(1)}, u32[]{:S(2)}, u32[]{:S(2)}) %collective-permute-start.4) | collective-permute-done | bytes 131104 | tf_op jit(solution)/shard_map/ppermute | solution.py:523
  63.7 0.0 collective-permute-done.5.refs_3_
  63.7 0.2 join.1.y_ref.sorted_ref
  63.9 0.0 all-to-all-done.1
  63.9 1.0 %couple.1 = bf16[4,64,128]{2,1,0:T(8,128)(2,1)} custom-call(bf16[128,2048]{1,0:T(8,128)(2,1)S(1)} %bitcast.13, bf16[128,2048]{1,0:T(8,128)(2,1)S(1)} %join.1.y_ref.sorted_ref), custom_call_target="tpu_custom_call" | custom-call | tf_op jit(solution)/shard_map/couple/pallas_call | solution.py:577
  64.9 4.2 %all-to-all-start.2 = ((bf16[4,64,128]{2,1,0:T(8,128)(2,1)}), bf16[4,64,128]{2,1,0:T(8,128)(2,1)S(1)}, u32[]{:S(2)}, u32[]{:S(2)}) async-start(bf16[4,64,128]{2,1,0:T(8,128)(2,1)} %couple.1), calls=%async_computation.2 | async-start | bytes 131072 | tf_op jit(solution)/shard_map/all_to_all | solution.py:585
  69.1 0.0 copy-done.3
  69.1 2.1 %unsort.1 = bf16[128,2048]{1,0:T(8,128)(2,1)} custom-call(bf16[128,2048]{1,0:T(8,128)(2,1)S(1)} %join.1.y_ref.sorted_ref, s32[1,2048]{1,0:T(1,128)S(1)} %copy-done.3), custom_call_target="tpu_custom_call" | custom-call | flops 1000000000 | bytes 10000000 | tf_op jit(solution)/shard_map/unsort/pallas_call | solution.py:586
  71.2 3.7 %all-to-all-done.2 = bf16[4,64,128]{2,1,0:T(8,128)(2,1)S(1)} async-done(((bf16[4,64,128]{2,1,0:T(8,128)(2,1)}), bf16[4,64,128]{2,1,0:T(8,128)(2,1)S(1)}, u32[]{:S(2)}, u32[]{:S(2)}) %all-to-all-start.2) | async-done | bytes 65568 | tf_op jit(solution)/shard_map/all_to_all | solution.py:585
  74.9 0.1 slice_bitcast_fusion.1
  75.0 0.6 maximum_multiply_fusion
  (1 shorter events, 0.0 us)
Async XLA Ops:
  6.1 14.9 %all-to-all-start = ((bf16[8,16,2048]{2,1,0:T(8,128)(2,1)}), bf16[8,16,2048]{2,1,0:T(8,128)(2,1)S(1)}, u32[]{:S(2)}, u32[]{:S(2)}) async-start(bf16[8,16,2048]{2,1,0:T(8,128)(2,1)} %bitcast.16), calls=%async_computation | async-start | bytes 1048576 | tf_op jit(solution)/shard_map/all_to_all | solution.py:539
  11.3 9.7 %copy-start = (s32[8]{0:T(128)S(1)}, s32[8]{0:T(128)}, u32[]{:S(2)}) copy-start(s32[8]{0:T(128)} %order_ref.1) | copy-start | bytes 100
  11.3 14.7 %collective-permute-start = (bf16[32,2304]{1,0:T(8,128)(2,1)}, bf16[32,2304]{1,0:T(8,128)(2,1)S(1)}, u32[]{:S(2)}, u32[]{:S(2)}) collective-permute-start(bf16[32,2304]{1,0:T(8,128)(2,1)} %get-tuple-element.16), channel_id=1, source_target_pairs={{0,1},{1,0},{2,3},{3,2},{4,5},{5,4},{6,7},{7,6},{8,9},{9,8},{10,11... | collective-permute-start | bytes 442376 | tf_op jit(solution)/shard_map/ppermute | solution.py:478
  12.9 14.2 %collective-permute-start.1 = (bf16[32,2304]{1,0:T(8,128)(2,1)}, bf16[32,2304]{1,0:T(8,128)(2,1)S(1)}, u32[]{:S(2)}, u32[]{:S(2)}) collective-permute-start(bf16[32,2304]{1,0:T(8,128)(2,1)} %get-tuple-element.17), channel_id=1, source_target_pairs={{0,2},{1,3},{2,0},{3,1},{4,6},{5,7},{6,4},{7,5},{8,10},{9,11},{10,... | collective-permute-start | bytes 442376 | tf_op jit(solution)/shard_map/ppermute | solution.py:478
  15.5 11.6 %collective-permute-start.2 = (bf16[32,2304]{1,0:T(8,128)(2,1)}, bf16[32,2304]{1,0:T(8,128)(2,1)S(1)}, u32[]{:S(2)}, u32[]{:S(2)}) collective-permute-start(bf16[32,2304]{1,0:T(8,128)(2,1)} %get-tuple-element.18), channel_id=1, source_target_pairs={{0,3},{1,2},{2,1},{3,0},{4,7},{5,6},{6,5},{7,4},{8,11},{9,10},{10,... | collective-permute-start | bytes 442376 | tf_op jit(solution)/shard_map/ppermute | solution.py:478
  15.7 1.6 %copy-start.1 = (f32[64,64,128]{2,1,0:T(8,128)S(1)}, f32[64,64,128]{2,1,0:T(8,128)}, u32[]{:S(2)}) copy-start(f32[64,64,128]{2,1,0:T(8,128)} %param.9) | copy-start | bytes 6291460
  17.3 0.8 %copy-start.5 = (bf16[64,256]{1,0:T(8,128)(2,1)S(1)}, bf16[64,256]{1,0:T(8,128)(2,1)}, u32[]{:S(2)}) copy-start(bf16[64,256]{1,0:T(8,128)(2,1)} %constant.13.clone.cs_ref.refs_5_) | copy-start | bytes 98308
  18.1 9.0 %copy-start.2 = (bf16[32,2304]{1,0:T(8,128)(2,1)S(1)}, bf16[32,2304]{1,0:T(8,128)(2,1)}, u32[]{:S(2)}) copy-start(bf16[32,2304]{1,0:T(8,128)(2,1)} %get-tuple-element.15.refs_0_) | copy-start | bytes 442372
  18.1 9.0 %copy-start.4 = (bf16[2,128,128]{2,1,0:T(8,128)(2,1)S(1)}, bf16[2,128,128]{2,1,0:T(8,128)(2,1)}, u32[]{:S(2)}) copy-start(bf16[2,128,128]{2,1,0:T(8,128)(2,1)} %constant.14.clone.refs_8_) | copy-start | bytes 196612
  18.1 9.0 %copy-start.6 = (bf16[64,256]{1,0:T(8,128)(2,1)S(1)}, bf16[64,256]{1,0:T(8,128)(2,1)}, u32[]{:S(2)}) copy-start(bf16[64,256]{1,0:T(8,128)(2,1)} %constant.13.clone.cs_ref.refs_5_) | copy-start | bytes 98308
  22.4 41.5 %all-to-all-start.1 = ((bf16[8,16,2048]{2,1,0:T(8,128)(2,1)}), bf16[8,16,2048]{2,1,0:T(8,128)(2,1)S(1)}, u32[]{:S(2)}, u32[]{:S(2)}) async-start(bf16[8,16,2048]{2,1,0:T(8,128)(2,1)} %select_partner.1), calls=%async_computation.1 | async-start | bytes 1048576 | tf_op jit(solution)/shard_map/all_to_all | solution.py:551
  48.3 20.8 %copy-start.3 = (s32[1,2048]{1,0:T(1,128)S(1)}, s32[1,2048]{1,0:T(1,128)}, u32[]{:S(2)}) copy-start(s32[1,2048]{1,0:T(1,128)} %get-tuple-element.26.rank_ref) | copy-start | bytes 24580
  48.3 7.3 %collective-permute-start.3 = (bf16[32,2048]{1,0:T(8,128)(2,1)S(1)}, bf16[32,2048]{1,0:T(8,128)(2,1)S(1)}, u32[]{:S(2)}, u32[]{:S(2)}) collective-permute-start(bf16[32,2048]{1,0:T(8,128)(2,1)S(1)} %get-tuple-element.23), channel_id=1, source_target_pairs={{0,1},{1,0},{2,3},{3,2},{4,5},{5,4},{6,7},{7,6},{8,9},{9,8},{10,11... | collective-permute-start | bytes 393224 | tf_op jit(solution)/shard_map/ppermute | solution.py:523
  51.3 12.4 %collective-permute-start.4 = (bf16[32,2048]{1,0:T(8,128)(2,1)S(1)}, bf16[32,2048]{1,0:T(8,128)(2,1)S(1)}, u32[]{:S(2)}, u32[]{:S(2)}) collective-permute-start(bf16[32,2048]{1,0:T(8,128)(2,1)S(1)} %get-tuple-element.24), channel_id=1, source_target_pairs={{0,2},{1,3},{2,0},{3,1},{4,6},{5,7},{6,4},{7,5},{8,10},{9,11},{10,... | collective-permute-start | bytes 393224 | tf_op jit(solution)/shard_map/ppermute | solution.py:523
  52.4 11.3 %collective-permute-start.5 = (bf16[32,2048]{1,0:T(8,128)(2,1)S(1)}, bf16[32,2048]{1,0:T(8,128)(2,1)S(1)}, u32[]{:S(2)}, u32[]{:S(2)}) collective-permute-start(bf16[32,2048]{1,0:T(8,128)(2,1)S(1)} %get-tuple-element.25), channel_id=1, source_target_pairs={{0,3},{1,2},{2,1},{3,0},{4,7},{5,6},{6,5},{7,4},{8,11},{9,10},{10,... | collective-permute-start | bytes 393224 | tf_op jit(solution)/shard_map/ppermute | solution.py:523
  64.9 9.9 %all-to-all-start.2 = ((bf16[4,64,128]{2,1,0:T(8,128)(2,1)}), bf16[4,64,128]{2,1,0:T(8,128)(2,1)S(1)}, u32[]{:S(2)}, u32[]{:S(2)}) async-start(bf16[4,64,128]{2,1,0:T(8,128)(2,1)} %couple.1), calls=%async_computation.2 | async-start | bytes 131072 | tf_op jit(solution)/shard_map/all_to_all | solution.py:585

commit v8 on v7

--- a/solution.py
+++ b/solution.py
@@ -11,7 +11,7 @@
 
 STICK_DEV = 64
 LANES = 128
-UNROLL = 8
+UNROLL = 16
 CHUNKS = 1
 BF16 = jnp.bfloat16
 F32 = jnp.float32
@@ -105,23 +105,26 @@
         outs[shift * CHUNKS][:, waves:] = extra
     fetch.wait()
     parts = waves // 256
-    for part in range(parts):
-        mask = jnp.where((rank >> 8) == part, 1.0, 0.0).astype(BF16)
-        wide[part * both : (part + 1) * both] = x_ref[...] * mask
-    pieces[...] = dot_nt(wide[...], low)
+    step = 2 if parts % 2 == 0 else 1
     half = share // CHUNKS
-    for part in range(parts):
-        here = slice(part * 256, (part + 1) * 256)
-        all_ref[:, here] = pieces[part * both : (part + 1) * both].astype(BF16)
-        for shift in range(groups):
-            begin = pl.multiple_of(part * both + (me_ref[0] ^ shift) * share, 8)
-            re = pieces[pl.ds(begin, share)]
-            im = pieces[pl.ds(begin + bands, share)]
-            for c in range(CHUNKS):
-                mine = slice(c * half, (c + 1) * half)
-                outs[shift * CHUNKS + c][:, here] = jnp.concatenate(
-                    [re[mine], im[mine]], axis=0
-                ).astype(BF16)
+    for first in range(0, parts, step):
+        for part in range(first, first + step):
+            mask = jnp.where((rank >> 8) == part, 1.0, 0.0).astype(BF16)
+            wide[part * both : (part + 1) * both] = x_ref[...] * mask
+        rows_now = slice(first * both, (first + step) * both)
+        pieces[rows_now] = dot_nt(wide[rows_now], low)
+        for part in range(first, first + step):
+            here = slice(part * 256, (part + 1) * 256)
+            all_ref[:, here] = pieces[part * both : (part + 1) * both].astype(BF16)
+            for shift in range(groups):
+                begin = pl.multiple_of(part * both + (me_ref[0] ^ shift) * share, 8)
+                re = pieces[pl.ds(begin, share)]
+                im = pieces[pl.ds(begin + bands, share)]
+                for c in range(CHUNKS):
+                    mine = slice(c * half, (c + 1) * half)
+                    outs[shift * CHUNKS + c][:, here] = jnp.concatenate(
+                        [re[mine], im[mine]], axis=0
+                    ).astype(BF16)
 
 
 def field_kernel(side, chunks, pot_ref, cs_ref, field_ref, cyr_ref, syr_ref):
@@ -398,10 +401,8 @@
 def couple_kernel(partner_ref, sorted_ref, g_ref):
     products = dot_nt(partner_ref[...], sorted_ref[...])
     half = products.shape[0] // 2
-    re = products[:half, :half] + products[half:, half:]
-    im = products[:half, half:] - products[half:, :half]
-    for i in range(g_ref.shape[0]):
-        g_ref[i] = jnp.concatenate([re, im], axis=1).astype(BF16)
+    g_ref[0] = (products[:half, :half] + products[half:, half:]).astype(BF16)
+    g_ref[1] = (products[:half, half:] - products[half:, :half]).astype(BF16)
 
 
 def unsort_kernel(y_ref, rank_ref, out_ref):
@@ -493,7 +494,7 @@
         name="field_pairs",
     )(potential.reshape(side * side, 2 * side), cs)
 
-    team = min(4, rows // 2)
+    team = min(8, rows // 2)
     scratch = [
         pltpu.VMEM((2, fft_count, rows, waves), F32),
         pltpu.VMEM((columns // LANES, rows * side, LANES), F32),
@@ -576,13 +577,13 @@
     )(me_row, *arranged, *returned[-1])
     sums = pl.pallas_call(
         couple_kernel,
-        out_shape=jax.ShapeDtypeStruct((fft_count, bands, 2 * bands), BF16),
+        out_shape=jax.ShapeDtypeStruct((2, bands, bands), BF16),
         in_specs=[whole(), whole()],
         out_specs=whole(),
         compiler_params=params(),
         name="couple",
     )(partner, sorted_response)
-    shares = lax.all_to_all(sums, "fft", 0, 0, tiled=True)
+    shares = [sums] + [lax.ppermute(sums, "fft", pairs[s]) for s in range(1, fft_count)]
     response = pl.pallas_call(
         unsort_kernel,
         out_shape=jax.ShapeDtypeStruct((2 * bands, waves), BF16),
@@ -592,8 +593,14 @@
         cost_estimate=pl.CostEstimate(flops=10**9, bytes_accessed=10**7, transcendentals=0),
         name="unsort",
     )(sorted_response, rank)
-    summed = jnp.sum(shares.astype(F32), axis=0)
-    summed = jnp.stack([summed[:, :bands], summed[:, bands:]])
+    summed = None
+    for d in range(fft_count):
+        offset = me ^ d
+        term = shares[0]
+        for s in range(1, fft_count):
+            term = jnp.where(offset == s, shares[s], term)
+        term = term.astype(F32)
+        summed = term if summed is None else summed + term
     coupling = (summed / jnp.sqrt(jnp.float32(waves * fft_count)))[:, None]
     return response.reshape(2, 1, bands, waves), coupling
 

time: 76.1 us -> 72.1 us (0.947)
  waiting for transfers between devices: 15.6 us -> 12.6 us
  Pallas kernels: 33.4 us -> 31.1 us
  local copies, waits for them, and re-layouts: 2.44 us -> 3.32 us
    ppermute x0 -> x3, starting transfers between devices: none -> 4.42 us  [shards(): lax.ppermute(sums, 'fft', pairs[s])]
    all_to_all x1 -> x0, starting transfers between devices: 4.2 us -> none  [shards(): shares = lax.all_to_all(sums, 'fft', 0, 0, tiled=True)]
    all_to_all x1 -> x0, waiting for transfers between devices: 3.66 us -> none  [shards(): shares = lax.all_to_all(sums, 'fft', 0, 0, tiled=True)]
    pallas_call x1, Pallas kernels: 21.2 us -> 19.4 us  [shards(): pl.pallas_call(functools.partial(box_first_kernel, side, chunks, team, wa...]
    unnamed x14 -> x18, local copies, waits for them, and re-layouts: 2.37 us -> 3.32 us
    ppermute x0 -> x3, waiting for transfers between devices: none -> 0.87 us  [shards(): lax.ppermute(sums, 'fft', pairs[s])]
  transfers between devices with their start and end apart: 9 -> 11, of which waited for: 5 -> 6; matrix products, arithmetic and copies ran while one was open for 0% -> 0% of each run, Pallas kernels for 36% -> 35%
where the time goes in v8:
time: 72.1 us; the launch traced here: 71.6 us
  Pallas kernels  31.1 us (43%)
  starting transfers between devices  23.2 us (32%)
  waiting for transfers between devices  12.6 us (17%)
  local copies, waits for them, and re-layouts  3.32 us (5%)
  between operations  0.76 us (1%)
    pallas_call x1, Pallas kernels, shards(): pl.pallas_call(functools.partial(box_first_kernel, side, chunks, team, wa...  19.4 us
    ppermute x3, waiting for transfers between devices, shards(): lax.ppermute(back[s], 'fft', pairs[s])  9.94 us
    pallas_call x1, Pallas kernels, shards(): pl.pallas_call(functools.partial(sort_kernel, side, fft_count), out_shape...  5.5 us
    ppermute x3, starting transfers between devices, shards(): lax.ppermute(back[s], 'fft', pairs[s])  5.48 us
    all_to_all x1, starting transfers between devices, shards(): lax.all_to_all(ordered_all.reshape(pool_count, 2 * bands // pool_count, w...  5.17 us
    ppermute x3, starting transfers between devices, shards(): lax.ppermute(ordered[s * CHUNKS + c], 'fft', pairs[s])  4.45 us
    ppermute x3, starting transfers between devices, shards(): lax.ppermute(sums, 'fft', pairs[s])  4.42 us
    all_to_all x1, starting transfers between devices, shards(): lax.all_to_all(chosen, 'pool', 0, 0, tiled=True).reshape(2 * bands, waves)  3.69 us
  transfers between devices with their start and end apart: 11, of which 6 were waited for; matrix products, arithmetic and copies ran while one was open for 0% of the time, Pallas kernels for 35%

profile of v8, /device:TPU:0, one launch (start us, length us, event | category | flops | bytes accessed | tf_op | source)
XLA Modules:
  0.0 71.6 jit_solution(11431951192207578194)
XLA Ops:
  0.6 5.5 %sort_waves.1 = (bf16[32,2304]{1,0:T(8,128)(2,1)}, bf16[32,2304]{1,0:T(8,128)(2,1)}, bf16[32,2304]{1,0:T(8,128)(2,1)}, bf16[32,2304]{1,0:T(8,128)(2,1)}, bf16[128,2048]{1,0:T(8,128)(2,1)}, /*index=5*/s32[1,2048]{1,0:T(1,128)}) custom-call(s32[1]{0:T(128)} %bitcast.me_ref, s32[1,2048]{1,0:T(1,128)} %bitcast.17, bf16[128,2048]{1,0:T(8,128)(2,1)} %bitcast.15), custom_call_target="tpu_custom_call" | custom-call | tf_op jit(solution)/shard_map/sort_waves/pallas_call | solution.py:456
  6.1 5.2 %all-to-all-start = ((bf16[8,16,2048]{2,1,0:T(8,128)(2,1)}), bf16[8,16,2048]{2,1,0:T(8,128)(2,1)S(1)}, u32[]{:S(2)}, u32[]{:S(2)}) async-start(bf16[8,16,2048]{2,1,0:T(8,128)(2,1)} %bitcast.16), calls=%async_computation | async-start | bytes 1048576 | tf_op jit(solution)/shard_map/all_to_all | solution.py:540
  11.3 0.0 copy-start
  11.3 1.6 %collective-permute-start = (bf16[32,2304]{1,0:T(8,128)(2,1)}, bf16[32,2304]{1,0:T(8,128)(2,1)S(1)}, u32[]{:S(2)}, u32[]{:S(2)}) collective-permute-start(bf16[32,2304]{1,0:T(8,128)(2,1)} %get-tuple-element.16), channel_id=1, source_target_pairs={{0,1},{1,0},{2,3},{3,2},{4,5},{5,4},{6,7},{7,6},{8,9},{9,8},{10,11... | collective-permute-start | bytes 442376 | tf_op jit(solution)/shard_map/ppermute | solution.py:479
  13.0 2.6 %collective-permute-start.1 = (bf16[32,2304]{1,0:T(8,128)(2,1)}, bf16[32,2304]{1,0:T(8,128)(2,1)S(1)}, u32[]{:S(2)}, u32[]{:S(2)}) collective-permute-start(bf16[32,2304]{1,0:T(8,128)(2,1)} %get-tuple-element.17), channel_id=1, source_target_pairs={{0,2},{1,3},{2,0},{3,1},{4,6},{5,7},{6,4},{7,5},{8,10},{9,11},{10,... | collective-permute-start | bytes 442376 | tf_op jit(solution)/shard_map/ppermute | solution.py:479
  15.6 0.2 collective-permute-start.2
  15.8 0.0 copy-start.1
  15.8 1.6 %copy-done.1 = f32[64,64,128]{2,1,0:T(8,128)S(1)} copy-done((f32[64,64,128]{2,1,0:T(8,128)S(1)}, f32[64,64,128]{2,1,0:T(8,128)}, u32[]{:S(2)}) %copy-start.1) | copy-done | bytes 2097176
  17.4 0.0 copy-start.5
  17.4 0.8 %copy-done.5 = bf16[64,256]{1,0:T(8,128)(2,1)S(1)} copy-done((bf16[64,256]{1,0:T(8,128)(2,1)S(1)}, bf16[64,256]{1,0:T(8,128)(2,1)}, u32[]{:S(2)}) %copy-start.5) | copy-done | bytes 32792
  18.1 0.0 copy-start.2
  18.1 0.0 copy-start.4
  18.1 0.0 copy-start.6
  18.1 2.1 %field_pairs.1 = (bf16[4,64,2176]{2,1,0:T(8,128)(2,1)S(1)}, bf16[64,2176]{1,0:T(8,128)(2,1)S(1)}, bf16[64,2176]{1,0:T(8,128)(2,1)S(1)}) custom-call(f32[4096,128]{1,0:T(8,128)S(1)} %bitcast.14, bf16[64,256]{1,0:T(8,128)(2,1)S(1)} %copy-done.5), custom_call_target="tpu_custom_call" | custom-call | flops 1000000000 | bytes 10000000 | tf_op jit(solution)/shard_map/field_pairs/pallas_call | solution.py:483
  20.2 0.0 copy-start.7
  20.2 0.8 %all-to-all-done.in_ref = bf16[8,16,2048]{2,1,0:T(8,128)(2,1)S(1)} async-done(((bf16[8,16,2048]{2,1,0:T(8,128)(2,1)}), bf16[8,16,2048]{2,1,0:T(8,128)(2,1)S(1)}, u32[]{:S(2)}, u32[]{:S(2)}) %all-to-all-start) | async-done | bytes 524320 | tf_op jit(solution)/shard_map/all_to_all | solution.py:540
  21.1 0.0 copy-done
  21.1 1.4 %select_partner.1 = bf16[8,16,2048]{2,1,0:T(8,128)(2,1)} custom-call(s32[8]{0:T(128)S(1)} %copy-done, bf16[8,16,2048]{2,1,0:T(8,128)(2,1)S(1)} %all-to-all-done.in_ref), custom_call_target="tpu_custom_call" | custom-call | tf_op jit(solution)/shard_map/select_partner/pallas_call | solution.py:543
  22.5 3.7 %all-to-all-start.1 = ((bf16[8,16,2048]{2,1,0:T(8,128)(2,1)}), bf16[8,16,2048]{2,1,0:T(8,128)(2,1)S(1)}, u32[]{:S(2)}, u32[]{:S(2)}) async-start(bf16[8,16,2048]{2,1,0:T(8,128)(2,1)} %select_partner.1), calls=%async_computation.1 | async-start | bytes 1048576 | tf_op jit(solution)/shard_map/all_to_all | solution.py:552
  26.2 0.0 collective-permute-done.refs_1_
  26.2 1.0 %collective-permute-done.1.refs_2_ = bf16[32,2304]{1,0:T(8,128)(2,1)S(1)} collective-permute-done((bf16[32,2304]{1,0:T(8,128)(2,1)}, bf16[32,2304]{1,0:T(8,128)(2,1)S(1)}, u32[]{:S(2)}, u32[]{:S(2)}) %collective-permute-start.1) | collective-permute-done | bytes 147488 | tf_op jit(solution)/shard_map/ppermute | solution.py:479
  27.1 0.0 collective-permute-done.2.refs_3_
  27.1 0.0 copy-done.7
  27.1 0.0 copy-done.2
  27.2 0.0 copy-done.4
  27.2 0.0 copy-done.6
  27.2 0.0 copy-start.8
  27.2 0.9 %copy-done.8 = bf16[64,2176]{1,0:T(8,128)(2,1)S(1)} copy-done((bf16[64,2176]{1,0:T(8,128)(2,1)S(1)}, bf16[64,2176]{1,0:T(8,128)(2,1)}, u32[]{:S(2)}) %copy-start.8) | copy-done | bytes 278552
  28.1 19.4 %box_first.1 = (bf16[32,2048]{1,0:T(8,128)(2,1)S(1)}, bf16[32,2048]{1,0:T(8,128)(2,1)S(1)}, bf16[32,2048]{1,0:T(8,128)(2,1)S(1)}, bf16[32,2048]{1,0:T(8,128)(2,1...) custom-call(bf16[32,2304]{1,0:T(8,128)(2,1)S(1)} %copy-done.2, ...), custom_call_target="tpu_custom_call" | custom-call | flops 10000000000 | bytes 10000000 | tf_op jit(solution)/shard_map/box_first/pallas_call | solution.py:507
  47.5 0.0 copy-start.3
  47.5 3.0 %collective-permute-start.3 = (bf16[32,2048]{1,0:T(8,128)(2,1)S(1)}, bf16[32,2048]{1,0:T(8,128)(2,1)S(1)}, u32[]{:S(2)}, u32[]{:S(2)}) collective-permute-start(bf16[32,2048]{1,0:T(8,128)(2,1)S(1)} %get-tuple-element.23), channel_id=1, source_target_pairs={{0,1},{1,0},{2,3},{3,2},{4,5},{5,4},{6,7},{7,6},{8,9},{9,8},{10,11... | collective-permute-start | bytes 393224 | tf_op jit(solution)/shard_map/ppermute | solution.py:524
  50.5 1.1 %collective-permute-start.4 = (bf16[32,2048]{1,0:T(8,128)(2,1)S(1)}, bf16[32,2048]{1,0:T(8,128)(2,1)S(1)}, u32[]{:S(2)}, u32[]{:S(2)}) collective-permute-start(bf16[32,2048]{1,0:T(8,128)(2,1)S(1)} %get-tuple-element.24), channel_id=1, source_target_pairs={{0,2},{1,3},{2,0},{3,1},{4,6},{5,7},{6,4},{7,5},{8,10},{9,11},{10,... | collective-permute-start | bytes 393224 | tf_op jit(solution)/shard_map/ppermute | solution.py:524
  51.6 1.4 %collective-permute-start.5 = (bf16[32,2048]{1,0:T(8,128)(2,1)S(1)}, bf16[32,2048]{1,0:T(8,128)(2,1)S(1)}, u32[]{:S(2)}, u32[]{:S(2)}) collective-permute-start(bf16[32,2048]{1,0:T(8,128)(2,1)S(1)} %get-tuple-element.25), channel_id=1, source_target_pairs={{0,3},{1,2},{2,1},{3,0},{4,7},{5,6},{6,5},{7,4},{8,11},{9,10},{10,... | collective-permute-start | bytes 393224 | tf_op jit(solution)/shard_map/ppermute | solution.py:524
  53.0 1.8 %collective-permute-done.3.refs_1_ = bf16[32,2048]{1,0:T(8,128)(2,1)S(1)} collective-permute-done((bf16[32,2048]{1,0:T(8,128)(2,1)S(1)}, bf16[32,2048]{1,0:T(8,128)(2,1)S(1)}, u32[]{:S(2)}, u32[]{:S(2)}) %collective-permute-start.3) | collective-permute-done | bytes 131104 | tf_op jit(solution)/shard_map/ppermute | solution.py:524
  54.8 8.1 %collective-permute-done.4.refs_2_ = bf16[32,2048]{1,0:T(8,128)(2,1)S(1)} collective-permute-done((bf16[32,2048]{1,0:T(8,128)(2,1)S(1)}, bf16[32,2048]{1,0:T(8,128)(2,1)S(1)}, u32[]{:S(2)}, u32[]{:S(2)}) %collective-permute-start.4) | collective-permute-done | bytes 131104 | tf_op jit(solution)/shard_map/ppermute | solution.py:524
  63.0 0.0 collective-permute-done.5.refs_3_
  63.0 0.2 join.1.y_ref.sorted_ref
  63.2 0.0 all-to-all-done.1
  63.2 0.4 couple.1
  63.6 2.0 %collective-permute-start.6 = (bf16[2,64,64]{2,1,0:T(8,128)(2,1)S(1)}, bf16[2,64,64]{2,1,0:T(8,128)(2,1)S(1)}, u32[]{:S(2)}, u32[]{:S(2)}) collective-permute-start(bf16[2,64,64]{2,1,0:T(8,128)(2,1)S(1)} %couple.1), channel_id=1, source_target_pairs={{0,3},{1,2},{2,1},{3,0},{4,7},{5,6},{6,5},{7,4},{8,11},{9,10},{10,... | collective-permute-start | bytes 49160 | tf_op jit(solution)/shard_map/ppermute | solution.py:586
  65.6 1.5 %collective-permute-start.7 = (bf16[2,64,64]{2,1,0:T(8,128)(2,1)S(1)}, bf16[2,64,64]{2,1,0:T(8,128)(2,1)S(1)}, u32[]{:S(2)}, u32[]{:S(2)}) collective-permute-start(bf16[2,64,64]{2,1,0:T(8,128)(2,1)S(1)} %couple.1), channel_id=1, source_target_pairs={{0,2},{1,3},{2,0},{3,1},{4,6},{5,7},{6,4},{7,5},{8,10},{9,11},{10,... | collective-permute-start | bytes 49160 | tf_op jit(solution)/shard_map/ppermute | solution.py:586
  67.1 1.0 %collective-permute-start.8 = (bf16[2,64,64]{2,1,0:T(8,128)(2,1)S(1)}, bf16[2,64,64]{2,1,0:T(8,128)(2,1)S(1)}, u32[]{:S(2)}, u32[]{:S(2)}) collective-permute-start(bf16[2,64,64]{2,1,0:T(8,128)(2,1)S(1)} %couple.1), channel_id=1, source_target_pairs={{0,1},{1,0},{2,3},{3,2},{4,5},{5,4},{6,7},{7,6},{8,9},{9,8},{10,11... | collective-permute-start | bytes 49160 | tf_op jit(solution)/shard_map/ppermute | solution.py:586
  68.0 0.0 copy-done.3
  68.0 2.1 %unsort.1 = bf16[128,2048]{1,0:T(8,128)(2,1)} custom-call(bf16[128,2048]{1,0:T(8,128)(2,1)S(1)} %join.1.y_ref.sorted_ref, s32[1,2048]{1,0:T(1,128)S(1)} %copy-done.3), custom_call_target="tpu_custom_call" | custom-call | flops 1000000000 | bytes 10000000 | tf_op jit(solution)/shard_map/unsort/pallas_call | solution.py:587
  70.1 0.0 collective-permute-done.6
  70.1 0.3 collective-permute-done.7
  70.4 0.6 collective-permute-done.8
  71.0 0.7 multiply_bitcast_fusion
Async XLA Ops:
  6.1 14.9 %all-to-all-start = ((bf16[8,16,2048]{2,1,0:T(8,128)(2,1)}), bf16[8,16,2048]{2,1,0:T(8,128)(2,1)S(1)}, u32[]{:S(2)}, u32[]{:S(2)}) async-start(bf16[8,16,2048]{2,1,0:T(8,128)(2,1)} %bitcast.16), calls=%async_computation | async-start | bytes 1048576 | tf_op jit(solution)/shard_map/all_to_all | solution.py:540
  11.3 9.7 %copy-start = (s32[8]{0:T(128)S(1)}, s32[8]{0:T(128)}, u32[]{:S(2)}) copy-start(s32[8]{0:T(128)} %order_ref.1) | copy-start | bytes 100
  11.3 14.8 %collective-permute-start = (bf16[32,2304]{1,0:T(8,128)(2,1)}, bf16[32,2304]{1,0:T(8,128)(2,1)S(1)}, u32[]{:S(2)}, u32[]{:S(2)}) collective-permute-start(bf16[32,2304]{1,0:T(8,128)(2,1)} %get-tuple-element.16), channel_id=1, source_target_pairs={{0,1},{1,0},{2,3},{3,2},{4,5},{5,4},{6,7},{7,6},{8,9},{9,8},{10,11... | collective-permute-start | bytes 442376 | tf_op jit(solution)/shard_map/ppermute | solution.py:479
  13.0 14.2 %collective-permute-start.1 = (bf16[32,2304]{1,0:T(8,128)(2,1)}, bf16[32,2304]{1,0:T(8,128)(2,1)S(1)}, u32[]{:S(2)}, u32[]{:S(2)}) collective-permute-start(bf16[32,2304]{1,0:T(8,128)(2,1)} %get-tuple-element.17), channel_id=1, source_target_pairs={{0,2},{1,3},{2,0},{3,1},{4,6},{5,7},{6,4},{7,5},{8,10},{9,11},{10,... | collective-permute-start | bytes 442376 | tf_op jit(solution)/shard_map/ppermute | solution.py:479
  15.6 11.6 %collective-permute-start.2 = (bf16[32,2304]{1,0:T(8,128)(2,1)}, bf16[32,2304]{1,0:T(8,128)(2,1)S(1)}, u32[]{:S(2)}, u32[]{:S(2)}) collective-permute-start(bf16[32,2304]{1,0:T(8,128)(2,1)} %get-tuple-element.18), channel_id=1, source_target_pairs={{0,3},{1,2},{2,1},{3,0},{4,7},{5,6},{6,5},{7,4},{8,11},{9,10},{10,... | collective-permute-start | bytes 442376 | tf_op jit(solution)/shard_map/ppermute | solution.py:479
  15.8 1.6 %copy-start.1 = (f32[64,64,128]{2,1,0:T(8,128)S(1)}, f32[64,64,128]{2,1,0:T(8,128)}, u32[]{:S(2)}) copy-start(f32[64,64,128]{2,1,0:T(8,128)} %param.9) | copy-start | bytes 6291460
  17.4 0.8 %copy-start.5 = (bf16[64,256]{1,0:T(8,128)(2,1)S(1)}, bf16[64,256]{1,0:T(8,128)(2,1)}, u32[]{:S(2)}) copy-start(bf16[64,256]{1,0:T(8,128)(2,1)} %constant.17.clone.cs_ref.refs_5_) | copy-start | bytes 98308
  18.1 9.0 %copy-start.2 = (bf16[32,2304]{1,0:T(8,128)(2,1)S(1)}, bf16[32,2304]{1,0:T(8,128)(2,1)}, u32[]{:S(2)}) copy-start(bf16[32,2304]{1,0:T(8,128)(2,1)} %get-tuple-element.15.refs_0_) | copy-start | bytes 442372
  18.1 9.0 %copy-start.4 = (bf16[2,128,128]{2,1,0:T(8,128)(2,1)S(1)}, bf16[2,128,128]{2,1,0:T(8,128)(2,1)}, u32[]{:S(2)}) copy-start(bf16[2,128,128]{2,1,0:T(8,128)(2,1)} %constant.18.clone.refs_8_) | copy-start | bytes 196612
  18.1 9.0 %copy-start.6 = (bf16[64,256]{1,0:T(8,128)(2,1)S(1)}, bf16[64,256]{1,0:T(8,128)(2,1)}, u32[]{:S(2)}) copy-start(bf16[64,256]{1,0:T(8,128)(2,1)} %constant.17.clone.cs_ref.refs_5_) | copy-start | bytes 98308
  20.2 6.9 %copy-start.7 = (bf16[64,2176]{1,0:T(8,128)(2,1)}, bf16[64,2176]{1,0:T(8,128)(2,1)S(1)}, u32[]{:S(2)}) copy-start(bf16[64,2176]{1,0:T(8,128)(2,1)S(1)} %get-tuple-element.21.refs_7_) | copy-start | bytes 835588
  22.5 40.7 %all-to-all-start.1 = ((bf16[8,16,2048]{2,1,0:T(8,128)(2,1)}), bf16[8,16,2048]{2,1,0:T(8,128)(2,1)S(1)}, u32[]{:S(2)}, u32[]{:S(2)}) async-start(bf16[8,16,2048]{2,1,0:T(8,128)(2,1)} %select_partner.1), calls=%async_computation.1 | async-start | bytes 1048576 | tf_op jit(solution)/shard_map/all_to_all | solution.py:552
  27.2 1.0 %copy-start.8 = (bf16[64,2176]{1,0:T(8,128)(2,1)S(1)}, bf16[64,2176]{1,0:T(8,128)(2,1)}, u32[]{:S(2)}) copy-start(bf16[64,2176]{1,0:T(8,128)(2,1)} %copy-done.7) | copy-start | bytes 835588
  47.5 20.5 %copy-start.3 = (s32[1,2048]{1,0:T(1,128)S(1)}, s32[1,2048]{1,0:T(1,128)}, u32[]{:S(2)}) copy-start(s32[1,2048]{1,0:T(1,128)} %get-tuple-element.26.rank_ref) | copy-start | bytes 24580
  47.5 7.3 %collective-permute-start.3 = (bf16[32,2048]{1,0:T(8,128)(2,1)S(1)}, bf16[32,2048]{1,0:T(8,128)(2,1)S(1)}, u32[]{:S(2)}, u32[]{:S(2)}) collective-permute-start(bf16[32,2048]{1,0:T(8,128)(2,1)S(1)} %get-tuple-element.23), channel_id=1, source_target_pairs={{0,1},{1,0},{2,3},{3,2},{4,5},{5,4},{6,7},{7,6},{8,9},{9,8},{10,11... | collective-permute-start | bytes 393224 | tf_op jit(solution)/shard_map/ppermute | solution.py:524
  50.5 12.4 %collective-permute-start.4 = (bf16[32,2048]{1,0:T(8,128)(2,1)S(1)}, bf16[32,2048]{1,0:T(8,128)(2,1)S(1)}, u32[]{:S(2)}, u32[]{:S(2)}) collective-permute-start(bf16[32,2048]{1,0:T(8,128)(2,1)S(1)} %get-tuple-element.24), channel_id=1, source_target_pairs={{0,2},{1,3},{2,0},{3,1},{4,6},{5,7},{6,4},{7,5},{8,10},{9,11},{10,... | collective-permute-start | bytes 393224 | tf_op jit(solution)/shard_map/ppermute | solution.py:524
  51.6 11.3 %collective-permute-start.5 = (bf16[32,2048]{1,0:T(8,128)(2,1)S(1)}, bf16[32,2048]{1,0:T(8,128)(2,1)S(1)}, u32[]{:S(2)}, u32[]{:S(2)}) collective-permute-start(bf16[32,2048]{1,0:T(8,128)(2,1)S(1)} %get-tuple-element.25), channel_id=1, source_target_pairs={{0,3},{1,2},{2,1},{3,0},{4,7},{5,6},{6,5},{7,4},{8,11},{9,10},{10,... | collective-permute-start | bytes 393224 | tf_op jit(solution)/shard_map/ppermute | solution.py:524
  63.6 6.5 %collective-permute-start.6 = (bf16[2,64,64]{2,1,0:T(8,128)(2,1)S(1)}, bf16[2,64,64]{2,1,0:T(8,128)(2,1)S(1)}, u32[]{:S(2)}, u32[]{:S(2)}) collective-permute-start(bf16[2,64,64]{2,1,0:T(8,128)(2,1)S(1)} %couple.1), channel_id=1, source_target_pairs={{0,3},{1,2},{2,1},{3,0},{4,7},{5,6},{6,5},{7,4},{8,11},{9,10},{10,... | collective-permute-start | bytes 49160 | tf_op jit(solution)/shard_map/ppermute | solution.py:586
  65.6 4.8 %collective-permute-start.7 = (bf16[2,64,64]{2,1,0:T(8,128)(2,1)S(1)}, bf16[2,64,64]{2,1,0:T(8,128)(2,1)S(1)}, u32[]{:S(2)}, u32[]{:S(2)}) collective-permute-start(bf16[2,64,64]{2,1,0:T(8,128)(2,1)S(1)} %couple.1), channel_id=1, source_target_pairs={{0,2},{1,3},{2,0},{3,1},{4,6},{5,7},{6,4},{7,5},{8,10},{9,11},{10,... | collective-permute-start | bytes 49160 | tf_op jit(solution)/shard_map/ppermute | solution.py:586
  67.1 3.9 %collective-permute-start.8 = (bf16[2,64,64]{2,1,0:T(8,128)(2,1)S(1)}, bf16[2,64,64]{2,1,0:T(8,128)(2,1)S(1)}, u32[]{:S(2)}, u32[]{:S(2)}) collective-permute-start(bf16[2,64,64]{2,1,0:T(8,128)(2,1)S(1)} %couple.1), channel_id=1, source_target_pairs={{0,1},{1,0},{2,3},{3,2},{4,5},{5,4},{6,7},{7,6},{8,9},{9,8},{10,11... | collective-permute-start | bytes 49160 | tf_op jit(solution)/shard_map/ppermute | solution.py:586

commit v9 on v8

--- a/solution.py
+++ b/solution.py
@@ -18,7 +18,8 @@
 VMEM_LIMIT = 24 * 1024 * 1024
 SORT_LIMIT = 60 * 1024 * 1024
 ARRANGE_COST = 3*10**9
-JOIN_COST = 10**7
+JOIN_COST = 10**11
+BOX_COST = 10**10
 
 
 def cos_sin(side):
@@ -77,7 +78,7 @@
 
 
 def sort_kernel(side, groups, me_ref, idx_ref, x_hbm, *refs):
-    outs, (all_ref, rank_ref, x_ref, wide, pieces, sem) = refs[: groups * CHUNKS], refs[groups * CHUNKS :]
+    outs, (re_ref, im_ref, rank_ref, x_ref, wide, pieces, sem) = refs[: groups * CHUNKS], refs[groups * CHUNKS :]
     fetch = pltpu.make_async_copy(x_hbm, x_ref, sem)
     fetch.start()
     xh, yh, ch, slot_of, cells, rank = locate(idx_ref[...], side)
@@ -115,7 +116,8 @@
         pieces[rows_now] = dot_nt(wide[rows_now], low)
         for part in range(first, first + step):
             here = slice(part * 256, (part + 1) * 256)
-            all_ref[:, here] = pieces[part * both : (part + 1) * both].astype(BF16)
+            re_ref[:, here] = pieces[part * both : part * both + bands].astype(BF16)
+            im_ref[:, here] = pieces[part * both + bands : (part + 1) * both].astype(BF16)
             for shift in range(groups):
                 begin = pl.multiple_of(part * both + (me_ref[0] ^ shift) * share, 8)
                 re = pieces[pl.ds(begin, share)]
@@ -127,16 +129,8 @@
                     ).astype(BF16)
 
 
-def field_kernel(side, chunks, pot_ref, cs_ref, field_ref, cyr_ref, syr_ref):
+def field_kernel(side, chunks, pot_ref, field_ref):
     half = side // 2
-    left = lax.broadcasted_iota(jnp.int32, (side, LANES), 1) < side
-    for ref, begin in ((cyr_ref, 0), (syr_ref, LANES)):
-        table = cs_ref[:, begin : begin + side].astype(F32)
-        for k in range(chunks):
-            ya, yb = (2 * k) % side, (2 * k + 1) % side
-            ref[:, k * LANES : (k + 1) * LANES] = jnp.where(
-                left, table[:, ya : ya + 1], table[:, yb : yb + 1]
-            ).astype(BF16)
     lane = lax.broadcasted_iota(jnp.int32, (side, LANES), 1)
     first = lane < side
     flipped = (lane & side) + ((side - (lane & (side - 1))) & (side - 1))
@@ -173,7 +167,47 @@
         copy.wait()
 
 
-def build_tables(side, chunks, waves, x_refs, cs_ref, cyr_ref, syr_ref, tab_ref, spot_ref, col_ref, start_ref):
+def choose(code, mask, sources, out_ref):
+    for name, source in sources.items():
+
+        @pl.when((code & mask) == name)
+        def _(source=source):
+            out_ref[...] = source[...]
+
+
+def stack_kernel(re_ref, im_ref, xn_ref, yn_ref, out_ref):
+    half = re_ref.shape[0]
+    for k, ref in enumerate((re_ref, im_ref, xn_ref, yn_ref)):
+        out_ref[k * half : (k + 1) * half] = ref[...]
+
+
+def seen(own_re, own_im, xn, yn, other):
+    half = own_re.shape[0]
+    sib_re, sib_im, xns, yns = [other.at[k * half : (k + 1) * half] for k in range(4)]
+    return {0: own_re, 1: sib_re, 2: xn, 3: xns}, {0: own_im, 1: sib_im, 4: yn, 5: yns}
+
+
+def route_kernel(order_ref, i_ref, own_re, own_im, xn, yn, other, re_ref, im_ref):
+    i = i_ref[0]
+    near_re, near_im = seen(own_re, own_im, xn, yn, other)
+    choose(order_ref[i ^ 4] ^ i, 3, near_re, re_ref)
+    choose(order_ref[i ^ 2] ^ i, 5, near_im, im_ref)
+
+
+def couple_routed_kernel(
+    order_ref, i_ref, own_re, own_im, xn, yn, other, far_re, far_im, sorted_ref, g_ref, partner,
+):
+    i = i_ref[0]
+    half = own_re.shape[0]
+    code = order_ref[i] ^ i
+    re_ref, im_ref = partner.at[:half], partner.at[half:]
+    near_re, near_im = seen(own_re, own_im, xn, yn, other)
+    choose(code, 7, {**near_re, **{4 + name: far_re for name in near_re}}, re_ref)
+    choose(code, 7, {**near_im, **{2 + name: far_im for name in near_im}}, im_ref)
+    couple_kernel(partner, sorted_ref, g_ref)
+
+
+def build_tables(side, chunks, waves, x_refs, cs_ref, tab_ref, spot_ref, col_ref, start_ref, cyr_ref, syr_ref):
     rows = x_refs[0].shape[0]
     parts = side // rows
     tiles = waves // LANES
@@ -185,6 +219,14 @@
         1.0, 0.0,
     ).astype(BF16)
     left = lax.broadcasted_iota(jnp.int32, (tiles, LANES), 1) < STICK_DEV
+    first = lax.broadcasted_iota(jnp.int32, (side, LANES), 1) < side
+    for ref, begin in ((cyr_ref, 0), (syr_ref, LANES)):
+        table = cs_ref[:, begin : begin + side].astype(F32)
+        for k in range(chunks):
+            ya, yb = (2 * k) % side, (2 * k + 1) % side
+            ref[:, k * LANES : (k + 1) * LANES] = jnp.where(
+                first, table[:, ya : ya + 1], table[:, yb : yb + 1]
+            ).astype(BF16)
     at_x, at_y = [], []
     for d, x_ref in enumerate(x_refs):
         cells = jnp.concatenate(
@@ -224,14 +266,14 @@
         tab_ref[:, base + LANES : base + 2 * LANES] = (cy * sx + sy * cx).astype(BF16)
 
 
-def box_first_kernel(side, chunks, team, waves, groups, *refs):
+def box_first_kernel(side, chunks, team, waves, groups, gates, *refs):
     x_refs, refs = refs[:groups], refs[groups:]
-    (field_ref, cs_ref, cyr_ref, syr_ref, wz_ref), refs = refs[:5], refs[5:]
+    (field_ref, cs_ref, wz_ref), refs = refs[:3], refs[3 + gates :]
     out_refs, refs = refs[:groups], refs[groups:]
     (tab_ref, spot_ref, col_ref, start_ref), refs = refs[:4], refs[4:]
-    *scratch, start_s, sem = refs
+    *scratch, cyr_ref, syr_ref, start_s, sem = refs
     build_tables(
-        side, chunks, waves, x_refs, cs_ref, cyr_ref, syr_ref, tab_ref, spot_ref, col_ref, start_ref
+        side, chunks, waves, x_refs, cs_ref, tab_ref, spot_ref, col_ref, start_ref, cyr_ref, syr_ref
     )
     to_scalars = pltpu.make_async_copy(start_ref, start_s, sem)
     to_scalars.start()
@@ -453,7 +495,7 @@
     packed = waves + side * STICK_DEV // rows + -(-(tiles + 8) // rows) * LANES
     scalars, blocks = whole(pltpu.SMEM), [whole()] * fft_count
 
-    *ordered, ordered_all, rank = pl.pallas_call(
+    *ordered, own_re, own_im, rank = pl.pallas_call(
         functools.partial(sort_kernel, side, fft_count),
         out_shape=[
             jax.ShapeDtypeStruct((rows, waves if c else packed), BF16)
@@ -461,11 +503,12 @@
             for c in range(CHUNKS)
         ]
         + [
-            jax.ShapeDtypeStruct((2 * bands, waves), BF16),
+            jax.ShapeDtypeStruct((bands, waves), BF16),
+            jax.ShapeDtypeStruct((bands, waves), BF16),
             jax.ShapeDtypeStruct((1, waves), jnp.int32),
         ],
         in_specs=[scalars, whole(), whole(pltpu.HBM)],
-        out_specs=blocks * CHUNKS + [whole(), whole()],
+        out_specs=blocks * CHUNKS + [whole()] * 3,
         scratch_shapes=[
             pltpu.VMEM((2 * bands, waves), BF16),
             pltpu.VMEM((waves // 256 * 2 * bands, waves), BF16),
@@ -480,20 +523,41 @@
         for c in range(CHUNKS)
     ]
 
-    field, cyr, syr = pl.pallas_call(
+    routed = pool_count == 8
+    half_rows = jax.ShapeDtypeStruct((bands, waves), BF16)
+    pool_row = lax.axis_index("pool").reshape(1)
+    if routed:
+        swaps = {m: [(i, i ^ m) for i in range(pool_count)] for m in (1, 2, 4)}
+        xn = lax.ppermute(own_re, "pool", swaps[2])
+        yn = lax.ppermute(own_im, "pool", swaps[4])
+        stacked = pl.pallas_call(
+            stack_kernel,
+            out_shape=jax.ShapeDtypeStruct((4 * bands, waves), BF16),
+            in_specs=[whole()] * 4,
+            out_specs=whole(),
+            compiler_params=params(),
+            name="stack",
+        )(own_re, own_im, xn, yn)
+        other = lax.ppermute(stacked, "pool", swaps[1])
+        near = [own_re, own_im, xn, yn, other]
+    else:
+        spread = lax.all_to_all(
+            jnp.concatenate([own_re, own_im]).reshape(pool_count, 2 * bands // pool_count, waves),
+            "pool", 0, 0, tiled=True,
+        )
+        near = []
+
+    field = pl.pallas_call(
         functools.partial(field_kernel, side, chunks),
-        out_shape=(
-            jax.ShapeDtypeStruct((4, side, chunks * LANES), BF16),
-            jax.ShapeDtypeStruct((side, chunks * LANES), BF16),
-            jax.ShapeDtypeStruct((side, chunks * LANES), BF16),
-        ),
-        in_specs=[whole()] * 2,
-        out_specs=(whole(),) * 3,
+        out_shape=jax.ShapeDtypeStruct((4, side, chunks * LANES), BF16),
+        in_specs=[whole()],
+        out_specs=whole(),
         compiler_params=params(),
-        cost_estimate=pl.CostEstimate(flops=10**9, bytes_accessed=10**7, transcendentals=0),
+        cost_estimate=pl.CostEstimate(flops=10**9, bytes_accessed=10**6, transcendentals=0),
         name="field_pairs",
-    )(potential.reshape(side * side, 2 * side), cs)
-
+    )(potential.reshape(side * side, 2 * side))
+
+    gates = [xn, yn] if routed else []
     team = min(8, rows // 2)
     scratch = [
         pltpu.VMEM((2, fft_count, rows, waves), F32),
@@ -502,10 +566,10 @@
         pltpu.VMEM((team * 2 * side, 2 * chunks * LANES), BF16),
         pltpu.VMEM((2, fft_count, rows, waves), F32),
     ]
-    cost = pl.CostEstimate(flops=10**10, bytes_accessed=10**7, transcendentals=0)
+    cost = pl.CostEstimate(flops=BOX_COST, bytes_accessed=10**7, transcendentals=0)
     shapes = [jax.ShapeDtypeStruct((rows, waves), BF16)] * fft_count
     *back, tab, spot, col, start = pl.pallas_call(
-        functools.partial(box_first_kernel, side, chunks, team, waves, fft_count),
+        functools.partial(box_first_kernel, side, chunks, team, waves, fft_count, len(gates)),
         out_shape=shapes
         + [
             jax.ShapeDtypeStruct((columns, 2 * chunks * LANES), BF16),
@@ -513,14 +577,15 @@
             jax.ShapeDtypeStruct((2, fft_count, tiles, LANES), jnp.int32),
             jax.ShapeDtypeStruct((fft_count, LANES), jnp.int32),
         ],
-        in_specs=blocks + [whole()] * 5,
+        in_specs=blocks + [whole()] * 3 + [whole(pl.ANY)] * len(gates),
         out_specs=blocks + [whole()] * 4,
         scratch_shapes=scratch
+        + [pltpu.VMEM((side, chunks * LANES), BF16)] * 2
         + [pltpu.SMEM((fft_count, LANES), jnp.int32), pltpu.SemaphoreType.DMA],
         compiler_params=params(),
         cost_estimate=cost,
         name="box_first",
-    )(*moved[0], field, cs, cyr, syr, wz)
+    )(*moved[0], field, cs, wz, *gates)
     returned = [[back[0]] + [lax.ppermute(back[s], "fft", pairs[s]) for s in range(1, fft_count)]]
     for c in range(1, CHUNKS):
         back = pl.pallas_call(
@@ -537,19 +602,28 @@
             [back[0]] + [lax.ppermute(back[s], "fft", pairs[s]) for s in range(1, fft_count)]
         )
 
-    spread = lax.all_to_all(
-        ordered_all.reshape(pool_count, 2 * bands // pool_count, waves), "pool", 0, 0, tiled=True
-    )
-    chosen = pl.pallas_call(
-        select_kernel,
-        out_shape=jax.ShapeDtypeStruct(spread.shape, BF16),
-        in_specs=[scalars, whole(pl.ANY)],
-        out_specs=whole(pl.ANY),
-        scratch_shapes=[pltpu.SemaphoreType.DMA((pool_count,))],
-        compiler_params=params(),
-        name="select_partner",
-    )(partner_pool, spread)
-    partner = lax.all_to_all(chosen, "pool", 0, 0, tiled=True).reshape(2 * bands, waves)
+    if not routed:
+        chosen = pl.pallas_call(
+            select_kernel,
+            out_shape=jax.ShapeDtypeStruct(spread.shape, BF16),
+            in_specs=[scalars, whole(pl.ANY)],
+            out_specs=whole(pl.ANY),
+            scratch_shapes=[pltpu.SemaphoreType.DMA((pool_count,))],
+            compiler_params=params(),
+            name="select_partner",
+        )(partner_pool, spread)
+        partner = lax.all_to_all(chosen, "pool", 0, 0, tiled=True).reshape(2 * bands, waves)
+    else:
+        far_re, far_im = pl.pallas_call(
+            route_kernel,
+            out_shape=(half_rows, half_rows),
+            in_specs=[scalars] * 2 + [whole()] * len(near),
+            out_specs=(whole(), whole()),
+            compiler_params=params(),
+            name="route_partner",
+        )(partner_pool, pool_row, *near)
+        far_re = lax.ppermute(far_re, "pool", swaps[4])
+        far_im = lax.ppermute(far_im, "pool", swaps[2])
 
     arranged = [
         pl.pallas_call(
@@ -575,14 +649,26 @@
         cost_estimate=pl.CostEstimate(flops=JOIN_COST, bytes_accessed=10**6, transcendentals=0),
         name="join",
     )(me_row, *arranged, *returned[-1])
-    sums = pl.pallas_call(
-        couple_kernel,
-        out_shape=jax.ShapeDtypeStruct((2, bands, bands), BF16),
-        in_specs=[whole(), whole()],
-        out_specs=whole(),
-        compiler_params=params(),
-        name="couple",
-    )(partner, sorted_response)
+    sums_shape = jax.ShapeDtypeStruct((2, bands, bands), BF16)
+    if routed:
+        sums = pl.pallas_call(
+            couple_routed_kernel,
+            out_shape=sums_shape,
+            in_specs=[scalars] * 2 + [whole()] * (len(near) + 3),
+            out_specs=whole(),
+            scratch_shapes=[pltpu.VMEM((2 * bands, waves), BF16)],
+            compiler_params=params(),
+            name="couple",
+        )(partner_pool, pool_row, *near, far_re, far_im, sorted_response)
+    else:
+        sums = pl.pallas_call(
+            couple_kernel,
+            out_shape=sums_shape,
+            in_specs=[whole(), whole()],
+            out_specs=whole(),
+            compiler_params=params(),
+            name="couple",
+        )(partner, sorted_response)
     shares = [sums] + [lax.ppermute(sums, "fft", pairs[s]) for s in range(1, fft_count)]
     response = pl.pallas_call(
         unsort_kernel,

time: 72.1 us -> 70.8 us (0.982)
  starting transfers between devices: 23.2 us -> 19.1 us
  waiting for transfers between devices: 12.6 us -> 15.7 us
  local copies, waits for them, and re-layouts: 3.32 us -> 2.28 us
  Pallas kernels: 31.1 us -> 32 us
    all_to_all x2 -> x0, starting transfers between devices: 8.86 us -> none  [the longest x1 5.17 us: shards(): lax.all_to_all(ordered_all.reshape(pool_count, 2 * bands // pool_count, w...]
    ppermute x3, waiting for transfers between devices: 0.98 us -> 7.46 us  [shards(): lax.ppermute(ordered[s * CHUNKS + c], 'fft', pairs[s])]
    ppermute x0 -> x5, starting transfers between devices: none -> 5.71 us  [the longest x1 3.01 us: shards(): xn = lax.ppermute(own_re, 'pool', swaps[2])]
    ppermute x3, waiting for transfers between devices: 9.94 us -> 7.38 us  [shards(): lax.ppermute(back[s], 'fft', pairs[s])]
    unnamed x18 -> x20, local copies, waits for them, and re-layouts: 3.32 us -> 2.28 us
    pallas_call x1, Pallas kernels: 0.19 us -> 1.22 us  [shards(): pl.pallas_call(functools.partial(join_kernel, fft_count), out_shape=jax.S...]
    ppermute x3, starting transfers between devices: 5.48 us -> 4.6 us  [shards(): lax.ppermute(back[s], 'fft', pairs[s])]
    all_to_all x2 -> x0, waiting for transfers between devices: 0.83 us -> none  [the longest x1 0.83 us: shards(): lax.all_to_all(ordered_all.reshape(pool_count, 2 * bands // pool_count, w...]
  transfers between devices with their start and end apart: 11 -> 14, of which waited for: 6 -> 5; matrix products, arithmetic and copies ran while one was open for 0% -> 0% of each run, Pallas kernels for 35% -> 36%
where the time goes in v9:
time: 70.8 us; the launch traced here: 70.6 us
  Pallas kernels  32 us (45%)
  starting transfers between devices  19.1 us (27%)
  waiting for transfers between devices  15.7 us (22%)
  local copies, waits for them, and re-layouts  2.28 us (3%)
  between operations  0.81 us (1%)
    pallas_call x1, Pallas kernels, shards(): pl.pallas_call(functools.partial(box_first_kernel, side, chunks, team, wa...  19.7 us
    ppermute x3, waiting for transfers between devices, shards(): lax.ppermute(ordered[s * CHUNKS + c], 'fft', pairs[s])  7.46 us
    ppermute x3, waiting for transfers between devices, shards(): lax.ppermute(back[s], 'fft', pairs[s])  7.38 us
    pallas_call x1, Pallas kernels, shards(): pl.pallas_call(functools.partial(sort_kernel, side, fft_count), out_shape...  5.49 us
    ppermute x3, starting transfers between devices, shards(): lax.ppermute(back[s], 'fft', pairs[s])  4.6 us
    ppermute x3, starting transfers between devices, shards(): lax.ppermute(sums, 'fft', pairs[s])  4.44 us
    ppermute x3, starting transfers between devices, shards(): lax.ppermute(ordered[s * CHUNKS + c], 'fft', pairs[s])  4.39 us
    ppermute x1, starting transfers between devices, shards(): xn = lax.ppermute(own_re, 'pool', swaps[2])  3.01 us
  transfers between devices with their start and end apart: 14, of which 5 were waited for; matrix products, arithmetic and copies ran while one was open for 0% of the time, Pallas kernels for 36%

profile of v9, /device:TPU:0, one launch (start us, length us, event | category | flops | bytes accessed | tf_op | source)
XLA Modules:
  0.0 70.6 jit_solution(7791569788646289942)
XLA Ops:
  0.6 5.5 %sort_waves.1 = (bf16[32,2304]{1,0:T(8,128)(2,1)}, bf16[32,2304]{1,0:T(8,128)(2,1)}, bf16[32,2304]{1,0:T(8,128)(2,1)}, bf16[32,2304]{1,0:T(8,128)(2,1)}, bf16[64...) custom-call(s32[1]{0:T(128)} %bitcast.me_ref, s32[1,2048]{1,0:T(1,128)} %bitcast.14, ...), custom_call_target="tpu_custom_call" | custom-call | tf_op jit(solution)/shard_map/sort_waves/pallas_call | solution.py:498
  6.1 0.0 copy-start
  6.1 0.0 copy-start.1
  6.2 3.0 %collective-permute-start.3 = (bf16[64,2048]{1,0:T(8,128)(2,1)}, bf16[64,2048]{1,0:T(8,128)(2,1)S(1)}, u32[]{:S(2)}, u32[]{:S(2)}) collective-permute-start(bf16[64,2048]{1,0:T(8,128)(2,1)} %get-tuple-element.19.re_ref.own_re), channel_id=1, source_target_pairs={{0,8},{4,12},{8,0},{12,4},{16,24},{20,28},{24,16},{28,20},{1,9},{5... | collective-permute-start | bytes 786440 | tf_op jit(solution)/shard_map/ppermute | solution.py:531
  9.2 1.5 %collective-permute-start.4 = (bf16[64,2048]{1,0:T(8,128)(2,1)}, bf16[64,2048]{1,0:T(8,128)(2,1)S(1)}, u32[]{:S(2)}, u32[]{:S(2)}) collective-permute-start(bf16[64,2048]{1,0:T(8,128)(2,1)} %get-tuple-element.20.im_ref.own_im), channel_id=1, source_target_pairs={{0,16},{4,20},{8,24},{12,28},{16,0},{20,4},{24,8},{28,12},{1,17},{... | collective-permute-start | bytes 786440 | tf_op jit(solution)/shard_map/ppermute | solution.py:532
  10.7 1.6 %collective-permute-start = (bf16[32,2304]{1,0:T(8,128)(2,1)}, bf16[32,2304]{1,0:T(8,128)(2,1)S(1)}, u32[]{:S(2)}, u32[]{:S(2)}) collective-permute-start(bf16[32,2304]{1,0:T(8,128)(2,1)} %get-tuple-element.16), channel_id=1, source_target_pairs={{0,1},{1,0},{2,3},{3,2},{4,5},{5,4},{6,7},{7,6},{8,9},{9,8},{10,11... | collective-permute-start | bytes 442376 | tf_op jit(solution)/shard_map/ppermute | solution.py:522
  12.3 2.6 %collective-permute-start.1 = (bf16[32,2304]{1,0:T(8,128)(2,1)}, bf16[32,2304]{1,0:T(8,128)(2,1)S(1)}, u32[]{:S(2)}, u32[]{:S(2)}) collective-permute-start(bf16[32,2304]{1,0:T(8,128)(2,1)} %get-tuple-element.17), channel_id=1, source_target_pairs={{0,2},{1,3},{2,0},{3,1},{4,6},{5,7},{6,4},{7,5},{8,10},{9,11},{10,... | collective-permute-start | bytes 442376 | tf_op jit(solution)/shard_map/ppermute | solution.py:522
  14.8 0.2 collective-permute-start.2
  15.1 0.0 copy-start.3
  15.1 1.6 %copy-done.3 = f32[64,64,128]{2,1,0:T(8,128)S(1)} copy-done((f32[64,64,128]{2,1,0:T(8,128)S(1)}, f32[64,64,128]{2,1,0:T(8,128)}, u32[]{:S(2)}) %copy-start.3) | copy-done | bytes 2097176
  16.7 0.0 copy-start.4
  16.7 0.0 copy-start.6
  16.7 0.0 copy-start.7
  16.7 1.7 %field_pairs.1.refs_4_ = bf16[4,64,2176]{2,1,0:T(8,128)(2,1)S(1)} custom-call(f32[4096,128]{1,0:T(8,128)S(1)} %bitcast.12), custom_call_target="tpu_custom_call" | custom-call | flops 1000000000 | bytes 1000000 | tf_op jit(solution)/shard_map/field_pairs/pallas_call | solution.py:550
  18.4 0.0 collective-permute-done.3.refs_7_.xn_ref.xn
  18.4 0.0 collective-permute-done.4.refs_8_.yn_ref.yn
  18.4 0.0 copy-done
  18.4 0.0 copy-done.1
  18.4 0.1 stack.1
  18.5 0.1 collective-permute-start.8
  18.6 0.0 collective-permute-done.refs_1_
  18.6 7.5 %collective-permute-done.1.refs_2_ = bf16[32,2304]{1,0:T(8,128)(2,1)S(1)} collective-permute-done((bf16[32,2304]{1,0:T(8,128)(2,1)}, bf16[32,2304]{1,0:T(8,128)(2,1)S(1)}, u32[]{:S(2)}, u32[]{:S(2)}) %collective-permute-start.1) | collective-permute-done | bytes 147488 | tf_op jit(solution)/shard_map/ppermute | solution.py:522
  26.1 0.0 collective-permute-done.2.refs_3_
  26.1 0.0 copy-done.4
  26.1 0.0 copy-done.6
  26.1 0.0 copy-done.7
  26.1 0.0 copy-start.2
  26.1 19.7 %box_first.1 = (bf16[32,2048]{1,0:T(8,128)(2,1)S(1)}, bf16[32,2048]{1,0:T(8,128)(2,1)S(1)}, bf16[32,2048]{1,0:T(8,128)(2,1)S(1)}, bf16[32,2048]{1,0:T(8,128)(2,1...) custom-call(bf16[32,2304]{1,0:T(8,128)(2,1)S(1)} %copy-done.4, ...), custom_call_target="tpu_custom_call" | custom-call | flops 10000000000 | bytes 10000000 | tf_op jit(solution)/shard_map/box_first/pallas_call | solution.py:571
  45.8 0.0 copy-start.8
  45.8 0.6 copy-done.8
  46.5 2.1 %collective-permute-start.5 = (bf16[32,2048]{1,0:T(8,128)(2,1)S(1)}, bf16[32,2048]{1,0:T(8,128)(2,1)}, u32[]{:S(2)}, u32[]{:S(2)}) collective-permute-start(bf16[32,2048]{1,0:T(8,128)(2,1)S(1)} %get-tuple-element.22), channel_id=1, source_target_pairs={{0,1},{1,0},{2,3},{3,2},{4,5},{5,4},{6,7},{7,6},{8,9},{9,8},{10,11... | collective-permute-start | bytes 393224 | tf_op jit(solution)/shard_map/ppermute | solution.py:589
  48.6 1.0 %collective-permute-start.6 = (bf16[32,2048]{1,0:T(8,128)(2,1)S(1)}, bf16[32,2048]{1,0:T(8,128)(2,1)}, u32[]{:S(2)}, u32[]{:S(2)}) collective-permute-start(bf16[32,2048]{1,0:T(8,128)(2,1)S(1)} %get-tuple-element.23), channel_id=1, source_target_pairs={{0,2},{1,3},{2,0},{3,1},{4,6},{5,7},{6,4},{7,5},{8,10},{9,11},{10,... | collective-permute-start | bytes 393224 | tf_op jit(solution)/shard_map/ppermute | solution.py:589
  49.6 1.5 %collective-permute-start.7 = (bf16[32,2048]{1,0:T(8,128)(2,1)S(1)}, bf16[32,2048]{1,0:T(8,128)(2,1)}, u32[]{:S(2)}, u32[]{:S(2)}) collective-permute-start(bf16[32,2048]{1,0:T(8,128)(2,1)S(1)} %get-tuple-element.24), channel_id=1, source_target_pairs={{0,3},{1,2},{2,1},{3,0},{4,7},{5,6},{6,5},{7,4},{8,11},{9,10},{10,... | collective-permute-start | bytes 393224 | tf_op jit(solution)/shard_map/ppermute | solution.py:589
  51.1 0.0 copy-start.9
  51.1 0.0 collective-permute-done.8.other
  51.1 0.0 copy-done.2
  51.1 0.6 route_partner.1
  51.7 0.6 collective-permute-start.9
  52.3 0.5 collective-permute-start.10
  52.8 0.1 collective-permute-done.5.refs_1_
  52.9 7.3 %collective-permute-done.6.refs_2_ = bf16[32,2048]{1,0:T(8,128)(2,1)} collective-permute-done((bf16[32,2048]{1,0:T(8,128)(2,1)S(1)}, bf16[32,2048]{1,0:T(8,128)(2,1)}, u32[]{:S(2)}, u32[]{:S(2)}) %collective-permute-start.6) | collective-permute-done | bytes 131104 | tf_op jit(solution)/shard_map/ppermute | solution.py:589
  60.2 0.0 collective-permute-done.7.refs_3_
  60.2 0.0 copy-done.9
  60.2 1.2 %join.1.y_ref.sorted_ref = bf16[128,2048]{1,0:T(8,128)(2,1)S(1)} custom-call(s32[1]{0:T(128)} %bitcast.me_ref, bf16[32,2048]{1,0:T(8,128)(2,1)S(1)} %copy-done.9, bf16[32,2048]{1,0:T(8,128)(2,1)} %collective-permute-done.5.refs_1_, bf16[32,2048]{1,0:T(8,128)(2,1)} %collective-permute-done.6.refs_2_, bf16[32,2048]{1,0:T(8,128)(2,1)} %collective-permute-done.7.refs_3_), custom_call_target="tpu_custom_call" | custom-call | flops 99999997952 | bytes 1000000 | tf_op jit(solution)/shard_map/join/pallas_call | solution.py:642
  61.4 0.0 copy-start.5
  61.4 0.0 collective-permute-done.9.far_re
  61.4 0.0 collective-permute-done.10.far_im
  61.5 1.1 %couple.1 = bf16[2,64,64]{2,1,0:T(8,128)(2,1)S(1)} custom-call(s32[8]{0:T(128)S(1)} %copy-done.2, s32[1]{0:T(128)} %bitcast.6.i_ref, bf16[64,2048]{1,0:T(8,128)(2,1)S(1)} %copy-done, bf16[64,2048]{1,0:T(8,128)(2,1)S(1)} %copy-done.1, bf16[64,2048]{1,0:T(8,128)(2,1)S(1)} %collective-permute-done.3.refs_7_.xn_ref.xn, ...), custom_call_target="tpu_custom_call" | custom-call | tf_op jit(solution)/shard_map/couple/pallas_call | solution.py:654
  62.5 1.8 %collective-permute-start.11 = (bf16[2,64,64]{2,1,0:T(8,128)(2,1)S(1)}, bf16[2,64,64]{2,1,0:T(8,128)(2,1)S(1)}, u32[]{:S(2)}, u32[]{:S(2)}) collective-permute-start(bf16[2,64,64]{2,1,0:T(8,128)(2,1)S(1)} %couple.1), channel_id=1, source_target_pairs={{0,3},{1,2},{2,1},{3,0},{4,7},{5,6},{6,5},{7,4},{8,11},{9,10},{10,... | collective-permute-start | bytes 49160 | tf_op jit(solution)/shard_map/ppermute | solution.py:672
  64.4 1.6 %collective-permute-start.12 = (bf16[2,64,64]{2,1,0:T(8,128)(2,1)S(1)}, bf16[2,64,64]{2,1,0:T(8,128)(2,1)S(1)}, u32[]{:S(2)}, u32[]{:S(2)}) collective-permute-start(bf16[2,64,64]{2,1,0:T(8,128)(2,1)S(1)} %couple.1), channel_id=1, source_target_pairs={{0,2},{1,3},{2,0},{3,1},{4,6},{5,7},{6,4},{7,5},{8,10},{9,11},{10,... | collective-permute-start | bytes 49160 | tf_op jit(solution)/shard_map/ppermute | solution.py:672
  66.0 1.0 %collective-permute-start.13 = (bf16[2,64,64]{2,1,0:T(8,128)(2,1)S(1)}, bf16[2,64,64]{2,1,0:T(8,128)(2,1)S(1)}, u32[]{:S(2)}, u32[]{:S(2)}) collective-permute-start(bf16[2,64,64]{2,1,0:T(8,128)(2,1)S(1)} %couple.1), channel_id=1, source_target_pairs={{0,1},{1,0},{2,3},{3,2},{4,5},{5,4},{6,7},{7,6},{8,9},{9,8},{10,11... | collective-permute-start | bytes 49160 | tf_op jit(solution)/shard_map/ppermute | solution.py:672
  67.0 0.0 copy-done.5
  67.0 2.1 %unsort.1 = bf16[128,2048]{1,0:T(8,128)(2,1)} custom-call(bf16[128,2048]{1,0:T(8,128)(2,1)S(1)} %join.1.y_ref.sorted_ref, s32[1,2048]{1,0:T(1,128)S(1)} %copy-done.5), custom_call_target="tpu_custom_call" | custom-call | flops 1000000000 | bytes 10000000 | tf_op jit(solution)/shard_map/unsort/pallas_call | solution.py:673
  69.1 0.0 collective-permute-done.11
  69.1 0.1 collective-permute-done.12
  69.2 0.7 %collective-permute-done.13 = bf16[2,64,64]{2,1,0:T(8,128)(2,1)S(1)} collective-permute-done((bf16[2,64,64]{2,1,0:T(8,128)(2,1)S(1)}, bf16[2,64,64]{2,1,0:T(8,128)(2,1)S(1)}, u32[]{:S(2)}, u32[]{:S(2)}) %collective-permute-start.13) | collective-permute-done | bytes 16416 | tf_op jit(solution)/shard_map/ppermute | solution.py:672
  69.9 0.7 multiply_bitcast_fusion
Async XLA Ops:
  6.1 12.3 %copy-start = (bf16[64,2048]{1,0:T(8,128)(2,1)S(1)}, bf16[64,2048]{1,0:T(8,128)(2,1)}, u32[]{:S(2)}) copy-start(bf16[64,2048]{1,0:T(8,128)(2,1)} %get-tuple-element.19.re_ref.own_re) | copy-start | bytes 786436
  6.1 12.3 %copy-start.1 = (bf16[64,2048]{1,0:T(8,128)(2,1)S(1)}, bf16[64,2048]{1,0:T(8,128)(2,1)}, u32[]{:S(2)}) copy-start(bf16[64,2048]{1,0:T(8,128)(2,1)} %get-tuple-element.20.im_ref.own_im) | copy-start | bytes 786436
  6.2 12.2 %collective-permute-start.3 = (bf16[64,2048]{1,0:T(8,128)(2,1)}, bf16[64,2048]{1,0:T(8,128)(2,1)S(1)}, u32[]{:S(2)}, u32[]{:S(2)}) collective-permute-start(bf16[64,2048]{1,0:T(8,128)(2,1)} %get-tuple-element.19.re_ref.own_re), channel_id=1, source_target_pairs={{0,8},{4,12},{8,0},{12,4},{16,24},{20,28},{24,16},{28,20},{1,9},{5... | collective-permute-start | bytes 786440 | tf_op jit(solution)/shard_map/ppermute | solution.py:531
  9.2 9.2 %collective-permute-start.4 = (bf16[64,2048]{1,0:T(8,128)(2,1)}, bf16[64,2048]{1,0:T(8,128)(2,1)S(1)}, u32[]{:S(2)}, u32[]{:S(2)}) collective-permute-start(bf16[64,2048]{1,0:T(8,128)(2,1)} %get-tuple-element.20.im_ref.own_im), channel_id=1, source_target_pairs={{0,16},{4,20},{8,24},{12,28},{16,0},{20,4},{24,8},{28,12},{1,17},{... | collective-permute-start | bytes 786440 | tf_op jit(solution)/shard_map/ppermute | solution.py:532
  10.7 7.9 %collective-permute-start = (bf16[32,2304]{1,0:T(8,128)(2,1)}, bf16[32,2304]{1,0:T(8,128)(2,1)S(1)}, u32[]{:S(2)}, u32[]{:S(2)}) collective-permute-start(bf16[32,2304]{1,0:T(8,128)(2,1)} %get-tuple-element.16), channel_id=1, source_target_pairs={{0,1},{1,0},{2,3},{3,2},{4,5},{5,4},{6,7},{7,6},{8,9},{9,8},{10,11... | collective-permute-start | bytes 442376 | tf_op jit(solution)/shard_map/ppermute | solution.py:522
  12.3 13.8 %collective-permute-start.1 = (bf16[32,2304]{1,0:T(8,128)(2,1)}, bf16[32,2304]{1,0:T(8,128)(2,1)S(1)}, u32[]{:S(2)}, u32[]{:S(2)}) collective-permute-start(bf16[32,2304]{1,0:T(8,128)(2,1)} %get-tuple-element.17), channel_id=1, source_target_pairs={{0,2},{1,3},{2,0},{3,1},{4,6},{5,7},{6,4},{7,5},{8,10},{9,11},{10,... | collective-permute-start | bytes 442376 | tf_op jit(solution)/shard_map/ppermute | solution.py:522
  14.8 11.2 %collective-permute-start.2 = (bf16[32,2304]{1,0:T(8,128)(2,1)}, bf16[32,2304]{1,0:T(8,128)(2,1)S(1)}, u32[]{:S(2)}, u32[]{:S(2)}) collective-permute-start(bf16[32,2304]{1,0:T(8,128)(2,1)} %get-tuple-element.18), channel_id=1, source_target_pairs={{0,3},{1,2},{2,1},{3,0},{4,7},{5,6},{6,5},{7,4},{8,11},{9,10},{10,... | collective-permute-start | bytes 442376 | tf_op jit(solution)/shard_map/ppermute | solution.py:522
  15.1 1.6 %copy-start.3 = (f32[64,64,128]{2,1,0:T(8,128)S(1)}, f32[64,64,128]{2,1,0:T(8,128)}, u32[]{:S(2)}) copy-start(f32[64,64,128]{2,1,0:T(8,128)} %param.9) | copy-start | bytes 6291460
  16.7 9.4 %copy-start.4 = (bf16[32,2304]{1,0:T(8,128)(2,1)S(1)}, bf16[32,2304]{1,0:T(8,128)(2,1)}, u32[]{:S(2)}) copy-start(bf16[32,2304]{1,0:T(8,128)(2,1)} %get-tuple-element.15.refs_0_) | copy-start | bytes 442372
  16.7 9.4 %copy-start.6 = (bf16[2,128,128]{2,1,0:T(8,128)(2,1)S(1)}, bf16[2,128,128]{2,1,0:T(8,128)(2,1)}, u32[]{:S(2)}) copy-start(bf16[2,128,128]{2,1,0:T(8,128)(2,1)} %constant.23.clone.refs_6_) | copy-start | bytes 196612
  16.7 9.4 %copy-start.7 = (bf16[64,256]{1,0:T(8,128)(2,1)S(1)}, bf16[64,256]{1,0:T(8,128)(2,1)}, u32[]{:S(2)}) copy-start(bf16[64,256]{1,0:T(8,128)(2,1)} %constant.22.clone.refs_5_) | copy-start | bytes 98308
  18.5 32.6 %collective-permute-start.8 = (bf16[256,2048]{1,0:T(8,128)(2,1)S(1)}, bf16[256,2048]{1,0:T(8,128)(2,1)S(1)}, u32[]{:S(2)}, u32[]{:S(2)}) collective-permute-start(bf16[256,2048]{1,0:T(8,128)(2,1)S(1)} %stack.1), channel_id=1, source_target_pairs={{0,4},{4,0},{8,12},{12,8},{16,20},{20,16},{24,28},{28,24},{1,5},{5... | collective-permute-start | bytes 3145736 | tf_op jit(solution)/shard_map/ppermute | solution.py:541
  26.1 25.0 %copy-start.2 = (s32[8]{0:T(128)S(1)}, s32[8]{0:T(128)}, u32[]{:S(2)}) copy-start(s32[8]{0:T(128)} %order_ref.3) | copy-start | bytes 100
  45.8 0.7 copy-start.8
  46.5 6.5 %collective-permute-start.5 = (bf16[32,2048]{1,0:T(8,128)(2,1)S(1)}, bf16[32,2048]{1,0:T(8,128)(2,1)}, u32[]{:S(2)}, u32[]{:S(2)}) collective-permute-start(bf16[32,2048]{1,0:T(8,128)(2,1)S(1)} %get-tuple-element.22), channel_id=1, source_target_pairs={{0,1},{1,0},{2,3},{3,2},{4,5},{5,4},{6,7},{7,6},{8,9},{9,8},{10,11... | collective-permute-start | bytes 393224 | tf_op jit(solution)/shard_map/ppermute | solution.py:589
  48.6 11.6 %collective-permute-start.6 = (bf16[32,2048]{1,0:T(8,128)(2,1)S(1)}, bf16[32,2048]{1,0:T(8,128)(2,1)}, u32[]{:S(2)}, u32[]{:S(2)}) collective-permute-start(bf16[32,2048]{1,0:T(8,128)(2,1)S(1)} %get-tuple-element.23), channel_id=1, source_target_pairs={{0,2},{1,3},{2,0},{3,1},{4,6},{5,7},{6,4},{7,5},{8,10},{9,11},{10,... | collective-permute-start | bytes 393224 | tf_op jit(solution)/shard_map/ppermute | solution.py:589
  49.6 10.6 %collective-permute-start.7 = (bf16[32,2048]{1,0:T(8,128)(2,1)S(1)}, bf16[32,2048]{1,0:T(8,128)(2,1)}, u32[]{:S(2)}, u32[]{:S(2)}) collective-permute-start(bf16[32,2048]{1,0:T(8,128)(2,1)S(1)} %get-tuple-element.24), channel_id=1, source_target_pairs={{0,3},{1,2},{2,1},{3,0},{4,7},{5,6},{6,5},{7,4},{8,11},{9,10},{10,... | collective-permute-start | bytes 393224 | tf_op jit(solution)/shard_map/ppermute | solution.py:589
  51.1 9.1 %copy-start.9 = (bf16[32,2048]{1,0:T(8,128)(2,1)S(1)}, bf16[32,2048]{1,0:T(8,128)(2,1)}, u32[]{:S(2)}) copy-start(bf16[32,2048]{1,0:T(8,128)(2,1)} %copy-done.8) | copy-start | bytes 393220
  51.7 9.7 %collective-permute-start.9 = (bf16[64,2048]{1,0:T(8,128)(2,1)S(1)}, bf16[64,2048]{1,0:T(8,128)(2,1)S(1)}, u32[]{:S(2)}, u32[]{:S(2)}) collective-permute-start(bf16[64,2048]{1,0:T(8,128)(2,1)S(1)} %get-tuple-element.26), channel_id=1, source_target_pairs={{0,16},{4,20},{8,24},{12,28},{16,0},{20,4},{24,8},{28,12},{1,17},{... | collective-permute-start | bytes 786440 | tf_op jit(solution)/shard_map/ppermute | solution.py:625
  52.3 9.2 %collective-permute-start.10 = (bf16[64,2048]{1,0:T(8,128)(2,1)S(1)}, bf16[64,2048]{1,0:T(8,128)(2,1)S(1)}, u32[]{:S(2)}, u32[]{:S(2)}) collective-permute-start(bf16[64,2048]{1,0:T(8,128)(2,1)S(1)} %get-tuple-element.27), channel_id=1, source_target_pairs={{0,8},{4,12},{8,0},{12,4},{16,24},{20,28},{24,16},{28,20},{1,9},{5... | collective-permute-start | bytes 786440 | tf_op jit(solution)/shard_map/ppermute | solution.py:626
  61.4 5.5 %copy-start.5 = (s32[1,2048]{1,0:T(1,128)S(1)}, s32[1,2048]{1,0:T(1,128)}, u32[]{:S(2)}) copy-start(s32[1,2048]{1,0:T(1,128)} %get-tuple-element.25.rank_ref) | copy-start | bytes 24580
  62.5 6.5 %collective-permute-start.11 = (bf16[2,64,64]{2,1,0:T(8,128)(2,1)S(1)}, bf16[2,64,64]{2,1,0:T(8,128)(2,1)S(1)}, u32[]{:S(2)}, u32[]{:S(2)}) collective-permute-start(bf16[2,64,64]{2,1,0:T(8,128)(2,1)S(1)} %couple.1), channel_id=1, source_target_pairs={{0,3},{1,2},{2,1},{3,0},{4,7},{5,6},{6,5},{7,4},{8,11},{9,10},{10,... | collective-permute-start | bytes 49160 | tf_op jit(solution)/shard_map/ppermute | solution.py:672
  64.4 4.8 %collective-permute-start.12 = (bf16[2,64,64]{2,1,0:T(8,128)(2,1)S(1)}, bf16[2,64,64]{2,1,0:T(8,128)(2,1)S(1)}, u32[]{:S(2)}, u32[]{:S(2)}) collective-permute-start(bf16[2,64,64]{2,1,0:T(8,128)(2,1)S(1)} %couple.1), channel_id=1, source_target_pairs={{0,2},{1,3},{2,0},{3,1},{4,6},{5,7},{6,4},{7,5},{8,10},{9,11},{10,... | collective-permute-start | bytes 49160 | tf_op jit(solution)/shard_map/ppermute | solution.py:672
  66.0 3.9 %collective-permute-start.13 = (bf16[2,64,64]{2,1,0:T(8,128)(2,1)S(1)}, bf16[2,64,64]{2,1,0:T(8,128)(2,1)S(1)}, u32[]{:S(2)}, u32[]{:S(2)}) collective-permute-start(bf16[2,64,64]{2,1,0:T(8,128)(2,1)S(1)} %couple.1), channel_id=1, source_target_pairs={{0,1},{1,0},{2,3},{3,2},{4,5},{5,4},{6,7},{7,6},{8,9},{9,8},{10,11... | collective-permute-start | bytes 49160 | tf_op jit(solution)/shard_map/ppermute | solution.py:672

commit v10 on v9

--- a/solution.py
+++ b/solution.py
@@ -12,13 +12,12 @@
 STICK_DEV = 64
 LANES = 128
 UNROLL = 16
-CHUNKS = 1
 BF16 = jnp.bfloat16
 F32 = jnp.float32
 VMEM_LIMIT = 24 * 1024 * 1024
-SORT_LIMIT = 60 * 1024 * 1024
-ARRANGE_COST = 3*10**9
+SORT_LIMIT = 24 * 1024 * 1024
 JOIN_COST = 10**11
+MARK_COST = 3*10**9
 BOX_COST = 10**10
 
 
@@ -78,7 +77,7 @@
 
 
 def sort_kernel(side, groups, me_ref, idx_ref, x_hbm, *refs):
-    outs, (re_ref, im_ref, rank_ref, x_ref, wide, pieces, sem) = refs[: groups * CHUNKS], refs[groups * CHUNKS :]
+    outs, (re_ref, im_ref, rank_ref, x_ref, wide, pieces, sem) = refs[:groups], refs[groups:]
     fetch = pltpu.make_async_copy(x_hbm, x_ref, sem)
     fetch.start()
     xh, yh, ch, slot_of, cells, rank = locate(idx_ref[...], side)
@@ -87,7 +86,7 @@
     both = x_ref.shape[0]
     bands = both // 2
     share = bands // groups
-    rows = 2 * share // CHUNKS
+    rows = 2 * share
     cells = jnp.concatenate([cells[i : i + rows] for i in range(0, side, rows)], axis=1)
     tiles = waves // LANES
     in_tile = one_hot(rank & (LANES - 1), LANES)
@@ -103,11 +102,10 @@
     extra = jnp.concatenate([cells] + lines, axis=1).astype(BF16)
     low = one_hot(rank & 255, 256)
     for shift in range(groups):
-        outs[shift * CHUNKS][:, waves:] = extra
+        outs[shift][:, waves:] = extra
     fetch.wait()
     parts = waves // 256
     step = 2 if parts % 2 == 0 else 1
-    half = share // CHUNKS
     for first in range(0, parts, step):
         for part in range(first, first + step):
             mask = jnp.where((rank >> 8) == part, 1.0, 0.0).astype(BF16)
@@ -122,11 +120,7 @@
                 begin = pl.multiple_of(part * both + (me_ref[0] ^ shift) * share, 8)
                 re = pieces[pl.ds(begin, share)]
                 im = pieces[pl.ds(begin + bands, share)]
-                for c in range(CHUNKS):
-                    mine = slice(c * half, (c + 1) * half)
-                    outs[shift * CHUNKS + c][:, here] = jnp.concatenate(
-                        [re[mine], im[mine]], axis=0
-                    ).astype(BF16)
+                outs[shift][:, here] = jnp.concatenate([re, im], axis=0).astype(BF16)
 
 
 def field_kernel(side, chunks, pot_ref, field_ref):
@@ -165,6 +159,10 @@
         copies.append(copy)
     for copy in copies:
         copy.wait()
+
+
+def mark_kernel(*refs):
+    refs[-1][...] = jnp.zeros(refs[-1].shape, F32)
 
 
 def choose(code, mask, sources, out_ref):
@@ -266,28 +264,17 @@
         tab_ref[:, base + LANES : base + 2 * LANES] = (cy * sx + sy * cx).astype(BF16)
 
 
-def box_first_kernel(side, chunks, team, waves, groups, gates, *refs):
-    x_refs, refs = refs[:groups], refs[groups:]
+def box_kernel(side, chunks, team, waves, groups, gates, *refs):
+    x_refs, refs = refs[:groups][::-1], refs[groups:]
     (field_ref, cs_ref, wz_ref), refs = refs[:3], refs[3 + gates :]
     out_refs, refs = refs[:groups], refs[groups:]
-    (tab_ref, spot_ref, col_ref, start_ref), refs = refs[:4], refs[4:]
-    *scratch, cyr_ref, syr_ref, start_s, sem = refs
+    *scratch, tab_ref, spot_ref, col_ref, start_ref, cyr_ref, syr_ref, start_s, sem = refs
     build_tables(
         side, chunks, waves, x_refs, cs_ref, tab_ref, spot_ref, col_ref, start_ref, cyr_ref, syr_ref
     )
     to_scalars = pltpu.make_async_copy(start_ref, start_s, sem)
     to_scalars.start()
     to_scalars.wait()
-    box_work(
-        side, chunks, team, waves, x_refs, field_ref, wz_ref, tab_ref, spot_ref, col_ref, start_s,
-        out_refs, *scratch,
-    )
-
-
-def box_next_kernel(side, chunks, team, waves, groups, *refs):
-    x_refs, refs = refs[:groups], refs[groups:]
-    (field_ref, wz_ref, tab_ref, spot_ref, col_ref, start_s), refs = refs[:6], refs[6:]
-    out_refs, scratch = refs[:groups], refs[groups:]
     box_work(
         side, chunks, team, waves, x_refs, field_ref, wz_ref, tab_ref, spot_ref, col_ref, start_s,
         out_refs, *scratch,
@@ -415,29 +402,23 @@
         out_refs[d][...] = (acc[0, d] + late).astype(BF16)
 
 
-def arrange_kernel(groups, me_ref, *refs):
-    y_refs, (rows_ref,) = refs[:groups], refs[groups:]
+def join_kernel(groups, me_ref, *refs):
+    y_refs, (sorted_ref,) = refs[:groups][::-1], refs[groups:]
     part = y_refs[0].shape[0] // 2
     half = groups * part
     me = me_ref[0]
+    even = (me & 1) == 0
     for j in range(groups // 2):
         one, other = y_refs[2 * j][...].astype(F32), y_refs[2 * j + 1][...].astype(F32)
-        low = jnp.where((me & 1) == 0, one, other)
-        high = jnp.where((me & 1) == 0, other, one)
-        begin = pl.multiple_of(((me >> 1) ^ j) * (2 * part), 8)
-        rows_ref[pl.ds(begin, 2 * part)] = jnp.concatenate([low[:part], high[:part]], axis=0)
-        rows_ref[pl.ds(begin + half, 2 * part)] = jnp.concatenate([low[part:], high[part:]], axis=0)
-
-
-def join_kernel(groups, me_ref, *refs):
-    rows_refs, refs = refs[: CHUNKS - 1], refs[CHUNKS - 1 :]
-    sorted_ref, rows_scr = refs[groups:]
-    arrange_kernel(groups, me_ref, *refs[:groups], rows_scr)
-    values = [ref[...] for ref in (*rows_refs, rows_scr)]
-    part = values[0].shape[0] // (2 * groups)
-    sorted_ref[...] = jnp.concatenate(
-        [v[i * part : (i + 1) * part] for i in range(2 * groups) for v in values], axis=0
-    ).astype(BF16)
+        low = jnp.where(even, one, other)
+        high = jnp.where(even, other, one)
+        begin = pl.multiple_of(((me >> 1) ^ j) * (2 * part), 16)
+        sorted_ref[pl.ds(begin, 2 * part)] = jnp.concatenate(
+            [low[:part], high[:part]], axis=0
+        ).astype(BF16)
+        sorted_ref[pl.ds(begin + half, 2 * part)] = jnp.concatenate(
+            [low[part:], high[part:]], axis=0
+        ).astype(BF16)
 
 
 def couple_kernel(partner_ref, sorted_ref, g_ref):
@@ -462,6 +443,13 @@
         out_ref[:, here] = total.astype(BF16)
 
 
+def exchange(blocks, pairs):
+    moved = list(blocks)
+    for s in range(len(blocks) - 1, 0, -1):
+        moved[s] = lax.ppermute(blocks[s], "fft", pairs[s])
+    return moved
+
+
 def whole(memory=pltpu.VMEM):
     return pl.BlockSpec(memory_space=memory)
 
@@ -490,7 +478,7 @@
     me_row = me.reshape(1)
     pairs = [[(i, i ^ s) for i in range(fft_count)] for s in range(fft_count)]
     pool_count = lax.axis_size("pool")
-    rows = 2 * share // CHUNKS
+    rows = 2 * share
     tiles = waves // LANES
     packed = waves + side * STICK_DEV // rows + -(-(tiles + 8) // rows) * LANES
     scalars, blocks = whole(pltpu.SMEM), [whole()] * fft_count
@@ -498,9 +486,8 @@
     *ordered, own_re, own_im, rank = pl.pallas_call(
         functools.partial(sort_kernel, side, fft_count),
         out_shape=[
-            jax.ShapeDtypeStruct((rows, waves if c else packed), BF16)
+            jax.ShapeDtypeStruct((rows, packed), BF16)
             for _ in range(fft_count)
-            for c in range(CHUNKS)
         ]
         + [
             jax.ShapeDtypeStruct((bands, waves), BF16),
@@ -508,7 +495,7 @@
             jax.ShapeDtypeStruct((1, waves), jnp.int32),
         ],
         in_specs=[scalars, whole(), whole(pltpu.HBM)],
-        out_specs=blocks * CHUNKS + [whole()] * 3,
+        out_specs=blocks + [whole()] * 3,
         scratch_shapes=[
             pltpu.VMEM((2 * bands, waves), BF16),
             pltpu.VMEM((waves // 256 * 2 * bands, waves), BF16),
@@ -518,10 +505,7 @@
         compiler_params=params(SORT_LIMIT),
         name="sort_waves",
     )(me_row, box_index.reshape(1, waves), coeffs)
-    moved = [
-        [ordered[c]] + [lax.ppermute(ordered[s * CHUNKS + c], "fft", pairs[s]) for s in range(1, fft_count)]
-        for c in range(CHUNKS)
-    ]
+    moved = exchange(ordered, pairs)
 
     routed = pool_count == 8
     half_rows = jax.ShapeDtypeStruct((bands, waves), BF16)
@@ -557,7 +541,16 @@
         name="field_pairs",
     )(potential.reshape(side * side, 2 * side))
 
-    gates = [xn, yn] if routed else []
+    mark = pl.pallas_call(
+        mark_kernel,
+        out_shape=jax.ShapeDtypeStruct((8, LANES), F32),
+        in_specs=[whole(pl.ANY)] * (fft_count - 1),
+        out_specs=whole(),
+        compiler_params=params(),
+        cost_estimate=pl.CostEstimate(flops=MARK_COST, bytes_accessed=10**4, transcendentals=0),
+        name="mark",
+    )(*moved[:0:-1])
+    gates = [mark, xn, yn] if routed else [mark]
     team = min(8, rows // 2)
     scratch = [
         pltpu.VMEM((2, fft_count, rows, waves), F32),
@@ -567,40 +560,27 @@
         pltpu.VMEM((2, fft_count, rows, waves), F32),
     ]
     cost = pl.CostEstimate(flops=BOX_COST, bytes_accessed=10**7, transcendentals=0)
-    shapes = [jax.ShapeDtypeStruct((rows, waves), BF16)] * fft_count
-    *back, tab, spot, col, start = pl.pallas_call(
-        functools.partial(box_first_kernel, side, chunks, team, waves, fft_count, len(gates)),
-        out_shape=shapes
+    back = pl.pallas_call(
+        functools.partial(box_kernel, side, chunks, team, waves, fft_count, len(gates)),
+        out_shape=[jax.ShapeDtypeStruct((rows, waves), BF16)] * fft_count,
+        in_specs=blocks + [whole()] * 3 + [whole(pl.ANY)] * len(gates),
+        out_specs=blocks,
+        scratch_shapes=scratch
         + [
-            jax.ShapeDtypeStruct((columns, 2 * chunks * LANES), BF16),
-            jax.ShapeDtypeStruct((fft_count, side, 2 * STICK_DEV), F32),
-            jax.ShapeDtypeStruct((2, fft_count, tiles, LANES), jnp.int32),
-            jax.ShapeDtypeStruct((fft_count, LANES), jnp.int32),
+            pltpu.VMEM((columns, 2 * chunks * LANES), BF16),
+            pltpu.VMEM((fft_count, side, 2 * STICK_DEV), F32),
+            pltpu.VMEM((2, fft_count, tiles, LANES), jnp.int32),
+            pltpu.VMEM((fft_count, LANES), jnp.int32),
+            pltpu.VMEM((side, chunks * LANES), BF16),
+            pltpu.VMEM((side, chunks * LANES), BF16),
+            pltpu.SMEM((fft_count, LANES), jnp.int32),
+            pltpu.SemaphoreType.DMA,
         ],
-        in_specs=blocks + [whole()] * 3 + [whole(pl.ANY)] * len(gates),
-        out_specs=blocks + [whole()] * 4,
-        scratch_shapes=scratch
-        + [pltpu.VMEM((side, chunks * LANES), BF16)] * 2
-        + [pltpu.SMEM((fft_count, LANES), jnp.int32), pltpu.SemaphoreType.DMA],
         compiler_params=params(),
         cost_estimate=cost,
-        name="box_first",
-    )(*moved[0], field, cs, wz, *gates)
-    returned = [[back[0]] + [lax.ppermute(back[s], "fft", pairs[s]) for s in range(1, fft_count)]]
-    for c in range(1, CHUNKS):
-        back = pl.pallas_call(
-            functools.partial(box_next_kernel, side, chunks, team, waves, fft_count),
-            out_shape=shapes,
-            in_specs=blocks + [whole()] * 5 + [scalars],
-            out_specs=blocks,
-            scratch_shapes=scratch,
-            compiler_params=params(),
-            cost_estimate=cost,
-            name="box_next",
-        )(*moved[c], field, wz, tab, spot, col, start)
-        returned.append(
-            [back[0]] + [lax.ppermute(back[s], "fft", pairs[s]) for s in range(1, fft_count)]
-        )
+        name="box_work",
+    )(*moved[::-1], field, cs, wz, *gates)
+    returned = exchange(back, pairs)
 
     if not routed:
         chosen = pl.pallas_call(
@@ -625,30 +605,15 @@
         far_re = lax.ppermute(far_re, "pool", swaps[4])
         far_im = lax.ppermute(far_im, "pool", swaps[2])
 
-    arranged = [
-        pl.pallas_call(
-            functools.partial(arrange_kernel, fft_count),
-            out_shape=jax.ShapeDtypeStruct((rows * fft_count, waves), F32),
-            in_specs=[scalars] + blocks,
-            out_specs=whole(),
-            compiler_params=params(),
-            cost_estimate=pl.CostEstimate(
-                flops=ARRANGE_COST, bytes_accessed=10**6, transcendentals=0
-            ),
-            name="arrange",
-        )(me_row, *returned[c])
-        for c in range(CHUNKS - 1)
-    ]
     sorted_response = pl.pallas_call(
         functools.partial(join_kernel, fft_count),
         out_shape=jax.ShapeDtypeStruct((2 * bands, waves), BF16),
-        in_specs=[scalars] + [whole()] * (CHUNKS - 1) + blocks,
+        in_specs=[scalars] + blocks,
         out_specs=whole(),
-        scratch_shapes=[pltpu.VMEM((rows * fft_count, waves), F32)],
         compiler_params=params(),
         cost_estimate=pl.CostEstimate(flops=JOIN_COST, bytes_accessed=10**6, transcendentals=0),
         name="join",
-    )(me_row, *arranged, *returned[-1])
+    )(me_row, *returned[::-1])
     sums_shape = jax.ShapeDtypeStruct((2, bands, bands), BF16)
     if routed:
         sums = pl.pallas_call(

time: 70.8 us -> 67.2 us (0.949)
  waiting for transfers between devices: 15.7 us -> 10.9 us
  Pallas kernels: 32 us -> 29.1 us
  local copies, waits for them, and re-layouts: 2.28 us -> 4.64 us
  starting transfers between devices: 19.1 us -> 20.9 us
    ppermute x6, waiting for transfers between devices: 14.8 us -> 10.2 us  [exchange(): moved[s] = lax.ppermute(blocks[s], 'fft', pairs[s])]
    unnamed x20 -> x16, local copies, waits for them, and re-layouts: 2.28 us -> 4.64 us
    pallas_call x1, Pallas kernels: 5.49 us -> 3.79 us  [shards(): pl.pallas_call(functools.partial(sort_kernel, side, fft_count), out_shape...]
    ppermute x1, starting transfers between devices: 3.01 us -> 1.64 us  [shards(): xn = lax.ppermute(own_re, 'pool', swaps[2])]
    ppermute x6, starting transfers between devices: 8.99 us -> 10.1 us  [exchange(): moved[s] = lax.ppermute(blocks[s], 'fft', pairs[s])]
    pallas_call x1 -> x2, Pallas kernels: 19.7 us -> 18.6 us  [the longest x1 18.6 us: shards(): pl.pallas_call(functools.partial(box_kernel, side, chunks, team, waves, f...]
    ppermute x1, starting transfers between devices: 0.57 us -> 1.58 us  [shards(): far_re = lax.ppermute(far_re, 'pool', swaps[4])]
    ppermute x1, starting transfers between devices: 0.54 us -> 1.48 us  [shards(): far_im = lax.ppermute(far_im, 'pool', swaps[2])]
  transfers between devices with their start and end apart: 14 -> 14, of which waited for: 5 -> 4; matrix products, arithmetic and copies ran while one was open for 0% -> 0% of each run, Pallas kernels for 36% -> 36%
where the time goes in v10:
time: 67.2 us; the launch traced here: 66.9 us
  Pallas kernels  29.1 us (43%)
  starting transfers between devices  20.9 us (31%)
  waiting for transfers between devices  10.9 us (16%)
  local copies, waits for them, and re-layouts  4.64 us (7%)
  between operations  0.77 us (1%)
    pallas_call x1, Pallas kernels, shards(): pl.pallas_call(functools.partial(box_kernel, side, chunks, team, waves, f...  18.6 us
    ppermute x6, waiting for transfers between devices, exchange(): moved[s] = lax.ppermute(blocks[s], 'fft', pairs[s])  10.2 us
    ppermute x6, starting transfers between devices, exchange(): moved[s] = lax.ppermute(blocks[s], 'fft', pairs[s])  10.1 us
    unnamed x16, local copies, waits for them, and re-layouts  4.64 us
    ppermute x3, starting transfers between devices, shards(): lax.ppermute(sums, 'fft', pairs[s])  4.44 us
    pallas_call x1, Pallas kernels, shards(): pl.pallas_call(functools.partial(sort_kernel, side, fft_count), out_shape...  3.79 us
    pallas_call x1, Pallas kernels, shards(): pl.pallas_call(unsort_kernel, out_shape=jax.ShapeDtypeStruct((2 * bands,...  2.08 us
    pallas_call x1, Pallas kernels, shards(): pl.pallas_call(functools.partial(field_kernel, side, chunks), out_shape=j...  1.72 us
  transfers between devices with their start and end apart: 14, of which 4 were waited for; matrix products, arithmetic and copies ran while one was open for 0% of the time, Pallas kernels for 36%

profile of v10, /device:TPU:0, one launch (start us, length us, event | category | flops | bytes accessed | tf_op | source)
XLA Modules:
  0.0 66.9 jit_solution(12710292605695042070)
XLA Ops:
  0.6 0.0 copy-start
  0.6 1.0 %copy-done = bf16[2,1,64,2048]{3,2,1,0:T(8,128)(2,1)S(1)} copy-done((bf16[2,1,64,2048]{3,2,1,0:T(8,128)(2,1)S(1)}, bf16[2,1,64,2048]{3,2,1,0:T(8,128)(2,1)}, u32[]{:S(2)}) %copy-start) | copy-done | bytes 524312
  1.7 0.0 copy-start.1
  1.7 0.7 %copy-done.1 = s32[2048]{0:T(1024)S(1)} copy-done((s32[2048]{0:T(1024)S(1)}, s32[2048]{0:T(1024)}, u32[]{:S(2)}) %copy-start.1) | copy-done | bytes 8216
  2.4 3.8 %sort_waves.1 = (bf16[32,2304]{1,0:T(8,128)(2,1)S(1)}, bf16[32,2304]{1,0:T(8,128)(2,1)S(1)}, bf16[32,2304]{1,0:T(8,128)(2,1)S(1)}, bf16[32,2304]{1,0:T(8,128)(2,...) custom-call(s32[1]{0:T(128)} %bitcast.me_ref, s32[1,2048]{1,0:T(1,128)S(1)} %bitcast.13, ...), custom_call_target="tpu_custom_call" | custom-call | tf_op jit(solution)/shard_map/sort_waves/pallas_call | solution.py:486
  6.2 5.1 %collective-permute-start = (bf16[32,2304]{1,0:T(8,128)(2,1)S(1)}, bf16[32,2304]{1,0:T(8,128)(2,1)S(1)}, u32[]{:S(2)}, u32[]{:S(2)}) collective-permute-start(bf16[32,2304]{1,0:T(8,128)(2,1)S(1)} %get-tuple-element.15), channel_id=1, source_target_pairs={{0,3},{1,2},{2,1},{3,0},{4,7},{5,6},{6,5},{7,4},{8,11},{9,10},{10,... | collective-permute-start | bytes 442376 | tf_op jit(solution)/shard_map/ppermute | solution.py:449
  11.3 0.0 collective-permute-start.1
  11.3 0.6 collective-permute-start.2
  11.9 1.6 %collective-permute-start.3 = (bf16[64,2048]{1,0:T(8,128)(2,1)S(1)}, bf16[64,2048]{1,0:T(8,128)(2,1)S(1)}, u32[]{:S(2)}, u32[]{:S(2)}) collective-permute-start(bf16[64,2048]{1,0:T(8,128)(2,1)S(1)} %get-tuple-element.19.re_ref.own_re), channel_id=1, source_target_pairs={{0,8},{4,12},{8,0},{12,4},{16,24},{20,28},{24,16},{28,20},{1,9},{5... | collective-permute-start | bytes 786440 | tf_op jit(solution)/shard_map/ppermute | solution.py:515
  13.6 1.5 %collective-permute-start.4 = (bf16[64,2048]{1,0:T(8,128)(2,1)S(1)}, bf16[64,2048]{1,0:T(8,128)(2,1)S(1)}, u32[]{:S(2)}, u32[]{:S(2)}) collective-permute-start(bf16[64,2048]{1,0:T(8,128)(2,1)S(1)} %get-tuple-element.20.im_ref.own_im), channel_id=1, source_target_pairs={{0,16},{4,20},{8,24},{12,28},{16,0},{20,4},{24,8},{28,12},{1,17},{... | collective-permute-start | bytes 786440 | tf_op jit(solution)/shard_map/ppermute | solution.py:516
  15.1 0.0 copy-start.3
  15.1 1.6 %copy-done.3 = f32[64,64,128]{2,1,0:T(8,128)S(1)} copy-done((f32[64,64,128]{2,1,0:T(8,128)S(1)}, f32[64,64,128]{2,1,0:T(8,128)}, u32[]{:S(2)}) %copy-start.3) | copy-done | bytes 2097176
  16.7 1.7 %field_pairs.1.refs_4_ = bf16[4,64,2176]{2,1,0:T(8,128)(2,1)S(1)} custom-call(f32[4096,128]{1,0:T(8,128)S(1)} %bitcast.14), custom_call_target="tpu_custom_call" | custom-call | flops 1000000000 | bytes 1000000 | tf_op jit(solution)/shard_map/field_pairs/pallas_call | solution.py:534
  18.4 0.0 collective-permute-done.refs_0_
  18.4 5.4 %collective-permute-done.1.refs_1_ = bf16[32,2304]{1,0:T(8,128)(2,1)S(1)} collective-permute-done((bf16[32,2304]{1,0:T(8,128)(2,1)S(1)}, bf16[32,2304]{1,0:T(8,128)(2,1)S(1)}, u32[]{:S(2)}, u32[]{:S(2)}) %collective-permute-start.1) | collective-permute-done | bytes 147488 | tf_op jit(solution)/shard_map/ppermute | solution.py:449
  23.8 0.0 collective-permute-done.2.refs_2_
  23.8 0.0 copy-start.4
  23.8 0.0 copy-start.5
  23.8 0.0 collective-permute-done.3.refs_8_.xn_ref.xn
  23.8 0.0 collective-permute-done.4.refs_9_.yn_ref.yn
  23.8 0.1 stack.1
  23.9 0.1 collective-permute-start.8
  24.0 0.7 copy-done.4
  24.6 0.0 copy-done.5
  24.6 0.0 copy-start.2
  24.6 18.6 %box_work.1 = (bf16[32,2048]{1,0:T(8,128)(2,1)S(1)}, bf16[32,2048]{1,0:T(8,128)(2,1)S(1)}, bf16[32,2048]{1,0:T(8,128)(2,1)S(1)}, bf16[32,2048]{1,0:T(8,128)(2,1)S(1)}) custom-call(bf16[32,2304]{1,0:T(8,128)(2,1)S(1)} %collective-permute-done.refs_0_, bf16[32,2304]{1,0:T(8,128)(2,1)S(1)} %collective-permute-done.1.refs_1_, ...), custom_call_target="tpu_custom_call" | custom-call | flops 10000000000 | bytes 10000000 | tf_op jit(solution)/shard_map/box_work/pallas_call | solution.py:563
  43.2 0.0 copy-start.6
  43.2 0.6 copy-done.6
  43.9 2.5 %collective-permute-start.5 = (bf16[32,2048]{1,0:T(8,128)(2,1)S(1)}, bf16[32,2048]{1,0:T(8,128)(2,1)}, u32[]{:S(2)}, u32[]{:S(2)}) collective-permute-start(bf16[32,2048]{1,0:T(8,128)(2,1)S(1)} %get-tuple-element.21), channel_id=1, source_target_pairs={{0,3},{1,2},{2,1},{3,0},{4,7},{5,6},{6,5},{7,4},{8,11},{9,10},{10,... | collective-permute-start | bytes 393224 | tf_op jit(solution)/shard_map/ppermute | solution.py:449
  46.4 0.0 collective-permute-start.6
  46.4 1.9 %collective-permute-start.7 = (bf16[32,2048]{1,0:T(8,128)(2,1)S(1)}, bf16[32,2048]{1,0:T(8,128)(2,1)}, u32[]{:S(2)}, u32[]{:S(2)}) collective-permute-start(bf16[32,2048]{1,0:T(8,128)(2,1)S(1)} %get-tuple-element.23), channel_id=1, source_target_pairs={{0,1},{1,0},{2,3},{3,2},{4,5},{5,4},{6,7},{7,6},{8,9},{9,8},{10,11... | collective-permute-start | bytes 393224 | tf_op jit(solution)/shard_map/ppermute | solution.py:449
  48.2 0.0 copy-start.7
  48.2 0.0 collective-permute-done.8.other
  48.2 0.0 copy-done.2
  48.3 0.6 route_partner.1
  48.9 1.6 %collective-permute-start.9 = (bf16[64,2048]{1,0:T(8,128)(2,1)S(1)}, bf16[64,2048]{1,0:T(8,128)(2,1)S(1)}, u32[]{:S(2)}, u32[]{:S(2)}) collective-permute-start(bf16[64,2048]{1,0:T(8,128)(2,1)S(1)} %get-tuple-element.26), channel_id=1, source_target_pairs={{0,16},{4,20},{8,24},{12,28},{16,0},{20,4},{24,8},{28,12},{1,17},{... | collective-permute-start | bytes 786440 | tf_op jit(solution)/shard_map/ppermute | solution.py:605
  50.5 1.5 %collective-permute-start.10 = (bf16[64,2048]{1,0:T(8,128)(2,1)S(1)}, bf16[64,2048]{1,0:T(8,128)(2,1)S(1)}, u32[]{:S(2)}, u32[]{:S(2)}) collective-permute-start(bf16[64,2048]{1,0:T(8,128)(2,1)S(1)} %get-tuple-element.27), channel_id=1, source_target_pairs={{0,8},{4,12},{8,0},{12,4},{16,24},{20,28},{24,16},{28,20},{1,9},{5... | collective-permute-start | bytes 786440 | tf_op jit(solution)/shard_map/ppermute | solution.py:606
  51.9 0.3 collective-permute-done.5.refs_0_
  52.2 4.5 %collective-permute-done.6.refs_1_ = bf16[32,2048]{1,0:T(8,128)(2,1)} collective-permute-done((bf16[32,2048]{1,0:T(8,128)(2,1)S(1)}, bf16[32,2048]{1,0:T(8,128)(2,1)}, u32[]{:S(2)}, u32[]{:S(2)}) %collective-permute-start.6) | collective-permute-done | bytes 131104 | tf_op jit(solution)/shard_map/ppermute | solution.py:449
  56.7 0.0 collective-permute-done.7.refs_2_
  56.7 0.0 copy-done.7
  56.7 1.1 %join.1.y_ref.sorted_ref = bf16[128,2048]{1,0:T(8,128)(2,1)S(1)} custom-call(s32[1]{0:T(128)} %bitcast.me_ref, bf16[32,2048]{1,0:T(8,128)(2,1)} %collective-permute-done.5.refs_0_, bf16[32,2048]{1,0:T(8,128)(2,1)} %collective-permute-done.6.refs_1_, bf16[32,2048]{1,0:T(8,128)(2,1)} %collective-permute-done.7.refs_2_, bf16[32,2048]{1,0:T(8,128)(2,1)S(1)} %copy-done.7), custom_call_target="tpu_custom_call" | custom-call | flops 99999997952 | bytes 1000000 | tf_op jit(solution)/shard_map/join/pallas_call | solution.py:608
  57.9 0.0 collective-permute-done.9.far_re
  57.9 0.0 collective-permute-done.10.far_im
  57.9 1.1 %couple.1 = bf16[2,64,64]{2,1,0:T(8,128)(2,1)S(1)} custom-call(s32[8]{0:T(128)S(1)} %copy-done.2, s32[1]{0:T(128)} %bitcast.6.i_ref, bf16[64,2048]{1,0:T(8,128)(2,1)S(1)} %get-tuple-element.19.re_ref.own_re, bf16[64,2048]{1,0:T(8,128)(2,1)S(1)} %get-tuple-element.20.im_ref.own_im, bf16[64,2048]{1,0:T(8,128)(2,1)S(1)} %collective-permute-done.3.refs_8_.xn_ref.xn, ...), custom_call_target="tpu_custom_call" | custom-call | tf_op jit(solution)/shard_map/couple/pallas_call | solution.py:619
  59.0 2.4 %collective-permute-start.11 = (bf16[2,64,64]{2,1,0:T(8,128)(2,1)S(1)}, bf16[2,64,64]{2,1,0:T(8,128)(2,1)S(1)}, u32[]{:S(2)}, u32[]{:S(2)}) collective-permute-start(bf16[2,64,64]{2,1,0:T(8,128)(2,1)S(1)} %couple.1), channel_id=1, source_target_pairs={{0,3},{1,2},{2,1},{3,0},{4,7},{5,6},{6,5},{7,4},{8,11},{9,10},{10,... | collective-permute-start | bytes 49160 | tf_op jit(solution)/shard_map/ppermute | solution.py:637
  61.4 0.0 collective-permute-start.12
  61.4 2.0 %collective-permute-start.13 = (bf16[2,64,64]{2,1,0:T(8,128)(2,1)S(1)}, bf16[2,64,64]{2,1,0:T(8,128)(2,1)S(1)}, u32[]{:S(2)}, u32[]{:S(2)}) collective-permute-start(bf16[2,64,64]{2,1,0:T(8,128)(2,1)S(1)} %couple.1), channel_id=1, source_target_pairs={{0,1},{1,0},{2,3},{3,2},{4,5},{5,4},{6,7},{7,6},{8,9},{9,8},{10,11... | collective-permute-start | bytes 49160 | tf_op jit(solution)/shard_map/ppermute | solution.py:637
  63.4 2.1 %unsort.1 = bf16[128,2048]{1,0:T(8,128)(2,1)} custom-call(bf16[128,2048]{1,0:T(8,128)(2,1)S(1)} %join.1.y_ref.sorted_ref, s32[1,2048]{1,0:T(1,128)S(1)} %get-tuple-element.25.rank_ref), custom_call_target="tpu_custom_call" | custom-call | flops 1000000000 | bytes 10000000 | tf_op jit(solution)/shard_map/unsort/pallas_call | solution.py:638
  65.5 0.0 collective-permute-done.11
  65.5 0.7 %collective-permute-done.12 = bf16[2,64,64]{2,1,0:T(8,128)(2,1)S(1)} collective-permute-done((bf16[2,64,64]{2,1,0:T(8,128)(2,1)S(1)}, bf16[2,64,64]{2,1,0:T(8,128)(2,1)S(1)}, u32[]{:S(2)}, u32[]{:S(2)}) %collective-permute-start.12) | collective-permute-done | bytes 16416 | tf_op jit(solution)/shard_map/ppermute | solution.py:637
  66.2 0.0 collective-permute-done.13
  66.3 0.7 %multiply_bitcast_fusion = f32[2,1,64,64]{3,2,1,0:T(8,128)} fusion(bf16[2,64,64]{2,1,0:T(8,128)(2,1)S(1)} %collective-permute-done.11, bf16[2,64,64]{2,1,0:T(8,128)(2,1)S(1)} %collective-permute-done.12, bf16[2,64,64]{2,1,0:T(8,128)(2,1)S(1)} %collective-permute-done.13, bf16[2,64,64]{2,1,0:T(8,128)(2,1)S(1)} %couple.1, pred[]{:T(512)S(6)} %eq.47, pred[]{:T(512)S(6)} %eq.46, ...), kind=kLoop, calls=%fused_computation | loop fusion | flops 163840 | bytes 98316
  (1 shorter events, 0.0 us)
Async XLA Ops:
  0.6 1.0 %copy-start = (bf16[2,1,64,2048]{3,2,1,0:T(8,128)(2,1)S(1)}, bf16[2,1,64,2048]{3,2,1,0:T(8,128)(2,1)}, u32[]{:S(2)}) copy-start(bf16[2,1,64,2048]{3,2,1,0:T(8,128)(2,1)} %param.6) | copy-start | bytes 1572868
  1.7 0.7 %copy-start.1 = (s32[2048]{0:T(1024)S(1)}, s32[2048]{0:T(1024)}, u32[]{:S(2)}) copy-start(s32[2048]{0:T(1024)} %param.7) | copy-start | bytes 24580
  6.2 12.2 %collective-permute-start = (bf16[32,2304]{1,0:T(8,128)(2,1)S(1)}, bf16[32,2304]{1,0:T(8,128)(2,1)S(1)}, u32[]{:S(2)}, u32[]{:S(2)}) collective-permute-start(bf16[32,2304]{1,0:T(8,128)(2,1)S(1)} %get-tuple-element.15), channel_id=1, source_target_pairs={{0,3},{1,2},{2,1},{3,0},{4,7},{5,6},{6,5},{7,4},{8,11},{9,10},{10,... | collective-permute-start | bytes 442376 | tf_op jit(solution)/shard_map/ppermute | solution.py:449
  11.3 12.5 %collective-permute-start.1 = (bf16[32,2304]{1,0:T(8,128)(2,1)S(1)}, bf16[32,2304]{1,0:T(8,128)(2,1)S(1)}, u32[]{:S(2)}, u32[]{:S(2)}) collective-permute-start(bf16[32,2304]{1,0:T(8,128)(2,1)S(1)} %get-tuple-element.16), channel_id=1, source_target_pairs={{0,2},{1,3},{2,0},{3,1},{4,6},{5,7},{6,4},{7,5},{8,10},{9,11},{10,... | collective-permute-start | bytes 442376 | tf_op jit(solution)/shard_map/ppermute | solution.py:449
  11.3 12.5 %collective-permute-start.2 = (bf16[32,2304]{1,0:T(8,128)(2,1)S(1)}, bf16[32,2304]{1,0:T(8,128)(2,1)S(1)}, u32[]{:S(2)}, u32[]{:S(2)}) collective-permute-start(bf16[32,2304]{1,0:T(8,128)(2,1)S(1)} %get-tuple-element.17), channel_id=1, source_target_pairs={{0,1},{1,0},{2,3},{3,2},{4,5},{5,4},{6,7},{7,6},{8,9},{9,8},{10,11... | collective-permute-start | bytes 442376 | tf_op jit(solution)/shard_map/ppermute | solution.py:449
  11.9 11.9 %collective-permute-start.3 = (bf16[64,2048]{1,0:T(8,128)(2,1)S(1)}, bf16[64,2048]{1,0:T(8,128)(2,1)S(1)}, u32[]{:S(2)}, u32[]{:S(2)}) collective-permute-start(bf16[64,2048]{1,0:T(8,128)(2,1)S(1)} %get-tuple-element.19.re_ref.own_re), channel_id=1, source_target_pairs={{0,8},{4,12},{8,0},{12,4},{16,24},{20,28},{24,16},{28,20},{1,9},{5... | collective-permute-start | bytes 786440 | tf_op jit(solution)/shard_map/ppermute | solution.py:515
  13.6 10.2 %collective-permute-start.4 = (bf16[64,2048]{1,0:T(8,128)(2,1)S(1)}, bf16[64,2048]{1,0:T(8,128)(2,1)S(1)}, u32[]{:S(2)}, u32[]{:S(2)}) collective-permute-start(bf16[64,2048]{1,0:T(8,128)(2,1)S(1)} %get-tuple-element.20.im_ref.own_im), channel_id=1, source_target_pairs={{0,16},{4,20},{8,24},{12,28},{16,0},{20,4},{24,8},{28,12},{1,17},{... | collective-permute-start | bytes 786440 | tf_op jit(solution)/shard_map/ppermute | solution.py:516
  15.1 1.6 %copy-start.3 = (f32[64,64,128]{2,1,0:T(8,128)S(1)}, f32[64,64,128]{2,1,0:T(8,128)}, u32[]{:S(2)}) copy-start(f32[64,64,128]{2,1,0:T(8,128)} %param.9) | copy-start | bytes 6291460
  23.8 0.8 %copy-start.4 = (bf16[2,128,128]{2,1,0:T(8,128)(2,1)S(1)}, bf16[2,128,128]{2,1,0:T(8,128)(2,1)}, u32[]{:S(2)}) copy-start(bf16[2,128,128]{2,1,0:T(8,128)(2,1)} %constant.23.clone.refs_6_) | copy-start | bytes 196612
  23.8 0.8 %copy-start.5 = (bf16[64,256]{1,0:T(8,128)(2,1)S(1)}, bf16[64,256]{1,0:T(8,128)(2,1)}, u32[]{:S(2)}) copy-start(bf16[64,256]{1,0:T(8,128)(2,1)} %constant.22.clone.refs_5_) | copy-start | bytes 98308
  23.9 24.4 %collective-permute-start.8 = (bf16[256,2048]{1,0:T(8,128)(2,1)S(1)}, bf16[256,2048]{1,0:T(8,128)(2,1)S(1)}, u32[]{:S(2)}, u32[]{:S(2)}) collective-permute-start(bf16[256,2048]{1,0:T(8,128)(2,1)S(1)} %stack.1), channel_id=1, source_target_pairs={{0,4},{4,0},{8,12},{12,8},{16,20},{20,16},{24,28},{28,24},{1,5},{5... | collective-permute-start | bytes 3145736 | tf_op jit(solution)/shard_map/ppermute | solution.py:525
  24.6 23.6 %copy-start.2 = (s32[8]{0:T(128)S(1)}, s32[8]{0:T(128)}, u32[]{:S(2)}) copy-start(s32[8]{0:T(128)} %order_ref.3) | copy-start | bytes 100
  43.2 0.7 copy-start.6
  43.9 8.3 %collective-permute-start.5 = (bf16[32,2048]{1,0:T(8,128)(2,1)S(1)}, bf16[32,2048]{1,0:T(8,128)(2,1)}, u32[]{:S(2)}, u32[]{:S(2)}) collective-permute-start(bf16[32,2048]{1,0:T(8,128)(2,1)S(1)} %get-tuple-element.21), channel_id=1, source_target_pairs={{0,3},{1,2},{2,1},{3,0},{4,7},{5,6},{6,5},{7,4},{8,11},{9,10},{10,... | collective-permute-start | bytes 393224 | tf_op jit(solution)/shard_map/ppermute | solution.py:449
  46.4 10.4 %collective-permute-start.6 = (bf16[32,2048]{1,0:T(8,128)(2,1)S(1)}, bf16[32,2048]{1,0:T(8,128)(2,1)}, u32[]{:S(2)}, u32[]{:S(2)}) collective-permute-start(bf16[32,2048]{1,0:T(8,128)(2,1)S(1)} %get-tuple-element.22), channel_id=1, source_target_pairs={{0,2},{1,3},{2,0},{3,1},{4,6},{5,7},{6,4},{7,5},{8,10},{9,11},{10,... | collective-permute-start | bytes 393224 | tf_op jit(solution)/shard_map/ppermute | solution.py:449
  46.4 10.4 %collective-permute-start.7 = (bf16[32,2048]{1,0:T(8,128)(2,1)S(1)}, bf16[32,2048]{1,0:T(8,128)(2,1)}, u32[]{:S(2)}, u32[]{:S(2)}) collective-permute-start(bf16[32,2048]{1,0:T(8,128)(2,1)S(1)} %get-tuple-element.23), channel_id=1, source_target_pairs={{0,1},{1,0},{2,3},{3,2},{4,5},{5,4},{6,7},{7,6},{8,9},{9,8},{10,11... | collective-permute-start | bytes 393224 | tf_op jit(solution)/shard_map/ppermute | solution.py:449
  48.2 8.5 %copy-start.7 = (bf16[32,2048]{1,0:T(8,128)(2,1)S(1)}, bf16[32,2048]{1,0:T(8,128)(2,1)}, u32[]{:S(2)}) copy-start(bf16[32,2048]{1,0:T(8,128)(2,1)} %copy-done.6) | copy-start | bytes 393220
  48.9 9.0 %collective-permute-start.9 = (bf16[64,2048]{1,0:T(8,128)(2,1)S(1)}, bf16[64,2048]{1,0:T(8,128)(2,1)S(1)}, u32[]{:S(2)}, u32[]{:S(2)}) collective-permute-start(bf16[64,2048]{1,0:T(8,128)(2,1)S(1)} %get-tuple-element.26), channel_id=1, source_target_pairs={{0,16},{4,20},{8,24},{12,28},{16,0},{20,4},{24,8},{28,12},{1,17},{... | collective-permute-start | bytes 786440 | tf_op jit(solution)/shard_map/ppermute | solution.py:605
  50.5 7.4 %collective-permute-start.10 = (bf16[64,2048]{1,0:T(8,128)(2,1)S(1)}, bf16[64,2048]{1,0:T(8,128)(2,1)S(1)}, u32[]{:S(2)}, u32[]{:S(2)}) collective-permute-start(bf16[64,2048]{1,0:T(8,128)(2,1)S(1)} %get-tuple-element.27), channel_id=1, source_target_pairs={{0,8},{4,12},{8,0},{12,4},{16,24},{20,28},{24,16},{28,20},{1,9},{5... | collective-permute-start | bytes 786440 | tf_op jit(solution)/shard_map/ppermute | solution.py:606
  59.0 6.5 %collective-permute-start.11 = (bf16[2,64,64]{2,1,0:T(8,128)(2,1)S(1)}, bf16[2,64,64]{2,1,0:T(8,128)(2,1)S(1)}, u32[]{:S(2)}, u32[]{:S(2)}) collective-permute-start(bf16[2,64,64]{2,1,0:T(8,128)(2,1)S(1)} %couple.1), channel_id=1, source_target_pairs={{0,3},{1,2},{2,1},{3,0},{4,7},{5,6},{6,5},{7,4},{8,11},{9,10},{10,... | collective-permute-start | bytes 49160 | tf_op jit(solution)/shard_map/ppermute | solution.py:637
  61.4 4.8 %collective-permute-start.12 = (bf16[2,64,64]{2,1,0:T(8,128)(2,1)S(1)}, bf16[2,64,64]{2,1,0:T(8,128)(2,1)S(1)}, u32[]{:S(2)}, u32[]{:S(2)}) collective-permute-start(bf16[2,64,64]{2,1,0:T(8,128)(2,1)S(1)} %couple.1), channel_id=1, source_target_pairs={{0,2},{1,3},{2,0},{3,1},{4,6},{5,7},{6,4},{7,5},{8,10},{9,11},{10,... | collective-permute-start | bytes 49160 | tf_op jit(solution)/shard_map/ppermute | solution.py:637
  61.4 4.8 %collective-permute-start.13 = (bf16[2,64,64]{2,1,0:T(8,128)(2,1)S(1)}, bf16[2,64,64]{2,1,0:T(8,128)(2,1)S(1)}, u32[]{:S(2)}, u32[]{:S(2)}) collective-permute-start(bf16[2,64,64]{2,1,0:T(8,128)(2,1)S(1)} %couple.1), channel_id=1, source_target_pairs={{0,1},{1,0},{2,3},{3,2},{4,5},{5,4},{6,7},{7,6},{8,9},{9,8},{10,11... | collective-permute-start | bytes 49160 | tf_op jit(solution)/shard_map/ppermute | solution.py:637

commit v11 on v10

--- a/solution.py
+++ b/solution.py
@@ -11,12 +11,14 @@
 
 STICK_DEV = 64
 LANES = 128
-UNROLL = 16
+UNROLL = 32
 BF16 = jnp.bfloat16
 F32 = jnp.float32
 VMEM_LIMIT = 24 * 1024 * 1024
+SMALL_LIMIT = 8 * 1024 * 1024
 SORT_LIMIT = 24 * 1024 * 1024
 JOIN_COST = 10**11
+RANK_COST = 5 * 10**9
 MARK_COST = 3*10**9
 BOX_COST = 10**10
 
@@ -76,17 +78,11 @@
     return xh, yh, ch, slot, cells, rank.astype(jnp.int32)
 
 
-def sort_kernel(side, groups, me_ref, idx_ref, x_hbm, *refs):
-    outs, (re_ref, im_ref, rank_ref, x_ref, wide, pieces, sem) = refs[:groups], refs[groups:]
-    fetch = pltpu.make_async_copy(x_hbm, x_ref, sem)
-    fetch.start()
+def rank_kernel(side, idx_ref, rank_ref, extra_ref):
     xh, yh, ch, slot_of, cells, rank = locate(idx_ref[...], side)
     rank_ref[...] = rank
     waves = rank.shape[1]
-    both = x_ref.shape[0]
-    bands = both // 2
-    share = bands // groups
-    rows = 2 * share
+    rows = extra_ref.shape[0]
     cells = jnp.concatenate([cells[i : i + rows] for i in range(0, side, rows)], axis=1)
     tiles = waves // LANES
     in_tile = one_hot(rank & (LANES - 1), LANES)
@@ -99,11 +95,19 @@
         lines.append(jnp.zeros((spare, LANES), F32))
     lines = jnp.concatenate(lines, axis=0)
     lines = [lines[i : i + rows] for i in range(0, lines.shape[0], rows)]
-    extra = jnp.concatenate([cells] + lines, axis=1).astype(BF16)
+    extra_ref[...] = jnp.concatenate([cells] + lines, axis=1).astype(BF16)
+
+
+def sort_kernel(side, groups, me_ref, rank_ref, extra_ref, x_ref, *refs):
+    outs, (re_ref, im_ref, wide, pieces) = refs[:groups], refs[groups:]
+    rank = rank_ref[...]
+    waves = rank.shape[1]
+    both = x_ref.shape[0]
+    bands = both // 2
+    share = bands // groups
     low = one_hot(rank & 255, 256)
-    for shift in range(groups):
-        outs[shift][:, waves:] = extra
-    fetch.wait()
+    for out in outs:
+        out[:, waves:] = extra_ref[...]
     parts = waves // 256
     step = 2 if parts % 2 == 0 else 1
     for first in range(0, parts, step):
@@ -123,7 +127,9 @@
                 outs[shift][:, here] = jnp.concatenate([re, im], axis=0).astype(BF16)
 
 
-def field_kernel(side, chunks, pot_ref, field_ref):
+def field_kernel(side, chunks, pot_ref, cs_ref, wz_ref, field_ref, cs_out, wz_out):
+    cs_out[...] = cs_ref[...]
+    wz_out[...] = wz_ref[...]
     half = side // 2
     lane = lax.broadcasted_iota(jnp.int32, (side, LANES), 1)
     first = lane < side
@@ -192,16 +198,18 @@
     choose(order_ref[i ^ 2] ^ i, 5, near_im, im_ref)
 
 
-def couple_routed_kernel(
-    order_ref, i_ref, own_re, own_im, xn, yn, other, far_re, far_im, sorted_ref, g_ref, partner,
-):
-    i = i_ref[0]
+def couple_routed_kernel(groups, me_ref, order_ref, i_ref, *refs):
+    y_refs, refs = refs[:groups], refs[groups:]
+    own_re, own_im, xn, yn, other, far_re, far_im, _, sorted_ref, g_ref, partner = refs
+    join_kernel(groups, me_ref, *y_refs, sorted_ref)
     half = own_re.shape[0]
-    code = order_ref[i] ^ i
+    code = order_ref[i_ref[0]] ^ i_ref[0]
+    near_re, near_im = seen(own_re, own_im, xn, yn, other)
     re_ref, im_ref = partner.at[:half], partner.at[half:]
-    near_re, near_im = seen(own_re, own_im, xn, yn, other)
-    choose(code, 7, {**near_re, **{4 + name: far_re for name in near_re}}, re_ref)
-    choose(code, 7, {**near_im, **{2 + name: far_im for name in near_im}}, im_ref)
+    choose(code, 7, near_re, re_ref)
+    choose(code, 4, {4: far_re}, re_ref)
+    choose(code, 7, near_im, im_ref)
+    choose(code, 2, {2: far_im}, im_ref)
     couple_kernel(partner, sorted_ref, g_ref)
 
 
@@ -483,28 +491,31 @@
     packed = waves + side * STICK_DEV // rows + -(-(tiles + 8) // rows) * LANES
     scalars, blocks = whole(pltpu.SMEM), [whole()] * fft_count
 
-    *ordered, own_re, own_im, rank = pl.pallas_call(
+    rank, extra = pl.pallas_call(
+        functools.partial(rank_kernel, side),
+        out_shape=(
+            jax.ShapeDtypeStruct((1, waves), jnp.int32),
+            jax.ShapeDtypeStruct((rows, packed - waves), BF16),
+        ),
+        in_specs=[whole()],
+        out_specs=(whole(), whole()),
+        compiler_params=params(SORT_LIMIT),
+        cost_estimate=pl.CostEstimate(flops=RANK_COST, bytes_accessed=10**4, transcendentals=0),
+        name="rank_waves",
+    )(box_index.reshape(1, waves))
+    *ordered, own_re, own_im = pl.pallas_call(
         functools.partial(sort_kernel, side, fft_count),
-        out_shape=[
-            jax.ShapeDtypeStruct((rows, packed), BF16)
-            for _ in range(fft_count)
-        ]
-        + [
-            jax.ShapeDtypeStruct((bands, waves), BF16),
-            jax.ShapeDtypeStruct((bands, waves), BF16),
-            jax.ShapeDtypeStruct((1, waves), jnp.int32),
-        ],
-        in_specs=[scalars, whole(), whole(pltpu.HBM)],
-        out_specs=blocks + [whole()] * 3,
+        out_shape=[jax.ShapeDtypeStruct((rows, packed), BF16)] * fft_count
+        + [jax.ShapeDtypeStruct((bands, waves), BF16)] * 2,
+        in_specs=[scalars, whole(), whole(), whole()],
+        out_specs=blocks + [whole()] * 2,
         scratch_shapes=[
-            pltpu.VMEM((2 * bands, waves), BF16),
             pltpu.VMEM((waves // 256 * 2 * bands, waves), BF16),
             pltpu.VMEM((waves // 256 * 2 * bands, 256), F32),
-            pltpu.SemaphoreType.DMA,
         ],
         compiler_params=params(SORT_LIMIT),
         name="sort_waves",
-    )(me_row, box_index.reshape(1, waves), coeffs)
+    )(me_row, rank, extra, coeffs)
     moved = exchange(ordered, pairs)
 
     routed = pool_count == 8
@@ -519,7 +530,7 @@
             out_shape=jax.ShapeDtypeStruct((4 * bands, waves), BF16),
             in_specs=[whole()] * 4,
             out_specs=whole(),
-            compiler_params=params(),
+            compiler_params=params(SMALL_LIMIT),
             name="stack",
         )(own_re, own_im, xn, yn)
         other = lax.ppermute(stacked, "pool", swaps[1])
@@ -531,22 +542,26 @@
         )
         near = []
 
-    field = pl.pallas_call(
+    field, cs, wz = pl.pallas_call(
         functools.partial(field_kernel, side, chunks),
-        out_shape=jax.ShapeDtypeStruct((4, side, chunks * LANES), BF16),
-        in_specs=[whole()],
-        out_specs=whole(),
+        out_shape=(
+            jax.ShapeDtypeStruct((4, side, chunks * LANES), BF16),
+            jax.ShapeDtypeStruct(cs.shape, BF16),
+            jax.ShapeDtypeStruct(wz.shape, BF16),
+        ),
+        in_specs=[whole()] * 3,
+        out_specs=(whole(),) * 3,
         compiler_params=params(),
         cost_estimate=pl.CostEstimate(flops=10**9, bytes_accessed=10**6, transcendentals=0),
         name="field_pairs",
-    )(potential.reshape(side * side, 2 * side))
+    )(potential.reshape(side * side, 2 * side), cs, wz)
 
     mark = pl.pallas_call(
         mark_kernel,
         out_shape=jax.ShapeDtypeStruct((8, LANES), F32),
         in_specs=[whole(pl.ANY)] * (fft_count - 1),
         out_specs=whole(),
-        compiler_params=params(),
+        compiler_params=params(SMALL_LIMIT),
         cost_estimate=pl.CostEstimate(flops=MARK_COST, bytes_accessed=10**4, transcendentals=0),
         name="mark",
     )(*moved[:0:-1])
@@ -599,39 +614,49 @@
             out_shape=(half_rows, half_rows),
             in_specs=[scalars] * 2 + [whole()] * len(near),
             out_specs=(whole(), whole()),
-            compiler_params=params(),
+            compiler_params=params(SMALL_LIMIT),
             name="route_partner",
         )(partner_pool, pool_row, *near)
         far_re = lax.ppermute(far_re, "pool", swaps[4])
         far_im = lax.ppermute(far_im, "pool", swaps[2])
 
-    sorted_response = pl.pallas_call(
-        functools.partial(join_kernel, fft_count),
-        out_shape=jax.ShapeDtypeStruct((2 * bands, waves), BF16),
-        in_specs=[scalars] + blocks,
-        out_specs=whole(),
-        compiler_params=params(),
-        cost_estimate=pl.CostEstimate(flops=JOIN_COST, bytes_accessed=10**6, transcendentals=0),
-        name="join",
-    )(me_row, *returned[::-1])
     sums_shape = jax.ShapeDtypeStruct((2, bands, bands), BF16)
+    sorted_shape = jax.ShapeDtypeStruct((2 * bands, waves), BF16)
+    blocks_home = [returned[s] for s in range(fft_count - 1, -1, -1)]
     if routed:
-        sums = pl.pallas_call(
-            couple_routed_kernel,
-            out_shape=sums_shape,
-            in_specs=[scalars] * 2 + [whole()] * (len(near) + 3),
+        home = pl.pallas_call(
+            mark_kernel,
+            out_shape=jax.ShapeDtypeStruct((8, LANES), F32),
+            in_specs=[whole(pl.ANY)] * (fft_count - 1),
             out_specs=whole(),
+            compiler_params=params(SMALL_LIMIT),
+            cost_estimate=pl.CostEstimate(flops=JOIN_COST, bytes_accessed=10**4, transcendentals=0),
+            name="mark_home",
+        )(*blocks_home[:-1])
+        sorted_response, sums = pl.pallas_call(
+            functools.partial(couple_routed_kernel, fft_count),
+            out_shape=(sorted_shape, sums_shape),
+            in_specs=[scalars] * 3 + blocks + [whole()] * (len(near) + 2) + [whole(pl.ANY)],
+            out_specs=(whole(), whole()),
             scratch_shapes=[pltpu.VMEM((2 * bands, waves), BF16)],
-            compiler_params=params(),
+            compiler_params=params(SMALL_LIMIT),
             name="couple",
-        )(partner_pool, pool_row, *near, far_re, far_im, sorted_response)
+        )(me_row, partner_pool, pool_row, *blocks_home, *near, far_re, far_im, home)
     else:
+        sorted_response = pl.pallas_call(
+            functools.partial(join_kernel, fft_count),
+            out_shape=sorted_shape,
+            in_specs=[scalars] + blocks,
+            out_specs=whole(),
+            compiler_params=params(SMALL_LIMIT),
+            name="join",
+        )(me_row, *blocks_home)
         sums = pl.pallas_call(
             couple_kernel,
             out_shape=sums_shape,
             in_specs=[whole(), whole()],
             out_specs=whole(),
-            compiler_params=params(),
+            compiler_params=params(SMALL_LIMIT),
             name="couple",
         )(partner, sorted_response)
     shares = [sums] + [lax.ppermute(sums, "fft", pairs[s]) for s in range(1, fft_count)]

time: 67.2 us -> 65.7 us (0.978)
  local copies, waits for them, and re-layouts: 4.64 us -> 0.71 us
  waiting for transfers between devices: 10.9 us -> 13.8 us
    unnamed x16 -> x12, local copies, waits for them, and re-layouts: 4.64 us -> 0.71 us
    pallas_call x1, Pallas kernels: 3.79 us -> 1.38 us  [shards(): pl.pallas_call(functools.partial(sort_kernel, side, fft_count), out_shape...]
    ppermute x6, waiting for transfers between devices: 10.2 us -> 12.5 us  [exchange(): moved[s] = lax.ppermute(blocks[s], 'fft', pairs[s])]
    pallas_call x3, Pallas kernels: 3.94 us -> 5.4 us  [the longest x1 2.15 us: shards(): pl.pallas_call(functools.partial(rank_kernel, side), out_shape=(jax.Shape...]
  transfers between devices with their start and end apart: 14 -> 14, of which waited for: 4 -> 5; matrix products, arithmetic and copies ran while one was open for 0% -> 0% of each run, Pallas kernels for 36% -> 36%
where the time goes in v11:
time: 65.7 us; the launch traced here: 65.5 us
  Pallas kernels  28.5 us (43%)
  starting transfers between devices  20.9 us (32%)
  waiting for transfers between devices  13.8 us (21%)
  between operations  0.74 us (1%)
  local copies, waits for them, and re-layouts  0.71 us (1%)
  other arithmetic  0.67 us (1%)
    pallas_call x1, Pallas kernels, shards(): pl.pallas_call(functools.partial(box_kernel, side, chunks, team, waves, f...  19 us
    ppermute x6, waiting for transfers between devices, exchange(): moved[s] = lax.ppermute(blocks[s], 'fft', pairs[s])  12.5 us
    ppermute x6, starting transfers between devices, exchange(): moved[s] = lax.ppermute(blocks[s], 'fft', pairs[s])  10.2 us
    ppermute x3, starting transfers between devices, shards(): lax.ppermute(sums, 'fft', pairs[s])  4.45 us
    pallas_call x1, Pallas kernels, shards(): pl.pallas_call(functools.partial(rank_kernel, side), out_shape=(jax.Shape...  2.15 us
    pallas_call x1, Pallas kernels, shards(): pl.pallas_call(unsort_kernel, out_shape=jax.ShapeDtypeStruct((2 * bands,...  2.08 us
    pallas_call x1, Pallas kernels, shards(): pl.pallas_call(functools.partial(field_kernel, side, chunks), out_shape=(...  1.73 us
    ppermute x1, starting transfers between devices, shards(): xn = lax.ppermute(own_re, 'pool', swaps[2])  1.63 us
  transfers between devices with their start and end apart: 14, of which 5 were waited for; matrix products, arithmetic and copies ran while one was open for 0% of the time, Pallas kernels for 36%

profile of v11, /device:TPU:0, one launch (start us, length us, event | category | flops | bytes accessed | tf_op | source)
XLA Modules:
  0.0 65.5 jit_solution(6018527318712135384)
XLA Ops:
  0.6 0.0 copy-start.3
  0.6 0.7 %copy-done.3 = s32[2048]{0:T(1024)S(1)} copy-done((s32[2048]{0:T(1024)S(1)}, s32[2048]{0:T(1024)}, u32[]{:S(2)}) %copy-start.3) | copy-done | bytes 8216
  1.3 0.0 copy-start
  1.3 0.0 copy-start.2
  1.3 0.0 copy-start.4
  1.3 0.0 copy-start.5
  1.3 2.2 %rank_waves.1 = (s32[1,2048]{1,0:T(1,128)S(1)}, bf16[32,256]{1,0:T(8,128)(2,1)S(1)}) custom-call(s32[1,2048]{1,0:T(1,128)S(1)} %bitcast.14), custom_call_target="tpu_custom_call" | custom-call | flops 5000000000 | bytes 10000 | tf_op jit(solution)/shard_map/rank_waves/pallas_call | solution.py:494
  3.5 0.0 copy-done
  3.5 1.4 %sort_waves.1 = (bf16[32,2304]{1,0:T(8,128)(2,1)S(1)}, bf16[32,2304]{1,0:T(8,128)(2,1)S(1)}, bf16[32,2304]{1,0:T(8,128)(2,1)S(1)}, bf16[32,2304]{1,0:T(8,128)(2,...) custom-call(s32[1]{0:T(128)} %bitcast.me_ref, s32[1,2048]{1,0:T(1,128)S(1)} %get-tuple-element.21.rank_ref, ...), custom_call_target="tpu_custom_call" | custom-call | tf_op jit(solution)/shard_map/sort_waves/pallas_call | solution.py:506
  4.9 5.1 %collective-permute-start = (bf16[32,2304]{1,0:T(8,128)(2,1)S(1)}, bf16[32,2304]{1,0:T(8,128)(2,1)S(1)}, u32[]{:S(2)}, u32[]{:S(2)}) collective-permute-start(bf16[32,2304]{1,0:T(8,128)(2,1)S(1)} %get-tuple-element.23), channel_id=1, source_target_pairs={{0,3},{1,2},{2,1},{3,0},{4,7},{5,6},{6,5},{7,4},{8,11},{9,10},{10,... | collective-permute-start | bytes 442376 | tf_op jit(solution)/shard_map/ppermute | solution.py:457
  10.0 0.0 collective-permute-start.1
  10.0 0.6 collective-permute-start.2
  10.7 1.6 %collective-permute-start.3 = (bf16[64,2048]{1,0:T(8,128)(2,1)S(1)}, bf16[64,2048]{1,0:T(8,128)(2,1)S(1)}, u32[]{:S(2)}, u32[]{:S(2)}) collective-permute-start(bf16[64,2048]{1,0:T(8,128)(2,1)S(1)} %get-tuple-element.30.re_ref.own_re.refs_4_), channel_id=1, source_target_pairs={{0,8},{4,12},{8,0},{12,4},{16,24},{20,28},{24,16},{28,20},{1,9},{5... | collective-permute-start | bytes 786440 | tf_op jit(solution)/shard_map/ppermute | solution.py:526
  12.3 1.5 %collective-permute-start.4 = (bf16[64,2048]{1,0:T(8,128)(2,1)S(1)}, bf16[64,2048]{1,0:T(8,128)(2,1)S(1)}, u32[]{:S(2)}, u32[]{:S(2)}) collective-permute-start(bf16[64,2048]{1,0:T(8,128)(2,1)S(1)} %get-tuple-element.31.im_ref.own_im.refs_5_), channel_id=1, source_target_pairs={{0,16},{4,20},{8,24},{12,28},{16,0},{20,4},{24,8},{28,12},{1,17},{... | collective-permute-start | bytes 786440 | tf_op jit(solution)/shard_map/ppermute | solution.py:527
  13.8 0.0 copy-done.2
  13.8 0.0 copy-done.4
  13.8 0.0 copy-done.5
  13.8 1.7 %field_pairs.1 = (bf16[4,64,2176]{2,1,0:T(8,128)(2,1)S(1)}, bf16[64,256]{1,0:T(8,128)(2,1)S(1)}, bf16[2,128,128]{2,1,0:T(8,128)(2,1)S(1)}) custom-call(f32[4096,128]{1,0:T(8,128)S(1)} %bitcast.13, bf16[64,256]{1,0:T(8,128)(2,1)S(1)} %copy-done.5, bf16[2,128,128]{2,1,0:T(8,128)(2,1)S(1)} %copy-done.4), custom_call_target="tpu_custom_call" | custom-call | flops 1000000000 | bytes 1000000 | tf_op jit(solution)/shard_map/field_pairs/pallas_call | solution.py:545
  15.5 0.0 collective-permute-done.refs_0_
  15.6 6.9 %collective-permute-done.1.refs_1_ = bf16[32,2304]{1,0:T(8,128)(2,1)S(1)} collective-permute-done((bf16[32,2304]{1,0:T(8,128)(2,1)S(1)}, bf16[32,2304]{1,0:T(8,128)(2,1)S(1)}, u32[]{:S(2)}, u32[]{:S(2)}) %collective-permute-start.1) | collective-permute-done | bytes 147488 | tf_op jit(solution)/shard_map/ppermute | solution.py:457
  22.5 0.0 collective-permute-done.2.refs_2_
  22.5 0.0 collective-permute-done.3.refs_8_.xn_ref.xn.refs_6_
  22.5 0.0 collective-permute-done.4.refs_9_.yn_ref.yn.refs_7_
  22.5 0.1 stack.1
  22.6 0.1 collective-permute-start.8
  22.7 0.0 copy-start.1
  22.7 19.0 %box_work.1 = (bf16[32,2048]{1,0:T(8,128)(2,1)S(1)}, bf16[32,2048]{1,0:T(8,128)(2,1)}, bf16[32,2048]{1,0:T(8,128)(2,1)}, bf16[32,2048]{1,0:T(8,128)(2,1)}) custom-call(bf16[32,2304]{1,0:T(8,128)(2,1)S(1)} %collective-permute-done.refs_0_, bf16[32,2304]{1,0:T(8,128)(2,1)S(1)} %collective-permute-done.1.refs_1_, ...), custom_call_target="tpu_custom_call" | custom-call | flops 10000000000 | bytes 10000000 | tf_op jit(solution)/shard_map/box_work/pallas_call | solution.py:578
  41.7 2.6 %collective-permute-start.5 = (bf16[32,2048]{1,0:T(8,128)(2,1)}, bf16[32,2048]{1,0:T(8,128)(2,1)S(1)}, u32[]{:S(2)}, u32[]{:S(2)}) collective-permute-start(bf16[32,2048]{1,0:T(8,128)(2,1)} %get-tuple-element.32), channel_id=1, source_target_pairs={{0,3},{1,2},{2,1},{3,0},{4,7},{5,6},{6,5},{7,4},{8,11},{9,10},{10,... | collective-permute-start | bytes 393224 | tf_op jit(solution)/shard_map/ppermute | solution.py:457
  44.2 0.0 collective-permute-start.6
  44.2 1.9 %collective-permute-start.7 = (bf16[32,2048]{1,0:T(8,128)(2,1)}, bf16[32,2048]{1,0:T(8,128)(2,1)}, u32[]{:S(2)}, u32[]{:S(2)}) collective-permute-start(bf16[32,2048]{1,0:T(8,128)(2,1)} %get-tuple-element.34), channel_id=1, source_target_pairs={{0,1},{1,0},{2,3},{3,2},{4,5},{5,4},{6,7},{7,6},{8,9},{9,8},{10,11... | collective-permute-start | bytes 393224 | tf_op jit(solution)/shard_map/ppermute | solution.py:457
  46.1 0.0 collective-permute-done.8.other.refs_8_
  46.1 0.0 copy-done.1
  46.1 0.6 route_partner.1
  46.8 1.5 %collective-permute-start.10 = (bf16[64,2048]{1,0:T(8,128)(2,1)S(1)}, bf16[64,2048]{1,0:T(8,128)(2,1)S(1)}, u32[]{:S(2)}, u32[]{:S(2)}) collective-permute-start(bf16[64,2048]{1,0:T(8,128)(2,1)S(1)} %get-tuple-element.37), channel_id=1, source_target_pairs={{0,8},{4,12},{8,0},{12,4},{16,24},{20,28},{24,16},{28,20},{1,9},{5... | collective-permute-start | bytes 786440 | tf_op jit(solution)/shard_map/ppermute | solution.py:621
  48.3 1.5 %collective-permute-start.9 = (bf16[64,2048]{1,0:T(8,128)(2,1)S(1)}, bf16[64,2048]{1,0:T(8,128)(2,1)S(1)}, u32[]{:S(2)}, u32[]{:S(2)}) collective-permute-start(bf16[64,2048]{1,0:T(8,128)(2,1)S(1)} %get-tuple-element.36), channel_id=1, source_target_pairs={{0,16},{4,20},{8,24},{12,28},{16,0},{20,4},{24,8},{28,12},{1,17},{... | collective-permute-start | bytes 786440 | tf_op jit(solution)/shard_map/ppermute | solution.py:620
  49.8 0.4 collective-permute-done.5.refs_0_
  50.2 5.2 %collective-permute-done.6.refs_1_ = bf16[32,2048]{1,0:T(8,128)(2,1)S(1)} collective-permute-done((bf16[32,2048]{1,0:T(8,128)(2,1)}, bf16[32,2048]{1,0:T(8,128)(2,1)S(1)}, u32[]{:S(2)}, u32[]{:S(2)}) %collective-permute-start.6) | collective-permute-done | bytes 131104 | tf_op jit(solution)/shard_map/ppermute | solution.py:457
  55.4 0.0 collective-permute-done.7.refs_2_
  55.4 0.0 collective-permute-done.10.refs_10_
  55.4 0.5 collective-permute-done.9.refs_9_
  55.9 1.5 %couple.1 = (bf16[128,2048]{1,0:T(8,128)(2,1)S(1)}, bf16[2,64,64]{2,1,0:T(8,128)(2,1)S(1)}) custom-call(s32[1]{0:T(128)} %bitcast.me_ref, s32[8]{0:T(128)S(1)} %copy-done.1, s32[1]{0:T(128)} %bitcast.1.i_ref, bf16[32,2048]{1,0:T(8,128)(2,1)S(1)} %collective-permute-done.5.refs_0_, bf16[32,2048]{1,0:T(8,128)(2,1)S(1)} %collective-permute-done.6.refs_1_, ...), custom_call_target="tpu_custom_call" | custom-call | tf_op jit(solution)/shard_map/couple/pallas_call | solution.py:636
  57.4 2.6 %collective-permute-start.11 = (bf16[2,64,64]{2,1,0:T(8,128)(2,1)S(1)}, bf16[2,64,64]{2,1,0:T(8,128)(2,1)S(1)}, u32[]{:S(2)}, u32[]{:S(2)}) collective-permute-start(bf16[2,64,64]{2,1,0:T(8,128)(2,1)S(1)} %get-tuple-element.39), channel_id=1, source_target_pairs={{0,3},{1,2},{2,1},{3,0},{4,7},{5,6},{6,5},{7,4},{8,11},{9,10},{10,... | collective-permute-start | bytes 49160 | tf_op jit(solution)/shard_map/ppermute | solution.py:662
  60.0 0.0 collective-permute-start.12
  60.0 1.9 %collective-permute-start.13 = (bf16[2,64,64]{2,1,0:T(8,128)(2,1)S(1)}, bf16[2,64,64]{2,1,0:T(8,128)(2,1)S(1)}, u32[]{:S(2)}, u32[]{:S(2)}) collective-permute-start(bf16[2,64,64]{2,1,0:T(8,128)(2,1)S(1)} %get-tuple-element.39), channel_id=1, source_target_pairs={{0,1},{1,0},{2,3},{3,2},{4,5},{5,4},{6,7},{7,6},{8,9},{9,8},{10,11... | collective-permute-start | bytes 49160 | tf_op jit(solution)/shard_map/ppermute | solution.py:662
  61.8 2.1 %unsort.1 = bf16[128,2048]{1,0:T(8,128)(2,1)} custom-call(bf16[128,2048]{1,0:T(8,128)(2,1)S(1)} %get-tuple-element.38.y_ref, s32[1,2048]{1,0:T(1,128)S(1)} %get-tuple-element.21.rank_ref), custom_call_target="tpu_custom_call" | custom-call | flops 1000000000 | bytes 10000000 | tf_op jit(solution)/shard_map/unsort/pallas_call | solution.py:663
  63.9 0.0 collective-permute-done.11
  63.9 0.8 %collective-permute-done.12 = bf16[2,64,64]{2,1,0:T(8,128)(2,1)S(1)} collective-permute-done((bf16[2,64,64]{2,1,0:T(8,128)(2,1)S(1)}, bf16[2,64,64]{2,1,0:T(8,128)(2,1)S(1)}, u32[]{:S(2)}, u32[]{:S(2)}) %collective-permute-start.12) | collective-permute-done | bytes 16416 | tf_op jit(solution)/shard_map/ppermute | solution.py:662
  64.8 0.0 collective-permute-done.13
  64.8 0.7 %multiply_bitcast_fusion = f32[2,1,64,64]{3,2,1,0:T(8,128)} fusion(bf16[2,64,64]{2,1,0:T(8,128)(2,1)S(1)} %collective-permute-done.11, bf16[2,64,64]{2,1,0:T(8,128)(2,1)S(1)} %collective-permute-done.12, bf16[2,64,64]{2,1,0:T(8,128)(2,1)S(1)} %collective-permute-done.13, bf16[2,64,64]{2,1,0:T(8,128)(2,1)S(1)} %get-tuple-element.39, pred[]{:T(512)S(6)} %eq.47, ...), kind=kLoop, calls=%fused_computation | loop fusion | flops 163840 | bytes 98316
  (2 shorter events, 0.0 us)
Async XLA Ops:
  0.6 0.7 %copy-start.3 = (s32[2048]{0:T(1024)S(1)}, s32[2048]{0:T(1024)}, u32[]{:S(2)}) copy-start(s32[2048]{0:T(1024)} %param.7) | copy-start | bytes 24580
  1.3 2.2 %copy-start = (bf16[2,1,64,2048]{3,2,1,0:T(8,128)(2,1)S(1)}, bf16[2,1,64,2048]{3,2,1,0:T(8,128)(2,1)}, u32[]{:S(2)}) copy-start(bf16[2,1,64,2048]{3,2,1,0:T(8,128)(2,1)} %param.6) | copy-start | bytes 1572868
  1.3 12.5 %copy-start.2 = (f32[64,64,128]{2,1,0:T(8,128)S(1)}, f32[64,64,128]{2,1,0:T(8,128)}, u32[]{:S(2)}) copy-start(f32[64,64,128]{2,1,0:T(8,128)} %param.9) | copy-start | bytes 6291460
  1.3 12.5 %copy-start.4 = (bf16[2,128,128]{2,1,0:T(8,128)(2,1)S(1)}, bf16[2,128,128]{2,1,0:T(8,128)(2,1)}, u32[]{:S(2)}) copy-start(bf16[2,128,128]{2,1,0:T(8,128)(2,1)} %constant.23.clone.wz_ref) | copy-start | bytes 196612
  1.3 12.5 %copy-start.5 = (bf16[64,256]{1,0:T(8,128)(2,1)S(1)}, bf16[64,256]{1,0:T(8,128)(2,1)}, u32[]{:S(2)}) copy-start(bf16[64,256]{1,0:T(8,128)(2,1)} %constant.22.clone.cs_ref) | copy-start | bytes 98308
  4.9 10.7 %collective-permute-start = (bf16[32,2304]{1,0:T(8,128)(2,1)S(1)}, bf16[32,2304]{1,0:T(8,128)(2,1)S(1)}, u32[]{:S(2)}, u32[]{:S(2)}) collective-permute-start(bf16[32,2304]{1,0:T(8,128)(2,1)S(1)} %get-tuple-element.23), channel_id=1, source_target_pairs={{0,3},{1,2},{2,1},{3,0},{4,7},{5,6},{6,5},{7,4},{8,11},{9,10},{10,... | collective-permute-start | bytes 442376 | tf_op jit(solution)/shard_map/ppermute | solution.py:457
  10.0 12.5 %collective-permute-start.1 = (bf16[32,2304]{1,0:T(8,128)(2,1)S(1)}, bf16[32,2304]{1,0:T(8,128)(2,1)S(1)}, u32[]{:S(2)}, u32[]{:S(2)}) collective-permute-start(bf16[32,2304]{1,0:T(8,128)(2,1)S(1)} %get-tuple-element.24), channel_id=1, source_target_pairs={{0,2},{1,3},{2,0},{3,1},{4,6},{5,7},{6,4},{7,5},{8,10},{9,11},{10,... | collective-permute-start | bytes 442376 | tf_op jit(solution)/shard_map/ppermute | solution.py:457
  10.0 12.5 %collective-permute-start.2 = (bf16[32,2304]{1,0:T(8,128)(2,1)S(1)}, bf16[32,2304]{1,0:T(8,128)(2,1)S(1)}, u32[]{:S(2)}, u32[]{:S(2)}) collective-permute-start(bf16[32,2304]{1,0:T(8,128)(2,1)S(1)} %get-tuple-element.25), channel_id=1, source_target_pairs={{0,1},{1,0},{2,3},{3,2},{4,5},{5,4},{6,7},{7,6},{8,9},{9,8},{10,11... | collective-permute-start | bytes 442376 | tf_op jit(solution)/shard_map/ppermute | solution.py:457
  10.7 11.8 %collective-permute-start.3 = (bf16[64,2048]{1,0:T(8,128)(2,1)S(1)}, bf16[64,2048]{1,0:T(8,128)(2,1)S(1)}, u32[]{:S(2)}, u32[]{:S(2)}) collective-permute-start(bf16[64,2048]{1,0:T(8,128)(2,1)S(1)} %get-tuple-element.30.re_ref.own_re.refs_4_), channel_id=1, source_target_pairs={{0,8},{4,12},{8,0},{12,4},{16,24},{20,28},{24,16},{28,20},{1,9},{5... | collective-permute-start | bytes 786440 | tf_op jit(solution)/shard_map/ppermute | solution.py:526
  12.3 10.2 %collective-permute-start.4 = (bf16[64,2048]{1,0:T(8,128)(2,1)S(1)}, bf16[64,2048]{1,0:T(8,128)(2,1)S(1)}, u32[]{:S(2)}, u32[]{:S(2)}) collective-permute-start(bf16[64,2048]{1,0:T(8,128)(2,1)S(1)} %get-tuple-element.31.im_ref.own_im.refs_5_), channel_id=1, source_target_pairs={{0,16},{4,20},{8,24},{12,28},{16,0},{20,4},{24,8},{28,12},{1,17},{... | collective-permute-start | bytes 786440 | tf_op jit(solution)/shard_map/ppermute | solution.py:527
  22.6 23.5 %collective-permute-start.8 = (bf16[256,2048]{1,0:T(8,128)(2,1)S(1)}, bf16[256,2048]{1,0:T(8,128)(2,1)S(1)}, u32[]{:S(2)}, u32[]{:S(2)}) collective-permute-start(bf16[256,2048]{1,0:T(8,128)(2,1)S(1)} %stack.1), channel_id=1, source_target_pairs={{0,4},{4,0},{8,12},{12,8},{16,20},{20,16},{24,28},{28,24},{1,5},{5... | collective-permute-start | bytes 3145736 | tf_op jit(solution)/shard_map/ppermute | solution.py:536
  22.7 23.5 %copy-start.1 = (s32[8]{0:T(128)S(1)}, s32[8]{0:T(128)}, u32[]{:S(2)}) copy-start(s32[8]{0:T(128)} %order_ref.3) | copy-start | bytes 100
  41.7 8.5 %collective-permute-start.5 = (bf16[32,2048]{1,0:T(8,128)(2,1)}, bf16[32,2048]{1,0:T(8,128)(2,1)S(1)}, u32[]{:S(2)}, u32[]{:S(2)}) collective-permute-start(bf16[32,2048]{1,0:T(8,128)(2,1)} %get-tuple-element.32), channel_id=1, source_target_pairs={{0,3},{1,2},{2,1},{3,0},{4,7},{5,6},{6,5},{7,4},{8,11},{9,10},{10,... | collective-permute-start | bytes 393224 | tf_op jit(solution)/shard_map/ppermute | solution.py:457
  44.2 11.1 %collective-permute-start.6 = (bf16[32,2048]{1,0:T(8,128)(2,1)}, bf16[32,2048]{1,0:T(8,128)(2,1)S(1)}, u32[]{:S(2)}, u32[]{:S(2)}) collective-permute-start(bf16[32,2048]{1,0:T(8,128)(2,1)} %get-tuple-element.33), channel_id=1, source_target_pairs={{0,2},{1,3},{2,0},{3,1},{4,6},{5,7},{6,4},{7,5},{8,10},{9,11},{10,... | collective-permute-start | bytes 393224 | tf_op jit(solution)/shard_map/ppermute | solution.py:457
  44.2 11.1 %collective-permute-start.7 = (bf16[32,2048]{1,0:T(8,128)(2,1)}, bf16[32,2048]{1,0:T(8,128)(2,1)}, u32[]{:S(2)}, u32[]{:S(2)}) collective-permute-start(bf16[32,2048]{1,0:T(8,128)(2,1)} %get-tuple-element.34), channel_id=1, source_target_pairs={{0,1},{1,0},{2,3},{3,2},{4,5},{5,4},{6,7},{7,6},{8,9},{9,8},{10,11... | collective-permute-start | bytes 393224 | tf_op jit(solution)/shard_map/ppermute | solution.py:457
  46.8 8.6 %collective-permute-start.10 = (bf16[64,2048]{1,0:T(8,128)(2,1)S(1)}, bf16[64,2048]{1,0:T(8,128)(2,1)S(1)}, u32[]{:S(2)}, u32[]{:S(2)}) collective-permute-start(bf16[64,2048]{1,0:T(8,128)(2,1)S(1)} %get-tuple-element.37), channel_id=1, source_target_pairs={{0,8},{4,12},{8,0},{12,4},{16,24},{20,28},{24,16},{28,20},{1,9},{5... | collective-permute-start | bytes 786440 | tf_op jit(solution)/shard_map/ppermute | solution.py:621
  48.3 7.6 %collective-permute-start.9 = (bf16[64,2048]{1,0:T(8,128)(2,1)S(1)}, bf16[64,2048]{1,0:T(8,128)(2,1)S(1)}, u32[]{:S(2)}, u32[]{:S(2)}) collective-permute-start(bf16[64,2048]{1,0:T(8,128)(2,1)S(1)} %get-tuple-element.36), channel_id=1, source_target_pairs={{0,16},{4,20},{8,24},{12,28},{16,0},{20,4},{24,8},{28,12},{1,17},{... | collective-permute-start | bytes 786440 | tf_op jit(solution)/shard_map/ppermute | solution.py:620
  57.4 6.5 %collective-permute-start.11 = (bf16[2,64,64]{2,1,0:T(8,128)(2,1)S(1)}, bf16[2,64,64]{2,1,0:T(8,128)(2,1)S(1)}, u32[]{:S(2)}, u32[]{:S(2)}) collective-permute-start(bf16[2,64,64]{2,1,0:T(8,128)(2,1)S(1)} %get-tuple-element.39), channel_id=1, source_target_pairs={{0,3},{1,2},{2,1},{3,0},{4,7},{5,6},{6,5},{7,4},{8,11},{9,10},{10,... | collective-permute-start | bytes 49160 | tf_op jit(solution)/shard_map/ppermute | solution.py:662
  60.0 4.8 %collective-permute-start.12 = (bf16[2,64,64]{2,1,0:T(8,128)(2,1)S(1)}, bf16[2,64,64]{2,1,0:T(8,128)(2,1)S(1)}, u32[]{:S(2)}, u32[]{:S(2)}) collective-permute-start(bf16[2,64,64]{2,1,0:T(8,128)(2,1)S(1)} %get-tuple-element.39), channel_id=1, source_target_pairs={{0,2},{1,3},{2,0},{3,1},{4,6},{5,7},{6,4},{7,5},{8,10},{9,11},{10,... | collective-permute-start | bytes 49160 | tf_op jit(solution)/shard_map/ppermute | solution.py:662
  60.0 4.8 %collective-permute-start.13 = (bf16[2,64,64]{2,1,0:T(8,128)(2,1)S(1)}, bf16[2,64,64]{2,1,0:T(8,128)(2,1)S(1)}, u32[]{:S(2)}, u32[]{:S(2)}) collective-permute-start(bf16[2,64,64]{2,1,0:T(8,128)(2,1)S(1)} %get-tuple-element.39), channel_id=1, source_target_pairs={{0,1},{1,0},{2,3},{3,2},{4,5},{5,4},{6,7},{7,6},{8,9},{9,8},{10,11... | collective-permute-start | bytes 49160 | tf_op jit(solution)/shard_map/ppermute | solution.py:662
